TPU v7x, 32 devices: a whole 2x2x4 slice. The times are simulated.
32 devices in a mesh: ctx: 8 (over z, core), dp: 4 (over y, x).
Axes of the slice: x: 2, y: 2, z: 4, core: 2. Of those that a mesh axis runs over, the one named last changes fastest.
Arguments:
- query: bfloat16 [8, 8, 64, 2048], P('ctx', 'dp'), parts along dimension 1, may hold values from -21 to 21
- key: bfloat16 [8, 8, 64, 256], P('ctx', 'dp'), parts along dimension 1, may hold values from -21 to 21
- value: bfloat16 [8, 8, 64, 256], P('ctx', 'dp'), parts along dimension 1, may hold values from -6 to 6
- out_grad: bfloat16 [8, 8, 64, 2048], P('ctx', 'dp'), parts along dimension 1, may hold values from -6 to 6
- attn_out: bfloat16 [8, 8, 64, 2048], P('ctx', 'dp'), parts along dimension 1, may hold values from -4 to 4
- doc_start: int32 [8, 8, 64], P('ctx', 'dp'), parts along dimension 1, may hold values from 0 to 1023, as said below
Outputs:
- q_grad: bfloat16 [8, 8, 64, 2048], P('ctx', 'dp'), parts along dimension 1
- k_grad: bfloat16 [8, 8, 64, 256], P('ctx', 'dp'), parts along dimension 1
- v_grad: bfloat16 [8, 8, 64, 256], P('ctx', 'dp'), parts along dimension 1
There are 4 independent parts, one for each index of `dp`. A program takes and returns all parts, laid end to end along the dimension named above; each array names one. Nothing has to cross between parts.
Inputs may be any that keep to these rules, and one draw needn't show every extreme that they name: Documents are runs of consecutive positions and doc_start(i) is the first position of the document that holds token i, so doc_start never falls along the sequence and doc_start(i) <= i.
All inputs are finite; a program needn't handle non-finite values.
Results may differ from a plain program's by a relative error of at most 0.0085.
Values may be sent and summed in bfloat16 or wider, within the bound.
No kernel may reach another device: no remote copies, remote signals or barrier semaphores. Data moves between devices by JAX's collectives and lax.ppermute only.
A program may use at most 64 MiB of HBM per device.

v0:
```python
import jax
import jax.numpy as jnp
from jax import lax
from jax.sharding import PartitionSpec as P

HEAD_SIZE = 128
STEPS = 4


def with_halo(block, sides, width):
    for axis, dim in sides:
        count = lax.axis_size(axis)
        forward = [(i, i + 1) for i in range(count - 1)]
        backward = [(target, source) for source, target in forward]
        low = lax.ppermute(
            lax.slice_in_dim(block, block.shape[dim] - width, None, axis=dim), axis, forward
        )
        high = lax.ppermute(lax.slice_in_dim(block, 0, width, axis=dim), axis, backward)
        block = jnp.concatenate([low, block, high], axis=dim)
    return block


def shards(query, key, value, out_grad, attn_out, doc_start):
    block_length = query.shape[2]
    heads = query.shape[3] // HEAD_SIZE
    kv_heads = key.shape[3] // HEAD_SIZE
    group = heads // kv_heads
    window_width = kv_heads * HEAD_SIZE
    scale = HEAD_SIZE ** (-0.5)
    ctx_count = lax.axis_size("ctx")
    ctx_index = lax.axis_index("ctx")
    is_last = ctx_index == ctx_count - 1
    window = STEPS * block_length
    total_length = (STEPS + 1) * block_length
    block_ids = jnp.stack([ctx_index, 2 * ctx_count - 1 - ctx_index])
    offsets = jnp.arange(block_length, dtype=jnp.int32)
    q_pos = block_ids[:, None] * block_length + offsets[None, :]
    starts = doc_start[0]
    query_matrix = query[0].reshape(2, block_length, kv_heads, group, HEAD_SIZE)
    grads_out = out_grad[0].reshape(2, block_length, kv_heads, group, HEAD_SIZE)
    output_rows = attn_out[0].reshape(2, block_length, kv_heads, group, HEAD_SIZE)
    current = jnp.concatenate([key[0], value[0]], axis=-1)
    blocks = [current]
    for hop_index in range(STEPS):
        padded = with_halo(
            jnp.concatenate([current[1], current[0]], axis=0), (("ctx", 0),), block_length
        )
        upper_half = jnp.where(is_last, current[0], padded[3 * block_length :])
        current = jnp.stack([padded[:block_length], upper_half])
        blocks.append(current)
    stored = jnp.concatenate(blocks[::-1], axis=1)
    keys_all = stored[..., :window_width].reshape(2, total_length, kv_heads, HEAD_SIZE)
    values_all = stored[..., window_width:].reshape(2, total_length, kv_heads, HEAD_SIZE)
    k_pos = (block_ids[:, None] - STEPS) * block_length + jnp.arange(total_length, dtype=jnp.int32)[
        None, :
    ]
    visible = (
        (k_pos[:, None, :] <= q_pos[:, :, None])
        & (q_pos[:, :, None] - k_pos[:, None, :] < window)
        & (k_pos[:, None, :] >= starts[:, :, None])
    )
    scores = (
        jnp.einsum("hqkgd,hpkd->hkgqp", query_matrix, keys_all, preferred_element_type=jnp.float32)
        * scale
    )
    scores = jnp.where(visible[:, None, None], scores, -jnp.inf)
    row_max = jnp.max(scores, axis=-1, keepdims=True)
    log_norm = row_max + jnp.log(jnp.sum(jnp.exp(scores - row_max), axis=-1, keepdims=True))
    probs = jnp.exp(scores - log_norm)
    probs_low = probs.astype(jnp.bfloat16)
    delta = jnp.transpose(
        jnp.sum(grads_out.astype(jnp.float32) * output_rows.astype(jnp.float32), axis=-1),
        (0, 2, 3, 1),
    )
    dprobs = jnp.einsum(
        "hqkgd,hpkd->hkgqp", grads_out, values_all, preferred_element_type=jnp.float32
    )
    dscores = (probs * (dprobs - delta[..., None])).astype(jnp.bfloat16)
    q_grad = (
        jnp.einsum("hkgqp,hpkd->hqkgd", dscores, keys_all, preferred_element_type=jnp.float32)
        * scale
    )
    q_out = q_grad.astype(jnp.bfloat16).reshape(1, 2, block_length, heads * HEAD_SIZE)
    k_part = (
        jnp.einsum("hkgqp,hqkgd->hpkd", dscores, query_matrix, preferred_element_type=jnp.float32)
        * scale
    )
    v_part = jnp.einsum(
        "hkgqp,hqkgd->hpkd", probs_low, grads_out, preferred_element_type=jnp.float32
    )
    partial_value = jnp.concatenate(
        [
            k_part.reshape(2, total_length, window_width),
            v_part.reshape(2, total_length, window_width),
        ],
        axis=-1,
    )
    partial_value = partial_value.reshape(2, STEPS + 1, block_length, 2 * window_width)
    summed = partial_value[:, 0]
    for hop_index in range(1, STEPS + 1):
        padded = with_halo(
            jnp.concatenate([summed[0], summed[1]], axis=0).astype(jnp.bfloat16),
            (("ctx", 0),),
            block_length,
        ).astype(jnp.float32)
        lower_half = jnp.where(is_last, summed[1], padded[3 * block_length :])
        summed = jnp.stack([lower_half, padded[:block_length]]) + partial_value[:, hop_index]
    k_out = (
        summed[..., :window_width].astype(jnp.bfloat16).reshape(1, 2, block_length, window_width)
    )
    v_out = (
        summed[..., window_width:].astype(jnp.bfloat16).reshape(1, 2, block_length, window_width)
    )
    return (q_out, k_out, v_out)


def solution(mesh):
    placed = (
        P("ctx", "dp", None, None),
        P("ctx", "dp", None, None),
        P("ctx", "dp", None, None),
        P("ctx", "dp", None, None),
        P("ctx", "dp", None, None),
        P("ctx", "dp", None),
    )
    return jax.shard_map(
        shards,
        mesh=mesh,
        in_specs=placed,
        out_specs=(
            P("ctx", "dp", None, None),
            P("ctx", "dp", None, None),
            P("ctx", "dp", None, None),
        ),
        check_vma=False,
    )
```

profile of v0, /device:TPU:13, one launch (start us, length us, event | category | flops | bytes accessed | tf_op | source)
XLA Modules:
  0.0 83.3 jit_solution(15425770405467710937)
XLA Ops:
  0.6 0.8 %fusion.48 = bf16[64,512]{1,0:T(8,128)(2,1)S(1)} fusion(bf16[2,64,256]{2,1,0:T(8,128)(2,1)} %bitcast.160, bf16[2,64,256]{2,1,0:T(8,128)(2,1)} %bitcast.163), kind=kLoop, calls=%fused_computation.82 | loop fusion | flops 131072 | bytes 196608 | tf_op jit(solution)/shard_map/squeeze | solution.py:46
  1.5 2.6 %collective-permute-start.4 = (bf16[64,512]{1,0:T(8,128)(2,1)S(1)}, bf16[64,512]{1,0:T(8,128)(2,1)S(1)}, u32[]{:S(2)}, u32[]{:S(2)}) collective-permute-start(bf16[64,512]{1,0:T(8,128)(2,1)S(1)} %fusion.48), channel_id=1, source_target_pairs={{4,0},{8,4},{12,8},{16,12},{20,16},{24,20},{28,24},{5,1},{9,5},{13... | collective-permute-start | bytes 196616 | tf_op jit(solution)/shard_map/ppermute | solution.py:18
  4.1 0.1 add_multiply_fusion
  4.2 3.0 %collective-permute-done.4 = bf16[64,512]{1,0:T(8,128)(2,1)S(1)} collective-permute-done((bf16[64,512]{1,0:T(8,128)(2,1)S(1)}, bf16[64,512]{1,0:T(8,128)(2,1)S(1)}, u32[]{:S(2)}, u32[]{:S(2)}) %collective-permute-start.4) | collective-permute-done | bytes 65568 | tf_op jit(solution)/shard_map/ppermute | solution.py:18
  7.2 0.8 broadcast_select_fusion.2
  8.0 1.9 %collective-permute-start = (bf16[64,512]{1,0:T(8,128)(2,1)S(1)}, bf16[64,512]{1,0:T(8,128)(2,1)S(1)}, u32[]{:S(2)}, u32[]{:S(2)}) collective-permute-start(bf16[64,512]{1,0:T(8,128)(2,1)S(1)} %get-tuple-element.4), channel_id=1, source_target_pairs={{0,4},{4,8},{8,12},{12,16},{16,20},{20,24},{24,28},{1,5},{5,9},{9,... | collective-permute-start | bytes 196616 | tf_op jit(solution)/shard_map/ppermute | solution.py:15
  9.9 2.4 %collective-permute-start.5 = (bf16[64,512]{1,0:T(8,128)(2,1)S(1)}, bf16[64,512]{1,0:T(8,128)(2,1)S(1)}, u32[]{:S(2)}, u32[]{:S(2)}) collective-permute-start(bf16[64,512]{1,0:T(8,128)(2,1)S(1)} %get-tuple-element.3), channel_id=1, source_target_pairs={{4,0},{8,4},{12,8},{16,12},{20,16},{24,20},{28,24},{5,1},{9,5},{13... | collective-permute-start | bytes 196616 | tf_op jit(solution)/shard_map/ppermute | solution.py:18
  12.4 3.1 %collective-permute-done.5 = bf16[64,512]{1,0:T(8,128)(2,1)S(1)} collective-permute-done((bf16[64,512]{1,0:T(8,128)(2,1)S(1)}, bf16[64,512]{1,0:T(8,128)(2,1)S(1)}, u32[]{:S(2)}, u32[]{:S(2)}) %collective-permute-start.5) | collective-permute-done | bytes 65568 | tf_op jit(solution)/shard_map/ppermute | solution.py:18
  15.5 1.9 %collective-permute-start.6 = (bf16[64,512]{1,0:T(8,128)(2,1)S(1)}, bf16[64,512]{1,0:T(8,128)(2,1)S(1)}, u32[]{:S(2)}, u32[]{:S(2)}) collective-permute-start(bf16[64,512]{1,0:T(8,128)(2,1)S(1)} %broadcast_select_fusion.1), channel_id=1, source_target_pairs={{4,0},{8,4},{12,8},{16,12},{20,16},{24,20},{28,24},{5,1},{9,5},{13... | collective-permute-start | bytes 196616 | tf_op jit(solution)/shard_map/ppermute | solution.py:18
  17.4 3.6 %collective-permute-start.1 = (bf16[64,512]{1,0:T(8,128)(2,1)S(1)}, bf16[64,512]{1,0:T(8,128)(2,1)S(1)}, u32[]{:S(2)}, u32[]{:S(2)}) collective-permute-start(bf16[64,512]{1,0:T(8,128)(2,1)S(1)} %collective-permute-done), channel_id=1, source_target_pairs={{0,4},{4,8},{8,12},{12,16},{16,20},{20,24},{24,28},{1,5},{5,9},{9,... | collective-permute-start | bytes 196616 | tf_op jit(solution)/shard_map/ppermute | solution.py:15
  21.1 0.8 fusion.31
  21.9 1.2 %copy.58 = f32[16,8,16,128]{3,2,1,0:T(8,128)S(1)} copy(bf16[16,8,16,128]{3,1,2,0:T(8,128)(2,1)} %bitcast.166) | data formatting | bytes 1572864
  23.1 1.1 %copy.57 = bf16[16,8,16,128]{3,2,1,0:T(8,128)(2,1)S(1)} copy(bf16[16,8,16,128]{3,1,2,0:T(8,128)(2,1)} %bitcast.167) | data formatting | bytes 1048576
  24.3 1.9 %collective-permute-start.7 = (bf16[64,512]{1,0:T(8,128)(2,1)S(1)}, bf16[64,512]{1,0:T(8,128)(2,1)S(1)}, u32[]{:S(2)}, u32[]{:S(2)}) collective-permute-start(bf16[64,512]{1,0:T(8,128)(2,1)S(1)} %broadcast_select_fusion), channel_id=1, source_target_pairs={{4,0},{8,4},{12,8},{16,12},{20,16},{24,20},{28,24},{5,1},{9,5},{13... | collective-permute-start | bytes 196616 | tf_op jit(solution)/shard_map/ppermute | solution.py:18
  26.2 3.6 %collective-permute-start.2 = (bf16[64,512]{1,0:T(8,128)(2,1)S(1)}, bf16[64,512]{1,0:T(8,128)(2,1)S(1)}, u32[]{:S(2)}, u32[]{:S(2)}) collective-permute-start(bf16[64,512]{1,0:T(8,128)(2,1)S(1)} %collective-permute-done.1), channel_id=1, source_target_pairs={{0,4},{4,8},{8,12},{12,16},{16,20},{20,24},{24,28},{1,5},{5,9},{9,... | collective-permute-start | bytes 196616 | tf_op jit(solution)/shard_map/ppermute | solution.py:15
  29.9 0.5 multiply_reduce_fusion
  30.4 0.9 %copy.56 = bf16[16,8,16,128]{3,2,1,0:T(8,128)(2,1)} copy(bf16[16,8,16,128]{3,1,2,0:T(8,128)(2,1)S(1)} %bitcast.168) | data formatting | bytes 1048576
  31.4 4.1 %collective-permute-start.3 = (bf16[64,512]{1,0:T(8,128)(2,1)S(1)}, bf16[64,512]{1,0:T(8,128)(2,1)S(1)}, u32[]{:S(2)}, u32[]{:S(2)}) collective-permute-start(bf16[64,512]{1,0:T(8,128)(2,1)S(1)} %collective-permute-done.2), channel_id=1, source_target_pairs={{0,4},{4,8},{8,12},{12,16},{16,20},{20,24},{24,28},{1,5},{5,9},{9,... | collective-permute-start | bytes 196616 | tf_op jit(solution)/shard_map/ppermute | solution.py:15
  35.5 1.3 %collective-permute-done.3 = bf16[64,512]{1,0:T(8,128)(2,1)S(1)} collective-permute-done((bf16[64,512]{1,0:T(8,128)(2,1)S(1)}, bf16[64,512]{1,0:T(8,128)(2,1)S(1)}, u32[]{:S(2)}, u32[]{:S(2)}) %collective-permute-start.3) | collective-permute-done | bytes 65568 | tf_op jit(solution)/shard_map/ppermute | solution.py:15
  36.9 0.8 fusion.52
  37.7 0.1 reshape.126
  37.8 1.8 %fusion.3 = (f32[2,2,8,64]{3,2,1,0:T(8,128)S(1)}, f32[2,2,320,64,8]{2,3,4,1,0:T(8,128)S(1)}) fusion(pred[2,64,320]{2,1,0:T(8,128)(4,1)S(1)} %fusion.31, bf16[2,64,2,8,128]{4,3,2,1,0:T(8,128)(2,1)} %bitcast.169, bf16[2,320,2,128,1]{3,2,1,0,4:T(2,128)(2,1)S(1)} %bitcast.158), kind=kOutput, calls=%fused_computation.7 | convolution fusion | flops 169736192 | bytes 3522560 | tf_op jit(solution)/shard_map/hqkgd,hpkd->hkgqp/dot_general | solution.py:63
  39.6 1.1 %exponential_reduce_fusion = f32[2,2,8,64]{3,2,1,0:T(8,128)S(1)} fusion(f32[2,2,320,64,8]{2,3,4,1,0:T(8,128)S(1)} %get-tuple-element.18, f32[2,2,8,64]{3,2,1,0:T(8,128)S(1)} %get-tuple-element.17, pred[2,64,320]{2,1,0:T(8,128)(4,1)S(1)} %fusion.31), kind=kLoop, calls=%fused_computation.5 | loop fusion | flops 2619392 | bytes 2678784 | tf_op jit(solution)/shard_map/reduce_sum | solution.py:68
  40.7 1.8 %reshape.127 = bf16[2,320,2,128]{3,2,1,0:T(2,128)(2,1)} reshape(bf16[2,320,256]{2,1,0:T(8,128)(2,1)} %get-tuple-element.7) | data formatting | bytes 655360 | tf_op jit(solution)/shard_map/reshape | solution.py:53
  42.4 3.2 %fusion.11 = f32[2,320,2,128]{3,1,2,0:T(8,128)} fusion(f32[2,2,320,64,8]{2,3,4,1,0:T(8,128)S(1)} %get-tuple-element.18, f32[2,2,8,64]{3,2,1,0:T(8,128)S(1)} %log_add_fusion, pred[2,64,320]{2,1,0:T(8,128)(4,1)S(1)} %fusion.31, bf16[2,64,2,8,128]{4,3,2,1,0:T(8,128)(2,1)} %bitcast.156), kind=kOutput, calls=%fused_computation.15 | convolution fusion | flops 170393600 | bytes 3850240 | tf_op jit(solution)/shard_map/hkgqp,hqkgd->hpkd/dot_general | solution.py:88
  45.6 1.1 %fusion.1 = bf16[2,2,8,64,320]{4,3,2,1,0:T(8,128)(2,1)S(1)} fusion(f32[2,2,320,64,8]{2,3,4,1,0:T(8,128)S(1)} %get-tuple-element.18, f32[2,2,8,64]{3,2,1,0:T(8,128)S(1)} %copy.32, f32[2,2,8,64]{3,2,1,0:T(8,128)S(1)} %log_add_fusion, pred[2,64,320]{2,1,0:T(8,128)(4,1)S(1)} %fusion.31, bf16[2,64,2,8,128]{4,3,2,1,0:T(8,128)(2,1)S(1)} %bitcast.157, ...), kind=kOutput, calls=%fused_computation.2 | convolution fusion | flops 171704320 | bytes 4841472 | tf_op jit(solution)/shard_map/hqkgd,hpkd->hkgqp/dot_general | solution.py:75
  46.8 0.7 fusion.15
  47.5 0.5 copy-done.2
  48.0 0.5 copy.36
  48.5 0.5 concatenate.48
  49.1 1.6 %copy.38 = f32[2,320,2,128]{3,2,1,0:T(2,128)S(1)} copy(f32[2,320,2,128]{3,1,2,0:T(8,128)} %fusion.11) | data formatting | bytes 1310720 | tf_op jit(solution)/shard_map/hkgqp,hqkgd->hpkd/transpose | solution.py:88
  50.7 0.5 concatenate.49
  51.2 0.1 constant_dynamic-update-slice_fusion
  51.4 3.2 %collective-permute-start.9 = (bf16[64,512]{1,0:T(8,128)(2,1)S(1)}, bf16[64,512]{1,0:T(8,128)(2,1)S(1)}, u32[]{:S(2)}, u32[]{:S(2)}) collective-permute-start(bf16[64,512]{1,0:T(8,128)(2,1)S(1)} %get-tuple-element.6), channel_id=1, source_target_pairs={{4,0},{8,4},{12,8},{16,12},{20,16},{24,20},{28,24},{5,1},{9,5},{13... | collective-permute-start | bytes 196616 | tf_op jit(solution)/shard_map/ppermute | solution.py:18
  54.6 3.1 %collective-permute-start.8 = (bf16[64,512]{1,0:T(8,128)(2,1)S(1)}, bf16[64,512]{1,0:T(8,128)(2,1)S(1)}, u32[]{:S(2)}, u32[]{:S(2)}) collective-permute-start(bf16[64,512]{1,0:T(8,128)(2,1)S(1)} %get-tuple-element.5), channel_id=1, source_target_pairs={{0,4},{4,8},{8,12},{12,16},{16,20},{20,24},{24,28},{1,5},{5,9},{9,... | collective-permute-start | bytes 196616 | tf_op jit(solution)/shard_map/ppermute | solution.py:15
  57.7 1.3 %collective-permute-done.8 = bf16[64,512]{1,0:T(8,128)(2,1)S(1)} collective-permute-done((bf16[64,512]{1,0:T(8,128)(2,1)S(1)}, bf16[64,512]{1,0:T(8,128)(2,1)S(1)}, u32[]{:S(2)}, u32[]{:S(2)}) %collective-permute-start.8) | collective-permute-done | bytes 65568 | tf_op jit(solution)/shard_map/ppermute | solution.py:15
  59.1 3.1 %collective-permute-start.11 = (bf16[64,512]{1,0:T(8,128)(2,1)S(1)}, bf16[64,512]{1,0:T(8,128)(2,1)S(1)}, u32[]{:S(2)}, u32[]{:S(2)}) collective-permute-start(bf16[64,512]{1,0:T(8,128)(2,1)S(1)} %get-tuple-element.14), channel_id=1, source_target_pairs={{4,0},{8,4},{12,8},{16,12},{20,16},{24,20},{28,24},{5,1},{9,5},{13... | collective-permute-start | bytes 196616 | tf_op jit(solution)/shard_map/ppermute | solution.py:18
  62.2 3.1 %collective-permute-start.10 = (bf16[64,512]{1,0:T(8,128)(2,1)S(1)}, bf16[64,512]{1,0:T(8,128)(2,1)S(1)}, u32[]{:S(2)}, u32[]{:S(2)}) collective-permute-start(bf16[64,512]{1,0:T(8,128)(2,1)S(1)} %get-tuple-element.13), channel_id=1, source_target_pairs={{0,4},{4,8},{8,12},{12,16},{16,20},{20,24},{24,28},{1,5},{5,9},{9,... | collective-permute-start | bytes 196616 | tf_op jit(solution)/shard_map/ppermute | solution.py:15
  65.3 1.3 %collective-permute-done.10 = bf16[64,512]{1,0:T(8,128)(2,1)S(1)} collective-permute-done((bf16[64,512]{1,0:T(8,128)(2,1)S(1)}, bf16[64,512]{1,0:T(8,128)(2,1)S(1)}, u32[]{:S(2)}, u32[]{:S(2)}) %collective-permute-start.10) | collective-permute-done | bytes 65568 | tf_op jit(solution)/shard_map/ppermute | solution.py:15
  66.7 3.1 %collective-permute-start.13 = (bf16[64,512]{1,0:T(8,128)(2,1)S(1)}, bf16[64,512]{1,0:T(8,128)(2,1)S(1)}, u32[]{:S(2)}, u32[]{:S(2)}) collective-permute-start(bf16[64,512]{1,0:T(8,128)(2,1)S(1)} %get-tuple-element.12), channel_id=1, source_target_pairs={{4,0},{8,4},{12,8},{16,12},{20,16},{24,20},{28,24},{5,1},{9,5},{13... | collective-permute-start | bytes 196616 | tf_op jit(solution)/shard_map/ppermute | solution.py:18
  69.8 3.1 %collective-permute-start.12 = (bf16[64,512]{1,0:T(8,128)(2,1)S(1)}, bf16[64,512]{1,0:T(8,128)(2,1)S(1)}, u32[]{:S(2)}, u32[]{:S(2)}) collective-permute-start(bf16[64,512]{1,0:T(8,128)(2,1)S(1)} %get-tuple-element.11), channel_id=1, source_target_pairs={{0,4},{4,8},{8,12},{12,16},{16,20},{20,24},{24,28},{1,5},{5,9},{9,... | collective-permute-start | bytes 196616 | tf_op jit(solution)/shard_map/ppermute | solution.py:15
  72.9 1.3 %collective-permute-done.12 = bf16[64,512]{1,0:T(8,128)(2,1)S(1)} collective-permute-done((bf16[64,512]{1,0:T(8,128)(2,1)S(1)}, bf16[64,512]{1,0:T(8,128)(2,1)S(1)}, u32[]{:S(2)}, u32[]{:S(2)}) %collective-permute-start.12) | collective-permute-done | bytes 65568 | tf_op jit(solution)/shard_map/ppermute | solution.py:15
  74.4 3.1 %collective-permute-start.15 = (bf16[64,512]{1,0:T(8,128)(2,1)S(1)}, bf16[64,512]{1,0:T(8,128)(2,1)S(1)}, u32[]{:S(2)}, u32[]{:S(2)}) collective-permute-start(bf16[64,512]{1,0:T(8,128)(2,1)S(1)} %get-tuple-element.10), channel_id=1, source_target_pairs={{4,0},{8,4},{12,8},{16,12},{20,16},{24,20},{28,24},{5,1},{9,5},{13... | collective-permute-start | bytes 196616 | tf_op jit(solution)/shard_map/ppermute | solution.py:18
  77.5 3.1 %collective-permute-start.14 = (bf16[64,512]{1,0:T(8,128)(2,1)S(1)}, bf16[64,512]{1,0:T(8,128)(2,1)S(1)}, u32[]{:S(2)}, u32[]{:S(2)}) collective-permute-start(bf16[64,512]{1,0:T(8,128)(2,1)S(1)} %get-tuple-element.9), channel_id=1, source_target_pairs={{0,4},{4,8},{8,12},{12,16},{16,20},{20,24},{24,28},{1,5},{5,9},{9,... | collective-permute-start | bytes 196616 | tf_op jit(solution)/shard_map/ppermute | solution.py:15
  80.6 0.6 fusion.16
  81.1 0.3 copy.34
  81.5 1.0 %reshape.128 = bf16[1,2,64,2048]{3,2,1,0:T(8,128)(2,1)} reshape(bf16[2,64,2,8,128]{4,3,2,1,0:T(8,128)(2,1)S(1)} %copy.34) | data formatting | bytes 1048576 | tf_op jit(solution)/shard_map/reshape | solution.py:83
  82.6 0.7 slice_bitcast_fusion.8
  (56 shorter events, 0.8 us)
Async XLA Ops:
  0.6 29.7 %copy-start.6 = (bf16[1,2,64,2048]{3,2,1,0:T(8,128)(2,1)S(1)}, bf16[1,2,64,2048]{3,2,1,0:T(8,128)(2,1)}, u32[]{:S(2)}) copy-start(bf16[1,2,64,2048]{3,2,1,0:T(8,128)(2,1)} %param.6) | copy-start | bytes 1572868
  1.5 5.7 %collective-permute-start.4 = (bf16[64,512]{1,0:T(8,128)(2,1)S(1)}, bf16[64,512]{1,0:T(8,128)(2,1)S(1)}, u32[]{:S(2)}, u32[]{:S(2)}) collective-permute-start(bf16[64,512]{1,0:T(8,128)(2,1)S(1)} %fusion.48), channel_id=1, source_target_pairs={{4,0},{8,4},{12,8},{16,12},{20,16},{24,20},{28,24},{5,1},{9,5},{13... | collective-permute-start | bytes 196616 | tf_op jit(solution)/shard_map/ppermute | solution.py:18
  8.0 4.4 %collective-permute-start = (bf16[64,512]{1,0:T(8,128)(2,1)S(1)}, bf16[64,512]{1,0:T(8,128)(2,1)S(1)}, u32[]{:S(2)}, u32[]{:S(2)}) collective-permute-start(bf16[64,512]{1,0:T(8,128)(2,1)S(1)} %get-tuple-element.4), channel_id=1, source_target_pairs={{0,4},{4,8},{8,12},{12,16},{16,20},{20,24},{24,28},{1,5},{5,9},{9,... | collective-permute-start | bytes 196616 | tf_op jit(solution)/shard_map/ppermute | solution.py:15
  9.9 5.6 %collective-permute-start.5 = (bf16[64,512]{1,0:T(8,128)(2,1)S(1)}, bf16[64,512]{1,0:T(8,128)(2,1)S(1)}, u32[]{:S(2)}, u32[]{:S(2)}) collective-permute-start(bf16[64,512]{1,0:T(8,128)(2,1)S(1)} %get-tuple-element.3), channel_id=1, source_target_pairs={{4,0},{8,4},{12,8},{16,12},{20,16},{24,20},{28,24},{5,1},{9,5},{13... | collective-permute-start | bytes 196616 | tf_op jit(solution)/shard_map/ppermute | solution.py:18
  15.5 8.8 %collective-permute-start.6 = (bf16[64,512]{1,0:T(8,128)(2,1)S(1)}, bf16[64,512]{1,0:T(8,128)(2,1)S(1)}, u32[]{:S(2)}, u32[]{:S(2)}) collective-permute-start(bf16[64,512]{1,0:T(8,128)(2,1)S(1)} %broadcast_select_fusion.1), channel_id=1, source_target_pairs={{4,0},{8,4},{12,8},{16,12},{20,16},{24,20},{28,24},{5,1},{9,5},{13... | collective-permute-start | bytes 196616 | tf_op jit(solution)/shard_map/ppermute | solution.py:18
  17.4 6.9 %collective-permute-start.1 = (bf16[64,512]{1,0:T(8,128)(2,1)S(1)}, bf16[64,512]{1,0:T(8,128)(2,1)S(1)}, u32[]{:S(2)}, u32[]{:S(2)}) collective-permute-start(bf16[64,512]{1,0:T(8,128)(2,1)S(1)} %collective-permute-done), channel_id=1, source_target_pairs={{0,4},{4,8},{8,12},{12,16},{16,20},{20,24},{24,28},{1,5},{5,9},{9,... | collective-permute-start | bytes 196616 | tf_op jit(solution)/shard_map/ppermute | solution.py:15
  21.9 15.0 %copy-start.4 = (bf16[1,2,64,256]{3,2,1,0:T(8,128)(2,1)S(1)}, bf16[1,2,64,256]{3,2,1,0:T(8,128)(2,1)}, u32[]{:S(2)}) copy-start(bf16[1,2,64,256]{3,2,1,0:T(8,128)(2,1)} %param.7) | copy-start | bytes 196612
  21.9 14.9 %copy-start.5 = (bf16[1,2,64,256]{3,2,1,0:T(8,128)(2,1)S(1)}, bf16[1,2,64,256]{3,2,1,0:T(8,128)(2,1)}, u32[]{:S(2)}) copy-start(bf16[1,2,64,256]{3,2,1,0:T(8,128)(2,1)} %param.8) | copy-start | bytes 196612
  24.3 6.1 %copy-start = (bf16[16,8,16,128]{3,2,1,0:T(8,128)(2,1)}, bf16[16,8,16,128]{3,2,1,0:T(8,128)(2,1)S(1)}, u32[]{:S(2)}) copy-start(bf16[16,8,16,128]{3,2,1,0:T(8,128)(2,1)S(1)} %copy.57) | copy-start | bytes 1572868
  24.3 11.2 %collective-permute-start.7 = (bf16[64,512]{1,0:T(8,128)(2,1)S(1)}, bf16[64,512]{1,0:T(8,128)(2,1)S(1)}, u32[]{:S(2)}, u32[]{:S(2)}) collective-permute-start(bf16[64,512]{1,0:T(8,128)(2,1)S(1)} %broadcast_select_fusion), channel_id=1, source_target_pairs={{4,0},{8,4},{12,8},{16,12},{20,16},{24,20},{28,24},{5,1},{9,5},{13... | collective-permute-start | bytes 196616 | tf_op jit(solution)/shard_map/ppermute | solution.py:18
  26.2 5.1 %collective-permute-start.2 = (bf16[64,512]{1,0:T(8,128)(2,1)S(1)}, bf16[64,512]{1,0:T(8,128)(2,1)S(1)}, u32[]{:S(2)}, u32[]{:S(2)}) collective-permute-start(bf16[64,512]{1,0:T(8,128)(2,1)S(1)} %collective-permute-done.1), channel_id=1, source_target_pairs={{0,4},{4,8},{8,12},{12,16},{16,20},{20,24},{24,28},{1,5},{5,9},{9,... | collective-permute-start | bytes 196616 | tf_op jit(solution)/shard_map/ppermute | solution.py:15
  31.4 5.4 %collective-permute-start.3 = (bf16[64,512]{1,0:T(8,128)(2,1)S(1)}, bf16[64,512]{1,0:T(8,128)(2,1)S(1)}, u32[]{:S(2)}, u32[]{:S(2)}) collective-permute-start(bf16[64,512]{1,0:T(8,128)(2,1)S(1)} %collective-permute-done.2), channel_id=1, source_target_pairs={{0,4},{4,8},{8,12},{12,16},{16,20},{20,24},{24,28},{1,5},{5,9},{9,... | collective-permute-start | bytes 196616 | tf_op jit(solution)/shard_map/ppermute | solution.py:15
  42.4 3.2 %copy-start.1 = (bf16[16,8,16,128]{3,2,1,0:T(8,128)(2,1)S(1)}, bf16[16,8,16,128]{3,2,1,0:T(8,128)(2,1)}, u32[]{:S(2)}) copy-start(bf16[16,8,16,128]{3,2,1,0:T(8,128)(2,1)} %copy-done) | copy-start | bytes 1572868
  42.4 3.2 %copy-start.8 = (bf16[2,320,2,128]{3,2,1,0:T(2,128)(2,1)S(1)}, bf16[2,320,2,128]{3,2,1,0:T(2,128)(2,1)}, u32[]{:S(2)}) copy-start(bf16[2,320,2,128]{3,2,1,0:T(2,128)(2,1)} %reshape.127) | copy-start | bytes 983044
  45.6 1.1 %copy-start.7 = (bf16[16,8,16,128]{3,2,1,0:T(8,128)(2,1)S(1)}, bf16[16,8,16,128]{3,2,1,0:T(8,128)(2,1)}, u32[]{:S(2)}) copy-start(bf16[16,8,16,128]{3,2,1,0:T(8,128)(2,1)} %copy.56) | copy-start | bytes 1572868
  46.8 1.2 %copy-start.2 = (bf16[2,2,8,64,320]{4,3,2,1,0:T(8,128)(2,1)}, bf16[2,2,8,64,320]{4,3,2,1,0:T(8,128)(2,1)S(1)}, u32[]{:S(2)}) copy-start(bf16[2,2,8,64,320]{4,3,2,1,0:T(8,128)(2,1)S(1)} %fusion.1) | copy-start | bytes 3932164
  51.3 29.3 %copy-start.3 = (bf16[2,2,8,64,320]{4,3,2,1,0:T(8,128)(2,1)S(1)}, bf16[2,2,8,64,320]{4,3,2,1,0:T(8,128)(2,1)}, u32[]{:S(2)}) copy-start(bf16[2,2,8,64,320]{4,3,2,1,0:T(8,128)(2,1)} %copy-done.2) | copy-start | bytes 3932164
  51.4 6.3 %collective-permute-start.9 = (bf16[64,512]{1,0:T(8,128)(2,1)S(1)}, bf16[64,512]{1,0:T(8,128)(2,1)S(1)}, u32[]{:S(2)}, u32[]{:S(2)}) collective-permute-start(bf16[64,512]{1,0:T(8,128)(2,1)S(1)} %get-tuple-element.6), channel_id=1, source_target_pairs={{4,0},{8,4},{12,8},{16,12},{20,16},{24,20},{28,24},{5,1},{9,5},{13... | collective-permute-start | bytes 196616 | tf_op jit(solution)/shard_map/ppermute | solution.py:18
  54.6 4.4 %collective-permute-start.8 = (bf16[64,512]{1,0:T(8,128)(2,1)S(1)}, bf16[64,512]{1,0:T(8,128)(2,1)S(1)}, u32[]{:S(2)}, u32[]{:S(2)}) collective-permute-start(bf16[64,512]{1,0:T(8,128)(2,1)S(1)} %get-tuple-element.5), channel_id=1, source_target_pairs={{0,4},{4,8},{8,12},{12,16},{16,20},{20,24},{24,28},{1,5},{5,9},{9,... | collective-permute-start | bytes 196616 | tf_op jit(solution)/shard_map/ppermute | solution.py:15
  59.1 6.2 %collective-permute-start.11 = (bf16[64,512]{1,0:T(8,128)(2,1)S(1)}, bf16[64,512]{1,0:T(8,128)(2,1)S(1)}, u32[]{:S(2)}, u32[]{:S(2)}) collective-permute-start(bf16[64,512]{1,0:T(8,128)(2,1)S(1)} %get-tuple-element.14), channel_id=1, source_target_pairs={{4,0},{8,4},{12,8},{16,12},{20,16},{24,20},{28,24},{5,1},{9,5},{13... | collective-permute-start | bytes 196616 | tf_op jit(solution)/shard_map/ppermute | solution.py:18
  62.2 4.4 %collective-permute-start.10 = (bf16[64,512]{1,0:T(8,128)(2,1)S(1)}, bf16[64,512]{1,0:T(8,128)(2,1)S(1)}, u32[]{:S(2)}, u32[]{:S(2)}) collective-permute-start(bf16[64,512]{1,0:T(8,128)(2,1)S(1)} %get-tuple-element.13), channel_id=1, source_target_pairs={{0,4},{4,8},{8,12},{12,16},{16,20},{20,24},{24,28},{1,5},{5,9},{9,... | collective-permute-start | bytes 196616 | tf_op jit(solution)/shard_map/ppermute | solution.py:15
  66.7 6.2 %collective-permute-start.13 = (bf16[64,512]{1,0:T(8,128)(2,1)S(1)}, bf16[64,512]{1,0:T(8,128)(2,1)S(1)}, u32[]{:S(2)}, u32[]{:S(2)}) collective-permute-start(bf16[64,512]{1,0:T(8,128)(2,1)S(1)} %get-tuple-element.12), channel_id=1, source_target_pairs={{4,0},{8,4},{12,8},{16,12},{20,16},{24,20},{28,24},{5,1},{9,5},{13... | collective-permute-start | bytes 196616 | tf_op jit(solution)/shard_map/ppermute | solution.py:18
  69.8 4.4 %collective-permute-start.12 = (bf16[64,512]{1,0:T(8,128)(2,1)S(1)}, bf16[64,512]{1,0:T(8,128)(2,1)S(1)}, u32[]{:S(2)}, u32[]{:S(2)}) collective-permute-start(bf16[64,512]{1,0:T(8,128)(2,1)S(1)} %get-tuple-element.11), channel_id=1, source_target_pairs={{0,4},{4,8},{8,12},{12,16},{16,20},{20,24},{24,28},{1,5},{5,9},{9,... | collective-permute-start | bytes 196616 | tf_op jit(solution)/shard_map/ppermute | solution.py:15
  74.4 8.1 %collective-permute-start.15 = (bf16[64,512]{1,0:T(8,128)(2,1)S(1)}, bf16[64,512]{1,0:T(8,128)(2,1)S(1)}, u32[]{:S(2)}, u32[]{:S(2)}) collective-permute-start(bf16[64,512]{1,0:T(8,128)(2,1)S(1)} %get-tuple-element.10), channel_id=1, source_target_pairs={{4,0},{8,4},{12,8},{16,12},{20,16},{24,20},{28,24},{5,1},{9,5},{13... | collective-permute-start | bytes 196616 | tf_op jit(solution)/shard_map/ppermute | solution.py:18
  77.5 5.1 %collective-permute-start.14 = (bf16[64,512]{1,0:T(8,128)(2,1)S(1)}, bf16[64,512]{1,0:T(8,128)(2,1)S(1)}, u32[]{:S(2)}, u32[]{:S(2)}) collective-permute-start(bf16[64,512]{1,0:T(8,128)(2,1)S(1)} %get-tuple-element.9), channel_id=1, source_target_pairs={{0,4},{4,8},{8,12},{12,16},{16,20},{20,24},{24,28},{1,5},{5,9},{9,... | collective-permute-start | bytes 196616 | tf_op jit(solution)/shard_map/ppermute | solution.py:15
where the time goes:
time: 84.9 us; the launch traced here: 83.3 us
  starting transfers between devices  47 us (55%)
  local copies, waits for them, and re-layouts  11.9 us (14%)
  waiting for transfers between devices  11.3 us (13%)
  matrix products  7.36 us (9%)
  other arithmetic  4.58 us (5%)
  between operations  1.16 us (1%)
    ppermute x8, starting transfers between devices, with_halo(): lax.ppermute(lax.slice_in_dim(block, block.shape[dim] - width, None, axis...  25.7 us
    ppermute x8, starting transfers between devices, with_halo(): lax.ppermute(lax.slice_in_dim(block, 0, width, axis=dim), axis, backward)  21.3 us
    ppermute x8, waiting for transfers between devices, with_halo(): lax.ppermute(lax.slice_in_dim(block, 0, width, axis=dim), axis, backward)  6.08 us
    ppermute x8, waiting for transfers between devices, with_halo(): lax.ppermute(lax.slice_in_dim(block, block.shape[dim] - width, None, axis...  5.19 us
    unnamed x22, local copies, waits for them, and re-layouts  3.81 us
    dot_general x1, matrix products, shards(): jnp.einsum('hkgqp,hqkgd->hpkd', probs_low, grads_out, preferred_element_t...  3.19 us
    dot_general x1, matrix products, shards(): jnp.einsum('hqkgd,hpkd->hkgqp', query_matrix, keys_all, preferred_element...  1.8 us
    reshape x1, local copies, waits for them, and re-layouts, shards(): stored[..., window_width:].reshape(2, total_length, kv_heads, HEAD_SIZE)  1.78 us
  transfers between devices with their start and end apart: 16, of which 6 were waited for; matrix products, arithmetic and copies ran while one was open for 8% of the time, Pallas kernels for 0%

commit v1 on v0

v1 whole, which is shorter than its diff:
```python
import functools

import jax
import jax.numpy as jnp
from jax import lax
from jax.experimental import pallas as pl
from jax.experimental.pallas import tpu as pltpu
from jax.sharding import PartitionSpec as P

HEAD_SIZE = 128
STEPS = 4
LOG2E = 1.4426950408889634
CONTRACT_LAST = (((1,), (1,)), ((), ()))
CONTRACT_ROWS = (((1,), (0,)), ((), ()))


def dot(a, b, dims=CONTRACT_ROWS):
    return lax.dot_general(a, b, dims, preferred_element_type=jnp.float32)


def stack_heads(rows, first, count):
    return jnp.concatenate(
        [rows[:, (first + a) * HEAD_SIZE : (first + a + 1) * HEAD_SIZE] for a in range(count)],
        axis=0,
    )


def attend(q, do, o, keys, values, low, high, group, scale):
    window = keys.shape[0]
    scores = dot(keys, q, CONTRACT_LAST) * (scale * LOG2E)
    row = lax.broadcasted_iota(jnp.int32, scores.shape, 0)
    scores = jnp.where((row >= low) & (row <= high), scores, -jnp.inf)
    top = jnp.max(scores, axis=0, keepdims=True)
    weights = jnp.exp2(scores - top)
    probs = weights * (1.0 / jnp.sum(weights, axis=0, keepdims=True))
    terms = do.astype(jnp.float32) * o.astype(jnp.float32)
    coarse = terms.astype(jnp.bfloat16)
    fine = (terms - coarse.astype(jnp.float32)).astype(jnp.bfloat16)
    ones = jnp.ones((8, 2 * HEAD_SIZE), jnp.bfloat16)
    delta = dot(ones, jnp.concatenate([coarse, fine], axis=1), CONTRACT_LAST)[:1]
    dprobs = dot(values, do, CONTRACT_LAST)
    dscores = (probs * (dprobs - delta)).astype(jnp.bfloat16)
    v_part = dot(probs.astype(jnp.bfloat16), do)
    k_part = dot(dscores, q) * scale
    q_grad_t = dot(keys.T, dscores) * scale
    return q_grad_t.astype(jnp.bfloat16), k_part, v_part


def kernel(
    block_ref, place_ref, q_ref, do_ref, o_ref, starts_ref, stored_ref,
    dq_ref, dkv_ref, window_ref, sems,
):
    units, tokens, width = q_ref.shape
    heads = width // HEAD_SIZE
    kv_width = stored_ref.shape[-1] // 2
    kv_heads = kv_width // HEAD_SIZE
    group = heads // kv_heads
    scale = HEAD_SIZE ** (-0.5)

    def copy(unit, step):
        place = place_ref[unit * (STEPS + 1) + step]
        return pltpu.make_async_copy(
            stored_ref.at[place],
            window_ref.at[unit, pl.ds(step * tokens, tokens)],
            sems.at[unit, step],
        )

    for unit in range(units):
        for step in range(STEPS + 1):
            copy(unit, step).start()
    dkv_ref[...] = jnp.zeros_like(dkv_ref)
    for unit in range(units):
        for step in range(STEPS + 1):
            copy(unit, step).wait()
        offset = lax.broadcasted_iota(jnp.int32, (1, tokens), 1)
        begin = (block_ref[unit] - STEPS) * tokens
        low = jnp.maximum(offset + 1, starts_ref[unit : unit + 1, :] - begin)
        high = offset + STEPS * tokens
        low = jnp.concatenate([low] * group, axis=1)
        high = jnp.concatenate([high] * group, axis=1)
        for g in range(kv_heads):
            keys = window_ref[unit, :, g * HEAD_SIZE : (g + 1) * HEAD_SIZE]
            values = window_ref[unit, :, kv_width + g * HEAD_SIZE : kv_width + (g + 1) * HEAD_SIZE]
            q = stack_heads(q_ref[unit], g * group, group)
            do = stack_heads(do_ref[unit], g * group, group)
            o = stack_heads(o_ref[unit], g * group, group)
            dq_t, k_part, v_part = attend(q, do, o, keys, values, low, high, group, scale)
            dq = dq_t.T
            for a in range(group):
                dq_ref[unit, :, (g * group + a) * HEAD_SIZE : (g * group + a + 1) * HEAD_SIZE] = (
                    dq[a * tokens : (a + 1) * tokens]
                )
            for step in range(STEPS + 1):
                place = place_ref[unit * (STEPS + 1) + step]
                rows = slice(step * tokens, (step + 1) * tokens)
                for part, at in ((k_part, g * HEAD_SIZE), (v_part, kv_width + g * HEAD_SIZE)):
                    held = dkv_ref[place, :, at : at + HEAD_SIZE].astype(jnp.float32)
                    dkv_ref[place, :, at : at + HEAD_SIZE] = (held + part[rows]).astype(jnp.bfloat16)


def window_backward(blocks, places, query, out_grad, attn_out, starts, stored):
    units, tokens, width = query.shape
    vmem = pl.BlockSpec(memory_space=pltpu.VMEM)
    smem = pl.BlockSpec(memory_space=pltpu.SMEM)
    return pl.pallas_call(
        kernel,
        out_shape=(
            jax.ShapeDtypeStruct((units, tokens, width), jnp.bfloat16),
            jax.ShapeDtypeStruct(stored.shape, jnp.bfloat16),
        ),
        in_specs=[smem, smem, vmem, vmem, vmem, vmem, pl.BlockSpec(memory_space=pl.ANY)],
        out_specs=(vmem, vmem),
        scratch_shapes=[
            pltpu.VMEM((units, (STEPS + 1) * tokens, stored.shape[-1]), jnp.bfloat16),
            pltpu.SemaphoreType.DMA((units, STEPS + 1)),
        ],
        compiler_params=pltpu.CompilerParams(vmem_limit_bytes=48 * 2**20),
        name="window_backward",
    )(blocks, places, query, out_grad, attn_out, starts, stored)


def neighbours(low, high, count):
    forward = [(i, i + 1) for i in range(count - 1)]
    backward = [(target, source) for source, target in forward]
    return lax.ppermute(low, "ctx", forward), lax.ppermute(high, "ctx", backward)


def shards(query, key, value, out_grad, attn_out, doc_start):
    count = lax.axis_size("ctx")
    index = lax.axis_index("ctx")
    blocks = jnp.stack([index, 2 * count - 1 - index]).astype(jnp.int32)
    pair = jnp.concatenate([key[0], value[0]], axis=-1)
    gathers = count <= 2 * STEPS
    is_last = index == count - 1
    if gathers:
        reach = blocks[:, None] - STEPS + jnp.arange(STEPS + 1, dtype=jnp.int32)
        reach = jnp.maximum(reach, 0)
        places = jnp.where(reach < count, 2 * reach, 2 * (2 * count - 1 - reach) + 1).reshape(-1)
        stored = lax.all_gather(pair, "ctx", axis=0, tiled=True)
    else:
        places = jnp.arange(2 * (STEPS + 1), dtype=jnp.int32)
        steps = [pair]
        for _ in range(STEPS):
            low, high = neighbours(steps[-1][0], steps[-1][1], count)
            steps.append(jnp.stack([low, jnp.where(is_last, steps[-1][0], high)]))
        stored = jnp.stack(steps[::-1], axis=1).reshape((-1,) + pair.shape[1:])
    dq, parts = window_backward(
        blocks, places, query[0], out_grad[0], attn_out[0], doc_start[0], stored
    )
    if gathers:
        total = lax.psum_scatter(parts, "ctx", scatter_dimension=0, tiled=True)
    else:
        parts = parts.reshape((2, STEPS + 1) + pair.shape[1:])
        total = parts[:, 0]
        for step in range(1, STEPS + 1):
            high, low = neighbours(total[1], total[0], count)
            total = jnp.stack([jnp.where(is_last, total[1], low), high])
            total = (total.astype(jnp.float32) + parts[:, step]).astype(jnp.bfloat16)
    half = pair.shape[-1] // 2
    return dq[None], total[None, ..., :half], total[None, ..., half:]


def solution(mesh):
    placed = (P("ctx", "dp", None, None),) * 5 + (P("ctx", "dp", None),)
    return jax.shard_map(
        shards,
        mesh=mesh,
        in_specs=placed,
        out_specs=(P("ctx", "dp", None, None),) * 3,
        check_vma=False,
    )
```

time: 84.9 us -> 86.8 us (1.022)
  the two profiles are of different devices: /device:TPU:13 before, /device:TPU:0 now
where the time goes in v1:
time: 86.8 us; the launch traced here: 86.4 us
  waiting for transfers between devices  58.2 us (67%)
  between operations  14.1 us (16%)
  local copies, waits for them, and re-layouts  6.64 us (8%)
  Pallas kernels  5.72 us (7%)
  other arithmetic  1.69 us (2%)
    reduce_scatter x1, waiting for transfers between devices, shards(): total = lax.psum_scatter(parts, 'ctx', scatter_dimension=0, tiled=True)  32.2 us
    all_gather x1, waiting for transfers between devices, shards(): stored = lax.all_gather(pair, 'ctx', axis=0, tiled=True)  25.9 us
    pallas_call x1, Pallas kernels, window_backward(): pl.pallas_call(kernel, out_shape=(jax.ShapeDtypeStruct((units, tokens, wi...  5.72 us
    unnamed x10, local copies, waits for them, and re-layouts  5.03 us
  transfers between devices with their start and end apart: 2, of which 2 were waited for; matrix products, arithmetic and copies ran while one was open for 0% of the time, Pallas kernels for 0%

profile of v1, /device:TPU:0, one launch (start us, length us, event | category | flops | bytes accessed | tf_op | source)
XLA Modules:
  0.0 86.4 jit_solution(9134166634873309161)
XLA Ops:
  7.2 0.0 all-gather.2.cloned.1.call-start
  7.2 1.5 %pad_maximum_fusion = bf16[2,64,512]{2,1,0:T(8,128)(2,1)} fusion(bf16[2,64,256]{2,1,0:T(8,128)(2,1)} %bitcast.17, bf16[2,64,256]{2,1,0:T(8,128)(2,1)} %bitcast.18), kind=kLoop, calls=%fused_computation | loop fusion | flops 262144 | bytes 262144 | tf_op jit(solution)/shard_map/concatenate | solution.py:132
  8.7 0.0 all-gather.2.cloned.1.call-update
  8.8 0.0 reduce-scatter.2.cloned.1.call-start
  8.8 0.1 broadcast_add_fusion
  8.9 0.1 compare_select_fusion
  9.0 0.1 reshape.40.place_ref
  9.1 25.9 %all-gather.2.cloned.1.call-done.stored_ref = bf16[16,64,512]{2,1,0:T(8,128)(2,1)} async-done(((bf16[2,64,512]{2,1,0:T(8,128)(2,1)}), bf16[16,64,512]{2,1,0:T(8,128)(2,1)}) %all-gather.2.cloned.1.call-update) | async-done | bytes 1048592 | tf_op jit(solution)/shard_map/all_gather | solution.py:139
  35.0 0.0 copy-start.4
  35.0 0.7 copy-done.4
  35.7 0.0 copy-start
  35.7 1.2 %copy-done = bf16[16,64,512]{2,1,0:T(8,128)(2,1)S(1)} copy-done((bf16[16,64,512]{2,1,0:T(8,128)(2,1)S(1)}, bf16[16,64,512]{2,1,0:T(8,128)(2,1)}, u32[]{:S(2)}) %copy-start) | copy-done | bytes 1048600
  36.9 0.0 copy-start.1
  36.9 1.0 %copy-done.1 = bf16[1,2,64,2048]{3,2,1,0:T(8,128)(2,1)S(1)} copy-done((bf16[1,2,64,2048]{3,2,1,0:T(8,128)(2,1)S(1)}, bf16[1,2,64,2048]{3,2,1,0:T(8,128)(2,1)}, u32[]{:S(2)}) %copy-start.1) | copy-done | bytes 524312
  38.0 0.0 copy-start.2
  38.0 1.0 %copy-done.2 = bf16[1,2,64,2048]{3,2,1,0:T(8,128)(2,1)S(1)} copy-done((bf16[1,2,64,2048]{3,2,1,0:T(8,128)(2,1)S(1)}, bf16[1,2,64,2048]{3,2,1,0:T(8,128)(2,1)}, u32[]{:S(2)}) %copy-start.2) | copy-done | bytes 524312
  39.0 0.0 copy-start.3
  39.0 1.0 %copy-done.3 = bf16[1,2,64,2048]{3,2,1,0:T(8,128)(2,1)S(1)} copy-done((bf16[1,2,64,2048]{3,2,1,0:T(8,128)(2,1)S(1)}, bf16[1,2,64,2048]{3,2,1,0:T(8,128)(2,1)}, u32[]{:S(2)}) %copy-start.3) | copy-done | bytes 524312
  40.0 5.7 %window_backward.1 = (bf16[2,64,2048]{2,1,0:T(8,128)(2,1)}, bf16[16,64,512]{2,1,0:T(8,128)(2,1)}) custom-call(s32[2]{0:T(128)S(1)} %get-tuple-element.8.block_ref, s32[10]{0:T(128)S(1)} %reshape.40.place_ref, bf16[2,64,2048]{2,1,0:T(8,128)(2,1)S(1)} %bitcast.13, bf16[2,64,2048]{2,1,0:T(8,128)(2,1)S(1)} %bitcast.14, bf16[2,64,2048]{2,1,0:T(8,128)(2,1)S(1)} %bitcast.15, ...), custom_call_target="tpu_custom_call" | custom-call | tf_op jit(solution)/shard_map/window_backward/pallas_call | solution.py:105
  45.8 0.0 reduce-scatter.2.cloned.1.call-update
  45.8 32.2 %reduce-scatter.2.cloned.1.call-done = bf16[2,64,512]{2,1,0:T(8,128)(2,1)} async-done(((bf16[16,64,512]{2,1,0:T(8,128)(2,1)}), bf16[2,64,512]{2,1,0:T(8,128)(2,1)}) %reduce-scatter.2.cloned.1.call-update) | async-done | bytes 131088 | tf_op jit(solution)/shard_map/reduce_scatter | solution.py:151
  78.0 1.5 %slice_bitcast_fusion = (bf16[1,2,64,256]{3,2,1,0:T(8,128)(2,1)}, bf16[1,2,64,256]{3,2,1,0:T(8,128)(2,1)}) fusion(bf16[2,64,512]{2,1,0:T(8,128)(2,1)} %reduce-scatter.2.cloned.1.call-done), kind=kLoop, calls=%fused_computation.1 | loop fusion | bytes 262144 | tf_op jit(solution)/shard_map/broadcast_in_dim | solution.py:160
Async XLA Ops:
  7.2 27.8 %all-gather.2.cloned.1.call-start = ((), (), s32[]{:S(2)}) async-start(), calls=%async_computation.1 | async-start | bytes 1179648 | tf_op jit(solution)/shard_map/all_gather | solution.py:139
  8.8 69.2 %reduce-scatter.2.cloned.1.call-start = ((), (), s32[]{:S(2)}) async-start(), calls=%async_computation.2 | async-start | bytes 1179648 | tf_op jit(solution)/shard_map/reduce_scatter | solution.py:151
  35.0 0.7 copy-start.4
  35.7 1.2 %copy-start = (bf16[16,64,512]{2,1,0:T(8,128)(2,1)S(1)}, bf16[16,64,512]{2,1,0:T(8,128)(2,1)}, u32[]{:S(2)}) copy-start(bf16[16,64,512]{2,1,0:T(8,128)(2,1)} %all-gather.2.cloned.1.call-done.stored_ref) | copy-start | bytes 3145732
  36.9 1.0 %copy-start.1 = (bf16[1,2,64,2048]{3,2,1,0:T(8,128)(2,1)S(1)}, bf16[1,2,64,2048]{3,2,1,0:T(8,128)(2,1)}, u32[]{:S(2)}) copy-start(bf16[1,2,64,2048]{3,2,1,0:T(8,128)(2,1)} %param.6) | copy-start | bytes 1572868
  38.0 1.0 %copy-start.2 = (bf16[1,2,64,2048]{3,2,1,0:T(8,128)(2,1)S(1)}, bf16[1,2,64,2048]{3,2,1,0:T(8,128)(2,1)}, u32[]{:S(2)}) copy-start(bf16[1,2,64,2048]{3,2,1,0:T(8,128)(2,1)} %param.9) | copy-start | bytes 1572868
  39.0 1.0 %copy-start.3 = (bf16[1,2,64,2048]{3,2,1,0:T(8,128)(2,1)S(1)}, bf16[1,2,64,2048]{3,2,1,0:T(8,128)(2,1)}, u32[]{:S(2)}) copy-start(bf16[1,2,64,2048]{3,2,1,0:T(8,128)(2,1)} %param.10) | copy-start | bytes 1572868
Sparse Core Ops, SparseCore 0:
  10.2 24.7 all-gather.1
  45.9 32.0 reduce-scatter.1

commit v2 on v1

v2 whole, which is shorter than its diff:
```python
import jax
import jax.numpy as jnp
from jax import lax
from jax.experimental import pallas as pl
from jax.experimental.pallas import tpu as pltpu
from jax.sharding import PartitionSpec as P

HEAD_SIZE = 128
STEPS = 4
LOG2E = 1.4426950408889634
CODE = 128
CODE_ROWS = 16
CONTRACT_LAST = (((1,), (1,)), ((), ()))
CONTRACT_ROWS = (((1,), (0,)), ((), ()))
VMEM = pl.BlockSpec(memory_space=pltpu.VMEM)
SMEM = pl.BlockSpec(memory_space=pltpu.SMEM)
ANY = pl.BlockSpec(memory_space=pl.ANY)
PARAMS = pltpu.CompilerParams(vmem_limit_bytes=48 * 2**20)


def dot(a, b, dims=CONTRACT_ROWS):
    return lax.dot_general(a, b, dims, preferred_element_type=jnp.float32)


def stack_heads(ref, first, count):
    return jnp.concatenate(
        [ref[:, (first + a) * HEAD_SIZE : (first + a + 1) * HEAD_SIZE] for a in range(count)],
        axis=0,
    )


def attend(q, do, o, keys, values, low, high, scale):
    scores = dot(keys, q, CONTRACT_LAST) * (scale * LOG2E)
    row = lax.broadcasted_iota(jnp.int32, scores.shape, 0)
    scores = jnp.where((row >= low) & (row <= high), scores, -jnp.inf)
    top = jnp.max(scores, axis=0, keepdims=True)
    weights = jnp.exp2(scores - top)
    probs = weights * (1.0 / jnp.sum(weights, axis=0, keepdims=True))
    terms = do.astype(jnp.float32) * o.astype(jnp.float32)
    coarse = terms.astype(jnp.bfloat16)
    fine = (terms - coarse.astype(jnp.float32)).astype(jnp.bfloat16)
    ones = jnp.ones((8, 2 * HEAD_SIZE), jnp.bfloat16)
    delta = dot(ones, jnp.concatenate([coarse, fine], axis=1), CONTRACT_LAST)[:1]
    dprobs = dot(values, do, CONTRACT_LAST)
    dscores = (probs * (dprobs - delta)).astype(jnp.bfloat16)
    v_part = dot(probs.astype(jnp.bfloat16), do)
    k_part = dot(dscores, q) * scale
    q_grad_t = dot(keys.T, dscores) * scale
    return q_grad_t.astype(jnp.bfloat16), k_part, v_part


def pack_pair_kernel(core_ref, starts_ref, key_ref, value_ref, keep_ref, send_ref, sems):
    core = core_ref[0]
    tokens, width = key_ref.shape[1:]
    copies = []
    for n, (slot, target) in enumerate(((core, keep_ref), (1 - core, send_ref))):
        for m, source in enumerate((key_ref, value_ref)):
            copies.append(
                pltpu.make_async_copy(
                    source.at[slot],
                    target.at[pl.ds(0, tokens), pl.ds(m * width, width)],
                    sems.at[n, m],
                )
            )
    for copy in copies:
        copy.start()
    starts = jnp.where(core == 0, starts_ref[1:2, :], starts_ref[0:1, :])
    coarse = starts // CODE
    coded = jnp.concatenate(
        [coarse, starts - coarse * CODE, jnp.zeros((CODE_ROWS - 2, tokens), jnp.int32)], axis=0
    ).astype(jnp.float32)
    padded = jnp.concatenate(
        [coded, jnp.zeros((CODE_ROWS, 2 * width - tokens), jnp.float32)], axis=1
    )
    send_ref[tokens:, :] = padded.astype(jnp.bfloat16)
    for copy in copies:
        copy.wait()


def pack_rows_kernel(core_ref, q_ref, do_ref, o_ref, send_ref, sems):
    slot = 1 - core_ref[0]
    copies = [
        pltpu.make_async_copy(source.at[slot], send_ref.at[n], sems.at[n])
        for n, source in enumerate((q_ref, do_ref, o_ref))
    ]
    for copy in copies:
        copy.start()
    for copy in copies:
        copy.wait()


def main_kernel(
    place_ref, starts_ref, q_ref, do_ref, o_ref, rows_ref, coded_ref, far_ref, near_ref, own_ref,
    dq_ref, dq_send_ref, far_part_ref, near_part_ref, own_part_ref,
    held_ref, dq_held_ref, window_ref, part_ref, sems, out_sem,
):
    core, begin = place_ref[0], place_ref[1]
    _, tokens, width = q_ref.shape
    heads = width // HEAD_SIZE
    kv_width = own_ref.shape[-1] // 2
    kv_heads = kv_width // HEAD_SIZE
    group = heads // kv_heads
    scale = HEAD_SIZE ** (-0.5)
    reach = (STEPS + 1) * tokens

    copies = []
    for n, source in enumerate((q_ref, do_ref, o_ref)):
        copies.append(
            pltpu.make_async_copy(source.at[core], held_ref.at[n, 0], sems.at[n, 0])
        )
        copies.append(
            pltpu.make_async_copy(rows_ref.at[n], held_ref.at[n, 1], sems.at[n, 1])
        )
    for copy in copies:
        copy.start()
    pair = 2 * tokens
    for n, source in enumerate((far_ref, near_ref, own_ref)):
        window_ref[n * pair : (n + 1) * pair, :] = source[...]
    part_ref[...] = jnp.zeros_like(part_ref)
    coded = coded_ref[tokens : tokens + CODE_ROWS, :tokens].astype(jnp.float32)
    own_starts = jnp.where(core == 0, starts_ref[0:1, :], starts_ref[1:2, :])
    sent_starts = (coded[0:1] * CODE + coded[1:2]).astype(jnp.int32)
    offset = lax.broadcasted_iota(jnp.int32, (1, tokens), 1)
    for copy in copies:
        copy.wait()
    for unit, starts in enumerate((own_starts, sent_starts)):
        first = unit * tokens
        low = jnp.maximum(offset + 1, starts - (begin + (unit - STEPS) * tokens))
        high = offset + STEPS * tokens
        low = jnp.concatenate([low] * group, axis=1)
        high = jnp.concatenate([high] * group, axis=1)
        for g in range(kv_heads):
            at = (g * HEAD_SIZE, kv_width + g * HEAD_SIZE)
            keys = window_ref[first : first + reach, at[0] : at[0] + HEAD_SIZE]
            values = window_ref[first : first + reach, at[1] : at[1] + HEAD_SIZE]
            q = stack_heads(held_ref.at[0, unit], g * group, group)
            do = stack_heads(held_ref.at[1, unit], g * group, group)
            o = stack_heads(held_ref.at[2, unit], g * group, group)
            dq_t, k_part, v_part = attend(q, do, o, keys, values, low, high, scale)
            dq = dq_t.T
            for a in range(group):
                column = (g * group + a) * HEAD_SIZE
                dq_held_ref[unit, :, column : column + HEAD_SIZE] = (
                    dq[a * tokens : (a + 1) * tokens]
                )
            for part, column in ((k_part, at[0]), (v_part, at[1])):
                part_ref[first : first + reach, column : column + HEAD_SIZE] += part
    stores = [
        pltpu.make_async_copy(dq_held_ref.at[0], dq_ref.at[core], out_sem.at[0]),
        pltpu.make_async_copy(dq_held_ref.at[1], dq_send_ref, out_sem.at[1]),
    ]
    for store in stores:
        store.start()
    far_part_ref[...] = part_ref[:pair, :].astype(jnp.bfloat16)
    near_part_ref[...] = part_ref[pair : 2 * pair, :].astype(jnp.bfloat16)
    own_part_ref[...] = part_ref[2 * pair :, :]
    for store in stores:
        store.wait()


def fill_kernel(core_ref, rows_ref, held_ref, out_ref, sem):
    copy = pltpu.make_async_copy(rows_ref, out_ref.at[1 - core_ref[0]], sem)
    copy.start()
    copy.wait()


def shards(query, key, value, out_grad, attn_out, doc_start):
    count = lax.axis_size("ctx")
    index = lax.axis_index("ctx")
    _, slots, tokens, width = query.shape
    kv_width = key.shape[-1]
    pair_width = 2 * kv_width
    pair = 2 * tokens
    core = (index % 2).astype(jnp.int32)
    stage = jnp.where(core == 0, index // 2, count - 1 - index // 2).astype(jnp.int32)
    core = core[None]
    place = jnp.stack([core[0], stage * pair])
    holder = [2 * s if 2 * s < count else 2 * count - 1 - 2 * s for s in range(count)]
    swap = [(i, i ^ 1) for i in range(count)]

    def shift(x, by):
        moves = [
            (holder[s], holder[s + by]) for s in range(count) if 0 <= s + by < count
        ]
        return lax.ppermute(x, "ctx", moves)

    bf16 = jnp.bfloat16
    keep, send = pl.pallas_call(
        pack_pair_kernel,
        out_shape=(
            jax.ShapeDtypeStruct((tokens, pair_width), bf16),
            jax.ShapeDtypeStruct((tokens + CODE_ROWS, pair_width), bf16),
        ),
        in_specs=[SMEM, VMEM, ANY, ANY],
        out_specs=(VMEM, VMEM),
        scratch_shapes=[pltpu.SemaphoreType.DMA((2, 2))],
        name="pack_pair",
    )(core, doc_start[0], key[0], value[0])
    coded = lax.ppermute(send, "ctx", swap)
    own = jnp.concatenate([keep, coded[:tokens]], axis=0)
    own, late_core = lax.optimization_barrier((own, core))
    near = shift(own, 1)
    far = shift(own, 2)
    rows_send = pl.pallas_call(
        pack_rows_kernel,
        out_shape=jax.ShapeDtypeStruct((3, tokens, width), bf16),
        in_specs=[SMEM, ANY, ANY, ANY],
        out_specs=ANY,
        scratch_shapes=[pltpu.SemaphoreType.DMA((3,))],
        name="pack_rows",
    )(late_core, query[0], out_grad[0], attn_out[0])
    rows = lax.ppermute(rows_send, "ctx", swap)
    dq, dq_send, far_part, near_part, own_part = pl.pallas_call(
        main_kernel,
        out_shape=(
            jax.ShapeDtypeStruct((slots, tokens, width), bf16),
            jax.ShapeDtypeStruct((tokens, width), bf16),
            jax.ShapeDtypeStruct((pair, pair_width), bf16),
            jax.ShapeDtypeStruct((pair, pair_width), bf16),
            jax.ShapeDtypeStruct((pair, pair_width), jnp.float32),
        ),
        in_specs=[SMEM, VMEM, ANY, ANY, ANY, ANY, VMEM, VMEM, VMEM, VMEM],
        out_specs=(ANY, ANY, VMEM, VMEM, VMEM),
        scratch_shapes=[
            pltpu.VMEM((3, slots, tokens, width), bf16),
            pltpu.VMEM((slots, tokens, width), bf16),
            pltpu.VMEM((3 * pair, pair_width), bf16),
            pltpu.VMEM((3 * pair, pair_width), jnp.float32),
            pltpu.SemaphoreType.DMA((3, 2)),
            pltpu.SemaphoreType.DMA((2,)),
        ],
        compiler_params=PARAMS,
        name="window_backward",
    )(
        place, doc_start[0], query[0], out_grad[0], attn_out[0], rows, coded, far, near, own
    )
    from_far = shift(far_part, -2)
    from_near = shift(near_part, -1)
    dq_rows = lax.ppermute(dq_send, "ctx", swap)
    dq = pl.pallas_call(
        fill_kernel,
        out_shape=jax.ShapeDtypeStruct(dq.shape, bf16),
        in_specs=[SMEM, ANY, ANY],
        out_specs=ANY,
        scratch_shapes=[pltpu.SemaphoreType.DMA],
        input_output_aliases={2: 0},
        name="fill_rows",
    )(core, dq_rows, dq)
    total = own_part + from_near.astype(jnp.float32) + from_far.astype(jnp.float32)
    total = total.astype(bf16)
    kept = total[:tokens]
    given = lax.ppermute(total[tokens:], "ctx", swap)
    both = jnp.where(core == 0, jnp.stack([kept, given]), jnp.stack([given, kept]))
    return dq[None], both[None, ..., :kv_width], both[None, ..., kv_width:]


def solution(mesh):
    placed = (P("ctx", "dp", None, None),) * 5 + (P("ctx", "dp", None),)
    return jax.shard_map(
        shards,
        mesh=mesh,
        in_specs=placed,
        out_specs=(P("ctx", "dp", None, None),) * 3,
        check_vma=False,
    )
```

time: 86.8 us -> 69.3 us (0.80)
  the two profiles are of different devices: /device:TPU:0 before, /device:TPU:13 now
where the time goes in v2:
time: 69.3 us; the launch traced here: 68.6 us
  Pallas kernels  40.6 us (59%)
  starting transfers between devices  16.9 us (24%)
  waiting for transfers between devices  8.8 us (13%)
  local copies, waits for them, and re-layouts  1.4 us (2%)
  between operations  0.82 us (1%)
    pallas_call x1, Pallas kernels, shards(): pl.pallas_call(pack_rows_kernel, out_shape=jax.ShapeDtypeStruct((3, token...  25 us
    ppermute x4, starting transfers between devices, shift(): return lax.ppermute(x, 'ctx', moves)  11.7 us
    pallas_call x1, Pallas kernels, shards(): pl.pallas_call(fill_kernel, out_shape=jax.ShapeDtypeStruct(dq.shape, bf16...  9.05 us
    ppermute x4, waiting for transfers between devices, shift(): return lax.ppermute(x, 'ctx', moves)  6.84 us
    pallas_call x1, Pallas kernels, shards(): pl.pallas_call(main_kernel, out_shape=(jax.ShapeDtypeStruct((slots, token...  4.41 us
    ppermute x1, starting transfers between devices, shards(): given = lax.ppermute(total[tokens:], 'ctx', swap)  3.95 us
    pallas_call x1, Pallas kernels, shards(): pl.pallas_call(pack_pair_kernel, out_shape=(jax.ShapeDtypeStruct((tokens,...  2.18 us
  transfers between devices with their start and end apart: 8, of which 5 were waited for; matrix products, arithmetic and copies ran while one was open for 1% of the time, Pallas kernels for 0%

profile of v2, /device:TPU:13, one launch (start us, length us, event | category | flops | bytes accessed | tf_op | source)
XLA Modules:
  0.0 68.6 jit_solution(1657823739461891769)
XLA Ops:
  0.6 2.2 %pack_pair.1 = (bf16[64,512]{1,0:T(8,128)(2,1)}, bf16[80,512]{1,0:T(8,128)(2,1)}) custom-call(s32[1]{0:T(128)} %bitcast.core_ref, s32[2,64]{1,0:T(2,128)} %bitcast.23, bf16[2,64,256]{2,1,0:T(8,128)(2,1)} %bitcast.26, bf16[2,64,256]{2,1,0:T(8,128)(2,1)} %bitcast.27), custom_call_target="tpu_custom_call" | custom-call | tf_op jit(solution)/shard_map/pack_pair/pallas_call | solution.py:188
  2.8 0.0 copy-start.5
  2.8 0.7 %collective-permute-start = (bf16[80,512]{1,0:T(8,128)(2,1)}, bf16[80,512]{1,0:T(8,128)(2,1)S(1)}, u32[]{:S(2)}, u32[]{:S(2)}) collective-permute-start(bf16[80,512]{1,0:T(8,128)(2,1)} %get-tuple-element.13), channel_id=1, source_target_pairs={{0,4},{4,0},{8,12},{12,8},{16,20},{20,16},{24,28},{28,24},{1,5},{5... | collective-permute-start | bytes 245768 | tf_op jit(solution)/shard_map/ppermute | solution.py:199
  3.6 1.1 %collective-permute-done.coded_ref = bf16[80,512]{1,0:T(8,128)(2,1)S(1)} collective-permute-done((bf16[80,512]{1,0:T(8,128)(2,1)}, bf16[80,512]{1,0:T(8,128)(2,1)S(1)}, u32[]{:S(2)}, u32[]{:S(2)}) %collective-permute-start) | collective-permute-done | bytes 81952 | tf_op jit(solution)/shard_map/ppermute | solution.py:199
  4.7 0.0 copy-done.5
  4.7 0.0 copy-start
  4.8 0.0 copy-start.1
  4.8 0.0 copy-start.2
  4.8 25.0 %pack_rows.1 = bf16[3,64,2048]{2,1,0:T(8,128)(2,1)} custom-call(s32[1]{0:T(128)} %bitcast.core_ref, bf16[2,64,2048]{2,1,0:T(8,128)(2,1)} %bitcast.17, bf16[2,64,2048]{2,1,0:T(8,128)(2,1)} %bitcast.19, bf16[2,64,2048]{2,1,0:T(8,128)(2,1)} %bitcast.21), custom_call_target="tpu_custom_call" | custom-call | tf_op jit(solution)/shard_map/pack_rows/pallas_call | solution.py:204
  29.7 0.4 collective-permute-start.1
  30.2 1.3 %collective-permute-start.2 = (bf16[128,512]{1,0:T(8,128)(2,1)S(1)}, bf16[128,512]{1,0:T(8,128)(2,1)S(1)}, u32[]{:S(2)}, u32[]{:S(2)}) collective-permute-start(bf16[128,512]{1,0:T(8,128)(2,1)S(1)} %pad_maximum_fusion.own_ref), channel_id=1, source_target_pairs={{0,16},{8,24},{16,28},{24,20},{28,12},{20,4},{1,17},{9,25},{17,29}... | collective-permute-start | bytes 393224 | tf_op jit(solution)/shard_map/ppermute | solution.py:185
  31.5 2.1 %collective-permute-start.3 = (bf16[128,512]{1,0:T(8,128)(2,1)S(1)}, bf16[128,512]{1,0:T(8,128)(2,1)S(1)}, u32[]{:S(2)}, u32[]{:S(2)}) collective-permute-start(bf16[128,512]{1,0:T(8,128)(2,1)S(1)} %pad_maximum_fusion.own_ref), channel_id=1, source_target_pairs={{0,8},{8,16},{16,24},{24,28},{28,20},{20,12},{12,4},{1,9},{9,17},{... | collective-permute-start | bytes 393224 | tf_op jit(solution)/shard_map/ppermute | solution.py:185
  33.6 0.0 copy-start.3
  33.6 0.1 pad_add_fusion.place_ref
  33.6 3.9 %collective-permute-done.2.far_ref = bf16[128,512]{1,0:T(8,128)(2,1)S(1)} collective-permute-done((bf16[128,512]{1,0:T(8,128)(2,1)S(1)}, bf16[128,512]{1,0:T(8,128)(2,1)S(1)}, u32[]{:S(2)}, u32[]{:S(2)}) %collective-permute-start.2) | collective-permute-done | bytes 131104 | tf_op jit(solution)/shard_map/ppermute | solution.py:185
  37.5 1.0 %collective-permute-done.3.near_ref = bf16[128,512]{1,0:T(8,128)(2,1)S(1)} collective-permute-done((bf16[128,512]{1,0:T(8,128)(2,1)S(1)}, bf16[128,512]{1,0:T(8,128)(2,1)S(1)}, u32[]{:S(2)}, u32[]{:S(2)}) %collective-permute-start.3) | collective-permute-done | bytes 131104 | tf_op jit(solution)/shard_map/ppermute | solution.py:185
  38.6 0.0 collective-permute-done.1.rows_ref
  38.6 0.0 copy-done
  38.6 0.0 copy-done.1
  38.6 0.0 copy-done.2
  38.6 0.0 copy-done.3
  38.6 4.4 %window_backward.1 = (bf16[2,64,2048]{2,1,0:T(8,128)(2,1)}, bf16[64,2048]{1,0:T(8,128)(2,1)S(1)}, bf16[128,512]{1,0:T(8,128)(2,1)S(1)}, bf16[128,512]{1,0:T(8,128)(2,1)S(1)}, f32[128,512]{1,0:T(8,128)S(1)}) custom-call(s32[2]{0:T(128)S(1)} %pad_add_fusion.place_ref, s32[2,64]{1,0:T(2,128)S(1)} %bitcast.24, bf16[2,64,2048]{2,1,0:T(8,128)(2,1)S(1)} %bitcast.18, ...), custom_call_target="tpu_custom_call" | custom-call | tf_op jit(solution)/shard_map/window_backward/pallas_call | solution.py:213
  43.0 3.2 %collective-permute-start.5 = (bf16[128,512]{1,0:T(8,128)(2,1)S(1)}, bf16[128,512]{1,0:T(8,128)(2,1)S(1)}, u32[]{:S(2)}, u32[]{:S(2)}) collective-permute-start(bf16[128,512]{1,0:T(8,128)(2,1)S(1)} %get-tuple-element.19), channel_id=1, source_target_pairs={{8,0},{16,8},{24,16},{28,24},{20,28},{12,20},{4,12},{9,1},{17,9},{... | collective-permute-start | bytes 393224 | tf_op jit(solution)/shard_map/ppermute | solution.py:185
  46.2 5.1 %collective-permute-start.6 = (bf16[128,512]{1,0:T(8,128)(2,1)S(1)}, bf16[128,512]{1,0:T(8,128)(2,1)S(1)}, u32[]{:S(2)}, u32[]{:S(2)}) collective-permute-start(bf16[128,512]{1,0:T(8,128)(2,1)S(1)} %get-tuple-element.20), channel_id=1, source_target_pairs={{16,0},{24,8},{28,16},{20,24},{12,28},{4,20},{17,1},{25,9},{29,17}... | collective-permute-start | bytes 393224 | tf_op jit(solution)/shard_map/ppermute | solution.py:185
  51.4 0.0 collective-permute-done.5
  51.4 1.9 %collective-permute-done.6 = bf16[128,512]{1,0:T(8,128)(2,1)S(1)} collective-permute-done((bf16[128,512]{1,0:T(8,128)(2,1)S(1)}, bf16[128,512]{1,0:T(8,128)(2,1)S(1)}, u32[]{:S(2)}, u32[]{:S(2)}) %collective-permute-start.6) | collective-permute-done | bytes 131104 | tf_op jit(solution)/shard_map/ppermute | solution.py:185
  53.3 0.1 add_convert_fusion
  53.4 4.0 %collective-permute-start.7 = (bf16[64,512]{1,0:T(8,128)(2,1)S(1)}, bf16[64,512]{1,0:T(8,128)(2,1)S(1)}, u32[]{:S(2)}, u32[]{:S(2)}) collective-permute-start(bf16[64,512]{1,0:T(8,128)(2,1)S(1)} %get-tuple-element.24), channel_id=1, source_target_pairs={{0,4},{4,0},{8,12},{12,8},{16,20},{20,16},{24,28},{28,24},{1,5},{5... | collective-permute-start | bytes 196616 | tf_op jit(solution)/shard_map/ppermute | solution.py:252
  57.3 0.1 collective-permute-start.4
  57.4 0.8 %collective-permute-done.7 = bf16[64,512]{1,0:T(8,128)(2,1)S(1)} collective-permute-done((bf16[64,512]{1,0:T(8,128)(2,1)S(1)}, bf16[64,512]{1,0:T(8,128)(2,1)S(1)}, u32[]{:S(2)}, u32[]{:S(2)}) %collective-permute-start.7) | collective-permute-done | bytes 65568 | tf_op jit(solution)/shard_map/ppermute | solution.py:252
  58.2 0.7 slice_bitcast_fusion
  58.9 0.0 collective-permute-done.4.rows_ref
  58.9 0.0 copy-start.4
  58.9 0.7 %copy-done.4 = bf16[64,2048]{1,0:T(8,128)(2,1)} copy-done((bf16[64,2048]{1,0:T(8,128)(2,1)}, bf16[64,2048]{1,0:T(8,128)(2,1)S(1)}, u32[]{:S(2)}) %copy-start.4) | copy-done | bytes 262168
  59.6 9.0 %fill_rows.1 = bf16[2,64,2048]{2,1,0:T(8,128)(2,1)} custom-call(s32[1]{0:T(128)} %bitcast.core_ref, bf16[64,2048]{1,0:T(8,128)(2,1)} %copy-done.4, bf16[2,64,2048]{2,1,0:T(8,128)(2,1)} %get-tuple-element.17.held_ref), custom_call_target="tpu_custom_call", output_to_operand_aliasing={{}: (2, {})} | custom-call | tf_op jit(solution)/shard_map/fill_rows/pallas_call | solution.py:240
  (4 shorter events, 0.0 us)
Async XLA Ops:
  2.8 1.9 %copy-start.5 = (bf16[64,512]{1,0:T(8,128)(2,1)S(1)}, bf16[64,512]{1,0:T(8,128)(2,1)}, u32[]{:S(2)}) copy-start(bf16[64,512]{1,0:T(8,128)(2,1)} %get-tuple-element.12) | copy-start | bytes 196612
  2.8 1.9 %collective-permute-start = (bf16[80,512]{1,0:T(8,128)(2,1)}, bf16[80,512]{1,0:T(8,128)(2,1)S(1)}, u32[]{:S(2)}, u32[]{:S(2)}) collective-permute-start(bf16[80,512]{1,0:T(8,128)(2,1)} %get-tuple-element.13), channel_id=1, source_target_pairs={{0,4},{4,0},{8,12},{12,8},{16,20},{20,16},{24,28},{28,24},{1,5},{5... | collective-permute-start | bytes 245768 | tf_op jit(solution)/shard_map/ppermute | solution.py:199
  4.7 33.8 %copy-start = (bf16[1,2,64,2048]{3,2,1,0:T(8,128)(2,1)S(1)}, bf16[1,2,64,2048]{3,2,1,0:T(8,128)(2,1)}, u32[]{:S(2)}) copy-start(bf16[1,2,64,2048]{3,2,1,0:T(8,128)(2,1)} %param.6) | copy-start | bytes 1572868
  4.8 33.8 %copy-start.1 = (bf16[1,2,64,2048]{3,2,1,0:T(8,128)(2,1)S(1)}, bf16[1,2,64,2048]{3,2,1,0:T(8,128)(2,1)}, u32[]{:S(2)}) copy-start(bf16[1,2,64,2048]{3,2,1,0:T(8,128)(2,1)} %param.9) | copy-start | bytes 1572868
  4.8 33.8 %copy-start.2 = (bf16[1,2,64,2048]{3,2,1,0:T(8,128)(2,1)S(1)}, bf16[1,2,64,2048]{3,2,1,0:T(8,128)(2,1)}, u32[]{:S(2)}) copy-start(bf16[1,2,64,2048]{3,2,1,0:T(8,128)(2,1)} %param.10) | copy-start | bytes 1572868
  29.7 8.8 %collective-permute-start.1 = (bf16[3,64,2048]{2,1,0:T(8,128)(2,1)}, bf16[3,64,2048]{2,1,0:T(8,128)(2,1)S(1)}, u32[]{:S(2)}, u32[]{:S(2)}) collective-permute-start(bf16[3,64,2048]{2,1,0:T(8,128)(2,1)} %pack_rows.1), channel_id=1, source_target_pairs={{0,4},{4,0},{8,12},{12,8},{16,20},{20,16},{24,28},{28,24},{1,5},{5... | collective-permute-start | bytes 2359304 | tf_op jit(solution)/shard_map/ppermute | solution.py:212
  30.2 7.4 %collective-permute-start.2 = (bf16[128,512]{1,0:T(8,128)(2,1)S(1)}, bf16[128,512]{1,0:T(8,128)(2,1)S(1)}, u32[]{:S(2)}, u32[]{:S(2)}) collective-permute-start(bf16[128,512]{1,0:T(8,128)(2,1)S(1)} %pad_maximum_fusion.own_ref), channel_id=1, source_target_pairs={{0,16},{8,24},{16,28},{24,20},{28,12},{20,4},{1,17},{9,25},{17,29}... | collective-permute-start | bytes 393224 | tf_op jit(solution)/shard_map/ppermute | solution.py:185
  31.5 7.1 %collective-permute-start.3 = (bf16[128,512]{1,0:T(8,128)(2,1)S(1)}, bf16[128,512]{1,0:T(8,128)(2,1)S(1)}, u32[]{:S(2)}, u32[]{:S(2)}) collective-permute-start(bf16[128,512]{1,0:T(8,128)(2,1)S(1)} %pad_maximum_fusion.own_ref), channel_id=1, source_target_pairs={{0,8},{8,16},{16,24},{24,28},{28,20},{20,12},{12,4},{1,9},{9,17},{... | collective-permute-start | bytes 393224 | tf_op jit(solution)/shard_map/ppermute | solution.py:185
  33.6 5.0 %copy-start.3 = (s32[1,2,64]{2,1,0:T(2,128)S(1)}, s32[1,2,64]{2,1,0:T(2,128)}, u32[]{:S(2)}) copy-start(s32[1,2,64]{2,1,0:T(2,128)} %param.11) | copy-start | bytes 1540
  43.0 8.4 %collective-permute-start.5 = (bf16[128,512]{1,0:T(8,128)(2,1)S(1)}, bf16[128,512]{1,0:T(8,128)(2,1)S(1)}, u32[]{:S(2)}, u32[]{:S(2)}) collective-permute-start(bf16[128,512]{1,0:T(8,128)(2,1)S(1)} %get-tuple-element.19), channel_id=1, source_target_pairs={{8,0},{16,8},{24,16},{28,24},{20,28},{12,20},{4,12},{9,1},{17,9},{... | collective-permute-start | bytes 393224 | tf_op jit(solution)/shard_map/ppermute | solution.py:185
  46.2 7.1 %collective-permute-start.6 = (bf16[128,512]{1,0:T(8,128)(2,1)S(1)}, bf16[128,512]{1,0:T(8,128)(2,1)S(1)}, u32[]{:S(2)}, u32[]{:S(2)}) collective-permute-start(bf16[128,512]{1,0:T(8,128)(2,1)S(1)} %get-tuple-element.20), channel_id=1, source_target_pairs={{16,0},{24,8},{28,16},{20,24},{12,28},{4,20},{17,1},{25,9},{29,17}... | collective-permute-start | bytes 393224 | tf_op jit(solution)/shard_map/ppermute | solution.py:185
  53.4 4.9 %collective-permute-start.7 = (bf16[64,512]{1,0:T(8,128)(2,1)S(1)}, bf16[64,512]{1,0:T(8,128)(2,1)S(1)}, u32[]{:S(2)}, u32[]{:S(2)}) collective-permute-start(bf16[64,512]{1,0:T(8,128)(2,1)S(1)} %get-tuple-element.24), channel_id=1, source_target_pairs={{0,4},{4,0},{8,12},{12,8},{16,20},{20,16},{24,28},{28,24},{1,5},{5... | collective-permute-start | bytes 196616 | tf_op jit(solution)/shard_map/ppermute | solution.py:252
  57.3 1.6 %collective-permute-start.4 = (bf16[64,2048]{1,0:T(8,128)(2,1)S(1)}, bf16[64,2048]{1,0:T(8,128)(2,1)S(1)}, u32[]{:S(2)}, u32[]{:S(2)}) collective-permute-start(bf16[64,2048]{1,0:T(8,128)(2,1)S(1)} %get-tuple-element.16), channel_id=1, source_target_pairs={{0,4},{4,0},{8,12},{12,8},{16,20},{20,16},{24,28},{28,24},{1,5},{5... | collective-permute-start | bytes 786440 | tf_op jit(solution)/shard_map/ppermute | solution.py:239
  58.9 0.7 %copy-start.4 = (bf16[64,2048]{1,0:T(8,128)(2,1)}, bf16[64,2048]{1,0:T(8,128)(2,1)S(1)}, u32[]{:S(2)}) copy-start(bf16[64,2048]{1,0:T(8,128)(2,1)S(1)} %collective-permute-done.4.rows_ref) | copy-start | bytes 786436

commit v3 on v2

v3 whole, which is shorter than its diff:
```python
import jax
import jax.numpy as jnp
from jax import lax
from jax.experimental import pallas as pl
from jax.experimental.pallas import tpu as pltpu
from jax.sharding import PartitionSpec as P

HEAD_SIZE = 128
STEPS = 4
LOG2E = 1.4426950408889634
CODE = 128
CODE_ROWS = 16
CONTRACT_LAST = (((1,), (1,)), ((), ()))
CONTRACT_ROWS = (((1,), (0,)), ((), ()))
VMEM = pl.BlockSpec(memory_space=pltpu.VMEM)
SMEM = pl.BlockSpec(memory_space=pltpu.SMEM)
ANY = pl.BlockSpec(memory_space=pl.ANY)
PARAMS = pltpu.CompilerParams(vmem_limit_bytes=48 * 2**20)


def dot(a, b, dims=CONTRACT_ROWS):
    return lax.dot_general(a, b, dims, preferred_element_type=jnp.float32)


def stack_heads(ref, first, count):
    return jnp.concatenate(
        [ref[:, (first + a) * HEAD_SIZE : (first + a + 1) * HEAD_SIZE] for a in range(count)],
        axis=0,
    )


def attend(q, do, o, keys, values, low, high, scale):
    scores = dot(keys, q, CONTRACT_LAST) * (scale * LOG2E)
    row = lax.broadcasted_iota(jnp.int32, scores.shape, 0)
    scores = jnp.where((row >= low) & (row <= high), scores, -jnp.inf)
    top = jnp.max(scores, axis=0, keepdims=True)
    weights = jnp.exp2(scores - top)
    probs = weights * (1.0 / jnp.sum(weights, axis=0, keepdims=True))
    terms = do.astype(jnp.float32) * o.astype(jnp.float32)
    coarse = terms.astype(jnp.bfloat16)
    fine = (terms - coarse.astype(jnp.float32)).astype(jnp.bfloat16)
    ones = jnp.ones((8, 2 * HEAD_SIZE), jnp.bfloat16)
    delta = dot(ones, jnp.concatenate([coarse, fine], axis=1), CONTRACT_LAST)[:1]
    dprobs = dot(values, do, CONTRACT_LAST)
    dscores = (probs * (dprobs - delta)).astype(jnp.bfloat16)
    return probs.astype(jnp.bfloat16), dscores


def pack_pair_kernel(
    core_ref, starts_ref, key_ref, value_ref, keep_ref, send_ref, held_ref, sems
):
    copies = [
        pltpu.make_async_copy(source, held_ref.at[n], sems.at[n])
        for n, source in enumerate((key_ref, value_ref))
    ]
    for copy in copies:
        copy.start()
    even = core_ref[0] == 0
    tokens, width = key_ref.shape[1:]
    starts = jnp.where(even, starts_ref[1:2, :], starts_ref[0:1, :])
    coarse = starts // CODE
    coded = jnp.concatenate(
        [coarse, starts - coarse * CODE, jnp.zeros((CODE_ROWS - 2, tokens), jnp.int32)], axis=0
    ).astype(jnp.float32)
    padded = jnp.concatenate(
        [coded, jnp.zeros((CODE_ROWS, 2 * width - tokens), jnp.float32)], axis=1
    )
    send_ref[tokens:, :] = padded.astype(jnp.bfloat16)
    for copy in copies:
        copy.wait()
    core = core_ref[0]
    for n in range(2):
        keep_ref[:, n * width : (n + 1) * width] = held_ref[n, core]
        send_ref[:tokens, n * width : (n + 1) * width] = held_ref[n, 1 - core]


def pack_rows_kernel(core_ref, q_ref, do_ref, o_ref, after_ref, send_ref, sems):
    slot = 1 - core_ref[0]
    copies = [
        pltpu.make_async_copy(source.at[slot], send_ref.at[n], sems.at[n])
        for n, source in enumerate((q_ref, do_ref, o_ref))
    ]
    for copy in copies:
        copy.start()
    for copy in copies:
        copy.wait()


def unit_sizes(rows_ref, pair_ref):
    heads = rows_ref.shape[-1] // HEAD_SIZE
    kv_width = pair_ref.shape[-1] // 2
    kv_heads = kv_width // HEAD_SIZE
    return kv_heads, kv_width, heads // kv_heads


def scores_kernel(
    place_ref, starts_ref, q_ref, do_ref, o_ref, rows_ref, coded_ref, far_ref, near_ref, own_ref,
    far_part_ref, near_part_ref, probs_ref, dscores_ref, window_ref, part_ref,
):
    core, begin = place_ref[0], place_ref[1]
    tokens = q_ref.shape[1]
    kv_heads, kv_width, group = unit_sizes(q_ref, own_ref)
    scale = HEAD_SIZE ** (-0.5)
    reach = (STEPS + 1) * tokens
    pair = 2 * tokens
    for n, source in enumerate((far_ref, near_ref, own_ref)):
        window_ref[n * pair : (n + 1) * pair, :] = source[...]
    coded = coded_ref[tokens : tokens + CODE_ROWS, :tokens].astype(jnp.float32)
    own_starts = jnp.where(core == 0, starts_ref[0:1, :], starts_ref[1:2, :])
    sent_starts = (coded[0:1] * CODE + coded[1:2]).astype(jnp.int32)
    offset = lax.broadcasted_iota(jnp.int32, (1, tokens), 1)
    for unit, starts in enumerate((own_starts, sent_starts)):
        first = unit * tokens
        low = jnp.maximum(offset + 1, starts - (begin + (unit - STEPS) * tokens))
        high = offset + STEPS * tokens
        low = jnp.concatenate([low] * group, axis=1)
        high = jnp.concatenate([high] * group, axis=1)
        sources = [r.at[core] for r in (q_ref, do_ref, o_ref)]
        if unit == 1:
            sources = [rows_ref.at[n] for n in range(3)]
        for g in range(kv_heads):
            at = (g * HEAD_SIZE, kv_width + g * HEAD_SIZE)
            keys = window_ref[first : first + reach, at[0] : at[0] + HEAD_SIZE]
            values = window_ref[first : first + reach, at[1] : at[1] + HEAD_SIZE]
            q, do, o = (stack_heads(r, g * group, group) for r in sources)
            probs, dscores = attend(q, do, o, keys, values, low, high, scale)
            probs_ref[unit, g] = probs
            dscores_ref[unit, g] = dscores
            before = 2 * pair - first
            for part, column in (
                (dot(dscores[:before], q) * scale, at[0]),
                (dot(probs[:before], do), at[1]),
            ):
                columns = slice(column, column + HEAD_SIZE)
                if unit == 0:
                    part_ref[:before, columns] = part
                else:
                    part_ref[first : 2 * pair, columns] += part
    far_part_ref[...] = part_ref[:pair, :].astype(jnp.bfloat16)
    near_part_ref[...] = part_ref[pair:, :].astype(jnp.bfloat16)


def rest_kernel(
    place_ref, q_ref, do_ref, rows_ref, far_ref, near_ref, own_ref, probs_ref, dscores_ref,
    dq_ref, dq_send_ref, own_part_ref, window_ref, held_ref, sem,
):
    core = place_ref[0]
    tokens = q_ref.shape[1]
    kv_heads, kv_width, group = unit_sizes(q_ref, own_ref)
    scale = HEAD_SIZE ** (-0.5)
    reach = (STEPS + 1) * tokens
    pair = 2 * tokens
    for n, source in enumerate((far_ref, near_ref, own_ref)):
        window_ref[n * pair : (n + 1) * pair, :] = source[:, :kv_width]
    store = pltpu.make_async_copy(held_ref, dq_ref.at[core], sem)
    for unit, target in ((1, dq_send_ref), (0, held_ref)):
        first = unit * tokens
        before = 2 * pair - first
        sources = (q_ref.at[core], do_ref.at[core])
        if unit == 1:
            sources = (rows_ref.at[0], rows_ref.at[1])
        for g in range(kv_heads):
            keys = window_ref[first : first + reach, g * HEAD_SIZE : (g + 1) * HEAD_SIZE]
            dq_t = dot(keys.T, dscores_ref[unit, g]) * scale
            dq = dq_t.astype(jnp.bfloat16).T
            for a in range(group):
                column = (g * group + a) * HEAD_SIZE
                target[:, column : column + HEAD_SIZE] = dq[a * tokens : (a + 1) * tokens]
            q, do = (stack_heads(r, g * group, group) for r in sources)
            at = (g * HEAD_SIZE, kv_width + g * HEAD_SIZE)
            for part, column in (
                (dot(dscores_ref[unit, g, before:, :], q) * scale, at[0]),
                (dot(probs_ref[unit, g, before:, :], do), at[1]),
            ):
                columns = slice(column, column + HEAD_SIZE)
                if unit == 1:
                    own_part_ref[:, columns] = part
                else:
                    own_part_ref[:tokens, columns] += part
    store.start()
    store.wait()


def fill_kernel(core_ref, rows_ref, held_ref, out_ref, sem):
    copy = pltpu.make_async_copy(rows_ref, out_ref.at[1 - core_ref[0]], sem)
    copy.start()
    copy.wait()


def shards(query, key, value, out_grad, attn_out, doc_start):
    count = lax.axis_size("ctx")
    index = lax.axis_index("ctx")
    _, slots, tokens, width = query.shape
    kv_width = key.shape[-1]
    pair_width = 2 * kv_width
    pair = 2 * tokens
    core = (index % 2).astype(jnp.int32)
    stage = jnp.where(core == 0, index // 2, count - 1 - index // 2).astype(jnp.int32)
    core = core[None]
    place = jnp.stack([core[0], stage * pair])
    holder = [2 * s if 2 * s < count else 2 * count - 1 - 2 * s for s in range(count)]
    swap = [(i, i ^ 1) for i in range(count)]

    def shift(x, by):
        moves = [
            (holder[s], holder[s + by]) for s in range(count) if 0 <= s + by < count
        ]
        return lax.ppermute(x, "ctx", moves)

    bf16 = jnp.bfloat16
    keep, send = pl.pallas_call(
        pack_pair_kernel,
        out_shape=(
            jax.ShapeDtypeStruct((tokens, pair_width), bf16),
            jax.ShapeDtypeStruct((tokens + CODE_ROWS, pair_width), bf16),
        ),
        in_specs=[SMEM, VMEM, ANY, ANY],
        out_specs=(VMEM, VMEM),
        scratch_shapes=[
            pltpu.VMEM((2, slots, tokens, kv_width), bf16),
            pltpu.SemaphoreType.DMA((2,)),
        ],
        name="pack_pair",
    )(core, doc_start[0], key[0], value[0])
    coded = lax.ppermute(send, "ctx", swap)
    rows_send = pl.pallas_call(
        pack_rows_kernel,
        out_shape=jax.ShapeDtypeStruct((3, tokens, width), bf16),
        in_specs=[SMEM, ANY, ANY, ANY, ANY],
        out_specs=VMEM,
        scratch_shapes=[pltpu.SemaphoreType.DMA((3,))],
        name="pack_rows",
    )(core, query[0], out_grad[0], attn_out[0], keep)
    coded, rows_send = lax.optimization_barrier((coded, rows_send))
    own = jnp.concatenate([keep, coded[:tokens]], axis=0)
    far = shift(own, 2)
    near = shift(own, 1)
    rows = lax.ppermute(rows_send, "ctx", swap)
    reach = (STEPS + 1) * tokens
    kv_heads = kv_width // HEAD_SIZE
    lanes = tokens * (width // kv_width)
    held = jax.ShapeDtypeStruct((slots, kv_heads, reach, lanes), bf16)
    far_part, near_part, probs, dscores = pl.pallas_call(
        scores_kernel,
        out_shape=(
            jax.ShapeDtypeStruct((pair, pair_width), bf16),
            jax.ShapeDtypeStruct((pair, pair_width), bf16),
            held,
            held,
        ),
        in_specs=[SMEM] + [VMEM] * 9,
        out_specs=(VMEM,) * 4,
        scratch_shapes=[
            pltpu.VMEM((3 * pair, pair_width), bf16),
            pltpu.VMEM((2 * pair, pair_width), jnp.float32),
        ],
        compiler_params=PARAMS,
        name="scores",
    )(
        place, doc_start[0], query[0], out_grad[0], attn_out[0], rows, coded, far, near, own
    )
    from_far = shift(far_part, -2)
    from_near = shift(near_part, -1)
    dq, dq_send, own_part = pl.pallas_call(
        rest_kernel,
        out_shape=(
            jax.ShapeDtypeStruct((slots, tokens, width), bf16),
            jax.ShapeDtypeStruct((tokens, width), bf16),
            jax.ShapeDtypeStruct((pair, pair_width), jnp.float32),
        ),
        in_specs=[SMEM] + [VMEM] * 8,
        out_specs=(ANY, VMEM, VMEM),
        scratch_shapes=[
            pltpu.VMEM((3 * pair, kv_width), bf16),
            pltpu.VMEM((tokens, width), bf16),
            pltpu.SemaphoreType.DMA,
        ],
        compiler_params=PARAMS,
        name="rest",
    )(place, query[0], out_grad[0], rows, far, near, own, probs, dscores)
    dq_rows = lax.ppermute(dq_send, "ctx", swap)
    dq = pl.pallas_call(
        fill_kernel,
        out_shape=jax.ShapeDtypeStruct(dq.shape, bf16),
        in_specs=[SMEM, VMEM, ANY],
        out_specs=ANY,
        scratch_shapes=[pltpu.SemaphoreType.DMA],
        input_output_aliases={2: 0},
        name="fill_rows",
    )(core, dq_rows, dq)
    total = own_part + from_near.astype(jnp.float32) + from_far.astype(jnp.float32)
    total = total.astype(bf16)
    kept = total[:tokens]
    given = lax.ppermute(total[tokens:], "ctx", swap)
    both = jnp.where(core == 0, jnp.stack([kept, given]), jnp.stack([given, kept]))
    return dq[None], both[None, ..., :kv_width], both[None, ..., kv_width:]


def solution(mesh):
    placed = (P("ctx", "dp", None, None),) * 5 + (P("ctx", "dp", None),)
    return jax.shard_map(
        shards,
        mesh=mesh,
        in_specs=placed,
        out_specs=(P("ctx", "dp", None, None),) * 3,
        check_vma=False,
    )
```

time: 69.3 us -> 36.6 us (0.53)
  Pallas kernels: 40.6 us -> 11 us
  waiting for transfers between devices: 8.8 us -> 5.75 us
    pallas_call x1, Pallas kernels: 25 us -> 2.15 us  [shards(): pl.pallas_call(pack_rows_kernel, out_shape=jax.ShapeDtypeStruct((3, token...]
    pallas_call x1, Pallas kernels: 9.05 us -> 1.66 us  [shards(): pl.pallas_call(fill_kernel, out_shape=jax.ShapeDtypeStruct(dq.shape, bf16...]
    ppermute x4, waiting for transfers between devices: 6.84 us -> 4.93 us  [shift(): return lax.ppermute(x, 'ctx', moves)]
    ppermute x1, waiting for transfers between devices: 1.13 us -> 0.01 us  [shards(): coded = lax.ppermute(send, 'ctx', swap)]
    pallas_call x1 -> x2, Pallas kernels: 4.41 us -> 4.99 us  [the longest x1 2.95 us: shards(): pl.pallas_call(scores_kernel, out_shape=(jax.ShapeDtypeStruct((pair, pair...]
  transfers between devices with their start and end apart: 8 -> 8, of which waited for: 5 -> 3; matrix products, arithmetic and copies ran while one was open for 1% -> 2% of each run, Pallas kernels for 0% -> 12%
where the time goes in v3:
time: 36.6 us; the launch traced here: 35.9 us
  starting transfers between devices  16.8 us (46%)
  Pallas kernels  11 us (30%)
  waiting for transfers between devices  5.75 us (16%)
  local copies, waits for them, and re-layouts  1.41 us (4%)
  between operations  0.82 us (2%)
    ppermute x4, starting transfers between devices, shift(): return lax.ppermute(x, 'ctx', moves)  11.7 us
    ppermute x4, waiting for transfers between devices, shift(): return lax.ppermute(x, 'ctx', moves)  4.93 us
    ppermute x1, starting transfers between devices, shards(): given = lax.ppermute(total[tokens:], 'ctx', swap)  4.11 us
    pallas_call x1, Pallas kernels, shards(): pl.pallas_call(scores_kernel, out_shape=(jax.ShapeDtypeStruct((pair, pair...  2.95 us
    pallas_call x1, Pallas kernels, shards(): pl.pallas_call(pack_pair_kernel, out_shape=(jax.ShapeDtypeStruct((tokens,...  2.23 us
    pallas_call x1, Pallas kernels, shards(): pl.pallas_call(pack_rows_kernel, out_shape=jax.ShapeDtypeStruct((3, token...  2.15 us
    pallas_call x1, Pallas kernels, shards(): pl.pallas_call(rest_kernel, out_shape=(jax.ShapeDtypeStruct((slots, token...  2.04 us
    pallas_call x1, Pallas kernels, shards(): pl.pallas_call(fill_kernel, out_shape=jax.ShapeDtypeStruct(dq.shape, bf16...  1.66 us
  transfers between devices with their start and end apart: 8, of which 3 were waited for; matrix products, arithmetic and copies ran while one was open for 2% of the time, Pallas kernels for 12%

profile of v3, /device:TPU:13, one launch (start us, length us, event | category | flops | bytes accessed | tf_op | source)
XLA Modules:
  0.0 35.9 jit_solution(15029607040264167108)
XLA Ops:
  0.6 2.2 %pack_pair.1 = (bf16[64,512]{1,0:T(8,128)(2,1)}, bf16[80,512]{1,0:T(8,128)(2,1)}) custom-call(s32[1]{0:T(128)} %bitcast.core_ref, s32[2,64]{1,0:T(2,128)} %bitcast.25, bf16[2,64,256]{2,1,0:T(8,128)(2,1)} %bitcast.28, bf16[2,64,256]{2,1,0:T(8,128)(2,1)} %bitcast.29), custom_call_target="tpu_custom_call" | custom-call | tf_op jit(solution)/shard_map/pack_pair/pallas_call | solution.py:211
  2.9 0.0 copy-start.5
  2.9 0.7 %collective-permute-start = (bf16[80,512]{1,0:T(8,128)(2,1)}, bf16[80,512]{1,0:T(8,128)(2,1)S(1)}, u32[]{:S(2)}, u32[]{:S(2)}) collective-permute-start(bf16[80,512]{1,0:T(8,128)(2,1)} %get-tuple-element.14), channel_id=1, source_target_pairs={{0,4},{4,0},{8,12},{12,8},{16,20},{20,16},{24,28},{28,24},{1,5},{5... | collective-permute-start | bytes 245768 | tf_op jit(solution)/shard_map/ppermute | solution.py:225
  3.6 0.0 copy-start
  3.6 0.0 copy-start.1
  3.6 0.0 copy-start.2
  3.6 0.0 copy-start.3
  3.6 2.1 %pack_rows.1 = bf16[3,64,2048]{2,1,0:T(8,128)(2,1)} custom-call(s32[1]{0:T(128)} %bitcast.core_ref, bf16[2,64,2048]{2,1,0:T(8,128)(2,1)} %bitcast.17, bf16[2,64,2048]{2,1,0:T(8,128)(2,1)} %bitcast.20, bf16[2,64,2048]{2,1,0:T(8,128)(2,1)} %bitcast.23, bf16[64,512]{1,0:T(8,128)(2,1)} %get-tuple-element.15.after_ref), custom_call_target="tpu_custom_call" | custom-call | tf_op jit(solution)/shard_map/pack_rows/pallas_call | solution.py:226
  5.8 0.0 collective-permute-done.coded_ref
  5.8 0.1 collective-permute-start.1
  5.9 0.0 copy-done.5
  6.0 1.3 %collective-permute-start.2 = (bf16[128,512]{1,0:T(8,128)(2,1)S(1)}, bf16[128,512]{1,0:T(8,128)(2,1)S(1)}, u32[]{:S(2)}, u32[]{:S(2)}) collective-permute-start(bf16[128,512]{1,0:T(8,128)(2,1)S(1)} %pad_maximum_fusion.own_ref), channel_id=1, source_target_pairs={{0,16},{8,24},{16,28},{24,20},{28,12},{20,4},{1,17},{9,25},{17,29}... | collective-permute-start | bytes 393224 | tf_op jit(solution)/shard_map/ppermute | solution.py:208
  7.3 2.1 %collective-permute-start.3 = (bf16[128,512]{1,0:T(8,128)(2,1)S(1)}, bf16[128,512]{1,0:T(8,128)(2,1)S(1)}, u32[]{:S(2)}, u32[]{:S(2)}) collective-permute-start(bf16[128,512]{1,0:T(8,128)(2,1)S(1)} %pad_maximum_fusion.own_ref), channel_id=1, source_target_pairs={{0,8},{8,16},{16,24},{24,28},{28,20},{20,12},{12,4},{1,9},{9,17},{... | collective-permute-start | bytes 393224 | tf_op jit(solution)/shard_map/ppermute | solution.py:208
  9.4 0.1 pad_add_fusion.place_ref
  9.4 3.9 %collective-permute-done.2.far_ref = bf16[128,512]{1,0:T(8,128)(2,1)S(1)} collective-permute-done((bf16[128,512]{1,0:T(8,128)(2,1)S(1)}, bf16[128,512]{1,0:T(8,128)(2,1)S(1)}, u32[]{:S(2)}, u32[]{:S(2)}) %collective-permute-start.2) | collective-permute-done | bytes 131104 | tf_op jit(solution)/shard_map/ppermute | solution.py:208
  13.3 1.0 %collective-permute-done.3.near_ref = bf16[128,512]{1,0:T(8,128)(2,1)S(1)} collective-permute-done((bf16[128,512]{1,0:T(8,128)(2,1)S(1)}, bf16[128,512]{1,0:T(8,128)(2,1)S(1)}, u32[]{:S(2)}, u32[]{:S(2)}) %collective-permute-start.3) | collective-permute-done | bytes 131104 | tf_op jit(solution)/shard_map/ppermute | solution.py:208
  14.4 0.0 collective-permute-done.1.rows_ref
  14.4 0.0 copy-done
  14.4 0.0 copy-done.1
  14.4 0.0 copy-done.2
  14.4 0.0 copy-done.3
  14.4 2.9 %scores.1 = (bf16[128,512]{1,0:T(8,128)(2,1)S(1)}, bf16[128,512]{1,0:T(8,128)(2,1)S(1)}, bf16[2,2,320,512]{3,2,1,0:T(8,128)(2,1)S(1)}, bf16[2,2,320,512]{3,2,1,0:T(8,128)(2,1)S(1)}) custom-call(s32[2]{0:T(128)S(1)} %pad_add_fusion.place_ref, s32[2,64]{1,0:T(2,128)S(1)} %bitcast.26, bf16[2,64,2048]{2,1,0:T(8,128)(2,1)S(1)} %bitcast.18, ...), custom_call_target="tpu_custom_call" | custom-call | tf_op jit(solution)/shard_map/scores/pallas_call | solution.py:243
  17.3 3.2 %collective-permute-start.5 = (bf16[128,512]{1,0:T(8,128)(2,1)S(1)}, bf16[128,512]{1,0:T(8,128)(2,1)S(1)}, u32[]{:S(2)}, u32[]{:S(2)}) collective-permute-start(bf16[128,512]{1,0:T(8,128)(2,1)S(1)} %get-tuple-element.23), channel_id=1, source_target_pairs={{8,0},{16,8},{24,16},{28,24},{20,28},{12,20},{4,12},{9,1},{17,9},{... | collective-permute-start | bytes 393224 | tf_op jit(solution)/shard_map/ppermute | solution.py:208
  20.5 5.2 %collective-permute-start.6 = (bf16[128,512]{1,0:T(8,128)(2,1)S(1)}, bf16[128,512]{1,0:T(8,128)(2,1)S(1)}, u32[]{:S(2)}, u32[]{:S(2)}) collective-permute-start(bf16[128,512]{1,0:T(8,128)(2,1)S(1)} %get-tuple-element.24), channel_id=1, source_target_pairs={{16,0},{24,8},{28,16},{20,24},{12,28},{4,20},{17,1},{25,9},{29,17}... | collective-permute-start | bytes 393224 | tf_op jit(solution)/shard_map/ppermute | solution.py:208
  25.7 2.0 %rest.1 = (bf16[2,64,2048]{2,1,0:T(8,128)(2,1)}, bf16[64,2048]{1,0:T(8,128)(2,1)S(1)}, f32[128,512]{1,0:T(8,128)S(1)}) custom-call(s32[2]{0:T(128)S(1)} %pad_add_fusion.place_ref, bf16[2,64,2048]{2,1,0:T(8,128)(2,1)S(1)} %bitcast.19, bf16[2,64,2048]{2,1,0:T(8,128)(2,1)S(1)} %bitcast.22, bf16[3,64,2048]{2,1,0:T(8,128)(2,1)S(1)} %collective-permute-done.1.rows_ref, ...), custom_call_target="tpu_custom_call" | custom-call | tf_op jit(solution)/shard_map/rest/pallas_call | solution.py:264
  27.8 0.0 collective-permute-done.5
  27.8 0.0 collective-permute-done.6
  27.9 4.1 %collective-permute-start.7 = (bf16[64,512]{1,0:T(8,128)(2,1)S(1)}, bf16[64,512]{1,0:T(8,128)(2,1)S(1)}, u32[]{:S(2)}, u32[]{:S(2)}) collective-permute-start(bf16[64,512]{1,0:T(8,128)(2,1)S(1)} %get-tuple-element.28), channel_id=1, source_target_pairs={{0,4},{4,0},{8,12},{12,8},{16,20},{20,16},{24,28},{28,24},{1,5},{5... | collective-permute-start | bytes 196616 | tf_op jit(solution)/shard_map/ppermute | solution.py:294
  32.0 0.1 collective-permute-start.4
  32.1 0.8 %collective-permute-done.7 = bf16[64,512]{1,0:T(8,128)(2,1)S(1)} collective-permute-done((bf16[64,512]{1,0:T(8,128)(2,1)S(1)}, bf16[64,512]{1,0:T(8,128)(2,1)S(1)}, u32[]{:S(2)}, u32[]{:S(2)}) %collective-permute-start.7) | collective-permute-done | bytes 65568 | tf_op jit(solution)/shard_map/ppermute | solution.py:294
  32.9 0.7 %slice_bitcast_fusion = (bf16[1,2,64,256]{3,2,1,0:T(8,128)(2,1)}, bf16[1,2,64,256]{3,2,1,0:T(8,128)(2,1)}) fusion(bf16[2,64,512]{2,1,0:T(8,128)(2,1)S(1)} %maximum_select_fusion), kind=kLoop, calls=%fused_computation.3 | loop fusion | bytes 262144 | tf_op jit(solution)/shard_map/broadcast_in_dim | solution.py:296
  33.5 0.0 collective-permute-done.4.rows_ref
  33.6 0.0 copy-start.4
  33.6 0.7 %copy-done.4 = bf16[64,2048]{1,0:T(8,128)(2,1)} copy-done((bf16[64,2048]{1,0:T(8,128)(2,1)}, bf16[64,2048]{1,0:T(8,128)(2,1)S(1)}, u32[]{:S(2)}) %copy-start.4) | copy-done | bytes 262168
  34.3 1.7 %fill_rows.1 = bf16[2,64,2048]{2,1,0:T(8,128)(2,1)} custom-call(s32[1]{0:T(128)} %bitcast.core_ref, bf16[64,2048]{1,0:T(8,128)(2,1)} %copy-done.4, bf16[2,64,2048]{2,1,0:T(8,128)(2,1)} %get-tuple-element.21.held_ref), custom_call_target="tpu_custom_call", output_to_operand_aliasing={{}: (2, {})} | custom-call | tf_op jit(solution)/shard_map/fill_rows/pallas_call | solution.py:282
  (5 shorter events, 0.1 us)
Async XLA Ops:
  2.9 3.0 %copy-start.5 = (bf16[64,512]{1,0:T(8,128)(2,1)S(1)}, bf16[64,512]{1,0:T(8,128)(2,1)}, u32[]{:S(2)}) copy-start(bf16[64,512]{1,0:T(8,128)(2,1)} %get-tuple-element.15.after_ref) | copy-start | bytes 196612
  2.9 2.9 %collective-permute-start = (bf16[80,512]{1,0:T(8,128)(2,1)}, bf16[80,512]{1,0:T(8,128)(2,1)S(1)}, u32[]{:S(2)}, u32[]{:S(2)}) collective-permute-start(bf16[80,512]{1,0:T(8,128)(2,1)} %get-tuple-element.14), channel_id=1, source_target_pairs={{0,4},{4,0},{8,12},{12,8},{16,20},{20,16},{24,28},{28,24},{1,5},{5... | collective-permute-start | bytes 245768 | tf_op jit(solution)/shard_map/ppermute | solution.py:225
  3.6 10.7 %copy-start = (bf16[1,2,64,2048]{3,2,1,0:T(8,128)(2,1)S(1)}, bf16[1,2,64,2048]{3,2,1,0:T(8,128)(2,1)}, u32[]{:S(2)}) copy-start(bf16[1,2,64,2048]{3,2,1,0:T(8,128)(2,1)} %param.6) | copy-start | bytes 1572868
  3.6 10.7 %copy-start.1 = (bf16[1,2,64,2048]{3,2,1,0:T(8,128)(2,1)S(1)}, bf16[1,2,64,2048]{3,2,1,0:T(8,128)(2,1)}, u32[]{:S(2)}) copy-start(bf16[1,2,64,2048]{3,2,1,0:T(8,128)(2,1)} %param.9) | copy-start | bytes 1572868
  3.6 10.7 %copy-start.2 = (bf16[1,2,64,2048]{3,2,1,0:T(8,128)(2,1)S(1)}, bf16[1,2,64,2048]{3,2,1,0:T(8,128)(2,1)}, u32[]{:S(2)}) copy-start(bf16[1,2,64,2048]{3,2,1,0:T(8,128)(2,1)} %param.10) | copy-start | bytes 1572868
  3.6 10.7 %copy-start.3 = (s32[1,2,64]{2,1,0:T(2,128)S(1)}, s32[1,2,64]{2,1,0:T(2,128)}, u32[]{:S(2)}) copy-start(s32[1,2,64]{2,1,0:T(2,128)} %param.11) | copy-start | bytes 1540
  5.8 8.5 %collective-permute-start.1 = (bf16[3,64,2048]{2,1,0:T(8,128)(2,1)}, bf16[3,64,2048]{2,1,0:T(8,128)(2,1)S(1)}, u32[]{:S(2)}, u32[]{:S(2)}) collective-permute-start(bf16[3,64,2048]{2,1,0:T(8,128)(2,1)} %pack_rows.1), channel_id=1, source_target_pairs={{0,4},{4,0},{8,12},{12,8},{16,20},{20,16},{24,28},{28,24},{1,5},{5... | collective-permute-start | bytes 2359304 | tf_op jit(solution)/shard_map/ppermute | solution.py:238
  6.0 7.4 %collective-permute-start.2 = (bf16[128,512]{1,0:T(8,128)(2,1)S(1)}, bf16[128,512]{1,0:T(8,128)(2,1)S(1)}, u32[]{:S(2)}, u32[]{:S(2)}) collective-permute-start(bf16[128,512]{1,0:T(8,128)(2,1)S(1)} %pad_maximum_fusion.own_ref), channel_id=1, source_target_pairs={{0,16},{8,24},{16,28},{24,20},{28,12},{20,4},{1,17},{9,25},{17,29}... | collective-permute-start | bytes 393224 | tf_op jit(solution)/shard_map/ppermute | solution.py:208
  7.3 7.1 %collective-permute-start.3 = (bf16[128,512]{1,0:T(8,128)(2,1)S(1)}, bf16[128,512]{1,0:T(8,128)(2,1)S(1)}, u32[]{:S(2)}, u32[]{:S(2)}) collective-permute-start(bf16[128,512]{1,0:T(8,128)(2,1)S(1)} %pad_maximum_fusion.own_ref), channel_id=1, source_target_pairs={{0,8},{8,16},{16,24},{24,28},{28,20},{20,12},{12,4},{1,9},{9,17},{... | collective-permute-start | bytes 393224 | tf_op jit(solution)/shard_map/ppermute | solution.py:208
  17.3 10.4 %collective-permute-start.5 = (bf16[128,512]{1,0:T(8,128)(2,1)S(1)}, bf16[128,512]{1,0:T(8,128)(2,1)S(1)}, u32[]{:S(2)}, u32[]{:S(2)}) collective-permute-start(bf16[128,512]{1,0:T(8,128)(2,1)S(1)} %get-tuple-element.23), channel_id=1, source_target_pairs={{8,0},{16,8},{24,16},{28,24},{20,28},{12,20},{4,12},{9,1},{17,9},{... | collective-permute-start | bytes 393224 | tf_op jit(solution)/shard_map/ppermute | solution.py:208
  20.5 7.2 %collective-permute-start.6 = (bf16[128,512]{1,0:T(8,128)(2,1)S(1)}, bf16[128,512]{1,0:T(8,128)(2,1)S(1)}, u32[]{:S(2)}, u32[]{:S(2)}) collective-permute-start(bf16[128,512]{1,0:T(8,128)(2,1)S(1)} %get-tuple-element.24), channel_id=1, source_target_pairs={{16,0},{24,8},{28,16},{20,24},{12,28},{4,20},{17,1},{25,9},{29,17}... | collective-permute-start | bytes 393224 | tf_op jit(solution)/shard_map/ppermute | solution.py:208
  27.9 5.0 %collective-permute-start.7 = (bf16[64,512]{1,0:T(8,128)(2,1)S(1)}, bf16[64,512]{1,0:T(8,128)(2,1)S(1)}, u32[]{:S(2)}, u32[]{:S(2)}) collective-permute-start(bf16[64,512]{1,0:T(8,128)(2,1)S(1)} %get-tuple-element.28), channel_id=1, source_target_pairs={{0,4},{4,0},{8,12},{12,8},{16,20},{20,16},{24,28},{28,24},{1,5},{5... | collective-permute-start | bytes 196616 | tf_op jit(solution)/shard_map/ppermute | solution.py:294
  32.0 1.6 %collective-permute-start.4 = (bf16[64,2048]{1,0:T(8,128)(2,1)S(1)}, bf16[64,2048]{1,0:T(8,128)(2,1)S(1)}, u32[]{:S(2)}, u32[]{:S(2)}) collective-permute-start(bf16[64,2048]{1,0:T(8,128)(2,1)S(1)} %get-tuple-element.20), channel_id=1, source_target_pairs={{0,4},{4,0},{8,12},{12,8},{16,20},{20,16},{24,28},{28,24},{1,5},{5... | collective-permute-start | bytes 786440 | tf_op jit(solution)/shard_map/ppermute | solution.py:281
  33.6 0.7 %copy-start.4 = (bf16[64,2048]{1,0:T(8,128)(2,1)}, bf16[64,2048]{1,0:T(8,128)(2,1)S(1)}, u32[]{:S(2)}) copy-start(bf16[64,2048]{1,0:T(8,128)(2,1)S(1)} %collective-permute-done.4.rows_ref) | copy-start | bytes 786436

commit v4 on v3

v4 whole, which is shorter than its diff:
```python
import jax
import jax.numpy as jnp
from jax import lax
from jax.experimental import pallas as pl
from jax.experimental.pallas import tpu as pltpu
from jax.sharding import PartitionSpec as P

HEAD_SIZE = 128
STEPS = 4
LOG2E = 1.4426950408889634
CONTRACT_LAST = (((1,), (1,)), ((), ()))
CONTRACT_ROWS = (((1,), (0,)), ((), ()))
VMEM = pl.BlockSpec(memory_space=pltpu.VMEM)
SMEM = pl.BlockSpec(memory_space=pltpu.SMEM)
HBM = pl.BlockSpec(memory_space=pltpu.HBM)
PARAMS = pltpu.CompilerParams(vmem_limit_bytes=24 * 2**20)
SMALL = pltpu.CompilerParams(vmem_limit_bytes=4 * 2**20)


def dot(a, b, dims=CONTRACT_ROWS):
    return lax.dot_general(a, b, dims, preferred_element_type=jnp.float32)


def stack_heads(ref, first, count):
    return jnp.concatenate(
        [ref[:, (first + a) * HEAD_SIZE : (first + a + 1) * HEAD_SIZE] for a in range(count)],
        axis=0,
    )


def attend(q, do, o, keys, values, low, high, scale):
    scores = dot(keys, q, CONTRACT_LAST) * (scale * LOG2E)
    row = lax.broadcasted_iota(jnp.int32, scores.shape, 0)
    scores = jnp.where((row >= low) & (row <= high), scores, -jnp.inf)
    top = jnp.max(scores, axis=0, keepdims=True)
    weights = jnp.exp2(scores - top)
    probs = weights * (1.0 / jnp.sum(weights, axis=0, keepdims=True))
    terms = do.astype(jnp.float32) * o.astype(jnp.float32)
    coarse = terms.astype(jnp.bfloat16)
    fine = (terms - coarse.astype(jnp.float32)).astype(jnp.bfloat16)
    ones = jnp.ones((8, 2 * HEAD_SIZE), jnp.bfloat16)
    delta = dot(ones, jnp.concatenate([coarse, fine], axis=1), CONTRACT_LAST)[:1]
    dprobs = dot(values, do, CONTRACT_LAST)
    dscores = (probs * (dprobs - delta)).astype(jnp.bfloat16)
    return probs.astype(jnp.bfloat16), dscores


def unit_sizes(rows_ref, pair_ref):
    heads = rows_ref.shape[-1] // HEAD_SIZE
    kv_width = pair_ref.shape[-1] // 2
    kv_heads = kv_width // HEAD_SIZE
    return kv_heads, kv_width, heads // kv_heads


def scores_kernel(
    place_ref, starts_ref, q_ref, do_ref, o_ref, starts_in_ref, q_in_ref, do_in_ref, o_in_ref,
    far_ref, near_ref, own_ref, far_part_ref, near_part_ref, probs_ref, dscores_ref,
    window_ref, part_ref,
):
    core, begin = place_ref[0], place_ref[1]
    tokens = q_ref.shape[1]
    kv_heads, kv_width, group = unit_sizes(q_ref, own_ref)
    scale = HEAD_SIZE ** (-0.5)
    reach = (STEPS + 1) * tokens
    pair = 2 * tokens
    for n, source in enumerate((far_ref, near_ref, own_ref)):
        window_ref[n * pair : (n + 1) * pair, :] = source[...]
    offset = lax.broadcasted_iota(jnp.int32, (1, tokens), 1)
    sides = ((starts_ref, q_ref, do_ref, o_ref), (starts_in_ref, q_in_ref, do_in_ref, o_in_ref))
    for unit, (starts_side, *sources) in enumerate(sides):
        starts = jnp.where(core == 0, starts_side[0:1, :], starts_side[1:2, :])
        first = unit * tokens
        low = jnp.maximum(offset + 1, starts - (begin + (unit - STEPS) * tokens))
        high = offset + STEPS * tokens
        low = jnp.concatenate([low] * group, axis=1)
        high = jnp.concatenate([high] * group, axis=1)
        for g in range(kv_heads):
            at = (g * HEAD_SIZE, kv_width + g * HEAD_SIZE)
            keys = window_ref[first : first + reach, at[0] : at[0] + HEAD_SIZE]
            values = window_ref[first : first + reach, at[1] : at[1] + HEAD_SIZE]
            q, do, o = (stack_heads(r.at[core], g * group, group) for r in sources)
            probs, dscores = attend(q, do, o, keys, values, low, high, scale)
            probs_ref[unit, g] = probs
            dscores_ref[unit, g] = dscores
            before = 2 * pair - first
            for part, column in (
                (dot(dscores[:before], q) * scale, at[0]),
                (dot(probs[:before], do), at[1]),
            ):
                columns = slice(column, column + HEAD_SIZE)
                if unit == 0:
                    part_ref[:before, columns] = part
                else:
                    part_ref[first : 2 * pair, columns] += part
    far_part_ref[...] = part_ref[:pair, :].astype(jnp.bfloat16)
    near_part_ref[...] = part_ref[pair:, :].astype(jnp.bfloat16)


def rest_kernel(
    place_ref, q_ref, do_ref, q_in_ref, do_in_ref, far_ref, near_ref, own_ref, probs_ref,
    dscores_ref, dq_ref, dq_send_ref, own_part_ref, window_ref, held_ref, sem,
):
    core = place_ref[0]
    tokens = q_ref.shape[1]
    kv_heads, kv_width, group = unit_sizes(q_ref, own_ref)
    scale = HEAD_SIZE ** (-0.5)
    reach = (STEPS + 1) * tokens
    pair = 2 * tokens
    for n, source in enumerate((far_ref, near_ref, own_ref)):
        window_ref[n * pair : (n + 1) * pair, :] = source[:, :kv_width]
    store = pltpu.make_async_copy(held_ref, dq_ref.at[core], sem)
    sides = ((1, dq_send_ref, q_in_ref, do_in_ref), (0, held_ref, q_ref, do_ref))
    for unit, target, *sources in sides:
        first = unit * tokens
        before = 2 * pair - first
        for g in range(kv_heads):
            keys = window_ref[first : first + reach, g * HEAD_SIZE : (g + 1) * HEAD_SIZE]
            dq_t = dot(keys.T, dscores_ref[unit, g]) * scale
            dq = dq_t.astype(jnp.bfloat16).T
            for a in range(group):
                column = (g * group + a) * HEAD_SIZE
                target[:, column : column + HEAD_SIZE] = dq[a * tokens : (a + 1) * tokens]
            if unit == 0 and g == kv_heads - 1:
                store.start()
            q, do = (stack_heads(r.at[core], g * group, group) for r in sources)
            at = (g * HEAD_SIZE, kv_width + g * HEAD_SIZE)
            for part, column in (
                (dot(dscores_ref[unit, g, before:, :], q) * scale, at[0]),
                (dot(probs_ref[unit, g, before:, :], do), at[1]),
            ):
                columns = slice(column, column + HEAD_SIZE)
                if unit == 1:
                    own_part_ref[:, columns] = part
                else:
                    own_part_ref[:tokens, columns] += part
    store.wait()


def store_kernel(
    core_ref, rows_ref, kept_ref, given_ref, held_ref, dq_ref, key_ref, value_ref, sems
):
    core = core_ref[0]
    width = key_ref.shape[-1]
    copies = [pltpu.make_async_copy(rows_ref, dq_ref.at[1 - core], sems.at[0, 0])]
    for n, (source, slot) in enumerate(((kept_ref, core), (given_ref, 1 - core))):
        for m, target in enumerate((key_ref, value_ref)):
            copies.append(
                pltpu.make_async_copy(
                    source.at[:, pl.ds(m * width, width)], target.at[slot], sems.at[n + 1, m]
                )
            )
    for copy in copies:
        copy.start()
    for copy in copies:
        copy.wait()


def shards(query, key, value, out_grad, attn_out, doc_start):
    count = lax.axis_size("ctx")
    index = lax.axis_index("ctx")
    _, slots, tokens, width = query.shape
    kv_width = key.shape[-1]
    pair_width = 2 * kv_width
    pair = 2 * tokens
    core = (index % 2).astype(jnp.int32)
    stage = jnp.where(core == 0, index // 2, count - 1 - index // 2).astype(jnp.int32)
    core = core[None]
    place = jnp.stack([core[0], stage * pair])
    holder = [2 * s if 2 * s < count else 2 * count - 1 - 2 * s for s in range(count)]
    swap = [(i, i ^ 1) for i in range(count)]

    def shift(x, by):
        moves = [
            (holder[s], holder[s + by]) for s in range(count) if 0 <= s + by < count
        ]
        return lax.ppermute(x, "ctx", moves)

    bf16 = jnp.bfloat16
    def swapped(x):
        return lax.ppermute(x, "ctx", swap)

    def mine(x):
        return jnp.where(core == 0, x[0], x[1])

    starts_in, key_in, value_in = (swapped(x[0]) for x in (doc_start, key, value))
    sides = ((key[0], value[0]), (key_in, value_in))
    own = jnp.concatenate(
        [jnp.concatenate([mine(x) for x in side], axis=-1) for side in sides], axis=0
    )
    own, starts_in, *late = lax.optimization_barrier(
        (own, starts_in, query, out_grad, attn_out)
    )
    sent = [starts_in] + [swapped(x[0]) for x in late]
    far = shift(own, 2)
    near = shift(own, 1)
    reach = (STEPS + 1) * tokens
    kv_heads = kv_width // HEAD_SIZE
    lanes = tokens * (width // kv_width)
    products = 2 * slots * tokens * reach * width

    def work(flops, moved):
        return pl.CostEstimate(flops=flops, bytes_accessed=moved, transcendentals=0)

    held = jax.ShapeDtypeStruct((slots, kv_heads, reach, lanes), bf16)
    far_part, near_part, probs, dscores = pl.pallas_call(
        scores_kernel,
        out_shape=(
            jax.ShapeDtypeStruct((pair, pair_width), bf16),
            jax.ShapeDtypeStruct((pair, pair_width), bf16),
            held,
            held,
        ),
        in_specs=[SMEM] + [VMEM] * 11,
        out_specs=(VMEM,) * 4,
        scratch_shapes=[
            pltpu.VMEM((3 * pair, pair_width), bf16),
            pltpu.VMEM((2 * pair, pair_width), jnp.float32),
        ],
        compiler_params=PARAMS,
        cost_estimate=work(3 * products, 12 * 2**20),
        name="scores",
    )(place, doc_start[0], query[0], out_grad[0], attn_out[0], *sent, far, near, own)
    from_far = shift(far_part, -2)
    from_near = shift(near_part, -1)
    dq, dq_send, own_part = pl.pallas_call(
        rest_kernel,
        out_shape=(
            jax.ShapeDtypeStruct((slots, tokens, width), bf16),
            jax.ShapeDtypeStruct((tokens, width), bf16),
            jax.ShapeDtypeStruct((pair, pair_width), jnp.float32),
        ),
        in_specs=[SMEM] + [VMEM] * 9,
        out_specs=(HBM, VMEM, VMEM),
        scratch_shapes=[
            pltpu.VMEM((3 * pair, kv_width), bf16),
            pltpu.VMEM((tokens, width), bf16),
            pltpu.SemaphoreType.DMA,
        ],
        compiler_params=PARAMS,
        cost_estimate=work(3 * products // 2, 8 * 2**20),
        name="rest",
    )(place, query[0], out_grad[0], *sent[1:3], far, near, own, probs, dscores)
    from_near, from_far, dq_send = lax.optimization_barrier((from_near, from_far, dq_send))
    dq_rows = swapped(dq_send)
    total = own_part + from_near.astype(jnp.float32) + from_far.astype(jnp.float32)
    total = total.astype(bf16)
    kept = total[:tokens]
    given = swapped(total[tokens:])
    dq, dk, dv = pl.pallas_call(
        store_kernel,
        out_shape=(
            jax.ShapeDtypeStruct(dq.shape, bf16),
            jax.ShapeDtypeStruct((slots, tokens, kv_width), bf16),
            jax.ShapeDtypeStruct((slots, tokens, kv_width), bf16),
        ),
        in_specs=[SMEM, VMEM, VMEM, VMEM, HBM],
        out_specs=(HBM,) * 3,
        scratch_shapes=[pltpu.SemaphoreType.DMA((3, 2))],
        input_output_aliases={4: 0},
        compiler_params=SMALL,
        name="store",
    )(core, dq_rows, kept, given, dq)
    return dq[None], dk[None], dv[None]


def solution(mesh):
    placed = (P("ctx", "dp", None, None),) * 5 + (P("ctx", "dp", None),)
    return jax.shard_map(
        shards,
        mesh=mesh,
        in_specs=placed,
        out_specs=(P("ctx", "dp", None, None),) * 3,
        check_vma=False,
    )
```

time: 36.6 us -> 36 us (0.984)
  Pallas kernels: 11 us -> 5.78 us
  local copies, waits for them, and re-layouts: 1.41 us -> 3.82 us
  other arithmetic: 0.15 us -> 0.97 us
  starting transfers between devices: 16.8 us -> 17.6 us
  waiting for transfers between devices: 5.75 us -> 6.34 us
    pallas_call x3 -> x1, Pallas kernels: 6.04 us -> 0.79 us  [shards(): pl.pallas_call(store_kernel, out_shape=(jax.ShapeDtypeStruct(dq.shape, bf...]
    unnamed x12, local copies, waits for them, and re-layouts: 0.73 us -> 3.8 us
    ppermute x4 -> x8, starting transfers between devices: 5.04 us -> 5.92 us  [swapped(): return lax.ppermute(x, 'ctx', swap)]
    select_n x1 -> x3, other arithmetic: 0.01 us -> 0.83 us  [mine(): return jnp.where(core == 0, x[0], x[1])]
    broadcast_in_dim x1 -> x0, local copies, waits for them, and re-layouts: 0.66 us -> none  [shards(): return (dq[None], both[None, ..., :kv_width], both[None, ..., kv_width:])]
    ppermute x4 -> x8, waiting for transfers between devices: 0.83 us -> 1.41 us  [swapped(): return lax.ppermute(x, 'ctx', swap)]
  transfers between devices with their start and end apart: 8 -> 12, of which waited for: 3 -> 5; matrix products, arithmetic and copies ran while one was open for 2% -> 3% of each run, Pallas kernels for 12% -> 6%
where the time goes in v4:
time: 36 us; the launch traced here: 35.4 us
  starting transfers between devices  17.6 us (49%)
  waiting for transfers between devices  6.34 us (18%)
  Pallas kernels  5.78 us (16%)
  local copies, waits for them, and re-layouts  3.82 us (11%)
  other arithmetic  0.97 us (3%)
  between operations  0.79 us (2%)
    ppermute x4, starting transfers between devices, shift(): return lax.ppermute(x, 'ctx', moves)  11.7 us
    ppermute x8, starting transfers between devices, swapped(): return lax.ppermute(x, 'ctx', swap)  5.92 us
    ppermute x4, waiting for transfers between devices, shift(): return lax.ppermute(x, 'ctx', moves)  4.93 us
    unnamed x12, local copies, waits for them, and re-layouts  3.8 us
    pallas_call x1, Pallas kernels, shards(): pl.pallas_call(scores_kernel, out_shape=(jax.ShapeDtypeStruct((pair, pair...  2.95 us
    pallas_call x1, Pallas kernels, shards(): pl.pallas_call(rest_kernel, out_shape=(jax.ShapeDtypeStruct((slots, token...  2.04 us
    ppermute x8, waiting for transfers between devices, swapped(): return lax.ppermute(x, 'ctx', swap)  1.41 us
    select_n x3, other arithmetic, mine(): return jnp.where(core == 0, x[0], x[1])  0.83 us
  transfers between devices with their start and end apart: 12, of which 5 were waited for; matrix products, arithmetic and copies ran while one was open for 3% of the time, Pallas kernels for 6%

profile of v4, /device:TPU:13, one launch (start us, length us, event | category | flops | bytes accessed | tf_op | source)
XLA Modules:
  0.0 35.4 jit_solution(13953563296539663950)
XLA Ops:
  0.6 0.7 %collective-permute-start.1 = (bf16[2,64,256]{2,1,0:T(8,128)(2,1)}, bf16[2,64,256]{2,1,0:T(8,128)(2,1)S(1)}, u32[]{:S(2)}, u32[]{:S(2)}) collective-permute-start(bf16[2,64,256]{2,1,0:T(8,128)(2,1)} %bitcast.34), channel_id=1, source_target_pairs={{0,4},{4,0},{8,12},{12,8},{16,20},{20,16},{24,28},{28,24},{1,5},{5... | collective-permute-start | bytes 196616 | tf_op jit(solution)/shard_map/ppermute | solution.py:180
  1.4 0.1 collective-permute-start
  1.4 0.4 %collective-permute-start.2 = (s32[2,64]{1,0:T(2,128)}, s32[2,64]{1,0:T(2,128)S(1)}, u32[]{:S(2)}, u32[]{:S(2)}) collective-permute-start(s32[2,64]{1,0:T(2,128)} %bitcast.31), channel_id=1, source_target_pairs={{0,4},{4,0},{8,12},{12,8},{16,20},{20,16},{24,28},{28,24},{1,5},{5... | collective-permute-start | bytes 1544 | tf_op jit(solution)/shard_map/ppermute | solution.py:180
  1.9 0.8 %select_bitcast_fusion = (bf16[64,256]{1,0:T(8,128)(2,1)S(1)}, bf16[64,256]{1,0:T(8,128)(2,1)S(1)}) fusion(bf16[1,2,64,256]{3,2,1,0:T(8,128)(2,1)} %param.8, pred[]{:T(512)} %bitcast.6, bf16[1,2,64,256]{3,2,1,0:T(8,128)(2,1)} %param.7), kind=kLoop, calls=%fused_computation.6 | loop fusion | flops 32768 | bytes 196609 | tf_op jit(solution)/shard_map/jit(_where)/select_n | solution.py:183
  2.7 0.0 collective-permute-done.1
  2.7 0.1 collective-permute-done
  2.9 0.1 collective-permute-done.2.starts_in_ref
  2.9 0.3 collective-permute-start.3
  3.2 0.2 collective-permute-start.4
  3.4 0.3 collective-permute-start.5
  3.7 1.3 %collective-permute-start.6 = (bf16[128,512]{1,0:T(8,128)(2,1)S(1)}, bf16[128,512]{1,0:T(8,128)(2,1)S(1)}, u32[]{:S(2)}, u32[]{:S(2)}) collective-permute-start(bf16[128,512]{1,0:T(8,128)(2,1)S(1)} %maximum_maximum_fusion.own_ref), channel_id=1, source_target_pairs={{0,16},{8,24},{16,28},{24,20},{28,12},{20,4},{1,17},{9,25},{17,29}... | collective-permute-start | bytes 393224 | tf_op jit(solution)/shard_map/ppermute | solution.py:176
  5.0 2.1 %collective-permute-start.7 = (bf16[128,512]{1,0:T(8,128)(2,1)S(1)}, bf16[128,512]{1,0:T(8,128)(2,1)S(1)}, u32[]{:S(2)}, u32[]{:S(2)}) collective-permute-start(bf16[128,512]{1,0:T(8,128)(2,1)S(1)} %maximum_maximum_fusion.own_ref), channel_id=1, source_target_pairs={{0,8},{8,16},{16,24},{24,28},{28,20},{20,12},{12,4},{1,9},{9,17},{... | collective-permute-start | bytes 393224 | tf_op jit(solution)/shard_map/ppermute | solution.py:176
  7.1 0.1 pad_add_fusion.place_ref
  7.2 3.9 %collective-permute-done.6.far_ref = bf16[128,512]{1,0:T(8,128)(2,1)S(1)} collective-permute-done((bf16[128,512]{1,0:T(8,128)(2,1)S(1)}, bf16[128,512]{1,0:T(8,128)(2,1)S(1)}, u32[]{:S(2)}, u32[]{:S(2)}) %collective-permute-start.6) | collective-permute-done | bytes 131104 | tf_op jit(solution)/shard_map/ppermute | solution.py:176
  11.1 1.0 %collective-permute-done.7.near_ref = bf16[128,512]{1,0:T(8,128)(2,1)S(1)} collective-permute-done((bf16[128,512]{1,0:T(8,128)(2,1)S(1)}, bf16[128,512]{1,0:T(8,128)(2,1)S(1)}, u32[]{:S(2)}, u32[]{:S(2)}) %collective-permute-start.7) | collective-permute-done | bytes 131104 | tf_op jit(solution)/shard_map/ppermute | solution.py:176
  12.1 0.0 collective-permute-done.3.q_in_ref
  12.1 0.0 collective-permute-done.4.do_in_ref
  12.1 0.0 collective-permute-done.5.o_in_ref
  12.2 0.0 copy-start
  12.2 1.0 %copy-done = bf16[1,2,64,2048]{3,2,1,0:T(8,128)(2,1)S(1)} copy-done((bf16[1,2,64,2048]{3,2,1,0:T(8,128)(2,1)S(1)}, bf16[1,2,64,2048]{3,2,1,0:T(8,128)(2,1)}, u32[]{:S(2)}) %copy-start) | copy-done | bytes 524312
  13.2 0.0 copy-start.2
  13.2 1.0 %copy-done.2 = bf16[1,2,64,2048]{3,2,1,0:T(8,128)(2,1)S(1)} copy-done((bf16[1,2,64,2048]{3,2,1,0:T(8,128)(2,1)S(1)}, bf16[1,2,64,2048]{3,2,1,0:T(8,128)(2,1)}, u32[]{:S(2)}) %copy-start.2) | copy-done | bytes 524312
  14.2 0.0 copy-start.4
  14.2 1.0 %copy-done.4 = bf16[1,2,64,2048]{3,2,1,0:T(8,128)(2,1)S(1)} copy-done((bf16[1,2,64,2048]{3,2,1,0:T(8,128)(2,1)S(1)}, bf16[1,2,64,2048]{3,2,1,0:T(8,128)(2,1)}, u32[]{:S(2)}) %copy-start.4) | copy-done | bytes 524312
  15.3 0.0 copy-start.5
  15.3 0.7 %copy-done.5 = s32[1,2,64]{2,1,0:T(2,128)S(1)} copy-done((s32[1,2,64]{2,1,0:T(2,128)S(1)}, s32[1,2,64]{2,1,0:T(2,128)}, u32[]{:S(2)}) %copy-start.5) | copy-done | bytes 536
  16.0 0.0 copy-start.1
  16.0 0.0 copy-start.3
  16.0 3.0 %scores.1 = (bf16[128,512]{1,0:T(8,128)(2,1)S(1)}, bf16[128,512]{1,0:T(8,128)(2,1)S(1)}, bf16[2,2,320,512]{3,2,1,0:T(8,128)(2,1)S(1)}, bf16[2,2,320,512]{3,2,1,0:T(8,128)(2,1)S(1)}) custom-call(s32[2]{0:T(128)S(1)} %pad_add_fusion.place_ref, s32[2,64]{1,0:T(2,128)S(1)} %bitcast.32, bf16[2,64,2048]{2,1,0:T(8,128)(2,1)S(1)} %bitcast.24, ...), custom_call_target="tpu_custom_call" | custom-call | flops 503316480 | bytes 12582912 | tf_op jit(solution)/shard_map/scores/pallas_call | solution.py:205
  18.9 3.2 %collective-permute-start.8 = (bf16[128,512]{1,0:T(8,128)(2,1)S(1)}, bf16[128,512]{1,0:T(8,128)(2,1)S(1)}, u32[]{:S(2)}, u32[]{:S(2)}) collective-permute-start(bf16[128,512]{1,0:T(8,128)(2,1)S(1)} %get-tuple-element.26), channel_id=1, source_target_pairs={{8,0},{16,8},{24,16},{28,24},{20,28},{12,20},{4,12},{9,1},{17,9},{... | collective-permute-start | bytes 393224 | tf_op jit(solution)/shard_map/ppermute | solution.py:176
  22.1 5.2 %collective-permute-start.9 = (bf16[128,512]{1,0:T(8,128)(2,1)S(1)}, bf16[128,512]{1,0:T(8,128)(2,1)S(1)}, u32[]{:S(2)}, u32[]{:S(2)}) collective-permute-start(bf16[128,512]{1,0:T(8,128)(2,1)S(1)} %get-tuple-element.27), channel_id=1, source_target_pairs={{16,0},{24,8},{28,16},{20,24},{12,28},{4,20},{17,1},{25,9},{29,17}... | collective-permute-start | bytes 393224 | tf_op jit(solution)/shard_map/ppermute | solution.py:176
  27.3 0.0 copy-done.1
  27.3 0.0 copy-done.3
  27.3 2.0 %rest.1 = (bf16[2,64,2048]{2,1,0:T(8,128)(2,1)}, bf16[64,2048]{1,0:T(8,128)(2,1)S(1)}, f32[128,512]{1,0:T(8,128)S(1)}) custom-call(s32[2]{0:T(128)S(1)} %pad_add_fusion.place_ref, bf16[2,64,2048]{2,1,0:T(8,128)(2,1)S(1)} %bitcast.25, bf16[2,64,2048]{2,1,0:T(8,128)(2,1)S(1)} %bitcast.28, bf16[2,64,2048]{2,1,0:T(8,128)(2,1)S(1)} %collective-permute-done.3.q_in_ref, ...), custom_call_target="tpu_custom_call" | custom-call | flops 251658240 | bytes 8388608 | tf_op jit(solution)/shard_map/rest/pallas_call | solution.py:225
  29.4 0.0 collective-permute-done.8
  29.4 0.0 collective-permute-done.9
  29.4 3.8 %collective-permute-start.10 = (bf16[64,2048]{1,0:T(8,128)(2,1)S(1)}, bf16[64,2048]{1,0:T(8,128)(2,1)S(1)}, u32[]{:S(2)}, u32[]{:S(2)}) collective-permute-start(bf16[64,2048]{1,0:T(8,128)(2,1)S(1)} %get-tuple-element.31), channel_id=1, source_target_pairs={{0,4},{4,0},{8,12},{12,8},{16,20},{20,16},{24,28},{28,24},{1,5},{5... | collective-permute-start | bytes 786440 | tf_op jit(solution)/shard_map/ppermute | solution.py:180
  33.2 0.1 add_convert_fusion
  33.2 0.1 collective-permute-start.11
  33.3 1.2 %collective-permute-done.11.given_ref = bf16[64,512]{1,0:T(8,128)(2,1)S(1)} collective-permute-done((bf16[64,512]{1,0:T(8,128)(2,1)S(1)}, bf16[64,512]{1,0:T(8,128)(2,1)S(1)}, u32[]{:S(2)}, u32[]{:S(2)}) %collective-permute-start.11) | collective-permute-done | bytes 65568 | tf_op jit(solution)/shard_map/ppermute | solution.py:180
  34.6 0.0 collective-permute-done.10.rows_ref
  34.6 0.8 %store.1 = (bf16[2,64,2048]{2,1,0:T(8,128)(2,1)}, bf16[2,64,256]{2,1,0:T(8,128)(2,1)}, bf16[2,64,256]{2,1,0:T(8,128)(2,1)}) custom-call(s32[1]{0:T(128)} %bitcast.core_ref, bf16[64,2048]{1,0:T(8,128)(2,1)S(1)} %collective-permute-done.10.rows_ref, bf16[64,512]{1,0:T(8,128)(2,1)S(1)} %get-tuple-element.40.kept_ref, ...), custom_call_target="tpu_custom_call", output_to_operand_aliasing={{0}: (4, {})} | custom-call | tf_op jit(solution)/shard_map/store/pallas_call | solution.py:249
  (4 shorter events, 0.0 us)
Async XLA Ops:
  0.6 2.1 %collective-permute-start.1 = (bf16[2,64,256]{2,1,0:T(8,128)(2,1)}, bf16[2,64,256]{2,1,0:T(8,128)(2,1)S(1)}, u32[]{:S(2)}, u32[]{:S(2)}) collective-permute-start(bf16[2,64,256]{2,1,0:T(8,128)(2,1)} %bitcast.34), channel_id=1, source_target_pairs={{0,4},{4,0},{8,12},{12,8},{16,20},{20,16},{24,28},{28,24},{1,5},{5... | collective-permute-start | bytes 196616 | tf_op jit(solution)/shard_map/ppermute | solution.py:180
  1.4 1.5 %collective-permute-start = (bf16[2,64,256]{2,1,0:T(8,128)(2,1)}, bf16[2,64,256]{2,1,0:T(8,128)(2,1)S(1)}, u32[]{:S(2)}, u32[]{:S(2)}) collective-permute-start(bf16[2,64,256]{2,1,0:T(8,128)(2,1)} %bitcast.35), channel_id=1, source_target_pairs={{0,4},{4,0},{8,12},{12,8},{16,20},{20,16},{24,28},{28,24},{1,5},{5... | collective-permute-start | bytes 196616 | tf_op jit(solution)/shard_map/ppermute | solution.py:180
  1.4 1.5 %collective-permute-start.2 = (s32[2,64]{1,0:T(2,128)}, s32[2,64]{1,0:T(2,128)S(1)}, u32[]{:S(2)}, u32[]{:S(2)}) collective-permute-start(s32[2,64]{1,0:T(2,128)} %bitcast.31), channel_id=1, source_target_pairs={{0,4},{4,0},{8,12},{12,8},{16,20},{20,16},{24,28},{28,24},{1,5},{5... | collective-permute-start | bytes 1544 | tf_op jit(solution)/shard_map/ppermute | solution.py:180
  2.9 9.2 %collective-permute-start.3 = (bf16[2,64,2048]{2,1,0:T(8,128)(2,1)}, bf16[2,64,2048]{2,1,0:T(8,128)(2,1)S(1)}, u32[]{:S(2)}, u32[]{:S(2)}) collective-permute-start(bf16[2,64,2048]{2,1,0:T(8,128)(2,1)} %bitcast.23), channel_id=1, source_target_pairs={{0,4},{4,0},{8,12},{12,8},{16,20},{20,16},{24,28},{28,24},{1,5},{5... | collective-permute-start | bytes 1572872 | tf_op jit(solution)/shard_map/ppermute | solution.py:180
  3.2 8.9 %collective-permute-start.4 = (bf16[2,64,2048]{2,1,0:T(8,128)(2,1)}, bf16[2,64,2048]{2,1,0:T(8,128)(2,1)S(1)}, u32[]{:S(2)}, u32[]{:S(2)}) collective-permute-start(bf16[2,64,2048]{2,1,0:T(8,128)(2,1)} %bitcast.26), channel_id=1, source_target_pairs={{0,4},{4,0},{8,12},{12,8},{16,20},{20,16},{24,28},{28,24},{1,5},{5... | collective-permute-start | bytes 1572872 | tf_op jit(solution)/shard_map/ppermute | solution.py:180
  3.4 8.7 %collective-permute-start.5 = (bf16[2,64,2048]{2,1,0:T(8,128)(2,1)}, bf16[2,64,2048]{2,1,0:T(8,128)(2,1)S(1)}, u32[]{:S(2)}, u32[]{:S(2)}) collective-permute-start(bf16[2,64,2048]{2,1,0:T(8,128)(2,1)} %bitcast.29), channel_id=1, source_target_pairs={{0,4},{4,0},{8,12},{12,8},{16,20},{20,16},{24,28},{28,24},{1,5},{5... | collective-permute-start | bytes 1572872 | tf_op jit(solution)/shard_map/ppermute | solution.py:180
  3.7 7.4 %collective-permute-start.6 = (bf16[128,512]{1,0:T(8,128)(2,1)S(1)}, bf16[128,512]{1,0:T(8,128)(2,1)S(1)}, u32[]{:S(2)}, u32[]{:S(2)}) collective-permute-start(bf16[128,512]{1,0:T(8,128)(2,1)S(1)} %maximum_maximum_fusion.own_ref), channel_id=1, source_target_pairs={{0,16},{8,24},{16,28},{24,20},{28,12},{20,4},{1,17},{9,25},{17,29}... | collective-permute-start | bytes 393224 | tf_op jit(solution)/shard_map/ppermute | solution.py:176
  5.0 7.1 %collective-permute-start.7 = (bf16[128,512]{1,0:T(8,128)(2,1)S(1)}, bf16[128,512]{1,0:T(8,128)(2,1)S(1)}, u32[]{:S(2)}, u32[]{:S(2)}) collective-permute-start(bf16[128,512]{1,0:T(8,128)(2,1)S(1)} %maximum_maximum_fusion.own_ref), channel_id=1, source_target_pairs={{0,8},{8,16},{16,24},{24,28},{28,20},{20,12},{12,4},{1,9},{9,17},{... | collective-permute-start | bytes 393224 | tf_op jit(solution)/shard_map/ppermute | solution.py:176
  12.2 1.0 %copy-start = (bf16[1,2,64,2048]{3,2,1,0:T(8,128)(2,1)S(1)}, bf16[1,2,64,2048]{3,2,1,0:T(8,128)(2,1)}, u32[]{:S(2)}) copy-start(bf16[1,2,64,2048]{3,2,1,0:T(8,128)(2,1)} %param.6) | copy-start | bytes 1572868
  13.2 1.0 %copy-start.2 = (bf16[1,2,64,2048]{3,2,1,0:T(8,128)(2,1)S(1)}, bf16[1,2,64,2048]{3,2,1,0:T(8,128)(2,1)}, u32[]{:S(2)}) copy-start(bf16[1,2,64,2048]{3,2,1,0:T(8,128)(2,1)} %param.9) | copy-start | bytes 1572868
  14.2 1.0 %copy-start.4 = (bf16[1,2,64,2048]{3,2,1,0:T(8,128)(2,1)S(1)}, bf16[1,2,64,2048]{3,2,1,0:T(8,128)(2,1)}, u32[]{:S(2)}) copy-start(bf16[1,2,64,2048]{3,2,1,0:T(8,128)(2,1)} %param.10) | copy-start | bytes 1572868
  15.3 0.7 %copy-start.5 = (s32[1,2,64]{2,1,0:T(2,128)S(1)}, s32[1,2,64]{2,1,0:T(2,128)}, u32[]{:S(2)}) copy-start(s32[1,2,64]{2,1,0:T(2,128)} %param.11) | copy-start | bytes 1540
  16.0 11.3 %copy-start.1 = (bf16[1,2,64,2048]{3,2,1,0:T(8,128)(2,1)S(1)}, bf16[1,2,64,2048]{3,2,1,0:T(8,128)(2,1)}, u32[]{:S(2)}) copy-start(bf16[1,2,64,2048]{3,2,1,0:T(8,128)(2,1)} %param.6) | copy-start | bytes 1572868
  16.0 11.4 %copy-start.3 = (bf16[1,2,64,2048]{3,2,1,0:T(8,128)(2,1)S(1)}, bf16[1,2,64,2048]{3,2,1,0:T(8,128)(2,1)}, u32[]{:S(2)}) copy-start(bf16[1,2,64,2048]{3,2,1,0:T(8,128)(2,1)} %param.9) | copy-start | bytes 1572868
  18.9 10.5 %collective-permute-start.8 = (bf16[128,512]{1,0:T(8,128)(2,1)S(1)}, bf16[128,512]{1,0:T(8,128)(2,1)S(1)}, u32[]{:S(2)}, u32[]{:S(2)}) collective-permute-start(bf16[128,512]{1,0:T(8,128)(2,1)S(1)} %get-tuple-element.26), channel_id=1, source_target_pairs={{8,0},{16,8},{24,16},{28,24},{20,28},{12,20},{4,12},{9,1},{17,9},{... | collective-permute-start | bytes 393224 | tf_op jit(solution)/shard_map/ppermute | solution.py:176
  22.1 7.3 %collective-permute-start.9 = (bf16[128,512]{1,0:T(8,128)(2,1)S(1)}, bf16[128,512]{1,0:T(8,128)(2,1)S(1)}, u32[]{:S(2)}, u32[]{:S(2)}) collective-permute-start(bf16[128,512]{1,0:T(8,128)(2,1)S(1)} %get-tuple-element.27), channel_id=1, source_target_pairs={{16,0},{24,8},{28,16},{20,24},{12,28},{4,20},{17,1},{25,9},{29,17}... | collective-permute-start | bytes 393224 | tf_op jit(solution)/shard_map/ppermute | solution.py:176
  29.4 5.2 %collective-permute-start.10 = (bf16[64,2048]{1,0:T(8,128)(2,1)S(1)}, bf16[64,2048]{1,0:T(8,128)(2,1)S(1)}, u32[]{:S(2)}, u32[]{:S(2)}) collective-permute-start(bf16[64,2048]{1,0:T(8,128)(2,1)S(1)} %get-tuple-element.31), channel_id=1, source_target_pairs={{0,4},{4,0},{8,12},{12,8},{16,20},{20,16},{24,28},{28,24},{1,5},{5... | collective-permute-start | bytes 786440 | tf_op jit(solution)/shard_map/ppermute | solution.py:180
  33.2 1.3 %collective-permute-start.11 = (bf16[64,512]{1,0:T(8,128)(2,1)S(1)}, bf16[64,512]{1,0:T(8,128)(2,1)S(1)}, u32[]{:S(2)}, u32[]{:S(2)}) collective-permute-start(bf16[64,512]{1,0:T(8,128)(2,1)S(1)} %get-tuple-element.39), channel_id=1, source_target_pairs={{0,4},{4,0},{8,12},{12,8},{16,20},{20,16},{24,28},{28,24},{1,5},{5... | collective-permute-start | bytes 196616 | tf_op jit(solution)/shard_map/ppermute | solution.py:180

commit v5 on v4

--- a/solution.py
+++ b/solution.py
@@ -53,7 +53,7 @@
 
 
 def scores_kernel(
-    place_ref, starts_ref, q_ref, do_ref, o_ref, starts_in_ref, q_in_ref, do_in_ref, o_in_ref,
+    place_ref, starts_ref, q_ref, do_ref, o_ref, q_in_ref, do_in_ref, o_in_ref,
     far_ref, near_ref, own_ref, far_part_ref, near_part_ref, probs_ref, dscores_ref,
     window_ref, part_ref,
 ):
@@ -66,8 +66,9 @@
     for n, source in enumerate((far_ref, near_ref, own_ref)):
         window_ref[n * pair : (n + 1) * pair, :] = source[...]
     offset = lax.broadcasted_iota(jnp.int32, (1, tokens), 1)
-    sides = ((starts_ref, q_ref, do_ref, o_ref), (starts_in_ref, q_in_ref, do_in_ref, o_in_ref))
-    for unit, (starts_side, *sources) in enumerate(sides):
+    sides = ((q_ref, do_ref, o_ref), (q_in_ref, do_in_ref, o_in_ref))
+    for unit, sources in enumerate(sides):
+        starts_side = starts_ref[2 * unit : 2 * unit + 2, :]
         starts = jnp.where(core == 0, starts_side[0:1, :], starts_side[1:2, :])
         first = unit * tokens
         low = jnp.maximum(offset + 1, starts - (begin + (unit - STEPS) * tokens))
@@ -187,10 +188,11 @@
     own = jnp.concatenate(
         [jnp.concatenate([mine(x) for x in side], axis=-1) for side in sides], axis=0
     )
-    own, starts_in, *late = lax.optimization_barrier(
-        (own, starts_in, query, out_grad, attn_out)
-    )
-    sent = [starts_in] + [swapped(x[0]) for x in late]
+    starts = jnp.concatenate([doc_start[0], starts_in], axis=0)
+    own, starts, *late = lax.optimization_barrier(
+        (own, starts, query[0], out_grad[0], attn_out[0])
+    )
+    sent = [swapped(x) for x in late]
     far = shift(own, 2)
     near = shift(own, 1)
     reach = (STEPS + 1) * tokens
@@ -210,7 +212,7 @@
             held,
             held,
         ),
-        in_specs=[SMEM] + [VMEM] * 11,
+        in_specs=[SMEM] + [VMEM] * 10,
         out_specs=(VMEM,) * 4,
         scratch_shapes=[
             pltpu.VMEM((3 * pair, pair_width), bf16),
@@ -219,7 +221,7 @@
         compiler_params=PARAMS,
         cost_estimate=work(3 * products, 12 * 2**20),
         name="scores",
-    )(place, doc_start[0], query[0], out_grad[0], attn_out[0], *sent, far, near, own)
+    )(place, starts, *late, *sent, far, near, own)
     from_far = shift(far_part, -2)
     from_near = shift(near_part, -1)
     dq, dq_send, own_part = pl.pallas_call(
@@ -239,7 +241,7 @@
         compiler_params=PARAMS,
         cost_estimate=work(3 * products // 2, 8 * 2**20),
         name="rest",
-    )(place, query[0], out_grad[0], *sent[1:3], far, near, own, probs, dscores)
+    )(place, *late[:2], *sent[:2], far, near, own, probs, dscores)
     from_near, from_far, dq_send = lax.optimization_barrier((from_near, from_far, dq_send))
     dq_rows = swapped(dq_send)
     total = own_part + from_near.astype(jnp.float32) + from_far.astype(jnp.float32)

time: 36 us -> 36.1 us (level)
  other arithmetic: 0.97 us -> 1.66 us
  local copies, waits for them, and re-layouts: 3.82 us -> 3.14 us
    concatenate x0 -> x1, other arithmetic: none -> 0.69 us  [shards(): starts = jnp.concatenate([doc_start[0], starts_in], axis=0)]
    unnamed x12 -> x10, local copies, waits for them, and re-layouts: 3.8 us -> 3.13 us
  transfers between devices with their start and end apart: 12 -> 12, of which waited for: 5 -> 4; matrix products, arithmetic and copies ran while one was open for 3% -> 5% of each run, Pallas kernels for 6% -> 6%
where the time goes in v5:
time: 36.1 us; the launch traced here: 35.5 us
  starting transfers between devices  17.7 us (49%)
  waiting for transfers between devices  6.4 us (18%)
  Pallas kernels  5.76 us (16%)
  local copies, waits for them, and re-layouts  3.14 us (9%)
  other arithmetic  1.66 us (5%)
  between operations  0.8 us (2%)
    ppermute x4, starting transfers between devices, shift(): return lax.ppermute(x, 'ctx', moves)  11.7 us
    ppermute x8, starting transfers between devices, swapped(): return lax.ppermute(x, 'ctx', swap)  5.98 us
    ppermute x4, waiting for transfers between devices, shift(): return lax.ppermute(x, 'ctx', moves)  4.93 us
    unnamed x10, local copies, waits for them, and re-layouts  3.13 us
    pallas_call x1, Pallas kernels, shards(): pl.pallas_call(scores_kernel, out_shape=(jax.ShapeDtypeStruct((pair, pair...  2.95 us
    pallas_call x1, Pallas kernels, shards(): pl.pallas_call(rest_kernel, out_shape=(jax.ShapeDtypeStruct((slots, token...  2.03 us
    ppermute x8, waiting for transfers between devices, swapped(): return lax.ppermute(x, 'ctx', swap)  1.47 us
    select_n x3, other arithmetic, mine(): return jnp.where(core == 0, x[0], x[1])  0.83 us
  transfers between devices with their start and end apart: 12, of which 4 were waited for; matrix products, arithmetic and copies ran while one was open for 5% of the time, Pallas kernels for 6%

profile of v5, /device:TPU:13, one launch (start us, length us, event | category | flops | bytes accessed | tf_op | source)
XLA Modules:
  0.0 35.5 jit_solution(8154523092546477530)
XLA Ops:
  0.6 0.7 %collective-permute-start.1 = (bf16[2,64,256]{2,1,0:T(8,128)(2,1)}, bf16[2,64,256]{2,1,0:T(8,128)(2,1)S(1)}, u32[]{:S(2)}, u32[]{:S(2)}) collective-permute-start(bf16[2,64,256]{2,1,0:T(8,128)(2,1)} %bitcast.29), channel_id=1, source_target_pairs={{0,4},{4,0},{8,12},{12,8},{16,20},{20,16},{24,28},{28,24},{1,5},{5... | collective-permute-start | bytes 196616 | tf_op jit(solution)/shard_map/ppermute | solution.py:181
  1.4 0.1 collective-permute-start
  1.4 0.4 %collective-permute-start.2 = (s32[2,64]{1,0:T(2,128)}, s32[2,64]{1,0:T(2,128)S(1)}, u32[]{:S(2)}, u32[]{:S(2)}) collective-permute-start(s32[2,64]{1,0:T(2,128)} %bitcast.31), channel_id=1, source_target_pairs={{0,4},{4,0},{8,12},{12,8},{16,20},{20,16},{24,28},{28,24},{1,5},{5... | collective-permute-start | bytes 1544 | tf_op jit(solution)/shard_map/ppermute | solution.py:181
  1.9 0.8 %select_bitcast_fusion = (bf16[64,256]{1,0:T(8,128)(2,1)S(1)}, bf16[64,256]{1,0:T(8,128)(2,1)S(1)}) fusion(bf16[1,2,64,256]{3,2,1,0:T(8,128)(2,1)} %param.8, pred[]{:T(512)} %bitcast.2, bf16[1,2,64,256]{3,2,1,0:T(8,128)(2,1)} %param.7), kind=kLoop, calls=%fused_computation.6 | loop fusion | flops 32768 | bytes 196609 | tf_op jit(solution)/shard_map/jit(_where)/select_n | solution.py:184
  2.7 0.2 collective-permute-done.2
  2.9 0.7 %pad_add_fusion.starts_ref = s32[4,64]{1,0:T(4,128)S(1)} fusion(s32[2,64]{1,0:T(2,128)S(1)} %collective-permute-done.2, s32[2,64]{1,0:T(2,128)} %bitcast.32), kind=kLoop, calls=%fused_computation.8 | loop fusion | flops 256 | bytes 2048 | tf_op jit(solution)/shard_map/concatenate | solution.py:191
  3.6 0.0 collective-permute-done.1
  3.6 0.0 collective-permute-done
  3.7 0.4 %collective-permute-start.3 = (bf16[2,64,2048]{2,1,0:T(8,128)(2,1)}, bf16[2,64,2048]{2,1,0:T(8,128)(2,1)S(1)}, u32[]{:S(2)}, u32[]{:S(2)}) collective-permute-start(bf16[2,64,2048]{2,1,0:T(8,128)(2,1)} %bitcast.20), channel_id=1, source_target_pairs={{0,4},{4,0},{8,12},{12,8},{16,20},{20,16},{24,28},{28,24},{1,5},{5... | collective-permute-start | bytes 1572872 | tf_op jit(solution)/shard_map/ppermute | solution.py:181
  4.1 0.2 collective-permute-start.4
  4.2 0.3 collective-permute-start.5
  4.6 1.3 %collective-permute-start.6 = (bf16[128,512]{1,0:T(8,128)(2,1)S(1)}, bf16[128,512]{1,0:T(8,128)(2,1)S(1)}, u32[]{:S(2)}, u32[]{:S(2)}) collective-permute-start(bf16[128,512]{1,0:T(8,128)(2,1)S(1)} %maximum_maximum_fusion.own_ref), channel_id=1, source_target_pairs={{0,16},{8,24},{16,28},{24,20},{28,12},{20,4},{1,17},{9,25},{17,29}... | collective-permute-start | bytes 393224 | tf_op jit(solution)/shard_map/ppermute | solution.py:177
  5.9 2.1 %collective-permute-start.7 = (bf16[128,512]{1,0:T(8,128)(2,1)S(1)}, bf16[128,512]{1,0:T(8,128)(2,1)S(1)}, u32[]{:S(2)}, u32[]{:S(2)}) collective-permute-start(bf16[128,512]{1,0:T(8,128)(2,1)S(1)} %maximum_maximum_fusion.own_ref), channel_id=1, source_target_pairs={{0,8},{8,16},{16,24},{24,28},{28,20},{20,12},{12,4},{1,9},{9,17},{... | collective-permute-start | bytes 393224 | tf_op jit(solution)/shard_map/ppermute | solution.py:177
  8.0 0.1 pad_add_fusion.1.place_ref
  8.0 3.9 %collective-permute-done.6.far_ref = bf16[128,512]{1,0:T(8,128)(2,1)S(1)} collective-permute-done((bf16[128,512]{1,0:T(8,128)(2,1)S(1)}, bf16[128,512]{1,0:T(8,128)(2,1)S(1)}, u32[]{:S(2)}, u32[]{:S(2)}) %collective-permute-start.6) | collective-permute-done | bytes 131104 | tf_op jit(solution)/shard_map/ppermute | solution.py:177
  11.9 1.0 %collective-permute-done.7.near_ref = bf16[128,512]{1,0:T(8,128)(2,1)S(1)} collective-permute-done((bf16[128,512]{1,0:T(8,128)(2,1)S(1)}, bf16[128,512]{1,0:T(8,128)(2,1)S(1)}, u32[]{:S(2)}, u32[]{:S(2)}) %collective-permute-start.7) | collective-permute-done | bytes 131104 | tf_op jit(solution)/shard_map/ppermute | solution.py:177
  13.0 0.0 collective-permute-done.3.q_in_ref
  13.0 0.0 collective-permute-done.4.do_in_ref
  13.0 0.0 collective-permute-done.5.o_in_ref
  13.0 0.0 copy-start
  13.0 1.0 %copy-done = bf16[1,2,64,2048]{3,2,1,0:T(8,128)(2,1)S(1)} copy-done((bf16[1,2,64,2048]{3,2,1,0:T(8,128)(2,1)S(1)}, bf16[1,2,64,2048]{3,2,1,0:T(8,128)(2,1)}, u32[]{:S(2)}) %copy-start) | copy-done | bytes 524312
  14.0 0.0 copy-start.2
  14.0 1.0 %copy-done.2 = bf16[1,2,64,2048]{3,2,1,0:T(8,128)(2,1)S(1)} copy-done((bf16[1,2,64,2048]{3,2,1,0:T(8,128)(2,1)S(1)}, bf16[1,2,64,2048]{3,2,1,0:T(8,128)(2,1)}, u32[]{:S(2)}) %copy-start.2) | copy-done | bytes 524312
  15.1 0.0 copy-start.4
  15.1 1.0 %copy-done.4 = bf16[1,2,64,2048]{3,2,1,0:T(8,128)(2,1)S(1)} copy-done((bf16[1,2,64,2048]{3,2,1,0:T(8,128)(2,1)S(1)}, bf16[1,2,64,2048]{3,2,1,0:T(8,128)(2,1)}, u32[]{:S(2)}) %copy-start.4) | copy-done | bytes 524312
  16.1 0.0 copy-start.1
  16.1 0.0 copy-start.3
  16.1 3.0 %scores.1 = (bf16[128,512]{1,0:T(8,128)(2,1)S(1)}, bf16[128,512]{1,0:T(8,128)(2,1)S(1)}, bf16[2,2,320,512]{3,2,1,0:T(8,128)(2,1)S(1)}, bf16[2,2,320,512]{3,2,1,0:T(8,128)(2,1)S(1)}) custom-call(s32[2]{0:T(128)S(1)} %pad_add_fusion.1.place_ref, s32[4,64]{1,0:T(4,128)S(1)} %pad_add_fusion.starts_ref, bf16[2,64,2048]{2,1,0:T(8,128)(2,1)S(1)} %bitcast.21, ...), custom_call_target="tpu_custom_call" | custom-call | flops 503316480 | bytes 12582912 | tf_op jit(solution)/shard_map/scores/pallas_call | solution.py:207
  19.1 3.2 %collective-permute-start.8 = (bf16[128,512]{1,0:T(8,128)(2,1)S(1)}, bf16[128,512]{1,0:T(8,128)(2,1)S(1)}, u32[]{:S(2)}, u32[]{:S(2)}) collective-permute-start(bf16[128,512]{1,0:T(8,128)(2,1)S(1)} %get-tuple-element.26), channel_id=1, source_target_pairs={{8,0},{16,8},{24,16},{28,24},{20,28},{12,20},{4,12},{9,1},{17,9},{... | collective-permute-start | bytes 393224 | tf_op jit(solution)/shard_map/ppermute | solution.py:177
  22.3 5.2 %collective-permute-start.9 = (bf16[128,512]{1,0:T(8,128)(2,1)S(1)}, bf16[128,512]{1,0:T(8,128)(2,1)S(1)}, u32[]{:S(2)}, u32[]{:S(2)}) collective-permute-start(bf16[128,512]{1,0:T(8,128)(2,1)S(1)} %get-tuple-element.27), channel_id=1, source_target_pairs={{16,0},{24,8},{28,16},{20,24},{12,28},{4,20},{17,1},{25,9},{29,17}... | collective-permute-start | bytes 393224 | tf_op jit(solution)/shard_map/ppermute | solution.py:177
  27.4 0.0 copy-done.1
  27.5 0.0 copy-done.3
  27.5 2.0 %rest.1 = (bf16[2,64,2048]{2,1,0:T(8,128)(2,1)}, bf16[64,2048]{1,0:T(8,128)(2,1)S(1)}, f32[128,512]{1,0:T(8,128)S(1)}) custom-call(s32[2]{0:T(128)S(1)} %pad_add_fusion.1.place_ref, bf16[2,64,2048]{2,1,0:T(8,128)(2,1)S(1)} %bitcast.22, bf16[2,64,2048]{2,1,0:T(8,128)(2,1)S(1)} %bitcast.25, bf16[2,64,2048]{2,1,0:T(8,128)(2,1)S(1)} %collective-permute-done.3.q_in_ref, ...), custom_call_target="tpu_custom_call" | custom-call | flops 251658240 | bytes 8388608 | tf_op jit(solution)/shard_map/rest/pallas_call | solution.py:227
  29.5 0.0 collective-permute-done.8
  29.5 0.0 collective-permute-done.9
  29.5 3.8 %collective-permute-start.10 = (bf16[64,2048]{1,0:T(8,128)(2,1)S(1)}, bf16[64,2048]{1,0:T(8,128)(2,1)S(1)}, u32[]{:S(2)}, u32[]{:S(2)}) collective-permute-start(bf16[64,2048]{1,0:T(8,128)(2,1)S(1)} %get-tuple-element.31), channel_id=1, source_target_pairs={{0,4},{4,0},{8,12},{12,8},{16,20},{20,16},{24,28},{28,24},{1,5},{5... | collective-permute-start | bytes 786440 | tf_op jit(solution)/shard_map/ppermute | solution.py:181
  33.3 0.1 add_convert_fusion
  33.4 0.1 collective-permute-start.11
  33.4 1.2 %collective-permute-done.11.given_ref = bf16[64,512]{1,0:T(8,128)(2,1)S(1)} collective-permute-done((bf16[64,512]{1,0:T(8,128)(2,1)S(1)}, bf16[64,512]{1,0:T(8,128)(2,1)S(1)}, u32[]{:S(2)}, u32[]{:S(2)}) %collective-permute-start.11) | collective-permute-done | bytes 65568 | tf_op jit(solution)/shard_map/ppermute | solution.py:181
  34.7 0.0 collective-permute-done.10.rows_ref
  34.7 0.8 %store.1 = (bf16[2,64,2048]{2,1,0:T(8,128)(2,1)}, bf16[2,64,256]{2,1,0:T(8,128)(2,1)}, bf16[2,64,256]{2,1,0:T(8,128)(2,1)}) custom-call(s32[1]{0:T(128)} %bitcast.core_ref, bf16[64,2048]{1,0:T(8,128)(2,1)S(1)} %collective-permute-done.10.rows_ref, bf16[64,512]{1,0:T(8,128)(2,1)S(1)} %get-tuple-element.40.kept_ref, ...), custom_call_target="tpu_custom_call", output_to_operand_aliasing={{0}: (4, {})} | custom-call | tf_op jit(solution)/shard_map/store/pallas_call | solution.py:251
  (4 shorter events, 0.0 us)
Async XLA Ops:
  0.6 3.0 %collective-permute-start.1 = (bf16[2,64,256]{2,1,0:T(8,128)(2,1)}, bf16[2,64,256]{2,1,0:T(8,128)(2,1)S(1)}, u32[]{:S(2)}, u32[]{:S(2)}) collective-permute-start(bf16[2,64,256]{2,1,0:T(8,128)(2,1)} %bitcast.29), channel_id=1, source_target_pairs={{0,4},{4,0},{8,12},{12,8},{16,20},{20,16},{24,28},{28,24},{1,5},{5... | collective-permute-start | bytes 196616 | tf_op jit(solution)/shard_map/ppermute | solution.py:181
  1.4 2.3 %collective-permute-start = (bf16[2,64,256]{2,1,0:T(8,128)(2,1)}, bf16[2,64,256]{2,1,0:T(8,128)(2,1)S(1)}, u32[]{:S(2)}, u32[]{:S(2)}) collective-permute-start(bf16[2,64,256]{2,1,0:T(8,128)(2,1)} %bitcast.30), channel_id=1, source_target_pairs={{0,4},{4,0},{8,12},{12,8},{16,20},{20,16},{24,28},{28,24},{1,5},{5... | collective-permute-start | bytes 196616 | tf_op jit(solution)/shard_map/ppermute | solution.py:181
  1.4 1.5 %collective-permute-start.2 = (s32[2,64]{1,0:T(2,128)}, s32[2,64]{1,0:T(2,128)S(1)}, u32[]{:S(2)}, u32[]{:S(2)}) collective-permute-start(s32[2,64]{1,0:T(2,128)} %bitcast.31), channel_id=1, source_target_pairs={{0,4},{4,0},{8,12},{12,8},{16,20},{20,16},{24,28},{28,24},{1,5},{5... | collective-permute-start | bytes 1544 | tf_op jit(solution)/shard_map/ppermute | solution.py:181
  3.7 9.3 %collective-permute-start.3 = (bf16[2,64,2048]{2,1,0:T(8,128)(2,1)}, bf16[2,64,2048]{2,1,0:T(8,128)(2,1)S(1)}, u32[]{:S(2)}, u32[]{:S(2)}) collective-permute-start(bf16[2,64,2048]{2,1,0:T(8,128)(2,1)} %bitcast.20), channel_id=1, source_target_pairs={{0,4},{4,0},{8,12},{12,8},{16,20},{20,16},{24,28},{28,24},{1,5},{5... | collective-permute-start | bytes 1572872 | tf_op jit(solution)/shard_map/ppermute | solution.py:181
  4.1 8.9 %collective-permute-start.4 = (bf16[2,64,2048]{2,1,0:T(8,128)(2,1)}, bf16[2,64,2048]{2,1,0:T(8,128)(2,1)S(1)}, u32[]{:S(2)}, u32[]{:S(2)}) collective-permute-start(bf16[2,64,2048]{2,1,0:T(8,128)(2,1)} %bitcast.23), channel_id=1, source_target_pairs={{0,4},{4,0},{8,12},{12,8},{16,20},{20,16},{24,28},{28,24},{1,5},{5... | collective-permute-start | bytes 1572872 | tf_op jit(solution)/shard_map/ppermute | solution.py:181
  4.2 8.7 %collective-permute-start.5 = (bf16[2,64,2048]{2,1,0:T(8,128)(2,1)}, bf16[2,64,2048]{2,1,0:T(8,128)(2,1)S(1)}, u32[]{:S(2)}, u32[]{:S(2)}) collective-permute-start(bf16[2,64,2048]{2,1,0:T(8,128)(2,1)} %bitcast.26), channel_id=1, source_target_pairs={{0,4},{4,0},{8,12},{12,8},{16,20},{20,16},{24,28},{28,24},{1,5},{5... | collective-permute-start | bytes 1572872 | tf_op jit(solution)/shard_map/ppermute | solution.py:181
  4.6 7.4 %collective-permute-start.6 = (bf16[128,512]{1,0:T(8,128)(2,1)S(1)}, bf16[128,512]{1,0:T(8,128)(2,1)S(1)}, u32[]{:S(2)}, u32[]{:S(2)}) collective-permute-start(bf16[128,512]{1,0:T(8,128)(2,1)S(1)} %maximum_maximum_fusion.own_ref), channel_id=1, source_target_pairs={{0,16},{8,24},{16,28},{24,20},{28,12},{20,4},{1,17},{9,25},{17,29}... | collective-permute-start | bytes 393224 | tf_op jit(solution)/shard_map/ppermute | solution.py:177
  5.9 7.1 %collective-permute-start.7 = (bf16[128,512]{1,0:T(8,128)(2,1)S(1)}, bf16[128,512]{1,0:T(8,128)(2,1)S(1)}, u32[]{:S(2)}, u32[]{:S(2)}) collective-permute-start(bf16[128,512]{1,0:T(8,128)(2,1)S(1)} %maximum_maximum_fusion.own_ref), channel_id=1, source_target_pairs={{0,8},{8,16},{16,24},{24,28},{28,20},{20,12},{12,4},{1,9},{9,17},{... | collective-permute-start | bytes 393224 | tf_op jit(solution)/shard_map/ppermute | solution.py:177
  13.0 1.0 %copy-start = (bf16[1,2,64,2048]{3,2,1,0:T(8,128)(2,1)S(1)}, bf16[1,2,64,2048]{3,2,1,0:T(8,128)(2,1)}, u32[]{:S(2)}) copy-start(bf16[1,2,64,2048]{3,2,1,0:T(8,128)(2,1)} %param.6) | copy-start | bytes 1572868
  14.0 1.0 %copy-start.2 = (bf16[1,2,64,2048]{3,2,1,0:T(8,128)(2,1)S(1)}, bf16[1,2,64,2048]{3,2,1,0:T(8,128)(2,1)}, u32[]{:S(2)}) copy-start(bf16[1,2,64,2048]{3,2,1,0:T(8,128)(2,1)} %param.9) | copy-start | bytes 1572868
  15.1 1.0 %copy-start.4 = (bf16[1,2,64,2048]{3,2,1,0:T(8,128)(2,1)S(1)}, bf16[1,2,64,2048]{3,2,1,0:T(8,128)(2,1)}, u32[]{:S(2)}) copy-start(bf16[1,2,64,2048]{3,2,1,0:T(8,128)(2,1)} %param.10) | copy-start | bytes 1572868
  16.1 11.3 %copy-start.1 = (bf16[1,2,64,2048]{3,2,1,0:T(8,128)(2,1)S(1)}, bf16[1,2,64,2048]{3,2,1,0:T(8,128)(2,1)}, u32[]{:S(2)}) copy-start(bf16[1,2,64,2048]{3,2,1,0:T(8,128)(2,1)} %param.6) | copy-start | bytes 1572868
  16.1 11.4 %copy-start.3 = (bf16[1,2,64,2048]{3,2,1,0:T(8,128)(2,1)S(1)}, bf16[1,2,64,2048]{3,2,1,0:T(8,128)(2,1)}, u32[]{:S(2)}) copy-start(bf16[1,2,64,2048]{3,2,1,0:T(8,128)(2,1)} %param.9) | copy-start | bytes 1572868
  19.1 10.4 %collective-permute-start.8 = (bf16[128,512]{1,0:T(8,128)(2,1)S(1)}, bf16[128,512]{1,0:T(8,128)(2,1)S(1)}, u32[]{:S(2)}, u32[]{:S(2)}) collective-permute-start(bf16[128,512]{1,0:T(8,128)(2,1)S(1)} %get-tuple-element.26), channel_id=1, source_target_pairs={{8,0},{16,8},{24,16},{28,24},{20,28},{12,20},{4,12},{9,1},{17,9},{... | collective-permute-start | bytes 393224 | tf_op jit(solution)/shard_map/ppermute | solution.py:177
  22.3 7.2 %collective-permute-start.9 = (bf16[128,512]{1,0:T(8,128)(2,1)S(1)}, bf16[128,512]{1,0:T(8,128)(2,1)S(1)}, u32[]{:S(2)}, u32[]{:S(2)}) collective-permute-start(bf16[128,512]{1,0:T(8,128)(2,1)S(1)} %get-tuple-element.27), channel_id=1, source_target_pairs={{16,0},{24,8},{28,16},{20,24},{12,28},{4,20},{17,1},{25,9},{29,17}... | collective-permute-start | bytes 393224 | tf_op jit(solution)/shard_map/ppermute | solution.py:177
  29.5 5.2 %collective-permute-start.10 = (bf16[64,2048]{1,0:T(8,128)(2,1)S(1)}, bf16[64,2048]{1,0:T(8,128)(2,1)S(1)}, u32[]{:S(2)}, u32[]{:S(2)}) collective-permute-start(bf16[64,2048]{1,0:T(8,128)(2,1)S(1)} %get-tuple-element.31), channel_id=1, source_target_pairs={{0,4},{4,0},{8,12},{12,8},{16,20},{20,16},{24,28},{28,24},{1,5},{5... | collective-permute-start | bytes 786440 | tf_op jit(solution)/shard_map/ppermute | solution.py:181
  33.4 1.3 %collective-permute-start.11 = (bf16[64,512]{1,0:T(8,128)(2,1)S(1)}, bf16[64,512]{1,0:T(8,128)(2,1)S(1)}, u32[]{:S(2)}, u32[]{:S(2)}) collective-permute-start(bf16[64,512]{1,0:T(8,128)(2,1)S(1)} %get-tuple-element.39), channel_id=1, source_target_pairs={{0,4},{4,0},{8,12},{12,8},{16,20},{20,16},{24,28},{28,24},{1,5},{5... | collective-permute-start | bytes 196616 | tf_op jit(solution)/shard_map/ppermute | solution.py:181

commit v6 on v5

--- a/solution.py
+++ b/solution.py
@@ -28,46 +28,52 @@
     )
 
 
-def attend(q, do, o, keys, values, low, high, scale):
+def attend(q, do, delta, keys, values, low, high, scale):
     scores = dot(keys, q, CONTRACT_LAST) * (scale * LOG2E)
     row = lax.broadcasted_iota(jnp.int32, scores.shape, 0)
     scores = jnp.where((row >= low) & (row <= high), scores, -jnp.inf)
     top = jnp.max(scores, axis=0, keepdims=True)
     weights = jnp.exp2(scores - top)
     probs = weights * (1.0 / jnp.sum(weights, axis=0, keepdims=True))
-    terms = do.astype(jnp.float32) * o.astype(jnp.float32)
-    coarse = terms.astype(jnp.bfloat16)
-    fine = (terms - coarse.astype(jnp.float32)).astype(jnp.bfloat16)
-    ones = jnp.ones((8, 2 * HEAD_SIZE), jnp.bfloat16)
-    delta = dot(ones, jnp.concatenate([coarse, fine], axis=1), CONTRACT_LAST)[:1]
     dprobs = dot(values, do, CONTRACT_LAST)
     dscores = (probs * (dprobs - delta)).astype(jnp.bfloat16)
     return probs.astype(jnp.bfloat16), dscores
 
 
-def unit_sizes(rows_ref, pair_ref):
-    heads = rows_ref.shape[-1] // HEAD_SIZE
-    kv_width = pair_ref.shape[-1] // 2
-    kv_heads = kv_width // HEAD_SIZE
-    return kv_heads, kv_width, heads // kv_heads
+def rows_kernel(core_ref, q_ref, do_ref, o_ref, q_out_ref, do_out_ref, delta_ref):
+    core = core_ref[0]
+    group = q_out_ref.shape[1] // q_ref.shape[1]
+    ones = jnp.ones((delta_ref.shape[1], 2 * HEAD_SIZE), jnp.bfloat16)
+    for g in range(q_out_ref.shape[0]):
+        q, do, o = (
+            stack_heads(r.at[core], g * group, group) for r in (q_ref, do_ref, o_ref)
+        )
+        terms = do.astype(jnp.float32) * o.astype(jnp.float32)
+        coarse = terms.astype(jnp.bfloat16)
+        fine = (terms - coarse.astype(jnp.float32)).astype(jnp.bfloat16)
+        delta_ref[g] = dot(ones, jnp.concatenate([coarse, fine], axis=1), CONTRACT_LAST)
+        q_out_ref[g] = q
+        do_out_ref[g] = do
 
 
 def scores_kernel(
-    place_ref, starts_ref, q_ref, do_ref, o_ref, q_in_ref, do_in_ref, o_in_ref,
+    place_ref, starts_ref, q_ref, do_ref, delta_ref, q_in_ref, do_in_ref, delta_in_ref,
     far_ref, near_ref, own_ref, far_part_ref, near_part_ref, probs_ref, dscores_ref,
     window_ref, part_ref,
 ):
     core, begin = place_ref[0], place_ref[1]
-    tokens = q_ref.shape[1]
-    kv_heads, kv_width, group = unit_sizes(q_ref, own_ref)
+    tokens = starts_ref.shape[1]
+    kv_heads, lanes = q_ref.shape[:2]
+    kv_width = kv_heads * HEAD_SIZE
+    group = lanes // tokens
     scale = HEAD_SIZE ** (-0.5)
     reach = (STEPS + 1) * tokens
     pair = 2 * tokens
     for n, source in enumerate((far_ref, near_ref, own_ref)):
         window_ref[n * pair : (n + 1) * pair, :] = source[...]
     offset = lax.broadcasted_iota(jnp.int32, (1, tokens), 1)
-    sides = ((q_ref, do_ref, o_ref), (q_in_ref, do_in_ref, o_in_ref))
-    for unit, sources in enumerate(sides):
+    sides = ((q_ref, do_ref, delta_ref), (q_in_ref, do_in_ref, delta_in_ref))
+    for unit, (q_side, do_side, delta_side) in enumerate(sides):
         starts_side = starts_ref[2 * unit : 2 * unit + 2, :]
         starts = jnp.where(core == 0, starts_side[0:1, :], starts_side[1:2, :])
         first = unit * tokens
@@ -79,8 +85,8 @@
             at = (g * HEAD_SIZE, kv_width + g * HEAD_SIZE)
             keys = window_ref[first : first + reach, at[0] : at[0] + HEAD_SIZE]
             values = window_ref[first : first + reach, at[1] : at[1] + HEAD_SIZE]
-            q, do, o = (stack_heads(r.at[core], g * group, group) for r in sources)
-            probs, dscores = attend(q, do, o, keys, values, low, high, scale)
+            q, do = q_side[g], do_side[g]
+            probs, dscores = attend(q, do, delta_side[g, :1], keys, values, low, high, scale)
             probs_ref[unit, g] = probs
             dscores_ref[unit, g] = dscores
             before = 2 * pair - first
@@ -102,8 +108,10 @@
     dscores_ref, dq_ref, dq_send_ref, own_part_ref, window_ref, held_ref, sem,
 ):
     core = place_ref[0]
-    tokens = q_ref.shape[1]
-    kv_heads, kv_width, group = unit_sizes(q_ref, own_ref)
+    tokens = dq_send_ref.shape[0]
+    kv_heads, lanes = q_ref.shape[:2]
+    kv_width = kv_heads * HEAD_SIZE
+    group = lanes // tokens
     scale = HEAD_SIZE ** (-0.5)
     reach = (STEPS + 1) * tokens
     pair = 2 * tokens
@@ -111,7 +119,7 @@
         window_ref[n * pair : (n + 1) * pair, :] = source[:, :kv_width]
     store = pltpu.make_async_copy(held_ref, dq_ref.at[core], sem)
     sides = ((1, dq_send_ref, q_in_ref, do_in_ref), (0, held_ref, q_ref, do_ref))
-    for unit, target, *sources in sides:
+    for unit, target, q_side, do_side in sides:
         first = unit * tokens
         before = 2 * pair - first
         for g in range(kv_heads):
@@ -123,11 +131,10 @@
                 target[:, column : column + HEAD_SIZE] = dq[a * tokens : (a + 1) * tokens]
             if unit == 0 and g == kv_heads - 1:
                 store.start()
-            q, do = (stack_heads(r.at[core], g * group, group) for r in sources)
             at = (g * HEAD_SIZE, kv_width + g * HEAD_SIZE)
             for part, column in (
-                (dot(dscores_ref[unit, g, before:, :], q) * scale, at[0]),
-                (dot(probs_ref[unit, g, before:, :], do), at[1]),
+                (dot(dscores_ref[unit, g, before:, :], q_side[g]) * scale, at[0]),
+                (dot(probs_ref[unit, g, before:, :], do_side[g]), at[1]),
             ):
                 columns = slice(column, column + HEAD_SIZE)
                 if unit == 1:
@@ -177,6 +184,9 @@
         return lax.ppermute(x, "ctx", moves)
 
     bf16 = jnp.bfloat16
+    def work(flops, moved):
+        return pl.CostEstimate(flops=flops, bytes_accessed=moved, transcendentals=0)
+
     def swapped(x):
         return lax.ppermute(x, "ctx", swap)
 
@@ -192,16 +202,31 @@
     own, starts, *late = lax.optimization_barrier(
         (own, starts, query[0], out_grad[0], attn_out[0])
     )
+    kv_heads = kv_width // HEAD_SIZE
+    lanes = tokens * (width // kv_width)
+
+    def arranged(sources):
+        stacked = jax.ShapeDtypeStruct((kv_heads, lanes, HEAD_SIZE), bf16)
+        return pl.pallas_call(
+            rows_kernel,
+            out_shape=(
+                stacked,
+                stacked,
+                jax.ShapeDtypeStruct((kv_heads, 8, lanes), jnp.float32),
+            ),
+            in_specs=[SMEM] + [VMEM] * 3,
+            out_specs=(VMEM,) * 3,
+            compiler_params=SMALL,
+            cost_estimate=work(2**20, 4 * 2**20),
+            name="rows",
+        )(core, *sources)
+
     sent = [swapped(x) for x in late]
+    rows, rows_in = arranged(late), arranged(sent)
     far = shift(own, 2)
     near = shift(own, 1)
     reach = (STEPS + 1) * tokens
-    kv_heads = kv_width // HEAD_SIZE
-    lanes = tokens * (width // kv_width)
     products = 2 * slots * tokens * reach * width
-
-    def work(flops, moved):
-        return pl.CostEstimate(flops=flops, bytes_accessed=moved, transcendentals=0)
 
     held = jax.ShapeDtypeStruct((slots, kv_heads, reach, lanes), bf16)
     far_part, near_part, probs, dscores = pl.pallas_call(
@@ -221,7 +246,7 @@
         compiler_params=PARAMS,
         cost_estimate=work(3 * products, 12 * 2**20),
         name="scores",
-    )(place, starts, *late, *sent, far, near, own)
+    )(place, starts, *rows, *rows_in, far, near, own)
     from_far = shift(far_part, -2)
     from_near = shift(near_part, -1)
     dq, dq_send, own_part = pl.pallas_call(
@@ -241,7 +266,7 @@
         compiler_params=PARAMS,
         cost_estimate=work(3 * products // 2, 8 * 2**20),
         name="rest",
-    )(place, *late[:2], *sent[:2], far, near, own, probs, dscores)
+    )(place, *rows[:2], *rows_in[:2], far, near, own, probs, dscores)
     from_near, from_far, dq_send = lax.optimization_barrier((from_near, from_far, dq_send))
     dq_rows = swapped(dq_send)
     total = own_part + from_near.astype(jnp.float32) + from_far.astype(jnp.float32)

time: 36.1 us -> 32.8 us (0.909)
  waiting for transfers between devices: 6.4 us -> 2.64 us
  Pallas kernels: 5.76 us -> 6.4 us
    ppermute x4, waiting for transfers between devices: 4.93 us -> 1.17 us  [shift(): return lax.ppermute(x, 'ctx', moves)]
    pallas_call x0 -> x2, Pallas kernels: none -> 0.6 us  [arranged(): pl.pallas_call(rows_kernel, out_shape=(stacked, stacked, jax.ShapeDtypeSt...]
    unnamed x10 -> x6, local copies, waits for them, and re-layouts: 3.13 us -> 3.12 us
  transfers between devices with their start and end apart: 12 -> 12, of which waited for: 4 -> 4; matrix products, arithmetic and copies ran while one was open for 5% -> 5% of each run, Pallas kernels for 6% -> 8%
where the time goes in v6:
time: 32.8 us; the launch traced here: 32.4 us
  starting transfers between devices  17.7 us (54%)
  Pallas kernels  6.4 us (20%)
  local copies, waits for them, and re-layouts  3.13 us (10%)
  waiting for transfers between devices  2.64 us (8%)
  other arithmetic  1.66 us (5%)
  between operations  0.8 us (2%)
    ppermute x4, starting transfers between devices, shift(): return lax.ppermute(x, 'ctx', moves)  11.7 us
    ppermute x8, starting transfers between devices, swapped(): return lax.ppermute(x, 'ctx', swap)  6.01 us
    unnamed x6, local copies, waits for them, and re-layouts  3.12 us
    pallas_call x1, Pallas kernels, shards(): pl.pallas_call(scores_kernel, out_shape=(jax.ShapeDtypeStruct((pair, pair...  2.98 us
    pallas_call x1, Pallas kernels, shards(): pl.pallas_call(rest_kernel, out_shape=(jax.ShapeDtypeStruct((slots, token...  2.03 us
    ppermute x8, waiting for transfers between devices, swapped(): return lax.ppermute(x, 'ctx', swap)  1.47 us
    ppermute x4, waiting for transfers between devices, shift(): return lax.ppermute(x, 'ctx', moves)  1.17 us
    select_n x3, other arithmetic, mine(): return jnp.where(core == 0, x[0], x[1])  0.83 us
  transfers between devices with their start and end apart: 12, of which 4 were waited for; matrix products, arithmetic and copies ran while one was open for 5% of the time, Pallas kernels for 8%

profile of v6, /device:TPU:13, one launch (start us, length us, event | category | flops | bytes accessed | tf_op | source)
XLA Modules:
  0.0 32.4 jit_solution(7067574939393771414)
XLA Ops:
  0.6 0.7 %collective-permute-start.1 = (bf16[2,64,256]{2,1,0:T(8,128)(2,1)}, bf16[2,64,256]{2,1,0:T(8,128)(2,1)S(1)}, u32[]{:S(2)}, u32[]{:S(2)}) collective-permute-start(bf16[2,64,256]{2,1,0:T(8,128)(2,1)} %bitcast.27), channel_id=1, source_target_pairs={{0,4},{4,0},{8,12},{12,8},{16,20},{20,16},{24,28},{28,24},{1,5},{5... | collective-permute-start | bytes 196616 | tf_op jit(solution)/shard_map/ppermute | solution.py:191
  1.4 0.1 collective-permute-start
  1.4 0.4 %collective-permute-start.2 = (s32[2,64]{1,0:T(2,128)}, s32[2,64]{1,0:T(2,128)S(1)}, u32[]{:S(2)}, u32[]{:S(2)}) collective-permute-start(s32[2,64]{1,0:T(2,128)} %bitcast.29), channel_id=1, source_target_pairs={{0,4},{4,0},{8,12},{12,8},{16,20},{20,16},{24,28},{28,24},{1,5},{5... | collective-permute-start | bytes 1544 | tf_op jit(solution)/shard_map/ppermute | solution.py:191
  1.9 0.8 %select_bitcast_fusion = (bf16[64,256]{1,0:T(8,128)(2,1)S(1)}, bf16[64,256]{1,0:T(8,128)(2,1)S(1)}) fusion(bf16[1,2,64,256]{3,2,1,0:T(8,128)(2,1)} %param.8, pred[]{:T(512)} %bitcast.2, bf16[1,2,64,256]{3,2,1,0:T(8,128)(2,1)} %param.7), kind=kLoop, calls=%fused_computation.6 | loop fusion | flops 32768 | bytes 196609 | tf_op jit(solution)/shard_map/jit(_where)/select_n | solution.py:194
  2.7 0.2 collective-permute-done.2
  2.9 0.7 %pad_add_fusion.starts_ref = s32[4,64]{1,0:T(4,128)S(1)} fusion(s32[2,64]{1,0:T(2,128)S(1)} %collective-permute-done.2, s32[2,64]{1,0:T(2,128)} %bitcast.30), kind=kLoop, calls=%fused_computation.8 | loop fusion | flops 256 | bytes 2048 | tf_op jit(solution)/shard_map/concatenate | solution.py:201
  3.6 0.0 collective-permute-done.1
  3.6 0.0 collective-permute-done
  3.7 0.4 %collective-permute-start.3 = (bf16[2,64,2048]{2,1,0:T(8,128)(2,1)}, bf16[2,64,2048]{2,1,0:T(8,128)(2,1)S(1)}, u32[]{:S(2)}, u32[]{:S(2)}) collective-permute-start(bf16[2,64,2048]{2,1,0:T(8,128)(2,1)} %bitcast.20), channel_id=1, source_target_pairs={{0,4},{4,0},{8,12},{12,8},{16,20},{20,16},{24,28},{28,24},{1,5},{5... | collective-permute-start | bytes 1572872 | tf_op jit(solution)/shard_map/ppermute | solution.py:191
  4.1 0.2 collective-permute-start.4
  4.2 0.3 collective-permute-start.5
  4.6 1.3 %collective-permute-start.6 = (bf16[128,512]{1,0:T(8,128)(2,1)S(1)}, bf16[128,512]{1,0:T(8,128)(2,1)S(1)}, u32[]{:S(2)}, u32[]{:S(2)}) collective-permute-start(bf16[128,512]{1,0:T(8,128)(2,1)S(1)} %maximum_maximum_fusion.own_ref), channel_id=1, source_target_pairs={{0,16},{8,24},{16,28},{24,20},{28,12},{20,4},{1,17},{9,25},{17,29}... | collective-permute-start | bytes 393224 | tf_op jit(solution)/shard_map/ppermute | solution.py:184
  5.9 2.1 %collective-permute-start.7 = (bf16[128,512]{1,0:T(8,128)(2,1)S(1)}, bf16[128,512]{1,0:T(8,128)(2,1)S(1)}, u32[]{:S(2)}, u32[]{:S(2)}) collective-permute-start(bf16[128,512]{1,0:T(8,128)(2,1)S(1)} %maximum_maximum_fusion.own_ref), channel_id=1, source_target_pairs={{0,8},{8,16},{16,24},{24,28},{28,20},{20,12},{12,4},{1,9},{9,17},{... | collective-permute-start | bytes 393224 | tf_op jit(solution)/shard_map/ppermute | solution.py:184
  8.0 0.1 pad_add_fusion.1.place_ref
  8.0 0.0 copy-start
  8.0 1.0 %copy-done = bf16[1,2,64,2048]{3,2,1,0:T(8,128)(2,1)S(1)} copy-done((bf16[1,2,64,2048]{3,2,1,0:T(8,128)(2,1)S(1)}, bf16[1,2,64,2048]{3,2,1,0:T(8,128)(2,1)}, u32[]{:S(2)}) %copy-start) | copy-done | bytes 524312
  9.1 0.0 copy-start.1
  9.1 1.0 %copy-done.1 = bf16[1,2,64,2048]{3,2,1,0:T(8,128)(2,1)S(1)} copy-done((bf16[1,2,64,2048]{3,2,1,0:T(8,128)(2,1)S(1)}, bf16[1,2,64,2048]{3,2,1,0:T(8,128)(2,1)}, u32[]{:S(2)}) %copy-start.1) | copy-done | bytes 524312
  10.1 0.0 copy-start.2
  10.1 1.0 %copy-done.2 = bf16[1,2,64,2048]{3,2,1,0:T(8,128)(2,1)S(1)} copy-done((bf16[1,2,64,2048]{3,2,1,0:T(8,128)(2,1)S(1)}, bf16[1,2,64,2048]{3,2,1,0:T(8,128)(2,1)}, u32[]{:S(2)}) %copy-start.2) | copy-done | bytes 524312
  11.2 0.3 rows.2
  11.5 0.0 collective-permute-done.3.q_ref
  11.5 0.0 collective-permute-done.4.do_ref
  11.5 0.0 collective-permute-done.5.o_ref
  11.5 0.3 rows.3
  11.8 0.1 collective-permute-done.6.far_ref
  11.9 1.0 %collective-permute-done.7.near_ref = bf16[128,512]{1,0:T(8,128)(2,1)S(1)} collective-permute-done((bf16[128,512]{1,0:T(8,128)(2,1)S(1)}, bf16[128,512]{1,0:T(8,128)(2,1)S(1)}, u32[]{:S(2)}, u32[]{:S(2)}) %collective-permute-start.7) | collective-permute-done | bytes 131104 | tf_op jit(solution)/shard_map/ppermute | solution.py:184
  13.0 3.0 %scores.1 = (bf16[128,512]{1,0:T(8,128)(2,1)S(1)}, bf16[128,512]{1,0:T(8,128)(2,1)S(1)}, bf16[2,2,320,512]{3,2,1,0:T(8,128)(2,1)S(1)}, bf16[2,2,320,512]{3,2,1,0:T(8,128)(2,1)S(1)}) custom-call(s32[2]{0:T(128)S(1)} %pad_add_fusion.1.place_ref, s32[4,64]{1,0:T(4,128)S(1)} %pad_add_fusion.starts_ref, bf16[2,512,128]{2,1,0:T(8,128)(2,1)S(1)} %get-tuple-element.31.q_ref, ...), custom_call_target="tpu_custom_call" | custom-call | flops 503316480 | bytes 12582912 | tf_op jit(solution)/shard_map/scores/pallas_call | solution.py:232
  15.9 3.2 %collective-permute-start.8 = (bf16[128,512]{1,0:T(8,128)(2,1)S(1)}, bf16[128,512]{1,0:T(8,128)(2,1)S(1)}, u32[]{:S(2)}, u32[]{:S(2)}) collective-permute-start(bf16[128,512]{1,0:T(8,128)(2,1)S(1)} %get-tuple-element.38), channel_id=1, source_target_pairs={{8,0},{16,8},{24,16},{28,24},{20,28},{12,20},{4,12},{9,1},{17,9},{... | collective-permute-start | bytes 393224 | tf_op jit(solution)/shard_map/ppermute | solution.py:184
  19.2 5.2 %collective-permute-start.9 = (bf16[128,512]{1,0:T(8,128)(2,1)S(1)}, bf16[128,512]{1,0:T(8,128)(2,1)S(1)}, u32[]{:S(2)}, u32[]{:S(2)}) collective-permute-start(bf16[128,512]{1,0:T(8,128)(2,1)S(1)} %get-tuple-element.39), channel_id=1, source_target_pairs={{16,0},{24,8},{28,16},{20,24},{12,28},{4,20},{17,1},{25,9},{29,17}... | collective-permute-start | bytes 393224 | tf_op jit(solution)/shard_map/ppermute | solution.py:184
  24.3 2.0 %rest.1 = (bf16[2,64,2048]{2,1,0:T(8,128)(2,1)}, bf16[64,2048]{1,0:T(8,128)(2,1)S(1)}, f32[128,512]{1,0:T(8,128)S(1)}) custom-call(s32[2]{0:T(128)S(1)} %pad_add_fusion.1.place_ref, bf16[2,512,128]{2,1,0:T(8,128)(2,1)S(1)} %get-tuple-element.31.q_ref, bf16[2,512,128]{2,1,0:T(8,128)(2,1)S(1)} %get-tuple-element.32.do_ref, ...), custom_call_target="tpu_custom_call" | custom-call | flops 251658240 | bytes 8388608 | tf_op jit(solution)/shard_map/rest/pallas_call | solution.py:252
  26.4 0.0 collective-permute-done.8
  26.4 0.0 collective-permute-done.9
  26.4 3.8 %collective-permute-start.10 = (bf16[64,2048]{1,0:T(8,128)(2,1)S(1)}, bf16[64,2048]{1,0:T(8,128)(2,1)S(1)}, u32[]{:S(2)}, u32[]{:S(2)}) collective-permute-start(bf16[64,2048]{1,0:T(8,128)(2,1)S(1)} %get-tuple-element.43), channel_id=1, source_target_pairs={{0,4},{4,0},{8,12},{12,8},{16,20},{20,16},{24,28},{28,24},{1,5},{5... | collective-permute-start | bytes 786440 | tf_op jit(solution)/shard_map/ppermute | solution.py:191
  30.2 0.1 add_convert_fusion
  30.3 0.1 collective-permute-start.11
  30.3 1.2 %collective-permute-done.11.given_ref = bf16[64,512]{1,0:T(8,128)(2,1)S(1)} collective-permute-done((bf16[64,512]{1,0:T(8,128)(2,1)S(1)}, bf16[64,512]{1,0:T(8,128)(2,1)S(1)}, u32[]{:S(2)}, u32[]{:S(2)}) %collective-permute-start.11) | collective-permute-done | bytes 65568 | tf_op jit(solution)/shard_map/ppermute | solution.py:191
  31.6 0.0 collective-permute-done.10.rows_ref
  31.6 0.8 %store.1 = (bf16[2,64,2048]{2,1,0:T(8,128)(2,1)}, bf16[2,64,256]{2,1,0:T(8,128)(2,1)}, bf16[2,64,256]{2,1,0:T(8,128)(2,1)}) custom-call(s32[1]{0:T(128)} %bitcast.core_ref, bf16[64,2048]{1,0:T(8,128)(2,1)S(1)} %collective-permute-done.10.rows_ref, bf16[64,512]{1,0:T(8,128)(2,1)S(1)} %get-tuple-element.52.kept_ref, ...), custom_call_target="tpu_custom_call", output_to_operand_aliasing={{0}: (4, {})} | custom-call | tf_op jit(solution)/shard_map/store/pallas_call | solution.py:276
  (4 shorter events, 0.0 us)
Async XLA Ops:
  0.6 3.0 %collective-permute-start.1 = (bf16[2,64,256]{2,1,0:T(8,128)(2,1)}, bf16[2,64,256]{2,1,0:T(8,128)(2,1)S(1)}, u32[]{:S(2)}, u32[]{:S(2)}) collective-permute-start(bf16[2,64,256]{2,1,0:T(8,128)(2,1)} %bitcast.27), channel_id=1, source_target_pairs={{0,4},{4,0},{8,12},{12,8},{16,20},{20,16},{24,28},{28,24},{1,5},{5... | collective-permute-start | bytes 196616 | tf_op jit(solution)/shard_map/ppermute | solution.py:191
  1.4 2.3 %collective-permute-start = (bf16[2,64,256]{2,1,0:T(8,128)(2,1)}, bf16[2,64,256]{2,1,0:T(8,128)(2,1)S(1)}, u32[]{:S(2)}, u32[]{:S(2)}) collective-permute-start(bf16[2,64,256]{2,1,0:T(8,128)(2,1)} %bitcast.28), channel_id=1, source_target_pairs={{0,4},{4,0},{8,12},{12,8},{16,20},{20,16},{24,28},{28,24},{1,5},{5... | collective-permute-start | bytes 196616 | tf_op jit(solution)/shard_map/ppermute | solution.py:191
  1.4 1.5 %collective-permute-start.2 = (s32[2,64]{1,0:T(2,128)}, s32[2,64]{1,0:T(2,128)S(1)}, u32[]{:S(2)}, u32[]{:S(2)}) collective-permute-start(s32[2,64]{1,0:T(2,128)} %bitcast.29), channel_id=1, source_target_pairs={{0,4},{4,0},{8,12},{12,8},{16,20},{20,16},{24,28},{28,24},{1,5},{5... | collective-permute-start | bytes 1544 | tf_op jit(solution)/shard_map/ppermute | solution.py:191
  3.7 7.8 %collective-permute-start.3 = (bf16[2,64,2048]{2,1,0:T(8,128)(2,1)}, bf16[2,64,2048]{2,1,0:T(8,128)(2,1)S(1)}, u32[]{:S(2)}, u32[]{:S(2)}) collective-permute-start(bf16[2,64,2048]{2,1,0:T(8,128)(2,1)} %bitcast.20), channel_id=1, source_target_pairs={{0,4},{4,0},{8,12},{12,8},{16,20},{20,16},{24,28},{28,24},{1,5},{5... | collective-permute-start | bytes 1572872 | tf_op jit(solution)/shard_map/ppermute | solution.py:191
  4.1 7.4 %collective-permute-start.4 = (bf16[2,64,2048]{2,1,0:T(8,128)(2,1)}, bf16[2,64,2048]{2,1,0:T(8,128)(2,1)S(1)}, u32[]{:S(2)}, u32[]{:S(2)}) collective-permute-start(bf16[2,64,2048]{2,1,0:T(8,128)(2,1)} %bitcast.22), channel_id=1, source_target_pairs={{0,4},{4,0},{8,12},{12,8},{16,20},{20,16},{24,28},{28,24},{1,5},{5... | collective-permute-start | bytes 1572872 | tf_op jit(solution)/shard_map/ppermute | solution.py:191
  4.2 7.2 %collective-permute-start.5 = (bf16[2,64,2048]{2,1,0:T(8,128)(2,1)}, bf16[2,64,2048]{2,1,0:T(8,128)(2,1)S(1)}, u32[]{:S(2)}, u32[]{:S(2)}) collective-permute-start(bf16[2,64,2048]{2,1,0:T(8,128)(2,1)} %bitcast.24), channel_id=1, source_target_pairs={{0,4},{4,0},{8,12},{12,8},{16,20},{20,16},{24,28},{28,24},{1,5},{5... | collective-permute-start | bytes 1572872 | tf_op jit(solution)/shard_map/ppermute | solution.py:191
  4.6 7.4 %collective-permute-start.6 = (bf16[128,512]{1,0:T(8,128)(2,1)S(1)}, bf16[128,512]{1,0:T(8,128)(2,1)S(1)}, u32[]{:S(2)}, u32[]{:S(2)}) collective-permute-start(bf16[128,512]{1,0:T(8,128)(2,1)S(1)} %maximum_maximum_fusion.own_ref), channel_id=1, source_target_pairs={{0,16},{8,24},{16,28},{24,20},{28,12},{20,4},{1,17},{9,25},{17,29}... | collective-permute-start | bytes 393224 | tf_op jit(solution)/shard_map/ppermute | solution.py:184
  5.9 7.1 %collective-permute-start.7 = (bf16[128,512]{1,0:T(8,128)(2,1)S(1)}, bf16[128,512]{1,0:T(8,128)(2,1)S(1)}, u32[]{:S(2)}, u32[]{:S(2)}) collective-permute-start(bf16[128,512]{1,0:T(8,128)(2,1)S(1)} %maximum_maximum_fusion.own_ref), channel_id=1, source_target_pairs={{0,8},{8,16},{16,24},{24,28},{28,20},{20,12},{12,4},{1,9},{9,17},{... | collective-permute-start | bytes 393224 | tf_op jit(solution)/shard_map/ppermute | solution.py:184
  8.0 1.0 %copy-start = (bf16[1,2,64,2048]{3,2,1,0:T(8,128)(2,1)S(1)}, bf16[1,2,64,2048]{3,2,1,0:T(8,128)(2,1)}, u32[]{:S(2)}) copy-start(bf16[1,2,64,2048]{3,2,1,0:T(8,128)(2,1)} %param.6) | copy-start | bytes 1572868
  9.1 1.0 %copy-start.1 = (bf16[1,2,64,2048]{3,2,1,0:T(8,128)(2,1)S(1)}, bf16[1,2,64,2048]{3,2,1,0:T(8,128)(2,1)}, u32[]{:S(2)}) copy-start(bf16[1,2,64,2048]{3,2,1,0:T(8,128)(2,1)} %param.9) | copy-start | bytes 1572868
  10.1 1.0 %copy-start.2 = (bf16[1,2,64,2048]{3,2,1,0:T(8,128)(2,1)S(1)}, bf16[1,2,64,2048]{3,2,1,0:T(8,128)(2,1)}, u32[]{:S(2)}) copy-start(bf16[1,2,64,2048]{3,2,1,0:T(8,128)(2,1)} %param.10) | copy-start | bytes 1572868
  15.9 10.4 %collective-permute-start.8 = (bf16[128,512]{1,0:T(8,128)(2,1)S(1)}, bf16[128,512]{1,0:T(8,128)(2,1)S(1)}, u32[]{:S(2)}, u32[]{:S(2)}) collective-permute-start(bf16[128,512]{1,0:T(8,128)(2,1)S(1)} %get-tuple-element.38), channel_id=1, source_target_pairs={{8,0},{16,8},{24,16},{28,24},{20,28},{12,20},{4,12},{9,1},{17,9},{... | collective-permute-start | bytes 393224 | tf_op jit(solution)/shard_map/ppermute | solution.py:184
  19.2 7.2 %collective-permute-start.9 = (bf16[128,512]{1,0:T(8,128)(2,1)S(1)}, bf16[128,512]{1,0:T(8,128)(2,1)S(1)}, u32[]{:S(2)}, u32[]{:S(2)}) collective-permute-start(bf16[128,512]{1,0:T(8,128)(2,1)S(1)} %get-tuple-element.39), channel_id=1, source_target_pairs={{16,0},{24,8},{28,16},{20,24},{12,28},{4,20},{17,1},{25,9},{29,17}... | collective-permute-start | bytes 393224 | tf_op jit(solution)/shard_map/ppermute | solution.py:184
  26.4 5.2 %collective-permute-start.10 = (bf16[64,2048]{1,0:T(8,128)(2,1)S(1)}, bf16[64,2048]{1,0:T(8,128)(2,1)S(1)}, u32[]{:S(2)}, u32[]{:S(2)}) collective-permute-start(bf16[64,2048]{1,0:T(8,128)(2,1)S(1)} %get-tuple-element.43), channel_id=1, source_target_pairs={{0,4},{4,0},{8,12},{12,8},{16,20},{20,16},{24,28},{28,24},{1,5},{5... | collective-permute-start | bytes 786440 | tf_op jit(solution)/shard_map/ppermute | solution.py:191
  30.3 1.3 %collective-permute-start.11 = (bf16[64,512]{1,0:T(8,128)(2,1)S(1)}, bf16[64,512]{1,0:T(8,128)(2,1)S(1)}, u32[]{:S(2)}, u32[]{:S(2)}) collective-permute-start(bf16[64,512]{1,0:T(8,128)(2,1)S(1)} %get-tuple-element.51), channel_id=1, source_target_pairs={{0,4},{4,0},{8,12},{12,8},{16,20},{20,16},{24,28},{28,24},{1,5},{5... | collective-permute-start | bytes 196616 | tf_op jit(solution)/shard_map/ppermute | solution.py:191

commit v7 on v6

v7 whole, which is shorter than its diff:
```python
import functools

import jax
import jax.numpy as jnp
from jax import lax
from jax.experimental import pallas as pl
from jax.experimental.pallas import tpu as pltpu
from jax.sharding import PartitionSpec as P

HEAD_SIZE = 128
STEPS = 4
LOG2E = 1.4426950408889634
CONTRACT_LAST = (((1,), (1,)), ((), ()))
CONTRACT_ROWS = (((1,), (0,)), ((), ()))
VMEM = pl.BlockSpec(memory_space=pltpu.VMEM)
SMEM = pl.BlockSpec(memory_space=pltpu.SMEM)
HBM = pl.BlockSpec(memory_space=pltpu.HBM)
PARAMS = pltpu.CompilerParams(vmem_limit_bytes=24 * 2**20)
SMALL = pltpu.CompilerParams(vmem_limit_bytes=4 * 2**20)


def dot(a, b, dims=CONTRACT_ROWS):
    return lax.dot_general(a, b, dims, preferred_element_type=jnp.float32)


def stack_heads(ref, first, count):
    return jnp.concatenate(
        [ref[:, (first + a) * HEAD_SIZE : (first + a + 1) * HEAD_SIZE] for a in range(count)],
        axis=0,
    )


def unit_starts(starts_ref, core, unit):
    side = starts_ref[2 * unit : 2 * unit + 2, :]
    return jnp.where(core == 0, side[0:1, :], side[1:2, :])


def rows_kernel(
    unit, place_ref, starts_ref, own_ref, q_ref, do_ref, o_ref,
    q_out_ref, do_out_ref, scores_ref, dprobs_ref, delta_ref,
):
    core, begin = place_ref[0], place_ref[1]
    tokens = q_ref.shape[1]
    kv_heads, reach, lanes = scores_ref.shape
    kv_width = kv_heads * HEAD_SIZE
    group = lanes // tokens
    factor = HEAD_SIZE ** (-0.5) * LOG2E
    ones = jnp.ones((delta_ref.shape[1], 2 * HEAD_SIZE), jnp.bfloat16)
    low = unit_starts(starts_ref, core, unit) - begin
    high = lax.broadcasted_iota(jnp.int32, (1, tokens), 1) + unit * tokens
    row = lax.broadcasted_iota(jnp.int32, (reach, tokens), 0)
    bias = jnp.where((row >= low) & (row <= high), 0.0, -jnp.inf)
    bias = jnp.concatenate([bias] * group, axis=1)
    for g in range(kv_heads):
        q, do, o = (
            stack_heads(r.at[core], g * group, group) for r in (q_ref, do_ref, o_ref)
        )
        keys = own_ref[:reach, g * HEAD_SIZE : (g + 1) * HEAD_SIZE]
        values = own_ref[:reach, kv_width + g * HEAD_SIZE : kv_width + (g + 1) * HEAD_SIZE]
        terms = do.astype(jnp.float32) * o.astype(jnp.float32)
        coarse = terms.astype(jnp.bfloat16)
        fine = (terms - coarse.astype(jnp.float32)).astype(jnp.bfloat16)
        delta = dot(ones, jnp.concatenate([coarse, fine], axis=1), CONTRACT_LAST)
        delta_ref[g] = delta
        scores_ref[g] = dot(keys, q, CONTRACT_LAST) * factor + bias
        dprobs_ref[g] = dot(values, do, CONTRACT_LAST) - delta[:1]
        q_out_ref[g] = q
        do_out_ref[g] = do


def scores_kernel(
    place_ref, starts_ref, q_ref, do_ref, held_ref, delta_ref, q_in_ref, do_in_ref, held_in_ref,
    delta_in_ref, far_ref, near_ref, far_part_ref, near_part_ref, dscores_ref, norm_ref,
    window_ref, part_ref,
):
    core, begin = place_ref[0], place_ref[1]
    tokens = starts_ref.shape[1]
    kv_heads, lanes = q_ref.shape[:2]
    kv_width = kv_heads * HEAD_SIZE
    group = lanes // tokens
    scale = HEAD_SIZE ** (-0.5)
    pair = 2 * tokens
    for n, source in enumerate((far_ref, near_ref)):
        window_ref[n * pair : (n + 1) * pair, :] = source[...]
    offset = lax.broadcasted_iota(jnp.int32, (1, tokens), 1)
    sides = (
        (q_ref, do_ref, held_ref, delta_ref), (q_in_ref, do_in_ref, held_in_ref, delta_in_ref)
    )
    for unit, (q_side, do_side, held_side, delta_side) in enumerate(sides):
        first = unit * tokens
        before = 2 * pair - first
        low = unit_starts(starts_ref, core, unit) - (begin + (unit - STEPS) * tokens)
        low = jnp.maximum(offset + 1, low)
        low = jnp.concatenate([low] * group, axis=1)
        for g in range(kv_heads):
            at = (g * HEAD_SIZE, kv_width + g * HEAD_SIZE)
            keys = window_ref[first:, at[0] : at[0] + HEAD_SIZE]
            values = window_ref[first:, at[1] : at[1] + HEAD_SIZE]
            q, do, held = q_side[g], do_side[g], held_side[g]
            scores = dot(keys, q, CONTRACT_LAST) * (scale * LOG2E)
            row = lax.broadcasted_iota(jnp.int32, scores.shape, 0)
            scores = jnp.where(row >= low, scores, -jnp.inf)
            top = jnp.maximum(
                jnp.max(scores, axis=0, keepdims=True), jnp.max(held, axis=0, keepdims=True)
            )
            weights = jnp.exp2(scores - top)
            total = jnp.sum(weights, axis=0, keepdims=True)
            total += jnp.sum(jnp.exp2(held - top), axis=0, keepdims=True)
            inverse = 1.0 / total
            probs = weights * inverse
            norm_ref[unit, g, 0:1] = top
            norm_ref[unit, g, 1:2] = inverse
            dprobs = dot(values, do, CONTRACT_LAST) - delta_side[g, :1]
            dscores = (probs * dprobs).astype(jnp.bfloat16)
            dscores_ref[unit, g, :before] = dscores
            for part, column in (
                (dot(dscores, q) * scale, at[0]),
                (dot(probs.astype(jnp.bfloat16), do), at[1]),
            ):
                columns = slice(column, column + HEAD_SIZE)
                if unit == 0:
                    part_ref[:, columns] = part
                else:
                    part_ref[first:, columns] += part
    far_part_ref[...] = part_ref[:pair, :].astype(jnp.bfloat16)
    near_part_ref[...] = part_ref[pair:, :].astype(jnp.bfloat16)


def rest_kernel(
    place_ref, q_ref, do_ref, held_ref, dprobs_ref, q_in_ref, do_in_ref, held_in_ref,
    dprobs_in_ref, far_ref, near_ref, own_ref, dscores_ref, norm_ref,
    dq_ref, dq_send_ref, own_part_ref, window_ref, rows_ref, sem,
):
    core = place_ref[0]
    tokens = dq_send_ref.shape[0]
    kv_heads, lanes = q_ref.shape[:2]
    kv_width = kv_heads * HEAD_SIZE
    group = lanes // tokens
    scale = HEAD_SIZE ** (-0.5)
    pair = 2 * tokens
    for n, source in enumerate((far_ref, near_ref)):
        window_ref[n * pair : (n + 1) * pair, :] = source[:, :kv_width]
    store = pltpu.make_async_copy(rows_ref, dq_ref.at[core], sem)
    sides = (
        (1, dq_send_ref, q_in_ref, do_in_ref, held_in_ref, dprobs_in_ref),
        (0, rows_ref, q_ref, do_ref, held_ref, dprobs_ref),
    )
    for unit, target, q_side, do_side, held_side, dprobs_side in sides:
        first = unit * tokens
        before = 2 * pair - first
        reach = held_side.shape[1]
        for g in range(kv_heads):
            at = (g * HEAD_SIZE, kv_width + g * HEAD_SIZE)
            top, inverse = norm_ref[unit, g, 0:1], norm_ref[unit, g, 1:2]
            probs = jnp.exp2(held_side[g] - top) * inverse
            dscores = (probs * dprobs_side[g]).astype(jnp.bfloat16)
            keys = window_ref[first:, at[0] : at[0] + HEAD_SIZE]
            own_keys = own_ref[:reach, at[0] : at[0] + HEAD_SIZE]
            dq_t = dot(keys.T, dscores_ref[unit, g, :before]) + dot(own_keys.T, dscores)
            dq = (dq_t * scale).astype(jnp.bfloat16).T
            for a in range(group):
                column = (g * group + a) * HEAD_SIZE
                target[:, column : column + HEAD_SIZE] = dq[a * tokens : (a + 1) * tokens]
            if unit == 0 and g == kv_heads - 1:
                store.start()
            for part, column in (
                (dot(dscores, q_side[g]) * scale, at[0]),
                (dot(probs.astype(jnp.bfloat16), do_side[g]), at[1]),
            ):
                columns = slice(column, column + HEAD_SIZE)
                if unit == 1:
                    own_part_ref[:, columns] = part
                else:
                    own_part_ref[:reach, columns] += part
    store.wait()


def store_kernel(
    core_ref, rows_ref, kept_ref, given_ref, held_ref, dq_ref, key_ref, value_ref, sems
):
    core = core_ref[0]
    width = key_ref.shape[-1]
    copies = [pltpu.make_async_copy(rows_ref, dq_ref.at[1 - core], sems.at[0, 0])]
    for n, (source, slot) in enumerate(((kept_ref, core), (given_ref, 1 - core))):
        for m, target in enumerate((key_ref, value_ref)):
            copies.append(
                pltpu.make_async_copy(
                    source.at[:, pl.ds(m * width, width)], target.at[slot], sems.at[n + 1, m]
                )
            )
    for copy in copies:
        copy.start()
    for copy in copies:
        copy.wait()


def shards(query, key, value, out_grad, attn_out, doc_start):
    count = lax.axis_size("ctx")
    index = lax.axis_index("ctx")
    _, slots, tokens, width = query.shape
    kv_width = key.shape[-1]
    pair_width = 2 * kv_width
    pair = 2 * tokens
    core = (index % 2).astype(jnp.int32)
    stage = jnp.where(core == 0, index // 2, count - 1 - index // 2).astype(jnp.int32)
    core = core[None]
    place = jnp.stack([core[0], stage * pair])
    holder = [2 * s if 2 * s < count else 2 * count - 1 - 2 * s for s in range(count)]
    swap = [(i, i ^ 1) for i in range(count)]

    def shift(x, by):
        moves = [
            (holder[s], holder[s + by]) for s in range(count) if 0 <= s + by < count
        ]
        return lax.ppermute(x, "ctx", moves)

    bf16 = jnp.bfloat16
    def work(flops, moved):
        return pl.CostEstimate(flops=flops, bytes_accessed=moved, transcendentals=0)

    def swapped(x):
        return lax.ppermute(x, "ctx", swap)

    def mine(x):
        return jnp.where(core == 0, x[0], x[1])

    starts_in, key_in, value_in = (swapped(x[0]) for x in (doc_start, key, value))
    sides = ((key[0], value[0]), (key_in, value_in))
    own = jnp.concatenate(
        [jnp.concatenate([mine(x) for x in side], axis=-1) for side in sides], axis=0
    )
    own, starts_in, starts, *late = lax.optimization_barrier(
        (own, starts_in, doc_start[0], query[0], out_grad[0], attn_out[0])
    )
    starts = jnp.concatenate([starts, starts_in], axis=0)
    kv_heads = kv_width // HEAD_SIZE
    lanes = tokens * (width // kv_width)
    products = 2 * slots * tokens * pair * width

    def arranged(unit, sources):
        stacked = jax.ShapeDtypeStruct((kv_heads, lanes, HEAD_SIZE), bf16)
        square = jax.ShapeDtypeStruct((kv_heads, (unit + 1) * tokens, lanes), jnp.float32)
        q, do, scores, dprobs, delta = pl.pallas_call(
            functools.partial(rows_kernel, unit),
            out_shape=(
                stacked,
                stacked,
                square,
                square,
                jax.ShapeDtypeStruct((kv_heads, 8, lanes), jnp.float32),
            ),
            in_specs=[SMEM] + [VMEM] * 5,
            out_specs=(VMEM,) * 5,
            compiler_params=SMALL,
            cost_estimate=work(products // 2, 4 * 2**20),
            name="rows",
        )(place, starts, own, *sources)
        return (q, do, scores, delta), (q, do, scores, dprobs)

    sent = [swapped(x) for x in late]
    far = shift(own, 2)
    near = shift(own, 1)
    sides = arranged(0, late), arranged(1, sent)
    far_part, near_part, dscores, norm = pl.pallas_call(
        scores_kernel,
        out_shape=(
            jax.ShapeDtypeStruct((pair, pair_width), bf16),
            jax.ShapeDtypeStruct((pair, pair_width), bf16),
            jax.ShapeDtypeStruct((slots, kv_heads, 2 * pair, lanes), bf16),
            jax.ShapeDtypeStruct((slots, kv_heads, 8, lanes), jnp.float32),
        ),
        in_specs=[SMEM] + [VMEM] * 11,
        out_specs=(VMEM,) * 4,
        scratch_shapes=[
            pltpu.VMEM((2 * pair, pair_width), bf16),
            pltpu.VMEM((2 * pair, pair_width), jnp.float32),
        ],
        compiler_params=PARAMS,
        cost_estimate=work(6 * products, 12 * 2**20),
        name="scores",
    )(place, starts, *sides[0][0], *sides[1][0], far, near)
    from_far = shift(far_part, -2)
    from_near = shift(near_part, -1)
    dq, dq_send, own_part = pl.pallas_call(
        rest_kernel,
        out_shape=(
            jax.ShapeDtypeStruct((slots, tokens, width), bf16),
            jax.ShapeDtypeStruct((tokens, width), bf16),
            jax.ShapeDtypeStruct((pair, pair_width), jnp.float32),
        ),
        in_specs=[SMEM] + [VMEM] * 13,
        out_specs=(HBM, VMEM, VMEM),
        scratch_shapes=[
            pltpu.VMEM((2 * pair, kv_width), bf16),
            pltpu.VMEM((tokens, width), bf16),
            pltpu.SemaphoreType.DMA,
        ],
        compiler_params=PARAMS,
        cost_estimate=work(3 * products, 8 * 2**20),
        name="rest",
    )(place, *sides[0][1], *sides[1][1], far, near, own, dscores, norm)
    from_near, from_far, dq_send = lax.optimization_barrier((from_near, from_far, dq_send))
    dq_rows = swapped(dq_send)
    total = own_part + from_near.astype(jnp.float32) + from_far.astype(jnp.float32)
    total = total.astype(bf16)
    kept = total[:tokens]
    given = swapped(total[tokens:])
    dq, dk, dv = pl.pallas_call(
        store_kernel,
        out_shape=(
            jax.ShapeDtypeStruct(dq.shape, bf16),
            jax.ShapeDtypeStruct((slots, tokens, kv_width), bf16),
            jax.ShapeDtypeStruct((slots, tokens, kv_width), bf16),
        ),
        in_specs=[SMEM, VMEM, VMEM, VMEM, HBM],
        out_specs=(HBM,) * 3,
        scratch_shapes=[pltpu.SemaphoreType.DMA((3, 2))],
        input_output_aliases={4: 0},
        compiler_params=SMALL,
        name="store",
    )(core, dq_rows, kept, given, dq)
    return dq[None], dk[None], dv[None]


def solution(mesh):
    placed = (P("ctx", "dp", None, None),) * 5 + (P("ctx", "dp", None),)
    return jax.shard_map(
        shards,
        mesh=mesh,
        in_specs=placed,
        out_specs=(P("ctx", "dp", None, None),) * 3,
        check_vma=False,
    )
```

time: 32.8 us -> 32.3 us (0.985)
  Pallas kernels: 6.4 us -> 7.57 us
  other arithmetic: 1.66 us -> 0.98 us
  local copies, waits for them, and re-layouts: 3.13 us -> 2.69 us
    pallas_call x2, Pallas kernels: 0.6 us -> 2.03 us  [arranged(): pl.pallas_call(functools.partial(rows_kernel, unit), out_shape=(stacked,...]
    concatenate x1, other arithmetic: 0.69 us -> 0.01 us  [shards(): starts = jnp.concatenate([starts, starts_in], axis=0)]
    unnamed x6 -> x8, local copies, waits for them, and re-layouts: 3.12 us -> 2.68 us
  transfers between devices with their start and end apart: 12 -> 12, of which waited for: 4 -> 5; matrix products, arithmetic and copies ran while one was open for 5% -> 3% of each run, Pallas kernels for 8% -> 13%
where the time goes in v7:
time: 32.3 us; the launch traced here: 31.9 us
  starting transfers between devices  17.5 us (54%)
  Pallas kernels  7.57 us (23%)
  local copies, waits for them, and re-layouts  2.69 us (8%)
  waiting for transfers between devices  2.36 us (7%)
  other arithmetic  0.98 us (3%)
  between operations  0.8 us (2%)
    ppermute x4, starting transfers between devices, shift(): return lax.ppermute(x, 'ctx', moves)  11.7 us
    ppermute x8, starting transfers between devices, swapped(): return lax.ppermute(x, 'ctx', swap)  5.77 us
    pallas_call x1, Pallas kernels, shards(): pl.pallas_call(scores_kernel, out_shape=(jax.ShapeDtypeStruct((pair, pair...  2.74 us
    unnamed x8, local copies, waits for them, and re-layouts  2.68 us
    pallas_call x2, Pallas kernels, arranged(): pl.pallas_call(functools.partial(rows_kernel, unit), out_shape=(stacked,...  2.03 us
    pallas_call x1, Pallas kernels, shards(): pl.pallas_call(rest_kernel, out_shape=(jax.ShapeDtypeStruct((slots, token...  2.02 us
    ppermute x8, waiting for transfers between devices, swapped(): return lax.ppermute(x, 'ctx', swap)  1.41 us
    ppermute x4, waiting for transfers between devices, shift(): return lax.ppermute(x, 'ctx', moves)  0.94 us
  transfers between devices with their start and end apart: 12, of which 5 were waited for; matrix products, arithmetic and copies ran while one was open for 3% of the time, Pallas kernels for 13%

profile of v7, /device:TPU:13, one launch (start us, length us, event | category | flops | bytes accessed | tf_op | source)
XLA Modules:
  0.0 31.9 jit_solution(13472010090164737861)
XLA Ops:
  0.6 0.0 copy-start
  0.6 0.7 %collective-permute-start.1 = (bf16[2,64,256]{2,1,0:T(8,128)(2,1)}, bf16[2,64,256]{2,1,0:T(8,128)(2,1)S(1)}, u32[]{:S(2)}, u32[]{:S(2)}) collective-permute-start(bf16[2,64,256]{2,1,0:T(8,128)(2,1)} %bitcast.27), channel_id=1, source_target_pairs={{0,4},{4,0},{8,12},{12,8},{16,20},{20,16},{24,28},{28,24},{1,5},{5... | collective-permute-start | bytes 196616 | tf_op jit(solution)/shard_map/ppermute | solution.py:222
  1.4 0.1 collective-permute-start
  1.5 0.4 %collective-permute-start.2 = (s32[2,64]{1,0:T(2,128)}, s32[2,64]{1,0:T(2,128)S(1)}, u32[]{:S(2)}, u32[]{:S(2)}) collective-permute-start(s32[2,64]{1,0:T(2,128)} %bitcast.29), channel_id=1, source_target_pairs={{0,4},{4,0},{8,12},{12,8},{16,20},{20,16},{24,28},{28,24},{1,5},{5... | collective-permute-start | bytes 1544 | tf_op jit(solution)/shard_map/ppermute | solution.py:222
  1.9 0.8 %select_bitcast_fusion = (bf16[64,256]{1,0:T(8,128)(2,1)S(1)}, bf16[64,256]{1,0:T(8,128)(2,1)S(1)}) fusion(bf16[1,2,64,256]{3,2,1,0:T(8,128)(2,1)} %param.8, pred[]{:T(512)} %bitcast.2, bf16[1,2,64,256]{3,2,1,0:T(8,128)(2,1)} %param.7), kind=kLoop, calls=%fused_computation.6 | loop fusion | flops 32768 | bytes 196609 | tf_op jit(solution)/shard_map/jit(_where)/select_n | solution.py:225
  2.7 0.0 collective-permute-done.1
  2.7 0.1 collective-permute-done
  2.9 0.1 collective-permute-done.2
  2.9 0.0 copy-done
  2.9 0.3 %collective-permute-start.3 = (bf16[2,64,2048]{2,1,0:T(8,128)(2,1)S(1)}, bf16[2,64,2048]{2,1,0:T(8,128)(2,1)S(1)}, u32[]{:S(2)}, u32[]{:S(2)}) collective-permute-start(bf16[2,64,2048]{2,1,0:T(8,128)(2,1)S(1)} %bitcast.20), channel_id=1, source_target_pairs={{0,4},{4,0},{8,12},{12,8},{16,20},{20,16},{24,28},{28,24},{1,5},{5... | collective-permute-start | bytes 1572872 | tf_op jit(solution)/shard_map/ppermute | solution.py:222
  3.2 0.2 collective-permute-start.4
  3.5 0.3 collective-permute-start.5
  3.8 1.3 %collective-permute-start.6 = (bf16[128,512]{1,0:T(8,128)(2,1)S(1)}, bf16[128,512]{1,0:T(8,128)(2,1)S(1)}, u32[]{:S(2)}, u32[]{:S(2)}) collective-permute-start(bf16[128,512]{1,0:T(8,128)(2,1)S(1)} %maximum_maximum_fusion.own_ref), channel_id=1, source_target_pairs={{0,16},{8,24},{16,28},{24,20},{28,12},{20,4},{1,17},{9,25},{17,29}... | collective-permute-start | bytes 393224 | tf_op jit(solution)/shard_map/ppermute | solution.py:215
  5.0 2.1 %collective-permute-start.7 = (bf16[128,512]{1,0:T(8,128)(2,1)S(1)}, bf16[128,512]{1,0:T(8,128)(2,1)S(1)}, u32[]{:S(2)}, u32[]{:S(2)}) collective-permute-start(bf16[128,512]{1,0:T(8,128)(2,1)S(1)} %maximum_maximum_fusion.own_ref), channel_id=1, source_target_pairs={{0,8},{8,16},{16,24},{24,28},{28,20},{20,12},{12,4},{1,9},{9,17},{... | collective-permute-start | bytes 393224 | tf_op jit(solution)/shard_map/ppermute | solution.py:215
  7.1 0.0 copy-start.3
  7.1 0.1 pad_add_fusion.1.place_ref
  7.2 0.6 %copy-done.3 = s32[1,2,64]{2,1,0:T(2,128)S(1)} copy-done((s32[1,2,64]{2,1,0:T(2,128)S(1)}, s32[1,2,64]{2,1,0:T(2,128)}, u32[]{:S(2)}) %copy-start.3) | copy-done | bytes 536
  7.8 0.0 copy-start.1
  7.8 1.0 %copy-done.1 = bf16[1,2,64,2048]{3,2,1,0:T(8,128)(2,1)S(1)} copy-done((bf16[1,2,64,2048]{3,2,1,0:T(8,128)(2,1)S(1)}, bf16[1,2,64,2048]{3,2,1,0:T(8,128)(2,1)}, u32[]{:S(2)}) %copy-start.1) | copy-done | bytes 524312
  8.9 0.0 copy-start.2
  8.9 1.0 %copy-done.2 = bf16[1,2,64,2048]{3,2,1,0:T(8,128)(2,1)S(1)} copy-done((bf16[1,2,64,2048]{3,2,1,0:T(8,128)(2,1)S(1)}, bf16[1,2,64,2048]{3,2,1,0:T(8,128)(2,1)}, u32[]{:S(2)}) %copy-start.2) | copy-done | bytes 524312
  9.9 1.0 %rows.2 = (bf16[2,512,128]{2,1,0:T(8,128)(2,1)S(1)}, bf16[2,512,128]{2,1,0:T(8,128)(2,1)S(1)}, f32[2,64,512]{2,1,0:T(8,128)S(1)}, f32[2,64,512]{2,1,0:T(8,128)S(1)}, f32[2,8,512]{2,1,0:T(8,128)S(1)}) custom-call(s32[2]{0:T(128)S(1)} %pad_add_fusion.1.place_ref, s32[4,64]{1,0:T(4,128)S(1)} %pad_add_fusion.starts_ref, ...), custom_call_target="tpu_custom_call" | custom-call | flops 33554432 | bytes 4194304 | tf_op jit(solution)/shard_map/rows/pallas_call | solution.py:243
  10.9 0.0 collective-permute-done.3.q_ref
  10.9 0.0 collective-permute-done.4.do_ref
  10.9 0.0 collective-permute-done.5.o_ref
  10.9 1.0 %rows.3 = (bf16[2,512,128]{2,1,0:T(8,128)(2,1)S(1)}, bf16[2,512,128]{2,1,0:T(8,128)(2,1)S(1)}, f32[2,128,512]{2,1,0:T(8,128)S(1)}, f32[2,128,512]{2,1,0:T(8,128)S(1)}, f32[2,8,512]{2,1,0:T(8,128)S(1)}) custom-call(s32[2]{0:T(128)S(1)} %pad_add_fusion.1.place_ref, s32[4,64]{1,0:T(4,128)S(1)} %pad_add_fusion.starts_ref, ...), custom_call_target="tpu_custom_call" | custom-call | flops 33554432 | bytes 4194304 | tf_op jit(solution)/shard_map/rows/pallas_call | solution.py:243
  12.0 0.0 collective-permute-done.6.far_ref
  12.0 0.2 collective-permute-done.7.near_ref
  12.2 2.7 %scores.1 = (bf16[128,512]{1,0:T(8,128)(2,1)S(1)}, bf16[128,512]{1,0:T(8,128)(2,1)S(1)}, bf16[2,2,256,512]{3,2,1,0:T(8,128)(2,1)S(1)}, f32[2,2,8,512]{3,2,1,0:T(8,128)S(1)}) custom-call(s32[2]{0:T(128)S(1)} %pad_add_fusion.1.place_ref, s32[4,64]{1,0:T(4,128)S(1)} %pad_add_fusion.starts_ref, bf16[2,512,128]{2,1,0:T(8,128)(2,1)S(1)} %get-tuple-element.38.q_ref, ...), custom_call_target="tpu_custom_call" | custom-call | flops 402653184 | bytes 12582912 | tf_op jit(solution)/shard_map/scores/pallas_call | solution.py:264
  14.9 3.6 %collective-permute-start.8 = (bf16[128,512]{1,0:T(8,128)(2,1)S(1)}, bf16[128,512]{1,0:T(8,128)(2,1)S(1)}, u32[]{:S(2)}, u32[]{:S(2)}) collective-permute-start(bf16[128,512]{1,0:T(8,128)(2,1)S(1)} %get-tuple-element.46), channel_id=1, source_target_pairs={{8,0},{16,8},{24,16},{28,24},{20,28},{12,20},{4,12},{9,1},{17,9},{... | collective-permute-start | bytes 393224 | tf_op jit(solution)/shard_map/ppermute | solution.py:215
  18.5 4.8 %collective-permute-start.9 = (bf16[128,512]{1,0:T(8,128)(2,1)S(1)}, bf16[128,512]{1,0:T(8,128)(2,1)S(1)}, u32[]{:S(2)}, u32[]{:S(2)}) collective-permute-start(bf16[128,512]{1,0:T(8,128)(2,1)S(1)} %get-tuple-element.47), channel_id=1, source_target_pairs={{16,0},{24,8},{28,16},{20,24},{12,28},{4,20},{17,1},{25,9},{29,17}... | collective-permute-start | bytes 393224 | tf_op jit(solution)/shard_map/ppermute | solution.py:215
  23.3 2.0 %rest.1 = (bf16[2,64,2048]{2,1,0:T(8,128)(2,1)}, bf16[64,2048]{1,0:T(8,128)(2,1)S(1)}, f32[128,512]{1,0:T(8,128)S(1)}) custom-call(s32[2]{0:T(128)S(1)} %pad_add_fusion.1.place_ref, bf16[2,512,128]{2,1,0:T(8,128)(2,1)S(1)} %get-tuple-element.38.q_ref, bf16[2,512,128]{2,1,0:T(8,128)(2,1)S(1)} %get-tuple-element.39.do_ref, ...), custom_call_target="tpu_custom_call" | custom-call | flops 201326592 | bytes 8388608 | tf_op jit(solution)/shard_map/rest/pallas_call | solution.py:284
  25.3 0.0 collective-permute-done.8
  25.3 0.8 %collective-permute-done.9 = bf16[128,512]{1,0:T(8,128)(2,1)S(1)} collective-permute-done((bf16[128,512]{1,0:T(8,128)(2,1)S(1)}, bf16[128,512]{1,0:T(8,128)(2,1)S(1)}, u32[]{:S(2)}, u32[]{:S(2)}) %collective-permute-start.9) | collective-permute-done | bytes 131104 | tf_op jit(solution)/shard_map/ppermute | solution.py:215
  26.1 3.6 %collective-permute-start.10 = (bf16[64,2048]{1,0:T(8,128)(2,1)S(1)}, bf16[64,2048]{1,0:T(8,128)(2,1)S(1)}, u32[]{:S(2)}, u32[]{:S(2)}) collective-permute-start(bf16[64,2048]{1,0:T(8,128)(2,1)S(1)} %get-tuple-element.53), channel_id=1, source_target_pairs={{0,4},{4,0},{8,12},{12,8},{16,20},{20,16},{24,28},{28,24},{1,5},{5... | collective-permute-start | bytes 786440 | tf_op jit(solution)/shard_map/ppermute | solution.py:222
  29.7 0.1 add_convert_fusion
  29.8 0.1 collective-permute-start.11
  29.9 1.2 %collective-permute-done.11.given_ref = bf16[64,512]{1,0:T(8,128)(2,1)S(1)} collective-permute-done((bf16[64,512]{1,0:T(8,128)(2,1)S(1)}, bf16[64,512]{1,0:T(8,128)(2,1)S(1)}, u32[]{:S(2)}, u32[]{:S(2)}) %collective-permute-start.11) | collective-permute-done | bytes 65568 | tf_op jit(solution)/shard_map/ppermute | solution.py:222
  31.1 0.0 collective-permute-done.10.rows_ref
  31.1 0.8 %store.1 = (bf16[2,64,2048]{2,1,0:T(8,128)(2,1)}, bf16[2,64,256]{2,1,0:T(8,128)(2,1)}, bf16[2,64,256]{2,1,0:T(8,128)(2,1)}) custom-call(s32[1]{0:T(128)} %bitcast.core_ref, bf16[64,2048]{1,0:T(8,128)(2,1)S(1)} %collective-permute-done.10.rows_ref, bf16[64,512]{1,0:T(8,128)(2,1)S(1)} %get-tuple-element.62.kept_ref, ...), custom_call_target="tpu_custom_call", output_to_operand_aliasing={{0}: (4, {})} | custom-call | tf_op jit(solution)/shard_map/store/pallas_call | solution.py:308
  (5 shorter events, 0.0 us)
Async XLA Ops:
  0.6 2.3 %copy-start = (bf16[1,2,64,2048]{3,2,1,0:T(8,128)(2,1)S(1)}, bf16[1,2,64,2048]{3,2,1,0:T(8,128)(2,1)}, u32[]{:S(2)}) copy-start(bf16[1,2,64,2048]{3,2,1,0:T(8,128)(2,1)} %param.6) | copy-start | bytes 1572868
  0.6 2.1 %collective-permute-start.1 = (bf16[2,64,256]{2,1,0:T(8,128)(2,1)}, bf16[2,64,256]{2,1,0:T(8,128)(2,1)S(1)}, u32[]{:S(2)}, u32[]{:S(2)}) collective-permute-start(bf16[2,64,256]{2,1,0:T(8,128)(2,1)} %bitcast.27), channel_id=1, source_target_pairs={{0,4},{4,0},{8,12},{12,8},{16,20},{20,16},{24,28},{28,24},{1,5},{5... | collective-permute-start | bytes 196616 | tf_op jit(solution)/shard_map/ppermute | solution.py:222
  1.4 1.5 %collective-permute-start = (bf16[2,64,256]{2,1,0:T(8,128)(2,1)}, bf16[2,64,256]{2,1,0:T(8,128)(2,1)S(1)}, u32[]{:S(2)}, u32[]{:S(2)}) collective-permute-start(bf16[2,64,256]{2,1,0:T(8,128)(2,1)} %bitcast.28), channel_id=1, source_target_pairs={{0,4},{4,0},{8,12},{12,8},{16,20},{20,16},{24,28},{28,24},{1,5},{5... | collective-permute-start | bytes 196616 | tf_op jit(solution)/shard_map/ppermute | solution.py:222
  1.5 1.5 %collective-permute-start.2 = (s32[2,64]{1,0:T(2,128)}, s32[2,64]{1,0:T(2,128)S(1)}, u32[]{:S(2)}, u32[]{:S(2)}) collective-permute-start(s32[2,64]{1,0:T(2,128)} %bitcast.29), channel_id=1, source_target_pairs={{0,4},{4,0},{8,12},{12,8},{16,20},{20,16},{24,28},{28,24},{1,5},{5... | collective-permute-start | bytes 1544 | tf_op jit(solution)/shard_map/ppermute | solution.py:222
  2.9 8.0 %collective-permute-start.3 = (bf16[2,64,2048]{2,1,0:T(8,128)(2,1)S(1)}, bf16[2,64,2048]{2,1,0:T(8,128)(2,1)S(1)}, u32[]{:S(2)}, u32[]{:S(2)}) collective-permute-start(bf16[2,64,2048]{2,1,0:T(8,128)(2,1)S(1)} %bitcast.20), channel_id=1, source_target_pairs={{0,4},{4,0},{8,12},{12,8},{16,20},{20,16},{24,28},{28,24},{1,5},{5... | collective-permute-start | bytes 1572872 | tf_op jit(solution)/shard_map/ppermute | solution.py:222
  3.2 7.7 %collective-permute-start.4 = (bf16[2,64,2048]{2,1,0:T(8,128)(2,1)}, bf16[2,64,2048]{2,1,0:T(8,128)(2,1)S(1)}, u32[]{:S(2)}, u32[]{:S(2)}) collective-permute-start(bf16[2,64,2048]{2,1,0:T(8,128)(2,1)} %bitcast.22), channel_id=1, source_target_pairs={{0,4},{4,0},{8,12},{12,8},{16,20},{20,16},{24,28},{28,24},{1,5},{5... | collective-permute-start | bytes 1572872 | tf_op jit(solution)/shard_map/ppermute | solution.py:222
  3.5 7.5 %collective-permute-start.5 = (bf16[2,64,2048]{2,1,0:T(8,128)(2,1)}, bf16[2,64,2048]{2,1,0:T(8,128)(2,1)S(1)}, u32[]{:S(2)}, u32[]{:S(2)}) collective-permute-start(bf16[2,64,2048]{2,1,0:T(8,128)(2,1)} %bitcast.24), channel_id=1, source_target_pairs={{0,4},{4,0},{8,12},{12,8},{16,20},{20,16},{24,28},{28,24},{1,5},{5... | collective-permute-start | bytes 1572872 | tf_op jit(solution)/shard_map/ppermute | solution.py:222
  3.8 8.2 %collective-permute-start.6 = (bf16[128,512]{1,0:T(8,128)(2,1)S(1)}, bf16[128,512]{1,0:T(8,128)(2,1)S(1)}, u32[]{:S(2)}, u32[]{:S(2)}) collective-permute-start(bf16[128,512]{1,0:T(8,128)(2,1)S(1)} %maximum_maximum_fusion.own_ref), channel_id=1, source_target_pairs={{0,16},{8,24},{16,28},{24,20},{28,12},{20,4},{1,17},{9,25},{17,29}... | collective-permute-start | bytes 393224 | tf_op jit(solution)/shard_map/ppermute | solution.py:215
  5.0 7.1 %collective-permute-start.7 = (bf16[128,512]{1,0:T(8,128)(2,1)S(1)}, bf16[128,512]{1,0:T(8,128)(2,1)S(1)}, u32[]{:S(2)}, u32[]{:S(2)}) collective-permute-start(bf16[128,512]{1,0:T(8,128)(2,1)S(1)} %maximum_maximum_fusion.own_ref), channel_id=1, source_target_pairs={{0,8},{8,16},{16,24},{24,28},{28,20},{20,12},{12,4},{1,9},{9,17},{... | collective-permute-start | bytes 393224 | tf_op jit(solution)/shard_map/ppermute | solution.py:215
  7.1 0.7 %copy-start.3 = (s32[1,2,64]{2,1,0:T(2,128)S(1)}, s32[1,2,64]{2,1,0:T(2,128)}, u32[]{:S(2)}) copy-start(s32[1,2,64]{2,1,0:T(2,128)} %param.11) | copy-start | bytes 1540
  7.8 1.0 %copy-start.1 = (bf16[1,2,64,2048]{3,2,1,0:T(8,128)(2,1)S(1)}, bf16[1,2,64,2048]{3,2,1,0:T(8,128)(2,1)}, u32[]{:S(2)}) copy-start(bf16[1,2,64,2048]{3,2,1,0:T(8,128)(2,1)} %param.9) | copy-start | bytes 1572868
  8.9 1.0 %copy-start.2 = (bf16[1,2,64,2048]{3,2,1,0:T(8,128)(2,1)S(1)}, bf16[1,2,64,2048]{3,2,1,0:T(8,128)(2,1)}, u32[]{:S(2)}) copy-start(bf16[1,2,64,2048]{3,2,1,0:T(8,128)(2,1)} %param.10) | copy-start | bytes 1572868
  14.9 10.4 %collective-permute-start.8 = (bf16[128,512]{1,0:T(8,128)(2,1)S(1)}, bf16[128,512]{1,0:T(8,128)(2,1)S(1)}, u32[]{:S(2)}, u32[]{:S(2)}) collective-permute-start(bf16[128,512]{1,0:T(8,128)(2,1)S(1)} %get-tuple-element.46), channel_id=1, source_target_pairs={{8,0},{16,8},{24,16},{28,24},{20,28},{12,20},{4,12},{9,1},{17,9},{... | collective-permute-start | bytes 393224 | tf_op jit(solution)/shard_map/ppermute | solution.py:215
  18.5 7.6 %collective-permute-start.9 = (bf16[128,512]{1,0:T(8,128)(2,1)S(1)}, bf16[128,512]{1,0:T(8,128)(2,1)S(1)}, u32[]{:S(2)}, u32[]{:S(2)}) collective-permute-start(bf16[128,512]{1,0:T(8,128)(2,1)S(1)} %get-tuple-element.47), channel_id=1, source_target_pairs={{16,0},{24,8},{28,16},{20,24},{12,28},{4,20},{17,1},{25,9},{29,17}... | collective-permute-start | bytes 393224 | tf_op jit(solution)/shard_map/ppermute | solution.py:215
  26.1 5.0 %collective-permute-start.10 = (bf16[64,2048]{1,0:T(8,128)(2,1)S(1)}, bf16[64,2048]{1,0:T(8,128)(2,1)S(1)}, u32[]{:S(2)}, u32[]{:S(2)}) collective-permute-start(bf16[64,2048]{1,0:T(8,128)(2,1)S(1)} %get-tuple-element.53), channel_id=1, source_target_pairs={{0,4},{4,0},{8,12},{12,8},{16,20},{20,16},{24,28},{28,24},{1,5},{5... | collective-permute-start | bytes 786440 | tf_op jit(solution)/shard_map/ppermute | solution.py:222
  29.8 1.3 %collective-permute-start.11 = (bf16[64,512]{1,0:T(8,128)(2,1)S(1)}, bf16[64,512]{1,0:T(8,128)(2,1)S(1)}, u32[]{:S(2)}, u32[]{:S(2)}) collective-permute-start(bf16[64,512]{1,0:T(8,128)(2,1)S(1)} %get-tuple-element.61), channel_id=1, source_target_pairs={{0,4},{4,0},{8,12},{12,8},{16,20},{20,16},{24,28},{28,24},{1,5},{5... | collective-permute-start | bytes 196616 | tf_op jit(solution)/shard_map/ppermute | solution.py:222

commit v8 on v7

--- a/solution.py
+++ b/solution.py
@@ -30,9 +30,8 @@
     )
 
 
-def unit_starts(starts_ref, core, unit):
-    side = starts_ref[2 * unit : 2 * unit + 2, :]
-    return jnp.where(core == 0, side[0:1, :], side[1:2, :])
+def unit_starts(starts_ref, core):
+    return jnp.where(core == 0, starts_ref[0:1, :], starts_ref[1:2, :])
 
 
 def rows_kernel(
@@ -46,7 +45,7 @@
     group = lanes // tokens
     factor = HEAD_SIZE ** (-0.5) * LOG2E
     ones = jnp.ones((delta_ref.shape[1], 2 * HEAD_SIZE), jnp.bfloat16)
-    low = unit_starts(starts_ref, core, unit) - begin
+    low = unit_starts(starts_ref, core) - begin
     high = lax.broadcasted_iota(jnp.int32, (1, tokens), 1) + unit * tokens
     row = lax.broadcasted_iota(jnp.int32, (reach, tokens), 0)
     bias = jnp.where((row >= low) & (row <= high), 0.0, -jnp.inf)
@@ -69,9 +68,9 @@
 
 
 def scores_kernel(
-    place_ref, starts_ref, q_ref, do_ref, held_ref, delta_ref, q_in_ref, do_in_ref, held_in_ref,
-    delta_in_ref, far_ref, near_ref, far_part_ref, near_part_ref, dscores_ref, norm_ref,
-    window_ref, part_ref,
+    place_ref, starts_ref, q_ref, do_ref, held_ref, delta_ref,
+    starts_in_ref, q_in_ref, do_in_ref, held_in_ref, delta_in_ref, far_ref, near_ref,
+    far_part_ref, near_part_ref, dscores_ref, norm_ref, window_ref, part_ref,
 ):
     core, begin = place_ref[0], place_ref[1]
     tokens = starts_ref.shape[1]
@@ -84,44 +83,53 @@
         window_ref[n * pair : (n + 1) * pair, :] = source[...]
     offset = lax.broadcasted_iota(jnp.int32, (1, tokens), 1)
     sides = (
-        (q_ref, do_ref, held_ref, delta_ref), (q_in_ref, do_in_ref, held_in_ref, delta_in_ref)
-    )
-    for unit, (q_side, do_side, held_side, delta_side) in enumerate(sides):
+        (starts_ref, q_ref, do_ref, held_ref, delta_ref),
+        (starts_in_ref, q_in_ref, do_in_ref, held_in_ref, delta_in_ref),
+    )
+
+    def products(unit, g):
+        starts, q_side, do_side, held_side, delta_side = sides[unit]
+        first = unit * tokens
+        columns = slice(g * HEAD_SIZE, (g + 1) * HEAD_SIZE)
+        values = window_ref[first:, kv_width + g * HEAD_SIZE : kv_width + (g + 1) * HEAD_SIZE]
+        low = unit_starts(starts, core) - (begin + (unit - STEPS) * tokens)
+        low = jnp.concatenate([jnp.maximum(offset + 1, low)] * group, axis=1)
+        scores = dot(window_ref[first:, columns], q_side[g], CONTRACT_LAST) * (scale * LOG2E)
+        row = lax.broadcasted_iota(jnp.int32, scores.shape, 0)
+        scores = jnp.where(row >= low, scores, -jnp.inf)
+        return scores, dot(values, do_side[g], CONTRACT_LAST)
+
+    order = [(unit, g) for unit in range(2) for g in range(kv_heads)]
+    ahead = products(*order[0])
+    for step, (unit, g) in enumerate(order):
+        scores, dprobs = ahead
+        if step + 1 < len(order):
+            ahead = products(*order[step + 1])
+        _, q_side, do_side, held_side, delta_side = sides[unit]
         first = unit * tokens
         before = 2 * pair - first
-        low = unit_starts(starts_ref, core, unit) - (begin + (unit - STEPS) * tokens)
-        low = jnp.maximum(offset + 1, low)
-        low = jnp.concatenate([low] * group, axis=1)
-        for g in range(kv_heads):
-            at = (g * HEAD_SIZE, kv_width + g * HEAD_SIZE)
-            keys = window_ref[first:, at[0] : at[0] + HEAD_SIZE]
-            values = window_ref[first:, at[1] : at[1] + HEAD_SIZE]
-            q, do, held = q_side[g], do_side[g], held_side[g]
-            scores = dot(keys, q, CONTRACT_LAST) * (scale * LOG2E)
-            row = lax.broadcasted_iota(jnp.int32, scores.shape, 0)
-            scores = jnp.where(row >= low, scores, -jnp.inf)
-            top = jnp.maximum(
-                jnp.max(scores, axis=0, keepdims=True), jnp.max(held, axis=0, keepdims=True)
-            )
-            weights = jnp.exp2(scores - top)
-            total = jnp.sum(weights, axis=0, keepdims=True)
-            total += jnp.sum(jnp.exp2(held - top), axis=0, keepdims=True)
-            inverse = 1.0 / total
-            probs = weights * inverse
-            norm_ref[unit, g, 0:1] = top
-            norm_ref[unit, g, 1:2] = inverse
-            dprobs = dot(values, do, CONTRACT_LAST) - delta_side[g, :1]
-            dscores = (probs * dprobs).astype(jnp.bfloat16)
-            dscores_ref[unit, g, :before] = dscores
-            for part, column in (
-                (dot(dscores, q) * scale, at[0]),
-                (dot(probs.astype(jnp.bfloat16), do), at[1]),
-            ):
-                columns = slice(column, column + HEAD_SIZE)
-                if unit == 0:
-                    part_ref[:, columns] = part
-                else:
-                    part_ref[first:, columns] += part
+        held = held_side[g]
+        top = jnp.maximum(
+            jnp.max(scores, axis=0, keepdims=True), jnp.max(held, axis=0, keepdims=True)
+        )
+        weights = jnp.exp2(scores - top)
+        total = jnp.sum(weights, axis=0, keepdims=True)
+        total += jnp.sum(jnp.exp2(held - top), axis=0, keepdims=True)
+        inverse = 1.0 / total
+        probs = weights * inverse
+        norm_ref[unit, g, 0:1] = top
+        norm_ref[unit, g, 1:2] = inverse
+        dscores = (probs * (dprobs - delta_side[g, :1])).astype(jnp.bfloat16)
+        dscores_ref[unit, g, :before] = dscores
+        for part, column in (
+            (dot(dscores, q_side[g]) * scale, g * HEAD_SIZE),
+            (dot(probs.astype(jnp.bfloat16), do_side[g]), kv_width + g * HEAD_SIZE),
+        ):
+            columns = slice(column, column + HEAD_SIZE)
+            if unit == 0:
+                part_ref[:, columns] = part
+            else:
+                part_ref[first:, columns] += part
     far_part_ref[...] = part_ref[:pair, :].astype(jnp.bfloat16)
     near_part_ref[...] = part_ref[pair:, :].astype(jnp.bfloat16)
 
@@ -232,12 +240,11 @@
     own, starts_in, starts, *late = lax.optimization_barrier(
         (own, starts_in, doc_start[0], query[0], out_grad[0], attn_out[0])
     )
-    starts = jnp.concatenate([starts, starts_in], axis=0)
     kv_heads = kv_width // HEAD_SIZE
     lanes = tokens * (width // kv_width)
     products = 2 * slots * tokens * pair * width
 
-    def arranged(unit, sources):
+    def arranged(unit, starts, sources):
         stacked = jax.ShapeDtypeStruct((kv_heads, lanes, HEAD_SIZE), bf16)
         square = jax.ShapeDtypeStruct((kv_heads, (unit + 1) * tokens, lanes), jnp.float32)
         q, do, scores, dprobs, delta = pl.pallas_call(
@@ -255,12 +262,14 @@
             cost_estimate=work(products // 2, 4 * 2**20),
             name="rows",
         )(place, starts, own, *sources)
-        return (q, do, scores, delta), (q, do, scores, dprobs)
+        return (starts, q, do, scores, delta), (q, do, scores, dprobs)
 
     sent = [swapped(x) for x in late]
     far = shift(own, 2)
     near = shift(own, 1)
-    sides = arranged(0, late), arranged(1, sent)
+    side_in = arranged(1, starts_in, sent)
+    *late, _ = lax.optimization_barrier((starts, *late, side_in[0][-1]))
+    side = arranged(0, late[0], late[1:])
     far_part, near_part, dscores, norm = pl.pallas_call(
         scores_kernel,
         out_shape=(
@@ -269,7 +278,7 @@
             jax.ShapeDtypeStruct((slots, kv_heads, 2 * pair, lanes), bf16),
             jax.ShapeDtypeStruct((slots, kv_heads, 8, lanes), jnp.float32),
         ),
-        in_specs=[SMEM] + [VMEM] * 11,
+        in_specs=[SMEM] + [VMEM] * 12,
         out_specs=(VMEM,) * 4,
         scratch_shapes=[
             pltpu.VMEM((2 * pair, pair_width), bf16),
@@ -278,7 +287,7 @@
         compiler_params=PARAMS,
         cost_estimate=work(6 * products, 12 * 2**20),
         name="scores",
-    )(place, starts, *sides[0][0], *sides[1][0], far, near)
+    )(place, *side[0], *side_in[0], far, near)
     from_far = shift(far_part, -2)
     from_near = shift(near_part, -1)
     dq, dq_send, own_part = pl.pallas_call(
@@ -298,7 +307,7 @@
         compiler_params=PARAMS,
         cost_estimate=work(3 * products, 8 * 2**20),
         name="rest",
-    )(place, *sides[0][1], *sides[1][1], far, near, own, dscores, norm)
+    )(place, *side[1], *side_in[1], far, near, own, dscores, norm)
     from_near, from_far, dq_send = lax.optimization_barrier((from_near, from_far, dq_send))
     dq_rows = swapped(dq_send)
     total = own_part + from_near.astype(jnp.float32) + from_far.astype(jnp.float32)

time: 32.3 us -> 31.6 us (0.978)
  local copies, waits for them, and re-layouts: 2.69 us -> 0.72 us
  waiting for transfers between devices: 2.36 us -> 3.56 us
    unnamed x8, local copies, waits for them, and re-layouts: 2.68 us -> 0.71 us
    ppermute x4, waiting for transfers between devices: 0.94 us -> 2.15 us  [shift(): return lax.ppermute(x, 'ctx', moves)]
where the time goes in v8:
time: 31.6 us; the launch traced here: 31 us
  starting transfers between devices  17.7 us (56%)
  Pallas kernels  7.26 us (23%)
  waiting for transfers between devices  3.56 us (11%)
  other arithmetic  0.97 us (3%)
  between operations  0.81 us (3%)
  local copies, waits for them, and re-layouts  0.72 us (2%)
    ppermute x4, starting transfers between devices, shift(): return lax.ppermute(x, 'ctx', moves)  11.7 us
    ppermute x8, starting transfers between devices, swapped(): return lax.ppermute(x, 'ctx', swap)  5.98 us
    pallas_call x1, Pallas kernels, shards(): pl.pallas_call(scores_kernel, out_shape=(jax.ShapeDtypeStruct((pair, pair...  2.43 us
    ppermute x4, waiting for transfers between devices, shift(): return lax.ppermute(x, 'ctx', moves)  2.15 us
    pallas_call x2, Pallas kernels, arranged(): pl.pallas_call(functools.partial(rows_kernel, unit), out_shape=(stacked,...  2.03 us
    pallas_call x1, Pallas kernels, shards(): pl.pallas_call(rest_kernel, out_shape=(jax.ShapeDtypeStruct((slots, token...  2.02 us
    ppermute x8, waiting for transfers between devices, swapped(): return lax.ppermute(x, 'ctx', swap)  1.41 us
    select_n x3, other arithmetic, mine(): return jnp.where(core == 0, x[0], x[1])  0.83 us
  transfers between devices with their start and end apart: 12, of which 5 were waited for; matrix products, arithmetic and copies ran while one was open for 3% of the time, Pallas kernels for 13%

profile of v8, /device:TPU:13, one launch (start us, length us, event | category | flops | bytes accessed | tf_op | source)
XLA Modules:
  0.0 31.0 jit_solution(8099966499296871992)
XLA Ops:
  0.6 0.0 copy-start
  0.6 0.7 %collective-permute-start.1 = (bf16[2,64,256]{2,1,0:T(8,128)(2,1)}, bf16[2,64,256]{2,1,0:T(8,128)(2,1)S(1)}, u32[]{:S(2)}, u32[]{:S(2)}) collective-permute-start(bf16[2,64,256]{2,1,0:T(8,128)(2,1)} %bitcast.30), channel_id=1, source_target_pairs={{0,4},{4,0},{8,12},{12,8},{16,20},{20,16},{24,28},{28,24},{1,5},{5... | collective-permute-start | bytes 196616 | tf_op jit(solution)/shard_map/ppermute | solution.py:230
  1.4 0.1 collective-permute-start
  1.5 0.4 %collective-permute-start.2 = (s32[2,64]{1,0:T(2,128)}, s32[2,64]{1,0:T(2,128)S(1)}, u32[]{:S(2)}, u32[]{:S(2)}) collective-permute-start(s32[2,64]{1,0:T(2,128)} %bitcast.26), channel_id=1, source_target_pairs={{0,4},{4,0},{8,12},{12,8},{16,20},{20,16},{24,28},{28,24},{1,5},{5... | collective-permute-start | bytes 1544 | tf_op jit(solution)/shard_map/ppermute | solution.py:230
  1.9 0.8 %select_bitcast_fusion = (bf16[64,256]{1,0:T(8,128)(2,1)S(1)}, bf16[64,256]{1,0:T(8,128)(2,1)S(1)}) fusion(bf16[1,2,64,256]{3,2,1,0:T(8,128)(2,1)} %param.8, pred[]{:T(512)} %bitcast.2, bf16[1,2,64,256]{3,2,1,0:T(8,128)(2,1)} %param.7), kind=kLoop, calls=%fused_computation.6 | loop fusion | flops 32768 | bytes 196609 | tf_op jit(solution)/shard_map/jit(_where)/select_n | solution.py:233
  2.7 0.0 collective-permute-done.1
  2.7 0.1 collective-permute-done
  2.9 0.1 collective-permute-done.2.starts_ref.starts_in_ref
  2.9 0.0 copy-done
  2.9 0.3 %collective-permute-start.3 = (bf16[2,64,2048]{2,1,0:T(8,128)(2,1)S(1)}, bf16[2,64,2048]{2,1,0:T(8,128)(2,1)S(1)}, u32[]{:S(2)}, u32[]{:S(2)}) collective-permute-start(bf16[2,64,2048]{2,1,0:T(8,128)(2,1)S(1)} %bitcast.20), channel_id=1, source_target_pairs={{0,4},{4,0},{8,12},{12,8},{16,20},{20,16},{24,28},{28,24},{1,5},{5... | collective-permute-start | bytes 1572872 | tf_op jit(solution)/shard_map/ppermute | solution.py:230
  3.2 0.2 collective-permute-start.4
  3.5 0.3 collective-permute-start.5
  3.8 1.3 %collective-permute-start.6 = (bf16[128,512]{1,0:T(8,128)(2,1)S(1)}, bf16[128,512]{1,0:T(8,128)(2,1)S(1)}, u32[]{:S(2)}, u32[]{:S(2)}) collective-permute-start(bf16[128,512]{1,0:T(8,128)(2,1)S(1)} %maximum_maximum_fusion.own_ref), channel_id=1, source_target_pairs={{0,16},{8,24},{16,28},{24,20},{28,12},{20,4},{1,17},{9,25},{17,29}... | collective-permute-start | bytes 393224 | tf_op jit(solution)/shard_map/ppermute | solution.py:223
  5.0 2.1 %collective-permute-start.7 = (bf16[128,512]{1,0:T(8,128)(2,1)S(1)}, bf16[128,512]{1,0:T(8,128)(2,1)S(1)}, u32[]{:S(2)}, u32[]{:S(2)}) collective-permute-start(bf16[128,512]{1,0:T(8,128)(2,1)S(1)} %maximum_maximum_fusion.own_ref), channel_id=1, source_target_pairs={{0,8},{8,16},{16,24},{24,28},{28,20},{20,12},{12,4},{1,9},{9,17},{... | collective-permute-start | bytes 393224 | tf_op jit(solution)/shard_map/ppermute | solution.py:223
  7.2 0.1 pad_add_fusion.place_ref
  7.2 0.0 copy-start.1
  7.2 0.0 copy-start.2
  7.2 0.0 collective-permute-done.3.q_ref
  7.2 0.0 collective-permute-done.4.do_ref
  7.2 0.0 collective-permute-done.5.o_ref
  7.3 1.0 %rows.2 = (bf16[2,512,128]{2,1,0:T(8,128)(2,1)S(1)}, bf16[2,512,128]{2,1,0:T(8,128)(2,1)S(1)}, f32[2,128,512]{2,1,0:T(8,128)S(1)}, f32[2,128,512]{2,1,0:T(8,128)S(1)}, f32[2,8,512]{2,1,0:T(8,128)S(1)}) custom-call(s32[2]{0:T(128)S(1)} %pad_add_fusion.place_ref, s32[2,64]{1,0:T(2,128)S(1)} %collective-permute-done.2.starts_ref.starts_in_ref, ...), custom_call_target="tpu_custom_call" | custom-call | flops 33554432 | bytes 4194304 | tf_op jit(solution)/shard_map/rows/pallas_call | solution.py:250
  8.3 0.0 copy-start.3
  8.3 0.0 copy-done.1
  8.3 0.1 copy-done.2
  8.4 0.6 %copy-done.3 = s32[1,2,64]{2,1,0:T(2,128)S(1)} copy-done((s32[1,2,64]{2,1,0:T(2,128)S(1)}, s32[1,2,64]{2,1,0:T(2,128)}, u32[]{:S(2)}) %copy-start.3) | copy-done | bytes 536
  9.0 1.0 %rows.3 = (bf16[2,512,128]{2,1,0:T(8,128)(2,1)S(1)}, bf16[2,512,128]{2,1,0:T(8,128)(2,1)S(1)}, f32[2,64,512]{2,1,0:T(8,128)S(1)}, f32[2,64,512]{2,1,0:T(8,128)S(1)}, f32[2,8,512]{2,1,0:T(8,128)S(1)}) custom-call(s32[2]{0:T(128)S(1)} %pad_add_fusion.place_ref, s32[2,64]{1,0:T(2,128)S(1)} %bitcast.27, bf16[128,512]{1,0:T(8,128)(2,1)S(1)} %maximum_maximum_fusion.own_ref, ...), custom_call_target="tpu_custom_call" | custom-call | flops 33554432 | bytes 4194304 | tf_op jit(solution)/shard_map/rows/pallas_call | solution.py:250
  10.0 1.1 %collective-permute-done.6.far_ref = bf16[128,512]{1,0:T(8,128)(2,1)S(1)} collective-permute-done((bf16[128,512]{1,0:T(8,128)(2,1)S(1)}, bf16[128,512]{1,0:T(8,128)(2,1)S(1)}, u32[]{:S(2)}, u32[]{:S(2)}) %collective-permute-start.6) | collective-permute-done | bytes 131104 | tf_op jit(solution)/shard_map/ppermute | solution.py:223
  11.1 1.0 %collective-permute-done.7.near_ref = bf16[128,512]{1,0:T(8,128)(2,1)S(1)} collective-permute-done((bf16[128,512]{1,0:T(8,128)(2,1)S(1)}, bf16[128,512]{1,0:T(8,128)(2,1)S(1)}, u32[]{:S(2)}, u32[]{:S(2)}) %collective-permute-start.7) | collective-permute-done | bytes 131104 | tf_op jit(solution)/shard_map/ppermute | solution.py:223
  12.2 2.4 %scores.1 = (bf16[128,512]{1,0:T(8,128)(2,1)S(1)}, bf16[128,512]{1,0:T(8,128)(2,1)S(1)}, bf16[2,2,256,512]{3,2,1,0:T(8,128)(2,1)S(1)}, f32[2,2,8,512]{3,2,1,0:T(8,128)S(1)}) custom-call(s32[2]{0:T(128)S(1)} %pad_add_fusion.place_ref, s32[2,64]{1,0:T(2,128)S(1)} %bitcast.28, bf16[2,512,128]{2,1,0:T(8,128)(2,1)S(1)} %get-tuple-element.47.q_ref, ...), custom_call_target="tpu_custom_call" | custom-call | flops 402653184 | bytes 12582912 | tf_op jit(solution)/shard_map/scores/pallas_call | solution.py:273
  14.6 3.2 %collective-permute-start.8 = (bf16[128,512]{1,0:T(8,128)(2,1)S(1)}, bf16[128,512]{1,0:T(8,128)(2,1)S(1)}, u32[]{:S(2)}, u32[]{:S(2)}) collective-permute-start(bf16[128,512]{1,0:T(8,128)(2,1)S(1)} %get-tuple-element.54), channel_id=1, source_target_pairs={{8,0},{16,8},{24,16},{28,24},{20,28},{12,20},{4,12},{9,1},{17,9},{... | collective-permute-start | bytes 393224 | tf_op jit(solution)/shard_map/ppermute | solution.py:223
  17.8 5.2 %collective-permute-start.9 = (bf16[128,512]{1,0:T(8,128)(2,1)S(1)}, bf16[128,512]{1,0:T(8,128)(2,1)S(1)}, u32[]{:S(2)}, u32[]{:S(2)}) collective-permute-start(bf16[128,512]{1,0:T(8,128)(2,1)S(1)} %get-tuple-element.55), channel_id=1, source_target_pairs={{16,0},{24,8},{28,16},{20,24},{12,28},{4,20},{17,1},{25,9},{29,17}... | collective-permute-start | bytes 393224 | tf_op jit(solution)/shard_map/ppermute | solution.py:223
  23.0 2.0 %rest.1 = (bf16[2,64,2048]{2,1,0:T(8,128)(2,1)}, bf16[64,2048]{1,0:T(8,128)(2,1)S(1)}, f32[128,512]{1,0:T(8,128)S(1)}) custom-call(s32[2]{0:T(128)S(1)} %pad_add_fusion.place_ref, bf16[2,512,128]{2,1,0:T(8,128)(2,1)S(1)} %get-tuple-element.47.q_ref, bf16[2,512,128]{2,1,0:T(8,128)(2,1)S(1)} %get-tuple-element.48.do_ref, ...), custom_call_target="tpu_custom_call" | custom-call | flops 201326592 | bytes 8388608 | tf_op jit(solution)/shard_map/rest/pallas_call | solution.py:293
  25.0 0.0 collective-permute-done.8
  25.0 0.0 collective-permute-done.9
  25.0 3.8 %collective-permute-start.10 = (bf16[64,2048]{1,0:T(8,128)(2,1)S(1)}, bf16[64,2048]{1,0:T(8,128)(2,1)S(1)}, u32[]{:S(2)}, u32[]{:S(2)}) collective-permute-start(bf16[64,2048]{1,0:T(8,128)(2,1)S(1)} %get-tuple-element.61), channel_id=1, source_target_pairs={{0,4},{4,0},{8,12},{12,8},{16,20},{20,16},{24,28},{28,24},{1,5},{5... | collective-permute-start | bytes 786440 | tf_op jit(solution)/shard_map/ppermute | solution.py:230
  28.8 0.1 add_convert_fusion
  28.9 0.1 collective-permute-start.11
  29.0 1.2 %collective-permute-done.11.given_ref = bf16[64,512]{1,0:T(8,128)(2,1)S(1)} collective-permute-done((bf16[64,512]{1,0:T(8,128)(2,1)S(1)}, bf16[64,512]{1,0:T(8,128)(2,1)S(1)}, u32[]{:S(2)}, u32[]{:S(2)}) %collective-permute-start.11) | collective-permute-done | bytes 65568 | tf_op jit(solution)/shard_map/ppermute | solution.py:230
  30.2 0.0 collective-permute-done.10.rows_ref
  30.2 0.8 %store.1 = (bf16[2,64,2048]{2,1,0:T(8,128)(2,1)}, bf16[2,64,256]{2,1,0:T(8,128)(2,1)}, bf16[2,64,256]{2,1,0:T(8,128)(2,1)}) custom-call(s32[1]{0:T(128)} %bitcast.core_ref, bf16[64,2048]{1,0:T(8,128)(2,1)S(1)} %collective-permute-done.10.rows_ref, bf16[64,512]{1,0:T(8,128)(2,1)S(1)} %get-tuple-element.70.kept_ref, ...), custom_call_target="tpu_custom_call", output_to_operand_aliasing={{0}: (4, {})} | custom-call | tf_op jit(solution)/shard_map/store/pallas_call | solution.py:317
  (4 shorter events, 0.0 us)
Async XLA Ops:
  0.6 2.3 %copy-start = (bf16[1,2,64,2048]{3,2,1,0:T(8,128)(2,1)S(1)}, bf16[1,2,64,2048]{3,2,1,0:T(8,128)(2,1)}, u32[]{:S(2)}) copy-start(bf16[1,2,64,2048]{3,2,1,0:T(8,128)(2,1)} %param.6) | copy-start | bytes 1572868
  0.6 2.1 %collective-permute-start.1 = (bf16[2,64,256]{2,1,0:T(8,128)(2,1)}, bf16[2,64,256]{2,1,0:T(8,128)(2,1)S(1)}, u32[]{:S(2)}, u32[]{:S(2)}) collective-permute-start(bf16[2,64,256]{2,1,0:T(8,128)(2,1)} %bitcast.30), channel_id=1, source_target_pairs={{0,4},{4,0},{8,12},{12,8},{16,20},{20,16},{24,28},{28,24},{1,5},{5... | collective-permute-start | bytes 196616 | tf_op jit(solution)/shard_map/ppermute | solution.py:230
  1.4 1.5 %collective-permute-start = (bf16[2,64,256]{2,1,0:T(8,128)(2,1)}, bf16[2,64,256]{2,1,0:T(8,128)(2,1)S(1)}, u32[]{:S(2)}, u32[]{:S(2)}) collective-permute-start(bf16[2,64,256]{2,1,0:T(8,128)(2,1)} %bitcast.31), channel_id=1, source_target_pairs={{0,4},{4,0},{8,12},{12,8},{16,20},{20,16},{24,28},{28,24},{1,5},{5... | collective-permute-start | bytes 196616 | tf_op jit(solution)/shard_map/ppermute | solution.py:230
  1.5 1.5 %collective-permute-start.2 = (s32[2,64]{1,0:T(2,128)}, s32[2,64]{1,0:T(2,128)S(1)}, u32[]{:S(2)}, u32[]{:S(2)}) collective-permute-start(s32[2,64]{1,0:T(2,128)} %bitcast.26), channel_id=1, source_target_pairs={{0,4},{4,0},{8,12},{12,8},{16,20},{20,16},{24,28},{28,24},{1,5},{5... | collective-permute-start | bytes 1544 | tf_op jit(solution)/shard_map/ppermute | solution.py:230
  2.9 4.3 %collective-permute-start.3 = (bf16[2,64,2048]{2,1,0:T(8,128)(2,1)S(1)}, bf16[2,64,2048]{2,1,0:T(8,128)(2,1)S(1)}, u32[]{:S(2)}, u32[]{:S(2)}) collective-permute-start(bf16[2,64,2048]{2,1,0:T(8,128)(2,1)S(1)} %bitcast.20), channel_id=1, source_target_pairs={{0,4},{4,0},{8,12},{12,8},{16,20},{20,16},{24,28},{28,24},{1,5},{5... | collective-permute-start | bytes 1572872 | tf_op jit(solution)/shard_map/ppermute | solution.py:230
  3.2 4.0 %collective-permute-start.4 = (bf16[2,64,2048]{2,1,0:T(8,128)(2,1)}, bf16[2,64,2048]{2,1,0:T(8,128)(2,1)S(1)}, u32[]{:S(2)}, u32[]{:S(2)}) collective-permute-start(bf16[2,64,2048]{2,1,0:T(8,128)(2,1)} %bitcast.22), channel_id=1, source_target_pairs={{0,4},{4,0},{8,12},{12,8},{16,20},{20,16},{24,28},{28,24},{1,5},{5... | collective-permute-start | bytes 1572872 | tf_op jit(solution)/shard_map/ppermute | solution.py:230
  3.5 3.8 %collective-permute-start.5 = (bf16[2,64,2048]{2,1,0:T(8,128)(2,1)}, bf16[2,64,2048]{2,1,0:T(8,128)(2,1)S(1)}, u32[]{:S(2)}, u32[]{:S(2)}) collective-permute-start(bf16[2,64,2048]{2,1,0:T(8,128)(2,1)} %bitcast.24), channel_id=1, source_target_pairs={{0,4},{4,0},{8,12},{12,8},{16,20},{20,16},{24,28},{28,24},{1,5},{5... | collective-permute-start | bytes 1572872 | tf_op jit(solution)/shard_map/ppermute | solution.py:230
  3.8 7.4 %collective-permute-start.6 = (bf16[128,512]{1,0:T(8,128)(2,1)S(1)}, bf16[128,512]{1,0:T(8,128)(2,1)S(1)}, u32[]{:S(2)}, u32[]{:S(2)}) collective-permute-start(bf16[128,512]{1,0:T(8,128)(2,1)S(1)} %maximum_maximum_fusion.own_ref), channel_id=1, source_target_pairs={{0,16},{8,24},{16,28},{24,20},{28,12},{20,4},{1,17},{9,25},{17,29}... | collective-permute-start | bytes 393224 | tf_op jit(solution)/shard_map/ppermute | solution.py:223
  5.0 7.1 %collective-permute-start.7 = (bf16[128,512]{1,0:T(8,128)(2,1)S(1)}, bf16[128,512]{1,0:T(8,128)(2,1)S(1)}, u32[]{:S(2)}, u32[]{:S(2)}) collective-permute-start(bf16[128,512]{1,0:T(8,128)(2,1)S(1)} %maximum_maximum_fusion.own_ref), channel_id=1, source_target_pairs={{0,8},{8,16},{16,24},{24,28},{28,20},{20,12},{12,4},{1,9},{9,17},{... | collective-permute-start | bytes 393224 | tf_op jit(solution)/shard_map/ppermute | solution.py:223
  7.2 1.1 %copy-start.1 = (bf16[1,2,64,2048]{3,2,1,0:T(8,128)(2,1)S(1)}, bf16[1,2,64,2048]{3,2,1,0:T(8,128)(2,1)}, u32[]{:S(2)}) copy-start(bf16[1,2,64,2048]{3,2,1,0:T(8,128)(2,1)} %param.9) | copy-start | bytes 1572868
  7.2 1.2 %copy-start.2 = (bf16[1,2,64,2048]{3,2,1,0:T(8,128)(2,1)S(1)}, bf16[1,2,64,2048]{3,2,1,0:T(8,128)(2,1)}, u32[]{:S(2)}) copy-start(bf16[1,2,64,2048]{3,2,1,0:T(8,128)(2,1)} %param.10) | copy-start | bytes 1572868
  8.3 0.7 %copy-start.3 = (s32[1,2,64]{2,1,0:T(2,128)S(1)}, s32[1,2,64]{2,1,0:T(2,128)}, u32[]{:S(2)}) copy-start(s32[1,2,64]{2,1,0:T(2,128)} %param.11) | copy-start | bytes 1540
  14.6 10.4 %collective-permute-start.8 = (bf16[128,512]{1,0:T(8,128)(2,1)S(1)}, bf16[128,512]{1,0:T(8,128)(2,1)S(1)}, u32[]{:S(2)}, u32[]{:S(2)}) collective-permute-start(bf16[128,512]{1,0:T(8,128)(2,1)S(1)} %get-tuple-element.54), channel_id=1, source_target_pairs={{8,0},{16,8},{24,16},{28,24},{20,28},{12,20},{4,12},{9,1},{17,9},{... | collective-permute-start | bytes 393224 | tf_op jit(solution)/shard_map/ppermute | solution.py:223
  17.8 7.2 %collective-permute-start.9 = (bf16[128,512]{1,0:T(8,128)(2,1)S(1)}, bf16[128,512]{1,0:T(8,128)(2,1)S(1)}, u32[]{:S(2)}, u32[]{:S(2)}) collective-permute-start(bf16[128,512]{1,0:T(8,128)(2,1)S(1)} %get-tuple-element.55), channel_id=1, source_target_pairs={{16,0},{24,8},{28,16},{20,24},{12,28},{4,20},{17,1},{25,9},{29,17}... | collective-permute-start | bytes 393224 | tf_op jit(solution)/shard_map/ppermute | solution.py:223
  25.0 5.2 %collective-permute-start.10 = (bf16[64,2048]{1,0:T(8,128)(2,1)S(1)}, bf16[64,2048]{1,0:T(8,128)(2,1)S(1)}, u32[]{:S(2)}, u32[]{:S(2)}) collective-permute-start(bf16[64,2048]{1,0:T(8,128)(2,1)S(1)} %get-tuple-element.61), channel_id=1, source_target_pairs={{0,4},{4,0},{8,12},{12,8},{16,20},{20,16},{24,28},{28,24},{1,5},{5... | collective-permute-start | bytes 786440 | tf_op jit(solution)/shard_map/ppermute | solution.py:230
  28.9 1.3 %collective-permute-start.11 = (bf16[64,512]{1,0:T(8,128)(2,1)S(1)}, bf16[64,512]{1,0:T(8,128)(2,1)S(1)}, u32[]{:S(2)}, u32[]{:S(2)}) collective-permute-start(bf16[64,512]{1,0:T(8,128)(2,1)S(1)} %get-tuple-element.69), channel_id=1, source_target_pairs={{0,4},{4,0},{8,12},{12,8},{16,20},{20,16},{24,28},{28,24},{1,5},{5... | collective-permute-start | bytes 196616 | tf_op jit(solution)/shard_map/ppermute | solution.py:230

commit v9 on v8

--- a/solution.py
+++ b/solution.py
@@ -67,69 +67,97 @@
         do_out_ref[g] = do
 
 
-def scores_kernel(
-    place_ref, starts_ref, q_ref, do_ref, held_ref, delta_ref,
-    starts_in_ref, q_in_ref, do_in_ref, held_in_ref, delta_in_ref, far_ref, near_ref,
-    far_part_ref, near_part_ref, dscores_ref, norm_ref, window_ref, part_ref,
-):
+def remote_products(place_ref, side, pair_ref, unit, g, skip, offset):
+    starts_ref, q_ref, do_ref, delta_ref = side
     core, begin = place_ref[0], place_ref[1]
     tokens = starts_ref.shape[1]
     kv_heads, lanes = q_ref.shape[:2]
     kv_width = kv_heads * HEAD_SIZE
-    group = lanes // tokens
+    columns = slice(g * HEAD_SIZE, (g + 1) * HEAD_SIZE)
+    values = pair_ref[skip:, kv_width + g * HEAD_SIZE : kv_width + (g + 1) * HEAD_SIZE]
+    low = unit_starts(starts_ref, core) - (begin + (unit - STEPS) * tokens)
+    low = jnp.maximum(lax.broadcasted_iota(jnp.int32, (1, tokens), 1) + 1, low) - offset
+    low = jnp.concatenate([low] * (lanes // tokens), axis=1)
+    factor = HEAD_SIZE ** (-0.5) * LOG2E
+    scores = dot(pair_ref[skip:, columns], q_ref[g], CONTRACT_LAST) * factor
+    row = lax.broadcasted_iota(jnp.int32, scores.shape, 0)
+    scores = jnp.where(row >= low, scores, -jnp.inf)
+    return scores, dot(values, do_ref[g], CONTRACT_LAST) - delta_ref[g, :1]
+
+
+def far_kernel(
+    place_ref, starts_ref, q_ref, do_ref, delta_ref,
+    starts_in_ref, q_in_ref, do_in_ref, delta_in_ref, far_ref,
+    scores_ref, dprobs_ref, scores_in_ref, dprobs_in_ref,
+):
+    tokens = starts_ref.shape[1]
+    sides = (
+        ((starts_ref, q_ref, do_ref, delta_ref), scores_ref, dprobs_ref),
+        ((starts_in_ref, q_in_ref, do_in_ref, delta_in_ref), scores_in_ref, dprobs_in_ref),
+    )
+    for unit, (side, scores, dprobs) in enumerate(sides):
+        for g in range(q_ref.shape[0]):
+            scores[g], dprobs[g] = remote_products(
+                place_ref, side, far_ref, unit, g, unit * tokens, 0
+            )
+
+
+def scores_kernel(
+    place_ref, starts_ref, q_ref, do_ref, held_ref, delta_ref,
+    starts_in_ref, q_in_ref, do_in_ref, held_in_ref, delta_in_ref,
+    far_scores_ref, far_dprobs_ref, far_scores_in_ref, far_dprobs_in_ref, near_ref,
+    far_part_ref, near_part_ref, dscores_ref, norm_ref, part_ref,
+):
+    tokens = starts_ref.shape[1]
+    kv_heads = q_ref.shape[0]
+    kv_width = kv_heads * HEAD_SIZE
     scale = HEAD_SIZE ** (-0.5)
     pair = 2 * tokens
-    for n, source in enumerate((far_ref, near_ref)):
-        window_ref[n * pair : (n + 1) * pair, :] = source[...]
-    offset = lax.broadcasted_iota(jnp.int32, (1, tokens), 1)
     sides = (
-        (starts_ref, q_ref, do_ref, held_ref, delta_ref),
-        (starts_in_ref, q_in_ref, do_in_ref, held_in_ref, delta_in_ref),
+        (starts_ref, q_ref, do_ref, delta_ref),
+        (starts_in_ref, q_in_ref, do_in_ref, delta_in_ref),
+    )
+    known = (
+        (held_ref, far_scores_ref, far_dprobs_ref),
+        (held_in_ref, far_scores_in_ref, far_dprobs_in_ref),
     )
 
     def products(unit, g):
-        starts, q_side, do_side, held_side, delta_side = sides[unit]
-        first = unit * tokens
-        columns = slice(g * HEAD_SIZE, (g + 1) * HEAD_SIZE)
-        values = window_ref[first:, kv_width + g * HEAD_SIZE : kv_width + (g + 1) * HEAD_SIZE]
-        low = unit_starts(starts, core) - (begin + (unit - STEPS) * tokens)
-        low = jnp.concatenate([jnp.maximum(offset + 1, low)] * group, axis=1)
-        scores = dot(window_ref[first:, columns], q_side[g], CONTRACT_LAST) * (scale * LOG2E)
-        row = lax.broadcasted_iota(jnp.int32, scores.shape, 0)
-        scores = jnp.where(row >= low, scores, -jnp.inf)
-        return scores, dot(values, do_side[g], CONTRACT_LAST)
+        return remote_products(place_ref, sides[unit], near_ref, unit, g, 0, pair - unit * tokens)
 
     order = [(unit, g) for unit in range(2) for g in range(kv_heads)]
     ahead = products(*order[0])
     for step, (unit, g) in enumerate(order):
-        scores, dprobs = ahead
+        near_scores, near_dprobs = ahead
         if step + 1 < len(order):
             ahead = products(*order[step + 1])
-        _, q_side, do_side, held_side, delta_side = sides[unit]
+        q, do = sides[unit][1][g], sides[unit][2][g]
+        held, far_scores, far_dprobs = (r[g] for r in known[unit])
         first = unit * tokens
-        before = 2 * pair - first
-        held = held_side[g]
-        top = jnp.maximum(
-            jnp.max(scores, axis=0, keepdims=True), jnp.max(held, axis=0, keepdims=True)
-        )
-        weights = jnp.exp2(scores - top)
-        total = jnp.sum(weights, axis=0, keepdims=True)
-        total += jnp.sum(jnp.exp2(held - top), axis=0, keepdims=True)
-        inverse = 1.0 / total
-        probs = weights * inverse
+        split, before = pair - first, 2 * pair - first
+        groups = (held, far_scores, near_scores)
+        tops = [jnp.max(x, axis=0, keepdims=True) for x in groups]
+        top = jnp.maximum(jnp.maximum(tops[0], tops[1]), tops[2])
+        own, far, near = (jnp.exp2(x - top) for x in groups)
+        inverse = 1.0 / sum(jnp.sum(x, axis=0, keepdims=True) for x in (own, far, near))
         norm_ref[unit, g, 0:1] = top
         norm_ref[unit, g, 1:2] = inverse
-        dscores = (probs * (dprobs - delta_side[g, :1])).astype(jnp.bfloat16)
-        dscores_ref[unit, g, :before] = dscores
-        for part, column in (
-            (dot(dscores, q_side[g]) * scale, g * HEAD_SIZE),
-            (dot(probs.astype(jnp.bfloat16), do_side[g]), kv_width + g * HEAD_SIZE),
-        ):
-            columns = slice(column, column + HEAD_SIZE)
-            if unit == 0:
-                part_ref[:, columns] = part
-            else:
-                part_ref[first:, columns] += part
+        parts = (
+            (far * inverse, far_dprobs, slice(0, split), slice(first, pair)),
+            (near * inverse, near_dprobs, slice(split, before), slice(pair, 2 * pair)),
+        )
+        for probs, dprobs, window_rows, pair_rows in parts:
+            dscores = (probs * dprobs).astype(jnp.bfloat16)
+            dscores_ref[unit, g, window_rows] = dscores
+            for part, column in (
+                (dot(dscores, q) * scale, g * HEAD_SIZE),
+                (dot(probs.astype(jnp.bfloat16), do), kv_width + g * HEAD_SIZE),
+            ):
+                columns = slice(column, column + HEAD_SIZE)
+                if unit == 0:
+                    part_ref[pair_rows, columns] = part
+                else:
+                    part_ref[pair_rows, columns] += part
     far_part_ref[...] = part_ref[:pair, :].astype(jnp.bfloat16)
     near_part_ref[...] = part_ref[pair:, :].astype(jnp.bfloat16)
 
@@ -270,6 +298,18 @@
     side_in = arranged(1, starts_in, sent)
     *late, _ = lax.optimization_barrier((starts, *late, side_in[0][-1]))
     side = arranged(0, late[0], late[1:])
+    def remote(rows):
+        return jax.ShapeDtypeStruct((kv_heads, rows, lanes), jnp.float32)
+
+    far_products = pl.pallas_call(
+        far_kernel,
+        out_shape=(remote(pair), remote(pair), remote(tokens), remote(tokens)),
+        in_specs=[SMEM] + [VMEM] * 9,
+        out_specs=(VMEM,) * 4,
+        compiler_params=SMALL,
+        cost_estimate=work(2 * products, 4 * 2**20),
+        name="far_scores",
+    )(place, *(x for part in (side[0], side_in[0]) for x in part[:3] + part[4:]), far)
     far_part, near_part, dscores, norm = pl.pallas_call(
         scores_kernel,
         out_shape=(
@@ -278,16 +318,13 @@
             jax.ShapeDtypeStruct((slots, kv_heads, 2 * pair, lanes), bf16),
             jax.ShapeDtypeStruct((slots, kv_heads, 8, lanes), jnp.float32),
         ),
-        in_specs=[SMEM] + [VMEM] * 12,
+        in_specs=[SMEM] + [VMEM] * 15,
         out_specs=(VMEM,) * 4,
-        scratch_shapes=[
-            pltpu.VMEM((2 * pair, pair_width), bf16),
-            pltpu.VMEM((2 * pair, pair_width), jnp.float32),
-        ],
+        scratch_shapes=[pltpu.VMEM((2 * pair, pair_width), jnp.float32)],
         compiler_params=PARAMS,
         cost_estimate=work(6 * products, 12 * 2**20),
         name="scores",
-    )(place, *side[0], *side_in[0], far, near)
+    )(place, *side[0], *side_in[0], *far_products, near)
     from_far = shift(far_part, -2)
     from_near = shift(near_part, -1)
     dq, dq_send, own_part = pl.pallas_call(

time: 31.6 us -> 32 us (1.013)
  Pallas kernels: 7.26 us -> 8.15 us
    pallas_call x0 -> x1, Pallas kernels: none -> 0.98 us  [shards(): pl.pallas_call(far_kernel, out_shape=(remote(pair), remote(pair), remote(...]
    ppermute x4, waiting for transfers between devices: 2.15 us -> 1.73 us  [shift(): return lax.ppermute(x, 'ctx', moves)]
  transfers between devices with their start and end apart: 12 -> 12, of which waited for: 5 -> 4; matrix products, arithmetic and copies ran while one was open for 3% -> 3% of each run, Pallas kernels for 13% -> 16%
where the time goes in v9:
time: 32 us; the launch traced here: 31.7 us
  starting transfers between devices  17.7 us (55%)
  Pallas kernels  8.15 us (25%)
  waiting for transfers between devices  3.27 us (10%)
  other arithmetic  0.97 us (3%)
  between operations  0.82 us (3%)
  local copies, waits for them, and re-layouts  0.81 us (3%)
    ppermute x4, starting transfers between devices, shift(): return lax.ppermute(x, 'ctx', moves)  11.7 us
    ppermute x8, starting transfers between devices, swapped(): return lax.ppermute(x, 'ctx', swap)  6 us
    pallas_call x1, Pallas kernels, shards(): pl.pallas_call(scores_kernel, out_shape=(jax.ShapeDtypeStruct((pair, pair...  2.33 us
    pallas_call x2, Pallas kernels, arranged(): pl.pallas_call(functools.partial(rows_kernel, unit), out_shape=(stacked,...  2.03 us
    pallas_call x1, Pallas kernels, shards(): pl.pallas_call(rest_kernel, out_shape=(jax.ShapeDtypeStruct((slots, token...  2.02 us
    ppermute x4, waiting for transfers between devices, shift(): return lax.ppermute(x, 'ctx', moves)  1.73 us
    ppermute x8, waiting for transfers between devices, swapped(): return lax.ppermute(x, 'ctx', swap)  1.54 us
    pallas_call x1, Pallas kernels, shards(): pl.pallas_call(far_kernel, out_shape=(remote(pair), remote(pair), remote(...  0.98 us
  transfers between devices with their start and end apart: 12, of which 4 were waited for; matrix products, arithmetic and copies ran while one was open for 3% of the time, Pallas kernels for 16%

profile of v9, /device:TPU:13, one launch (start us, length us, event | category | flops | bytes accessed | tf_op | source)
XLA Modules:
  0.0 31.7 jit_solution(1071091232555230267)
XLA Ops:
  0.6 0.0 copy-start.3
  0.6 0.0 copy-start
  0.7 0.7 %copy-done.3 = s32[1,2,64]{2,1,0:T(2,128)S(1)} copy-done((s32[1,2,64]{2,1,0:T(2,128)S(1)}, s32[1,2,64]{2,1,0:T(2,128)}, u32[]{:S(2)}) %copy-start.3) | copy-done | bytes 536
  1.3 0.7 %collective-permute-start.2 = (s32[2,64]{1,0:T(2,128)S(1)}, s32[2,64]{1,0:T(2,128)S(1)}, u32[]{:S(2)}, u32[]{:S(2)}) collective-permute-start(s32[2,64]{1,0:T(2,128)S(1)} %bitcast.26), channel_id=1, source_target_pairs={{0,4},{4,0},{8,12},{12,8},{16,20},{20,16},{24,28},{28,24},{1,5},{5... | collective-permute-start | bytes 1544 | tf_op jit(solution)/shard_map/ppermute | solution.py:258
  2.0 0.0 collective-permute-start.1
  2.0 0.5 %collective-permute-start = (bf16[2,64,256]{2,1,0:T(8,128)(2,1)}, bf16[2,64,256]{2,1,0:T(8,128)(2,1)S(1)}, u32[]{:S(2)}, u32[]{:S(2)}) collective-permute-start(bf16[2,64,256]{2,1,0:T(8,128)(2,1)} %bitcast.32), channel_id=1, source_target_pairs={{0,4},{4,0},{8,12},{12,8},{16,20},{20,16},{24,28},{28,24},{1,5},{5... | collective-permute-start | bytes 196616 | tf_op jit(solution)/shard_map/ppermute | solution.py:258
  2.5 0.8 %select_bitcast_fusion = (bf16[64,256]{1,0:T(8,128)(2,1)S(1)}, bf16[64,256]{1,0:T(8,128)(2,1)S(1)}) fusion(bf16[1,2,64,256]{3,2,1,0:T(8,128)(2,1)} %param.8, pred[]{:T(512)} %bitcast.2, bf16[1,2,64,256]{3,2,1,0:T(8,128)(2,1)} %param.7), kind=kLoop, calls=%fused_computation.6 | loop fusion | flops 32768 | bytes 196609 | tf_op jit(solution)/shard_map/jit(_where)/select_n | solution.py:261
  3.3 0.1 collective-permute-done.1
  3.5 0.1 collective-permute-done
  3.6 0.0 collective-permute-done.2.starts_ref.starts_in_ref
  3.6 0.0 copy-done
  3.7 0.4 %collective-permute-start.3 = (bf16[2,64,2048]{2,1,0:T(8,128)(2,1)S(1)}, bf16[2,64,2048]{2,1,0:T(8,128)(2,1)S(1)}, u32[]{:S(2)}, u32[]{:S(2)}) collective-permute-start(bf16[2,64,2048]{2,1,0:T(8,128)(2,1)S(1)} %bitcast.20), channel_id=1, source_target_pairs={{0,4},{4,0},{8,12},{12,8},{16,20},{20,16},{24,28},{28,24},{1,5},{5... | collective-permute-start | bytes 1572872 | tf_op jit(solution)/shard_map/ppermute | solution.py:258
  4.1 0.2 collective-permute-start.4
  4.2 0.4 %collective-permute-start.5 = (bf16[2,64,2048]{2,1,0:T(8,128)(2,1)}, bf16[2,64,2048]{2,1,0:T(8,128)(2,1)S(1)}, u32[]{:S(2)}, u32[]{:S(2)}) collective-permute-start(bf16[2,64,2048]{2,1,0:T(8,128)(2,1)} %bitcast.24), channel_id=1, source_target_pairs={{0,4},{4,0},{8,12},{12,8},{16,20},{20,16},{24,28},{28,24},{1,5},{5... | collective-permute-start | bytes 1572872 | tf_op jit(solution)/shard_map/ppermute | solution.py:258
  4.6 1.3 %collective-permute-start.6 = (bf16[128,512]{1,0:T(8,128)(2,1)S(1)}, bf16[128,512]{1,0:T(8,128)(2,1)S(1)}, u32[]{:S(2)}, u32[]{:S(2)}) collective-permute-start(bf16[128,512]{1,0:T(8,128)(2,1)S(1)} %maximum_maximum_fusion.own_ref), channel_id=1, source_target_pairs={{0,16},{8,24},{16,28},{24,20},{28,12},{20,4},{1,17},{9,25},{17,29}... | collective-permute-start | bytes 393224 | tf_op jit(solution)/shard_map/ppermute | solution.py:251
  5.9 2.1 %collective-permute-start.7 = (bf16[128,512]{1,0:T(8,128)(2,1)S(1)}, bf16[128,512]{1,0:T(8,128)(2,1)S(1)}, u32[]{:S(2)}, u32[]{:S(2)}) collective-permute-start(bf16[128,512]{1,0:T(8,128)(2,1)S(1)} %maximum_maximum_fusion.own_ref), channel_id=1, source_target_pairs={{0,8},{8,16},{16,24},{24,28},{28,20},{20,12},{12,4},{1,9},{9,17},{... | collective-permute-start | bytes 393224 | tf_op jit(solution)/shard_map/ppermute | solution.py:251
  8.0 0.1 pad_add_fusion.place_ref
  8.1 0.0 copy-start.1
  8.1 0.0 copy-start.2
  8.1 0.0 collective-permute-done.3.q_ref
  8.1 0.0 collective-permute-done.4.do_ref
  8.1 0.0 collective-permute-done.5.o_ref
  8.1 1.0 %rows.2 = (bf16[2,512,128]{2,1,0:T(8,128)(2,1)S(1)}, bf16[2,512,128]{2,1,0:T(8,128)(2,1)S(1)}, f32[2,128,512]{2,1,0:T(8,128)S(1)}, f32[2,128,512]{2,1,0:T(8,128)S(1)}, f32[2,8,512]{2,1,0:T(8,128)S(1)}) custom-call(s32[2]{0:T(128)S(1)} %pad_add_fusion.place_ref, s32[2,64]{1,0:T(2,128)S(1)} %collective-permute-done.2.starts_ref.starts_in_ref, ...), custom_call_target="tpu_custom_call" | custom-call | flops 33554432 | bytes 4194304 | tf_op jit(solution)/shard_map/rows/pallas_call | solution.py:278
  9.1 0.0 copy-done.1
  9.1 0.1 copy-done.2
  9.3 1.0 %rows.3 = (bf16[2,512,128]{2,1,0:T(8,128)(2,1)S(1)}, bf16[2,512,128]{2,1,0:T(8,128)(2,1)S(1)}, f32[2,64,512]{2,1,0:T(8,128)S(1)}, f32[2,64,512]{2,1,0:T(8,128)S(1)}, f32[2,8,512]{2,1,0:T(8,128)S(1)}) custom-call(s32[2]{0:T(128)S(1)} %pad_add_fusion.place_ref, s32[2,64]{1,0:T(2,128)S(1)} %bitcast.27, bf16[128,512]{1,0:T(8,128)(2,1)S(1)} %maximum_maximum_fusion.own_ref, ...), custom_call_target="tpu_custom_call" | custom-call | flops 33554432 | bytes 4194304 | tf_op jit(solution)/shard_map/rows/pallas_call | solution.py:278
  10.3 1.7 %collective-permute-done.6.far_ref = bf16[128,512]{1,0:T(8,128)(2,1)S(1)} collective-permute-done((bf16[128,512]{1,0:T(8,128)(2,1)S(1)}, bf16[128,512]{1,0:T(8,128)(2,1)S(1)}, u32[]{:S(2)}, u32[]{:S(2)}) %collective-permute-start.6) | collective-permute-done | bytes 131104 | tf_op jit(solution)/shard_map/ppermute | solution.py:251
  11.9 1.0 %far_scores.1 = (f32[2,128,512]{2,1,0:T(8,128)S(1)}, f32[2,128,512]{2,1,0:T(8,128)S(1)}, f32[2,64,512]{2,1,0:T(8,128)S(1)}, f32[2,64,512]{2,1,0:T(8,128)S(1)}) custom-call(s32[2]{0:T(128)S(1)} %pad_add_fusion.place_ref, s32[2,64]{1,0:T(2,128)S(1)} %bitcast.28, bf16[2,512,128]{2,1,0:T(8,128)(2,1)S(1)} %get-tuple-element.51.q_ref, ...), custom_call_target="tpu_custom_call" | custom-call | flops 134217728 | bytes 4194304 | tf_op jit(solution)/shard_map/far_scores/pallas_call | solution.py:304
  12.9 0.0 collective-permute-done.7.near_ref
  13.0 2.3 %scores.1 = (bf16[128,512]{1,0:T(8,128)(2,1)S(1)}, bf16[128,512]{1,0:T(8,128)(2,1)S(1)}, bf16[2,2,256,512]{3,2,1,0:T(8,128)(2,1)S(1)}, f32[2,2,8,512]{3,2,1,0:T(8,128)S(1)}) custom-call(s32[2]{0:T(128)S(1)} %pad_add_fusion.place_ref, s32[2,64]{1,0:T(2,128)S(1)} %bitcast.29, bf16[2,512,128]{2,1,0:T(8,128)(2,1)S(1)} %get-tuple-element.51.q_ref, ...), custom_call_target="tpu_custom_call" | custom-call | flops 402653184 | bytes 12582912 | tf_op jit(solution)/shard_map/scores/pallas_call | solution.py:313
  15.3 3.5 %collective-permute-start.8 = (bf16[128,512]{1,0:T(8,128)(2,1)S(1)}, bf16[128,512]{1,0:T(8,128)(2,1)S(1)}, u32[]{:S(2)}, u32[]{:S(2)}) collective-permute-start(bf16[128,512]{1,0:T(8,128)(2,1)S(1)} %get-tuple-element.62), channel_id=1, source_target_pairs={{8,0},{16,8},{24,16},{28,24},{20,28},{12,20},{4,12},{9,1},{17,9},{... | collective-permute-start | bytes 393224 | tf_op jit(solution)/shard_map/ppermute | solution.py:251
  18.8 4.9 %collective-permute-start.9 = (bf16[128,512]{1,0:T(8,128)(2,1)S(1)}, bf16[128,512]{1,0:T(8,128)(2,1)S(1)}, u32[]{:S(2)}, u32[]{:S(2)}) collective-permute-start(bf16[128,512]{1,0:T(8,128)(2,1)S(1)} %get-tuple-element.63), channel_id=1, source_target_pairs={{16,0},{24,8},{28,16},{20,24},{12,28},{4,20},{17,1},{25,9},{29,17}... | collective-permute-start | bytes 393224 | tf_op jit(solution)/shard_map/ppermute | solution.py:251
  23.7 2.0 %rest.1 = (bf16[2,64,2048]{2,1,0:T(8,128)(2,1)}, bf16[64,2048]{1,0:T(8,128)(2,1)S(1)}, f32[128,512]{1,0:T(8,128)S(1)}) custom-call(s32[2]{0:T(128)S(1)} %pad_add_fusion.place_ref, bf16[2,512,128]{2,1,0:T(8,128)(2,1)S(1)} %get-tuple-element.51.q_ref, bf16[2,512,128]{2,1,0:T(8,128)(2,1)S(1)} %get-tuple-element.52.do_ref, ...), custom_call_target="tpu_custom_call" | custom-call | flops 201326592 | bytes 8388608 | tf_op jit(solution)/shard_map/rest/pallas_call | solution.py:330
  25.7 0.0 collective-permute-done.8
  25.7 0.0 collective-permute-done.9
  25.7 3.8 %collective-permute-start.10 = (bf16[64,2048]{1,0:T(8,128)(2,1)S(1)}, bf16[64,2048]{1,0:T(8,128)(2,1)S(1)}, u32[]{:S(2)}, u32[]{:S(2)}) collective-permute-start(bf16[64,2048]{1,0:T(8,128)(2,1)S(1)} %get-tuple-element.69), channel_id=1, source_target_pairs={{0,4},{4,0},{8,12},{12,8},{16,20},{20,16},{24,28},{28,24},{1,5},{5... | collective-permute-start | bytes 786440 | tf_op jit(solution)/shard_map/ppermute | solution.py:258
  29.5 0.1 add_convert_fusion
  29.6 0.1 collective-permute-start.11
  29.7 1.2 %collective-permute-done.11.given_ref = bf16[64,512]{1,0:T(8,128)(2,1)S(1)} collective-permute-done((bf16[64,512]{1,0:T(8,128)(2,1)S(1)}, bf16[64,512]{1,0:T(8,128)(2,1)S(1)}, u32[]{:S(2)}, u32[]{:S(2)}) %collective-permute-start.11) | collective-permute-done | bytes 65568 | tf_op jit(solution)/shard_map/ppermute | solution.py:258
  30.9 0.0 collective-permute-done.10.rows_ref
  30.9 0.8 %store.1 = (bf16[2,64,2048]{2,1,0:T(8,128)(2,1)}, bf16[2,64,256]{2,1,0:T(8,128)(2,1)}, bf16[2,64,256]{2,1,0:T(8,128)(2,1)}) custom-call(s32[1]{0:T(128)} %bitcast.core_ref, bf16[64,2048]{1,0:T(8,128)(2,1)S(1)} %collective-permute-done.10.rows_ref, bf16[64,512]{1,0:T(8,128)(2,1)S(1)} %get-tuple-element.78.kept_ref, ...), custom_call_target="tpu_custom_call", output_to_operand_aliasing={{0}: (4, {})} | custom-call | tf_op jit(solution)/shard_map/store/pallas_call | solution.py:354
  (4 shorter events, 0.0 us)
Async XLA Ops:
  0.6 0.7 %copy-start.3 = (s32[1,2,64]{2,1,0:T(2,128)S(1)}, s32[1,2,64]{2,1,0:T(2,128)}, u32[]{:S(2)}) copy-start(s32[1,2,64]{2,1,0:T(2,128)} %param.11) | copy-start | bytes 1540
  0.6 3.0 %copy-start = (bf16[1,2,64,2048]{3,2,1,0:T(8,128)(2,1)S(1)}, bf16[1,2,64,2048]{3,2,1,0:T(8,128)(2,1)}, u32[]{:S(2)}) copy-start(bf16[1,2,64,2048]{3,2,1,0:T(8,128)(2,1)} %param.6) | copy-start | bytes 1572868
  1.3 2.3 %collective-permute-start.2 = (s32[2,64]{1,0:T(2,128)S(1)}, s32[2,64]{1,0:T(2,128)S(1)}, u32[]{:S(2)}, u32[]{:S(2)}) collective-permute-start(s32[2,64]{1,0:T(2,128)S(1)} %bitcast.26), channel_id=1, source_target_pairs={{0,4},{4,0},{8,12},{12,8},{16,20},{20,16},{24,28},{28,24},{1,5},{5... | collective-permute-start | bytes 1544 | tf_op jit(solution)/shard_map/ppermute | solution.py:258
  2.0 1.5 %collective-permute-start.1 = (bf16[2,64,256]{2,1,0:T(8,128)(2,1)}, bf16[2,64,256]{2,1,0:T(8,128)(2,1)S(1)}, u32[]{:S(2)}, u32[]{:S(2)}) collective-permute-start(bf16[2,64,256]{2,1,0:T(8,128)(2,1)} %bitcast.31), channel_id=1, source_target_pairs={{0,4},{4,0},{8,12},{12,8},{16,20},{20,16},{24,28},{28,24},{1,5},{5... | collective-permute-start | bytes 196616 | tf_op jit(solution)/shard_map/ppermute | solution.py:258
  2.0 1.6 %collective-permute-start = (bf16[2,64,256]{2,1,0:T(8,128)(2,1)}, bf16[2,64,256]{2,1,0:T(8,128)(2,1)S(1)}, u32[]{:S(2)}, u32[]{:S(2)}) collective-permute-start(bf16[2,64,256]{2,1,0:T(8,128)(2,1)} %bitcast.32), channel_id=1, source_target_pairs={{0,4},{4,0},{8,12},{12,8},{16,20},{20,16},{24,28},{28,24},{1,5},{5... | collective-permute-start | bytes 196616 | tf_op jit(solution)/shard_map/ppermute | solution.py:258
  3.7 4.4 %collective-permute-start.3 = (bf16[2,64,2048]{2,1,0:T(8,128)(2,1)S(1)}, bf16[2,64,2048]{2,1,0:T(8,128)(2,1)S(1)}, u32[]{:S(2)}, u32[]{:S(2)}) collective-permute-start(bf16[2,64,2048]{2,1,0:T(8,128)(2,1)S(1)} %bitcast.20), channel_id=1, source_target_pairs={{0,4},{4,0},{8,12},{12,8},{16,20},{20,16},{24,28},{28,24},{1,5},{5... | collective-permute-start | bytes 1572872 | tf_op jit(solution)/shard_map/ppermute | solution.py:258
  4.1 4.0 %collective-permute-start.4 = (bf16[2,64,2048]{2,1,0:T(8,128)(2,1)}, bf16[2,64,2048]{2,1,0:T(8,128)(2,1)S(1)}, u32[]{:S(2)}, u32[]{:S(2)}) collective-permute-start(bf16[2,64,2048]{2,1,0:T(8,128)(2,1)} %bitcast.22), channel_id=1, source_target_pairs={{0,4},{4,0},{8,12},{12,8},{16,20},{20,16},{24,28},{28,24},{1,5},{5... | collective-permute-start | bytes 1572872 | tf_op jit(solution)/shard_map/ppermute | solution.py:258
  4.2 3.8 %collective-permute-start.5 = (bf16[2,64,2048]{2,1,0:T(8,128)(2,1)}, bf16[2,64,2048]{2,1,0:T(8,128)(2,1)S(1)}, u32[]{:S(2)}, u32[]{:S(2)}) collective-permute-start(bf16[2,64,2048]{2,1,0:T(8,128)(2,1)} %bitcast.24), channel_id=1, source_target_pairs={{0,4},{4,0},{8,12},{12,8},{16,20},{20,16},{24,28},{28,24},{1,5},{5... | collective-permute-start | bytes 1572872 | tf_op jit(solution)/shard_map/ppermute | solution.py:258
  4.6 7.4 %collective-permute-start.6 = (bf16[128,512]{1,0:T(8,128)(2,1)S(1)}, bf16[128,512]{1,0:T(8,128)(2,1)S(1)}, u32[]{:S(2)}, u32[]{:S(2)}) collective-permute-start(bf16[128,512]{1,0:T(8,128)(2,1)S(1)} %maximum_maximum_fusion.own_ref), channel_id=1, source_target_pairs={{0,16},{8,24},{16,28},{24,20},{28,12},{20,4},{1,17},{9,25},{17,29}... | collective-permute-start | bytes 393224 | tf_op jit(solution)/shard_map/ppermute | solution.py:251
  5.9 7.1 %collective-permute-start.7 = (bf16[128,512]{1,0:T(8,128)(2,1)S(1)}, bf16[128,512]{1,0:T(8,128)(2,1)S(1)}, u32[]{:S(2)}, u32[]{:S(2)}) collective-permute-start(bf16[128,512]{1,0:T(8,128)(2,1)S(1)} %maximum_maximum_fusion.own_ref), channel_id=1, source_target_pairs={{0,8},{8,16},{16,24},{24,28},{28,20},{20,12},{12,4},{1,9},{9,17},{... | collective-permute-start | bytes 393224 | tf_op jit(solution)/shard_map/ppermute | solution.py:251
  8.1 1.1 %copy-start.1 = (bf16[1,2,64,2048]{3,2,1,0:T(8,128)(2,1)S(1)}, bf16[1,2,64,2048]{3,2,1,0:T(8,128)(2,1)}, u32[]{:S(2)}) copy-start(bf16[1,2,64,2048]{3,2,1,0:T(8,128)(2,1)} %param.9) | copy-start | bytes 1572868
  8.1 1.2 %copy-start.2 = (bf16[1,2,64,2048]{3,2,1,0:T(8,128)(2,1)S(1)}, bf16[1,2,64,2048]{3,2,1,0:T(8,128)(2,1)}, u32[]{:S(2)}) copy-start(bf16[1,2,64,2048]{3,2,1,0:T(8,128)(2,1)} %param.10) | copy-start | bytes 1572868
  15.3 10.4 %collective-permute-start.8 = (bf16[128,512]{1,0:T(8,128)(2,1)S(1)}, bf16[128,512]{1,0:T(8,128)(2,1)S(1)}, u32[]{:S(2)}, u32[]{:S(2)}) collective-permute-start(bf16[128,512]{1,0:T(8,128)(2,1)S(1)} %get-tuple-element.62), channel_id=1, source_target_pairs={{8,0},{16,8},{24,16},{28,24},{20,28},{12,20},{4,12},{9,1},{17,9},{... | collective-permute-start | bytes 393224 | tf_op jit(solution)/shard_map/ppermute | solution.py:251
  18.8 6.9 %collective-permute-start.9 = (bf16[128,512]{1,0:T(8,128)(2,1)S(1)}, bf16[128,512]{1,0:T(8,128)(2,1)S(1)}, u32[]{:S(2)}, u32[]{:S(2)}) collective-permute-start(bf16[128,512]{1,0:T(8,128)(2,1)S(1)} %get-tuple-element.63), channel_id=1, source_target_pairs={{16,0},{24,8},{28,16},{20,24},{12,28},{4,20},{17,1},{25,9},{29,17}... | collective-permute-start | bytes 393224 | tf_op jit(solution)/shard_map/ppermute | solution.py:251
  25.7 5.2 %collective-permute-start.10 = (bf16[64,2048]{1,0:T(8,128)(2,1)S(1)}, bf16[64,2048]{1,0:T(8,128)(2,1)S(1)}, u32[]{:S(2)}, u32[]{:S(2)}) collective-permute-start(bf16[64,2048]{1,0:T(8,128)(2,1)S(1)} %get-tuple-element.69), channel_id=1, source_target_pairs={{0,4},{4,0},{8,12},{12,8},{16,20},{20,16},{24,28},{28,24},{1,5},{5... | collective-permute-start | bytes 786440 | tf_op jit(solution)/shard_map/ppermute | solution.py:258
  29.6 1.3 %collective-permute-start.11 = (bf16[64,512]{1,0:T(8,128)(2,1)S(1)}, bf16[64,512]{1,0:T(8,128)(2,1)S(1)}, u32[]{:S(2)}, u32[]{:S(2)}) collective-permute-start(bf16[64,512]{1,0:T(8,128)(2,1)S(1)} %get-tuple-element.77), channel_id=1, source_target_pairs={{0,4},{4,0},{8,12},{12,8},{16,20},{20,16},{24,28},{28,24},{1,5},{5... | collective-permute-start | bytes 196616 | tf_op jit(solution)/shard_map/ppermute | solution.py:258

commit v10 on v8

--- a/solution.py
+++ b/solution.py
@@ -233,13 +233,13 @@
         return jnp.where(core == 0, x[0], x[1])
 
     starts_in, key_in, value_in = (swapped(x[0]) for x in (doc_start, key, value))
+    key_in, *late = lax.optimization_barrier((key_in, query[0], out_grad[0], attn_out[0]))
+    sent = [swapped(x) for x in late]
     sides = ((key[0], value[0]), (key_in, value_in))
     own = jnp.concatenate(
         [jnp.concatenate([mine(x) for x in side], axis=-1) for side in sides], axis=0
     )
-    own, starts_in, starts, *late = lax.optimization_barrier(
-        (own, starts_in, doc_start[0], query[0], out_grad[0], attn_out[0])
-    )
+    own, starts_in, starts = lax.optimization_barrier((own, starts_in, doc_start[0]))
     kv_heads = kv_width // HEAD_SIZE
     lanes = tokens * (width // kv_width)
     products = 2 * slots * tokens * pair * width
@@ -264,7 +264,6 @@
         )(place, starts, own, *sources)
         return (starts, q, do, scores, delta), (q, do, scores, dprobs)
 
-    sent = [swapped(x) for x in late]
     far = shift(own, 2)
     near = shift(own, 1)
     side_in = arranged(1, starts_in, sent)

time: 31.6 us -> 31.7 us (level)
    ppermute x4, waiting for transfers between devices: 2.15 us -> 2.57 us  [shift(): return lax.ppermute(x, 'ctx', moves)]
    unnamed x8 -> x10, local copies, waits for them, and re-layouts: 0.71 us -> 0.9 us
    select_n x3 -> x4, other arithmetic: 0.83 us -> 0.84 us  [mine(): return jnp.where(core == 0, x[0], x[1])]
  transfers between devices with their start and end apart: 12 -> 12, of which waited for: 5 -> 3; matrix products, arithmetic and copies ran while one was open for 3% -> 3% of each run, Pallas kernels for 13% -> 13%
where the time goes in v10:
time: 31.7 us; the launch traced here: 31.2 us
  starting transfers between devices  17.4 us (55%)
  Pallas kernels  7.25 us (23%)
  waiting for transfers between devices  3.83 us (12%)
  other arithmetic  0.98 us (3%)
  local copies, waits for them, and re-layouts  0.92 us (3%)
  between operations  0.82 us (3%)
    ppermute x4, starting transfers between devices, shift(): return lax.ppermute(x, 'ctx', moves)  11.6 us
    ppermute x8, starting transfers between devices, swapped(): return lax.ppermute(x, 'ctx', swap)  5.77 us
    ppermute x4, waiting for transfers between devices, shift(): return lax.ppermute(x, 'ctx', moves)  2.57 us
    pallas_call x1, Pallas kernels, shards(): pl.pallas_call(scores_kernel, out_shape=(jax.ShapeDtypeStruct((pair, pair...  2.42 us
    pallas_call x2, Pallas kernels, arranged(): pl.pallas_call(functools.partial(rows_kernel, unit), out_shape=(stacked,...  2.02 us
    pallas_call x1, Pallas kernels, shards(): pl.pallas_call(rest_kernel, out_shape=(jax.ShapeDtypeStruct((slots, token...  2.02 us
    ppermute x8, waiting for transfers between devices, swapped(): return lax.ppermute(x, 'ctx', swap)  1.26 us
    unnamed x10, local copies, waits for them, and re-layouts  0.9 us
  transfers between devices with their start and end apart: 12, of which 3 were waited for; matrix products, arithmetic and copies ran while one was open for 3% of the time, Pallas kernels for 13%

profile of v10, /device:TPU:13, one launch (start us, length us, event | category | flops | bytes accessed | tf_op | source)
XLA Modules:
  0.0 31.2 jit_solution(9131101418586170756)
XLA Ops:
  0.6 0.7 %collective-permute-start.1 = (bf16[2,64,256]{2,1,0:T(8,128)(2,1)}, bf16[2,64,256]{2,1,0:T(8,128)(2,1)S(1)}, u32[]{:S(2)}, u32[]{:S(2)}) collective-permute-start(bf16[2,64,256]{2,1,0:T(8,128)(2,1)} %bitcast.31), channel_id=1, source_target_pairs={{0,4},{4,0},{8,12},{12,8},{16,20},{20,16},{24,28},{28,24},{1,5},{5... | collective-permute-start | bytes 196616 | tf_op jit(solution)/shard_map/ppermute | solution.py:230
  1.4 0.0 copy-start.3
  1.4 0.1 collective-permute-start
  1.5 0.6 %copy-done.3 = s32[1,2,64]{2,1,0:T(2,128)S(1)} copy-done((s32[1,2,64]{2,1,0:T(2,128)S(1)}, s32[1,2,64]{2,1,0:T(2,128)}, u32[]{:S(2)}) %copy-start.3) | copy-done | bytes 536
  2.1 0.0 collective-permute-start.2
  2.1 0.0 copy-start.4
  2.1 0.8 %select_bitcast_fusion.1 = bf16[64,256]{1,0:T(8,128)(2,1)S(1)} fusion(bf16[1,2,64,256]{3,2,1,0:T(8,128)(2,1)} %param.8, pred[]{:T(512)} %bitcast.2), kind=kLoop, calls=%fused_computation.5 | loop fusion | flops 16384 | bytes 98305 | tf_op jit(solution)/shard_map/jit(_where)/select_n | solution.py:233
  2.9 0.0 copy-done.4
  2.9 0.0 collective-permute-done
  2.9 0.6 %collective-permute-start.3 = (bf16[2,64,2048]{2,1,0:T(8,128)(2,1)}, bf16[2,64,2048]{2,1,0:T(8,128)(2,1)S(1)}, u32[]{:S(2)}, u32[]{:S(2)}) collective-permute-start(bf16[2,64,2048]{2,1,0:T(8,128)(2,1)} %bitcast.20), channel_id=1, source_target_pairs={{0,4},{4,0},{8,12},{12,8},{16,20},{20,16},{24,28},{28,24},{1,5},{5... | collective-permute-start | bytes 1572872 | tf_op jit(solution)/shard_map/ppermute | solution.py:230
  3.5 0.1 collective-permute-start.4
  3.6 0.4 %collective-permute-start.5 = (bf16[2,64,2048]{2,1,0:T(8,128)(2,1)}, bf16[2,64,2048]{2,1,0:T(8,128)(2,1)S(1)}, u32[]{:S(2)}, u32[]{:S(2)}) collective-permute-start(bf16[2,64,2048]{2,1,0:T(8,128)(2,1)} %bitcast.24), channel_id=1, source_target_pairs={{0,4},{4,0},{8,12},{12,8},{16,20},{20,16},{24,28},{28,24},{1,5},{5... | collective-permute-start | bytes 1572872 | tf_op jit(solution)/shard_map/ppermute | solution.py:230
  4.0 0.0 collective-permute-done.1
  4.0 0.0 collective-permute-done.2.starts_ref.starts_in_ref
  4.1 1.3 %collective-permute-start.6 = (bf16[128,512]{1,0:T(8,128)(2,1)S(1)}, bf16[128,512]{1,0:T(8,128)(2,1)S(1)}, u32[]{:S(2)}, u32[]{:S(2)}) collective-permute-start(bf16[128,512]{1,0:T(8,128)(2,1)S(1)} %maximum_maximum_fusion.own_ref), channel_id=1, source_target_pairs={{0,16},{8,24},{16,28},{24,20},{28,12},{20,4},{1,17},{9,25},{17,29}... | collective-permute-start | bytes 393224 | tf_op jit(solution)/shard_map/ppermute | solution.py:223
  5.4 2.1 %collective-permute-start.7 = (bf16[128,512]{1,0:T(8,128)(2,1)S(1)}, bf16[128,512]{1,0:T(8,128)(2,1)S(1)}, u32[]{:S(2)}, u32[]{:S(2)}) collective-permute-start(bf16[128,512]{1,0:T(8,128)(2,1)S(1)} %maximum_maximum_fusion.own_ref), channel_id=1, source_target_pairs={{0,8},{8,16},{16,24},{24,28},{28,20},{20,12},{12,4},{1,9},{9,17},{... | collective-permute-start | bytes 393224 | tf_op jit(solution)/shard_map/ppermute | solution.py:223
  7.5 0.1 pad_add_fusion.place_ref
  7.5 0.0 copy-start
  7.5 0.0 copy-start.1
  7.5 0.0 copy-start.2
  7.5 0.0 collective-permute-done.3.q_ref
  7.5 0.0 collective-permute-done.4.do_ref
  7.6 0.0 collective-permute-done.5.o_ref
  7.6 1.0 %rows.2 = (bf16[2,512,128]{2,1,0:T(8,128)(2,1)S(1)}, bf16[2,512,128]{2,1,0:T(8,128)(2,1)S(1)}, f32[2,128,512]{2,1,0:T(8,128)S(1)}, f32[2,128,512]{2,1,0:T(8,128)S(1)}, f32[2,8,512]{2,1,0:T(8,128)S(1)}) custom-call(s32[2]{0:T(128)S(1)} %pad_add_fusion.place_ref, s32[2,64]{1,0:T(2,128)S(1)} %collective-permute-done.2.starts_ref.starts_in_ref, ...), custom_call_target="tpu_custom_call" | custom-call | flops 33554432 | bytes 4194304 | tf_op jit(solution)/shard_map/rows/pallas_call | solution.py:250
  8.6 0.0 copy-done
  8.6 0.1 copy-done.1
  8.7 0.2 copy-done.2
  8.9 1.0 %rows.3 = (bf16[2,512,128]{2,1,0:T(8,128)(2,1)S(1)}, bf16[2,512,128]{2,1,0:T(8,128)(2,1)S(1)}, f32[2,64,512]{2,1,0:T(8,128)S(1)}, f32[2,64,512]{2,1,0:T(8,128)S(1)}, f32[2,8,512]{2,1,0:T(8,128)S(1)}) custom-call(s32[2]{0:T(128)S(1)} %pad_add_fusion.place_ref, s32[2,64]{1,0:T(2,128)S(1)} %bitcast.27, bf16[128,512]{1,0:T(8,128)(2,1)S(1)} %maximum_maximum_fusion.own_ref, ...), custom_call_target="tpu_custom_call" | custom-call | flops 33554432 | bytes 4194304 | tf_op jit(solution)/shard_map/rows/pallas_call | solution.py:250
  9.9 1.5 %collective-permute-done.6.far_ref = bf16[128,512]{1,0:T(8,128)(2,1)S(1)} collective-permute-done((bf16[128,512]{1,0:T(8,128)(2,1)S(1)}, bf16[128,512]{1,0:T(8,128)(2,1)S(1)}, u32[]{:S(2)}, u32[]{:S(2)}) %collective-permute-start.6) | collective-permute-done | bytes 131104 | tf_op jit(solution)/shard_map/ppermute | solution.py:223
  11.4 1.0 %collective-permute-done.7.near_ref = bf16[128,512]{1,0:T(8,128)(2,1)S(1)} collective-permute-done((bf16[128,512]{1,0:T(8,128)(2,1)S(1)}, bf16[128,512]{1,0:T(8,128)(2,1)S(1)}, u32[]{:S(2)}, u32[]{:S(2)}) %collective-permute-start.7) | collective-permute-done | bytes 131104 | tf_op jit(solution)/shard_map/ppermute | solution.py:223
  12.5 2.4 %scores.1 = (bf16[128,512]{1,0:T(8,128)(2,1)S(1)}, bf16[128,512]{1,0:T(8,128)(2,1)S(1)}, bf16[2,2,256,512]{3,2,1,0:T(8,128)(2,1)S(1)}, f32[2,2,8,512]{3,2,1,0:T(8,128)S(1)}) custom-call(s32[2]{0:T(128)S(1)} %pad_add_fusion.place_ref, s32[2,64]{1,0:T(2,128)S(1)} %bitcast.28, bf16[2,512,128]{2,1,0:T(8,128)(2,1)S(1)} %get-tuple-element.49.q_ref, ...), custom_call_target="tpu_custom_call" | custom-call | flops 402653184 | bytes 12582912 | tf_op jit(solution)/shard_map/scores/pallas_call | solution.py:272
  14.9 3.2 %collective-permute-start.8 = (bf16[128,512]{1,0:T(8,128)(2,1)S(1)}, bf16[128,512]{1,0:T(8,128)(2,1)S(1)}, u32[]{:S(2)}, u32[]{:S(2)}) collective-permute-start(bf16[128,512]{1,0:T(8,128)(2,1)S(1)} %get-tuple-element.56), channel_id=1, source_target_pairs={{8,0},{16,8},{24,16},{28,24},{20,28},{12,20},{4,12},{9,1},{17,9},{... | collective-permute-start | bytes 393224 | tf_op jit(solution)/shard_map/ppermute | solution.py:223
  18.1 5.1 %collective-permute-start.9 = (bf16[128,512]{1,0:T(8,128)(2,1)S(1)}, bf16[128,512]{1,0:T(8,128)(2,1)S(1)}, u32[]{:S(2)}, u32[]{:S(2)}) collective-permute-start(bf16[128,512]{1,0:T(8,128)(2,1)S(1)} %get-tuple-element.57), channel_id=1, source_target_pairs={{16,0},{24,8},{28,16},{20,24},{12,28},{4,20},{17,1},{25,9},{29,17}... | collective-permute-start | bytes 393224 | tf_op jit(solution)/shard_map/ppermute | solution.py:223
  23.2 2.0 %rest.1 = (bf16[2,64,2048]{2,1,0:T(8,128)(2,1)}, bf16[64,2048]{1,0:T(8,128)(2,1)S(1)}, f32[128,512]{1,0:T(8,128)S(1)}) custom-call(s32[2]{0:T(128)S(1)} %pad_add_fusion.place_ref, bf16[2,512,128]{2,1,0:T(8,128)(2,1)S(1)} %get-tuple-element.49.q_ref, bf16[2,512,128]{2,1,0:T(8,128)(2,1)S(1)} %get-tuple-element.50.do_ref, ...), custom_call_target="tpu_custom_call" | custom-call | flops 201326592 | bytes 8388608 | tf_op jit(solution)/shard_map/rest/pallas_call | solution.py:292
  25.2 0.0 collective-permute-done.8
  25.2 0.0 collective-permute-done.9
  25.2 3.8 %collective-permute-start.10 = (bf16[64,2048]{1,0:T(8,128)(2,1)S(1)}, bf16[64,2048]{1,0:T(8,128)(2,1)S(1)}, u32[]{:S(2)}, u32[]{:S(2)}) collective-permute-start(bf16[64,2048]{1,0:T(8,128)(2,1)S(1)} %get-tuple-element.63), channel_id=1, source_target_pairs={{0,4},{4,0},{8,12},{12,8},{16,20},{20,16},{24,28},{28,24},{1,5},{5... | collective-permute-start | bytes 786440 | tf_op jit(solution)/shard_map/ppermute | solution.py:230
  29.0 0.1 add_convert_fusion
  29.1 0.1 collective-permute-start.11
  29.2 1.2 %collective-permute-done.11.given_ref = bf16[64,512]{1,0:T(8,128)(2,1)S(1)} collective-permute-done((bf16[64,512]{1,0:T(8,128)(2,1)S(1)}, bf16[64,512]{1,0:T(8,128)(2,1)S(1)}, u32[]{:S(2)}, u32[]{:S(2)}) %collective-permute-start.11) | collective-permute-done | bytes 65568 | tf_op jit(solution)/shard_map/ppermute | solution.py:230
  30.4 0.0 collective-permute-done.10.rows_ref
  30.4 0.8 %store.1 = (bf16[2,64,2048]{2,1,0:T(8,128)(2,1)}, bf16[2,64,256]{2,1,0:T(8,128)(2,1)}, bf16[2,64,256]{2,1,0:T(8,128)(2,1)}) custom-call(s32[1]{0:T(128)} %bitcast.core_ref, bf16[64,2048]{1,0:T(8,128)(2,1)S(1)} %collective-permute-done.10.rows_ref, bf16[64,512]{1,0:T(8,128)(2,1)S(1)} %get-tuple-element.72.kept_ref, ...), custom_call_target="tpu_custom_call", output_to_operand_aliasing={{0}: (4, {})} | custom-call | tf_op jit(solution)/shard_map/store/pallas_call | solution.py:316
  (5 shorter events, 0.0 us)
Async XLA Ops:
  0.6 3.4 %collective-permute-start.1 = (bf16[2,64,256]{2,1,0:T(8,128)(2,1)}, bf16[2,64,256]{2,1,0:T(8,128)(2,1)S(1)}, u32[]{:S(2)}, u32[]{:S(2)}) collective-permute-start(bf16[2,64,256]{2,1,0:T(8,128)(2,1)} %bitcast.31), channel_id=1, source_target_pairs={{0,4},{4,0},{8,12},{12,8},{16,20},{20,16},{24,28},{28,24},{1,5},{5... | collective-permute-start | bytes 196616 | tf_op jit(solution)/shard_map/ppermute | solution.py:230
  1.4 0.7 %copy-start.3 = (s32[1,2,64]{2,1,0:T(2,128)S(1)}, s32[1,2,64]{2,1,0:T(2,128)}, u32[]{:S(2)}) copy-start(s32[1,2,64]{2,1,0:T(2,128)} %param.11) | copy-start | bytes 1540
  1.4 1.5 %collective-permute-start = (bf16[2,64,256]{2,1,0:T(8,128)(2,1)}, bf16[2,64,256]{2,1,0:T(8,128)(2,1)S(1)}, u32[]{:S(2)}, u32[]{:S(2)}) collective-permute-start(bf16[2,64,256]{2,1,0:T(8,128)(2,1)} %bitcast.30), channel_id=1, source_target_pairs={{0,4},{4,0},{8,12},{12,8},{16,20},{20,16},{24,28},{28,24},{1,5},{5... | collective-permute-start | bytes 196616 | tf_op jit(solution)/shard_map/ppermute | solution.py:230
  2.1 2.0 %collective-permute-start.2 = (s32[2,64]{1,0:T(2,128)S(1)}, s32[2,64]{1,0:T(2,128)S(1)}, u32[]{:S(2)}, u32[]{:S(2)}) collective-permute-start(s32[2,64]{1,0:T(2,128)S(1)} %bitcast.26), channel_id=1, source_target_pairs={{0,4},{4,0},{8,12},{12,8},{16,20},{20,16},{24,28},{28,24},{1,5},{5... | collective-permute-start | bytes 1544 | tf_op jit(solution)/shard_map/ppermute | solution.py:230
  2.1 0.8 %copy-start.4 = (bf16[1,2,64,256]{3,2,1,0:T(8,128)(2,1)S(1)}, bf16[1,2,64,256]{3,2,1,0:T(8,128)(2,1)}, u32[]{:S(2)}) copy-start(bf16[1,2,64,256]{3,2,1,0:T(8,128)(2,1)} %param.7) | copy-start | bytes 196612
  2.9 4.6 %collective-permute-start.3 = (bf16[2,64,2048]{2,1,0:T(8,128)(2,1)}, bf16[2,64,2048]{2,1,0:T(8,128)(2,1)S(1)}, u32[]{:S(2)}, u32[]{:S(2)}) collective-permute-start(bf16[2,64,2048]{2,1,0:T(8,128)(2,1)} %bitcast.20), channel_id=1, source_target_pairs={{0,4},{4,0},{8,12},{12,8},{16,20},{20,16},{24,28},{28,24},{1,5},{5... | collective-permute-start | bytes 1572872 | tf_op jit(solution)/shard_map/ppermute | solution.py:230
  3.5 4.1 %collective-permute-start.4 = (bf16[2,64,2048]{2,1,0:T(8,128)(2,1)}, bf16[2,64,2048]{2,1,0:T(8,128)(2,1)S(1)}, u32[]{:S(2)}, u32[]{:S(2)}) collective-permute-start(bf16[2,64,2048]{2,1,0:T(8,128)(2,1)} %bitcast.22), channel_id=1, source_target_pairs={{0,4},{4,0},{8,12},{12,8},{16,20},{20,16},{24,28},{28,24},{1,5},{5... | collective-permute-start | bytes 1572872 | tf_op jit(solution)/shard_map/ppermute | solution.py:230
  3.6 4.0 %collective-permute-start.5 = (bf16[2,64,2048]{2,1,0:T(8,128)(2,1)}, bf16[2,64,2048]{2,1,0:T(8,128)(2,1)S(1)}, u32[]{:S(2)}, u32[]{:S(2)}) collective-permute-start(bf16[2,64,2048]{2,1,0:T(8,128)(2,1)} %bitcast.24), channel_id=1, source_target_pairs={{0,4},{4,0},{8,12},{12,8},{16,20},{20,16},{24,28},{28,24},{1,5},{5... | collective-permute-start | bytes 1572872 | tf_op jit(solution)/shard_map/ppermute | solution.py:230
  4.1 7.4 %collective-permute-start.6 = (bf16[128,512]{1,0:T(8,128)(2,1)S(1)}, bf16[128,512]{1,0:T(8,128)(2,1)S(1)}, u32[]{:S(2)}, u32[]{:S(2)}) collective-permute-start(bf16[128,512]{1,0:T(8,128)(2,1)S(1)} %maximum_maximum_fusion.own_ref), channel_id=1, source_target_pairs={{0,16},{8,24},{16,28},{24,20},{28,12},{20,4},{1,17},{9,25},{17,29}... | collective-permute-start | bytes 393224 | tf_op jit(solution)/shard_map/ppermute | solution.py:223
  5.4 7.1 %collective-permute-start.7 = (bf16[128,512]{1,0:T(8,128)(2,1)S(1)}, bf16[128,512]{1,0:T(8,128)(2,1)S(1)}, u32[]{:S(2)}, u32[]{:S(2)}) collective-permute-start(bf16[128,512]{1,0:T(8,128)(2,1)S(1)} %maximum_maximum_fusion.own_ref), channel_id=1, source_target_pairs={{0,8},{8,16},{16,24},{24,28},{28,20},{20,12},{12,4},{1,9},{9,17},{... | collective-permute-start | bytes 393224 | tf_op jit(solution)/shard_map/ppermute | solution.py:223
  7.5 1.1 %copy-start = (bf16[1,2,64,2048]{3,2,1,0:T(8,128)(2,1)S(1)}, bf16[1,2,64,2048]{3,2,1,0:T(8,128)(2,1)}, u32[]{:S(2)}) copy-start(bf16[1,2,64,2048]{3,2,1,0:T(8,128)(2,1)} %param.6) | copy-start | bytes 1572868
  7.5 1.2 %copy-start.1 = (bf16[1,2,64,2048]{3,2,1,0:T(8,128)(2,1)S(1)}, bf16[1,2,64,2048]{3,2,1,0:T(8,128)(2,1)}, u32[]{:S(2)}) copy-start(bf16[1,2,64,2048]{3,2,1,0:T(8,128)(2,1)} %param.9) | copy-start | bytes 1572868
  7.5 1.4 %copy-start.2 = (bf16[1,2,64,2048]{3,2,1,0:T(8,128)(2,1)S(1)}, bf16[1,2,64,2048]{3,2,1,0:T(8,128)(2,1)}, u32[]{:S(2)}) copy-start(bf16[1,2,64,2048]{3,2,1,0:T(8,128)(2,1)} %param.10) | copy-start | bytes 1572868
  14.9 10.3 %collective-permute-start.8 = (bf16[128,512]{1,0:T(8,128)(2,1)S(1)}, bf16[128,512]{1,0:T(8,128)(2,1)S(1)}, u32[]{:S(2)}, u32[]{:S(2)}) collective-permute-start(bf16[128,512]{1,0:T(8,128)(2,1)S(1)} %get-tuple-element.56), channel_id=1, source_target_pairs={{8,0},{16,8},{24,16},{28,24},{20,28},{12,20},{4,12},{9,1},{17,9},{... | collective-permute-start | bytes 393224 | tf_op jit(solution)/shard_map/ppermute | solution.py:223
  18.1 7.1 %collective-permute-start.9 = (bf16[128,512]{1,0:T(8,128)(2,1)S(1)}, bf16[128,512]{1,0:T(8,128)(2,1)S(1)}, u32[]{:S(2)}, u32[]{:S(2)}) collective-permute-start(bf16[128,512]{1,0:T(8,128)(2,1)S(1)} %get-tuple-element.57), channel_id=1, source_target_pairs={{16,0},{24,8},{28,16},{20,24},{12,28},{4,20},{17,1},{25,9},{29,17}... | collective-permute-start | bytes 393224 | tf_op jit(solution)/shard_map/ppermute | solution.py:223
  25.2 5.2 %collective-permute-start.10 = (bf16[64,2048]{1,0:T(8,128)(2,1)S(1)}, bf16[64,2048]{1,0:T(8,128)(2,1)S(1)}, u32[]{:S(2)}, u32[]{:S(2)}) collective-permute-start(bf16[64,2048]{1,0:T(8,128)(2,1)S(1)} %get-tuple-element.63), channel_id=1, source_target_pairs={{0,4},{4,0},{8,12},{12,8},{16,20},{20,16},{24,28},{28,24},{1,5},{5... | collective-permute-start | bytes 786440 | tf_op jit(solution)/shard_map/ppermute | solution.py:230
  29.1 1.3 %collective-permute-start.11 = (bf16[64,512]{1,0:T(8,128)(2,1)S(1)}, bf16[64,512]{1,0:T(8,128)(2,1)S(1)}, u32[]{:S(2)}, u32[]{:S(2)}) collective-permute-start(bf16[64,512]{1,0:T(8,128)(2,1)S(1)} %get-tuple-element.71), channel_id=1, source_target_pairs={{0,4},{4,0},{8,12},{12,8},{16,20},{20,16},{24,28},{28,24},{1,5},{5... | collective-permute-start | bytes 196616 | tf_op jit(solution)/shard_map/ppermute | solution.py:230

commit v11 on v8

--- a/solution.py
+++ b/solution.py
@@ -308,7 +308,6 @@
         cost_estimate=work(3 * products, 8 * 2**20),
         name="rest",
     )(place, *side[1], *side_in[1], far, near, own, dscores, norm)
-    from_near, from_far, dq_send = lax.optimization_barrier((from_near, from_far, dq_send))
     dq_rows = swapped(dq_send)
     total = own_part + from_near.astype(jnp.float32) + from_far.astype(jnp.float32)
     total = total.astype(bf16)

time: 31.6 us -> 31.4 us (level)
  starting transfers between devices: 17.7 us -> 15.7 us
  waiting for transfers between devices: 3.56 us -> 5.51 us
    ppermute x4, waiting for transfers between devices: 2.15 us -> 4.31 us  [shift(): return lax.ppermute(x, 'ctx', moves)]
    ppermute x8, starting transfers between devices: 5.98 us -> 4.03 us  [swapped(): return lax.ppermute(x, 'ctx', swap)]
  transfers between devices with their start and end apart: 12 -> 12, of which waited for: 5 -> 6; matrix products, arithmetic and copies ran while one was open for 3% -> 3% of each run, Pallas kernels for 13% -> 13%
where the time goes in v11:
time: 31.4 us; the launch traced here: 31.1 us
  starting transfers between devices  15.7 us (50%)
  Pallas kernels  7.25 us (23%)
  waiting for transfers between devices  5.51 us (18%)
  other arithmetic  0.97 us (3%)
  local copies, waits for them, and re-layouts  0.81 us (3%)
  between operations  0.8 us (3%)
    ppermute x4, starting transfers between devices, shift(): return lax.ppermute(x, 'ctx', moves)  11.7 us
    ppermute x4, waiting for transfers between devices, shift(): return lax.ppermute(x, 'ctx', moves)  4.31 us
    ppermute x8, starting transfers between devices, swapped(): return lax.ppermute(x, 'ctx', swap)  4.03 us
    pallas_call x1, Pallas kernels, shards(): pl.pallas_call(scores_kernel, out_shape=(jax.ShapeDtypeStruct((pair, pair...  2.42 us
    pallas_call x2, Pallas kernels, arranged(): pl.pallas_call(functools.partial(rows_kernel, unit), out_shape=(stacked,...  2.03 us
    pallas_call x1, Pallas kernels, shards(): pl.pallas_call(rest_kernel, out_shape=(jax.ShapeDtypeStruct((slots, token...  2.02 us
    ppermute x8, waiting for transfers between devices, swapped(): return lax.ppermute(x, 'ctx', swap)  1.2 us
    select_n x3, other arithmetic, mine(): return jnp.where(core == 0, x[0], x[1])  0.83 us
  transfers between devices with their start and end apart: 12, of which 6 were waited for; matrix products, arithmetic and copies ran while one was open for 3% of the time, Pallas kernels for 13%

profile of v11, /device:TPU:13, one launch (start us, length us, event | category | flops | bytes accessed | tf_op | source)
XLA Modules:
  0.0 31.1 jit_solution(10054494341011035987)
XLA Ops:
  0.6 0.0 copy-start.3
  0.6 0.0 copy-start
  0.7 0.7 %copy-done.3 = s32[1,2,64]{2,1,0:T(2,128)S(1)} copy-done((s32[1,2,64]{2,1,0:T(2,128)S(1)}, s32[1,2,64]{2,1,0:T(2,128)}, u32[]{:S(2)}) %copy-start.3) | copy-done | bytes 536
  1.3 0.7 %collective-permute-start.2 = (s32[2,64]{1,0:T(2,128)S(1)}, s32[2,64]{1,0:T(2,128)S(1)}, u32[]{:S(2)}, u32[]{:S(2)}) collective-permute-start(s32[2,64]{1,0:T(2,128)S(1)} %bitcast.26), channel_id=1, source_target_pairs={{0,4},{4,0},{8,12},{12,8},{16,20},{20,16},{24,28},{28,24},{1,5},{5... | collective-permute-start | bytes 1544 | tf_op jit(solution)/shard_map/ppermute | solution.py:230
  2.0 0.0 collective-permute-start.1
  2.0 0.5 %collective-permute-start = (bf16[2,64,256]{2,1,0:T(8,128)(2,1)}, bf16[2,64,256]{2,1,0:T(8,128)(2,1)S(1)}, u32[]{:S(2)}, u32[]{:S(2)}) collective-permute-start(bf16[2,64,256]{2,1,0:T(8,128)(2,1)} %bitcast.31), channel_id=1, source_target_pairs={{0,4},{4,0},{8,12},{12,8},{16,20},{20,16},{24,28},{28,24},{1,5},{5... | collective-permute-start | bytes 196616 | tf_op jit(solution)/shard_map/ppermute | solution.py:230
  2.5 0.8 %select_bitcast_fusion = (bf16[64,256]{1,0:T(8,128)(2,1)S(1)}, bf16[64,256]{1,0:T(8,128)(2,1)S(1)}) fusion(bf16[1,2,64,256]{3,2,1,0:T(8,128)(2,1)} %param.8, pred[]{:T(512)} %bitcast.2, bf16[1,2,64,256]{3,2,1,0:T(8,128)(2,1)} %param.7), kind=kLoop, calls=%fused_computation.6 | loop fusion | flops 32768 | bytes 196609 | tf_op jit(solution)/shard_map/jit(_where)/select_n | solution.py:233
  3.3 0.1 collective-permute-done.1
  3.5 0.1 collective-permute-done
  3.6 0.0 collective-permute-done.2.starts_ref.starts_in_ref
  3.6 0.0 copy-done
  3.7 0.4 %collective-permute-start.3 = (bf16[2,64,2048]{2,1,0:T(8,128)(2,1)S(1)}, bf16[2,64,2048]{2,1,0:T(8,128)(2,1)S(1)}, u32[]{:S(2)}, u32[]{:S(2)}) collective-permute-start(bf16[2,64,2048]{2,1,0:T(8,128)(2,1)S(1)} %bitcast.20), channel_id=1, source_target_pairs={{0,4},{4,0},{8,12},{12,8},{16,20},{20,16},{24,28},{28,24},{1,5},{5... | collective-permute-start | bytes 1572872 | tf_op jit(solution)/shard_map/ppermute | solution.py:230
  4.1 0.2 collective-permute-start.4
  4.2 0.4 %collective-permute-start.5 = (bf16[2,64,2048]{2,1,0:T(8,128)(2,1)}, bf16[2,64,2048]{2,1,0:T(8,128)(2,1)S(1)}, u32[]{:S(2)}, u32[]{:S(2)}) collective-permute-start(bf16[2,64,2048]{2,1,0:T(8,128)(2,1)} %bitcast.24), channel_id=1, source_target_pairs={{0,4},{4,0},{8,12},{12,8},{16,20},{20,16},{24,28},{28,24},{1,5},{5... | collective-permute-start | bytes 1572872 | tf_op jit(solution)/shard_map/ppermute | solution.py:230
  4.6 2.1 %collective-permute-start.7 = (bf16[128,512]{1,0:T(8,128)(2,1)S(1)}, bf16[128,512]{1,0:T(8,128)(2,1)S(1)}, u32[]{:S(2)}, u32[]{:S(2)}) collective-permute-start(bf16[128,512]{1,0:T(8,128)(2,1)S(1)} %maximum_maximum_fusion.own_ref), channel_id=1, source_target_pairs={{0,8},{8,16},{16,24},{24,28},{28,20},{20,12},{12,4},{1,9},{9,17},{... | collective-permute-start | bytes 393224 | tf_op jit(solution)/shard_map/ppermute | solution.py:223
  6.7 1.3 %collective-permute-start.6 = (bf16[128,512]{1,0:T(8,128)(2,1)S(1)}, bf16[128,512]{1,0:T(8,128)(2,1)S(1)}, u32[]{:S(2)}, u32[]{:S(2)}) collective-permute-start(bf16[128,512]{1,0:T(8,128)(2,1)S(1)} %maximum_maximum_fusion.own_ref), channel_id=1, source_target_pairs={{0,16},{8,24},{16,28},{24,20},{28,12},{20,4},{1,17},{9,25},{17,29}... | collective-permute-start | bytes 393224 | tf_op jit(solution)/shard_map/ppermute | solution.py:223
  8.0 0.1 pad_add_fusion.place_ref
  8.1 0.0 copy-start.1
  8.1 0.0 copy-start.2
  8.1 0.0 collective-permute-done.3.q_ref
  8.1 0.0 collective-permute-done.4.do_ref
  8.1 0.0 collective-permute-done.5.o_ref
  8.1 1.0 %rows.2 = (bf16[2,512,128]{2,1,0:T(8,128)(2,1)S(1)}, bf16[2,512,128]{2,1,0:T(8,128)(2,1)S(1)}, f32[2,128,512]{2,1,0:T(8,128)S(1)}, f32[2,128,512]{2,1,0:T(8,128)S(1)}, f32[2,8,512]{2,1,0:T(8,128)S(1)}) custom-call(s32[2]{0:T(128)S(1)} %pad_add_fusion.place_ref, s32[2,64]{1,0:T(2,128)S(1)} %collective-permute-done.2.starts_ref.starts_in_ref, ...), custom_call_target="tpu_custom_call" | custom-call | flops 33554432 | bytes 4194304 | tf_op jit(solution)/shard_map/rows/pallas_call | solution.py:250
  9.1 0.0 copy-done.1
  9.1 0.1 copy-done.2
  9.3 1.0 %rows.3 = (bf16[2,512,128]{2,1,0:T(8,128)(2,1)S(1)}, bf16[2,512,128]{2,1,0:T(8,128)(2,1)S(1)}, f32[2,64,512]{2,1,0:T(8,128)S(1)}, f32[2,64,512]{2,1,0:T(8,128)S(1)}, f32[2,8,512]{2,1,0:T(8,128)S(1)}) custom-call(s32[2]{0:T(128)S(1)} %pad_add_fusion.place_ref, s32[2,64]{1,0:T(2,128)S(1)} %bitcast.27, bf16[128,512]{1,0:T(8,128)(2,1)S(1)} %maximum_maximum_fusion.own_ref, ...), custom_call_target="tpu_custom_call" | custom-call | flops 33554432 | bytes 4194304 | tf_op jit(solution)/shard_map/rows/pallas_call | solution.py:250
  10.3 0.3 %collective-permute-done.7.near_ref = bf16[128,512]{1,0:T(8,128)(2,1)S(1)} collective-permute-done((bf16[128,512]{1,0:T(8,128)(2,1)S(1)}, bf16[128,512]{1,0:T(8,128)(2,1)S(1)}, u32[]{:S(2)}, u32[]{:S(2)}) %collective-permute-start.7) | collective-permute-done | bytes 131104 | tf_op jit(solution)/shard_map/ppermute | solution.py:223
  10.6 3.4 %collective-permute-done.6.far_ref = bf16[128,512]{1,0:T(8,128)(2,1)S(1)} collective-permute-done((bf16[128,512]{1,0:T(8,128)(2,1)S(1)}, bf16[128,512]{1,0:T(8,128)(2,1)S(1)}, u32[]{:S(2)}, u32[]{:S(2)}) %collective-permute-start.6) | collective-permute-done | bytes 131104 | tf_op jit(solution)/shard_map/ppermute | solution.py:223
  14.0 2.4 %scores.1 = (bf16[128,512]{1,0:T(8,128)(2,1)S(1)}, bf16[128,512]{1,0:T(8,128)(2,1)S(1)}, bf16[2,2,256,512]{3,2,1,0:T(8,128)(2,1)S(1)}, f32[2,2,8,512]{3,2,1,0:T(8,128)S(1)}) custom-call(s32[2]{0:T(128)S(1)} %pad_add_fusion.place_ref, s32[2,64]{1,0:T(2,128)S(1)} %bitcast.28, bf16[2,512,128]{2,1,0:T(8,128)(2,1)S(1)} %get-tuple-element.44.q_ref, ...), custom_call_target="tpu_custom_call" | custom-call | flops 402653184 | bytes 12582912 | tf_op jit(solution)/shard_map/scores/pallas_call | solution.py:273
  16.5 2.8 %collective-permute-start.9 = (bf16[128,512]{1,0:T(8,128)(2,1)S(1)}, bf16[128,512]{1,0:T(8,128)(2,1)S(1)}, u32[]{:S(2)}, u32[]{:S(2)}) collective-permute-start(bf16[128,512]{1,0:T(8,128)(2,1)S(1)} %get-tuple-element.57), channel_id=1, source_target_pairs={{8,0},{16,8},{24,16},{28,24},{20,28},{12,20},{4,12},{9,1},{17,9},{... | collective-permute-start | bytes 393224 | tf_op jit(solution)/shard_map/ppermute | solution.py:223
  19.3 5.5 %collective-permute-start.10 = (bf16[128,512]{1,0:T(8,128)(2,1)S(1)}, bf16[128,512]{1,0:T(8,128)(2,1)S(1)}, u32[]{:S(2)}, u32[]{:S(2)}) collective-permute-start(bf16[128,512]{1,0:T(8,128)(2,1)S(1)} %get-tuple-element.58), channel_id=1, source_target_pairs={{16,0},{24,8},{28,16},{20,24},{12,28},{4,20},{17,1},{25,9},{29,17}... | collective-permute-start | bytes 393224 | tf_op jit(solution)/shard_map/ppermute | solution.py:223
  24.8 2.0 %rest.1 = (bf16[2,64,2048]{2,1,0:T(8,128)(2,1)}, bf16[64,2048]{1,0:T(8,128)(2,1)S(1)}, f32[128,512]{1,0:T(8,128)S(1)}) custom-call(s32[2]{0:T(128)S(1)} %pad_add_fusion.place_ref, bf16[2,512,128]{2,1,0:T(8,128)(2,1)S(1)} %get-tuple-element.44.q_ref, bf16[2,512,128]{2,1,0:T(8,128)(2,1)S(1)} %get-tuple-element.45.do_ref, ...), custom_call_target="tpu_custom_call" | custom-call | flops 201326592 | bytes 8388608 | tf_op jit(solution)/shard_map/rest/pallas_call | solution.py:293
  26.8 0.1 collective-permute-start.8
  26.9 0.0 collective-permute-done.9
  26.9 0.5 %collective-permute-done.10 = bf16[128,512]{1,0:T(8,128)(2,1)S(1)} collective-permute-done((bf16[128,512]{1,0:T(8,128)(2,1)S(1)}, bf16[128,512]{1,0:T(8,128)(2,1)S(1)}, u32[]{:S(2)}, u32[]{:S(2)}) %collective-permute-start.10) | collective-permute-done | bytes 131104 | tf_op jit(solution)/shard_map/ppermute | solution.py:223
  27.5 0.1 add_convert_fusion
  27.5 1.8 %collective-permute-start.11 = (bf16[64,512]{1,0:T(8,128)(2,1)S(1)}, bf16[64,512]{1,0:T(8,128)(2,1)S(1)}, u32[]{:S(2)}, u32[]{:S(2)}) collective-permute-start(bf16[64,512]{1,0:T(8,128)(2,1)S(1)} %get-tuple-element.63), channel_id=1, source_target_pairs={{0,4},{4,0},{8,12},{12,8},{16,20},{20,16},{24,28},{28,24},{1,5},{5... | collective-permute-start | bytes 196616 | tf_op jit(solution)/shard_map/ppermute | solution.py:230
  29.4 0.9 %collective-permute-done.11.given_ref = bf16[64,512]{1,0:T(8,128)(2,1)S(1)} collective-permute-done((bf16[64,512]{1,0:T(8,128)(2,1)S(1)}, bf16[64,512]{1,0:T(8,128)(2,1)S(1)}, u32[]{:S(2)}, u32[]{:S(2)}) %collective-permute-start.11) | collective-permute-done | bytes 65568 | tf_op jit(solution)/shard_map/ppermute | solution.py:230
  30.3 0.0 collective-permute-done.8.rows_ref
  30.3 0.8 %store.1 = (bf16[2,64,2048]{2,1,0:T(8,128)(2,1)}, bf16[2,64,256]{2,1,0:T(8,128)(2,1)}, bf16[2,64,256]{2,1,0:T(8,128)(2,1)}) custom-call(s32[1]{0:T(128)} %bitcast.core_ref, bf16[64,2048]{1,0:T(8,128)(2,1)S(1)} %collective-permute-done.8.rows_ref, bf16[64,512]{1,0:T(8,128)(2,1)S(1)} %get-tuple-element.64.kept_ref, ...), custom_call_target="tpu_custom_call", output_to_operand_aliasing={{0}: (4, {})} | custom-call | tf_op jit(solution)/shard_map/store/pallas_call | solution.py:316
  (4 shorter events, 0.0 us)
Async XLA Ops:
  0.6 0.7 %copy-start.3 = (s32[1,2,64]{2,1,0:T(2,128)S(1)}, s32[1,2,64]{2,1,0:T(2,128)}, u32[]{:S(2)}) copy-start(s32[1,2,64]{2,1,0:T(2,128)} %param.11) | copy-start | bytes 1540
  0.6 3.0 %copy-start = (bf16[1,2,64,2048]{3,2,1,0:T(8,128)(2,1)S(1)}, bf16[1,2,64,2048]{3,2,1,0:T(8,128)(2,1)}, u32[]{:S(2)}) copy-start(bf16[1,2,64,2048]{3,2,1,0:T(8,128)(2,1)} %param.6) | copy-start | bytes 1572868
  1.3 2.3 %collective-permute-start.2 = (s32[2,64]{1,0:T(2,128)S(1)}, s32[2,64]{1,0:T(2,128)S(1)}, u32[]{:S(2)}, u32[]{:S(2)}) collective-permute-start(s32[2,64]{1,0:T(2,128)S(1)} %bitcast.26), channel_id=1, source_target_pairs={{0,4},{4,0},{8,12},{12,8},{16,20},{20,16},{24,28},{28,24},{1,5},{5... | collective-permute-start | bytes 1544 | tf_op jit(solution)/shard_map/ppermute | solution.py:230
  2.0 1.5 %collective-permute-start.1 = (bf16[2,64,256]{2,1,0:T(8,128)(2,1)}, bf16[2,64,256]{2,1,0:T(8,128)(2,1)S(1)}, u32[]{:S(2)}, u32[]{:S(2)}) collective-permute-start(bf16[2,64,256]{2,1,0:T(8,128)(2,1)} %bitcast.30), channel_id=1, source_target_pairs={{0,4},{4,0},{8,12},{12,8},{16,20},{20,16},{24,28},{28,24},{1,5},{5... | collective-permute-start | bytes 196616 | tf_op jit(solution)/shard_map/ppermute | solution.py:230
  2.0 1.6 %collective-permute-start = (bf16[2,64,256]{2,1,0:T(8,128)(2,1)}, bf16[2,64,256]{2,1,0:T(8,128)(2,1)S(1)}, u32[]{:S(2)}, u32[]{:S(2)}) collective-permute-start(bf16[2,64,256]{2,1,0:T(8,128)(2,1)} %bitcast.31), channel_id=1, source_target_pairs={{0,4},{4,0},{8,12},{12,8},{16,20},{20,16},{24,28},{28,24},{1,5},{5... | collective-permute-start | bytes 196616 | tf_op jit(solution)/shard_map/ppermute | solution.py:230
  3.7 4.4 %collective-permute-start.3 = (bf16[2,64,2048]{2,1,0:T(8,128)(2,1)S(1)}, bf16[2,64,2048]{2,1,0:T(8,128)(2,1)S(1)}, u32[]{:S(2)}, u32[]{:S(2)}) collective-permute-start(bf16[2,64,2048]{2,1,0:T(8,128)(2,1)S(1)} %bitcast.20), channel_id=1, source_target_pairs={{0,4},{4,0},{8,12},{12,8},{16,20},{20,16},{24,28},{28,24},{1,5},{5... | collective-permute-start | bytes 1572872 | tf_op jit(solution)/shard_map/ppermute | solution.py:230
  4.1 4.0 %collective-permute-start.4 = (bf16[2,64,2048]{2,1,0:T(8,128)(2,1)}, bf16[2,64,2048]{2,1,0:T(8,128)(2,1)S(1)}, u32[]{:S(2)}, u32[]{:S(2)}) collective-permute-start(bf16[2,64,2048]{2,1,0:T(8,128)(2,1)} %bitcast.22), channel_id=1, source_target_pairs={{0,4},{4,0},{8,12},{12,8},{16,20},{20,16},{24,28},{28,24},{1,5},{5... | collective-permute-start | bytes 1572872 | tf_op jit(solution)/shard_map/ppermute | solution.py:230
  4.2 3.8 %collective-permute-start.5 = (bf16[2,64,2048]{2,1,0:T(8,128)(2,1)}, bf16[2,64,2048]{2,1,0:T(8,128)(2,1)S(1)}, u32[]{:S(2)}, u32[]{:S(2)}) collective-permute-start(bf16[2,64,2048]{2,1,0:T(8,128)(2,1)} %bitcast.24), channel_id=1, source_target_pairs={{0,4},{4,0},{8,12},{12,8},{16,20},{20,16},{24,28},{28,24},{1,5},{5... | collective-permute-start | bytes 1572872 | tf_op jit(solution)/shard_map/ppermute | solution.py:230
  4.6 6.0 %collective-permute-start.7 = (bf16[128,512]{1,0:T(8,128)(2,1)S(1)}, bf16[128,512]{1,0:T(8,128)(2,1)S(1)}, u32[]{:S(2)}, u32[]{:S(2)}) collective-permute-start(bf16[128,512]{1,0:T(8,128)(2,1)S(1)} %maximum_maximum_fusion.own_ref), channel_id=1, source_target_pairs={{0,8},{8,16},{16,24},{24,28},{28,20},{20,12},{12,4},{1,9},{9,17},{... | collective-permute-start | bytes 393224 | tf_op jit(solution)/shard_map/ppermute | solution.py:223
  6.7 7.4 %collective-permute-start.6 = (bf16[128,512]{1,0:T(8,128)(2,1)S(1)}, bf16[128,512]{1,0:T(8,128)(2,1)S(1)}, u32[]{:S(2)}, u32[]{:S(2)}) collective-permute-start(bf16[128,512]{1,0:T(8,128)(2,1)S(1)} %maximum_maximum_fusion.own_ref), channel_id=1, source_target_pairs={{0,16},{8,24},{16,28},{24,20},{28,12},{20,4},{1,17},{9,25},{17,29}... | collective-permute-start | bytes 393224 | tf_op jit(solution)/shard_map/ppermute | solution.py:223
  8.1 1.1 %copy-start.1 = (bf16[1,2,64,2048]{3,2,1,0:T(8,128)(2,1)S(1)}, bf16[1,2,64,2048]{3,2,1,0:T(8,128)(2,1)}, u32[]{:S(2)}) copy-start(bf16[1,2,64,2048]{3,2,1,0:T(8,128)(2,1)} %param.9) | copy-start | bytes 1572868
  8.1 1.2 %copy-start.2 = (bf16[1,2,64,2048]{3,2,1,0:T(8,128)(2,1)S(1)}, bf16[1,2,64,2048]{3,2,1,0:T(8,128)(2,1)}, u32[]{:S(2)}) copy-start(bf16[1,2,64,2048]{3,2,1,0:T(8,128)(2,1)} %param.10) | copy-start | bytes 1572868
  16.5 10.4 %collective-permute-start.9 = (bf16[128,512]{1,0:T(8,128)(2,1)S(1)}, bf16[128,512]{1,0:T(8,128)(2,1)S(1)}, u32[]{:S(2)}, u32[]{:S(2)}) collective-permute-start(bf16[128,512]{1,0:T(8,128)(2,1)S(1)} %get-tuple-element.57), channel_id=1, source_target_pairs={{8,0},{16,8},{24,16},{28,24},{20,28},{12,20},{4,12},{9,1},{17,9},{... | collective-permute-start | bytes 393224 | tf_op jit(solution)/shard_map/ppermute | solution.py:223
  19.3 8.1 %collective-permute-start.10 = (bf16[128,512]{1,0:T(8,128)(2,1)S(1)}, bf16[128,512]{1,0:T(8,128)(2,1)S(1)}, u32[]{:S(2)}, u32[]{:S(2)}) collective-permute-start(bf16[128,512]{1,0:T(8,128)(2,1)S(1)} %get-tuple-element.58), channel_id=1, source_target_pairs={{16,0},{24,8},{28,16},{20,24},{12,28},{4,20},{17,1},{25,9},{29,17}... | collective-permute-start | bytes 393224 | tf_op jit(solution)/shard_map/ppermute | solution.py:223
  26.8 3.5 %collective-permute-start.8 = (bf16[64,2048]{1,0:T(8,128)(2,1)S(1)}, bf16[64,2048]{1,0:T(8,128)(2,1)S(1)}, u32[]{:S(2)}, u32[]{:S(2)}) collective-permute-start(bf16[64,2048]{1,0:T(8,128)(2,1)S(1)} %get-tuple-element.55), channel_id=1, source_target_pairs={{0,4},{4,0},{8,12},{12,8},{16,20},{20,16},{24,28},{28,24},{1,5},{5... | collective-permute-start | bytes 786440 | tf_op jit(solution)/shard_map/ppermute | solution.py:230
  27.5 2.7 %collective-permute-start.11 = (bf16[64,512]{1,0:T(8,128)(2,1)S(1)}, bf16[64,512]{1,0:T(8,128)(2,1)S(1)}, u32[]{:S(2)}, u32[]{:S(2)}) collective-permute-start(bf16[64,512]{1,0:T(8,128)(2,1)S(1)} %get-tuple-element.63), channel_id=1, source_target_pairs={{0,4},{4,0},{8,12},{12,8},{16,20},{20,16},{24,28},{28,24},{1,5},{5... | collective-permute-start | bytes 196616 | tf_op jit(solution)/shard_map/ppermute | solution.py:230

commit v12 on v11

--- a/solution.py
+++ b/solution.py
@@ -232,14 +232,14 @@
     def mine(x):
         return jnp.where(core == 0, x[0], x[1])
 
-    starts_in, key_in, value_in = (swapped(x[0]) for x in (doc_start, key, value))
-    sides = ((key[0], value[0]), (key_in, value_in))
-    own = jnp.concatenate(
-        [jnp.concatenate([mine(x) for x in side], axis=-1) for side in sides], axis=0
-    )
-    own, starts_in, starts, *late = lax.optimization_barrier(
-        (own, starts_in, doc_start[0], query[0], out_grad[0], attn_out[0])
-    )
+    key_in, value_in = swapped(key[0]), swapped(value[0])
+    keep, starts = lax.optimization_barrier(
+        (jnp.concatenate([mine(key[0]), mine(value[0])], axis=-1), doc_start[0])
+    )
+    starts_in = swapped(starts)
+    given = jnp.concatenate([mine(key_in), mine(value_in)], axis=-1)
+    own = jnp.concatenate([keep, given], axis=0)
+    own, *late = lax.optimization_barrier((own, query[0], out_grad[0], attn_out[0]))
     kv_heads = kv_width // HEAD_SIZE
     lanes = tokens * (width // kv_width)
     products = 2 * slots * tokens * pair * width

time: 31.4 us -> 30.7 us (0.978)
  local copies, waits for them, and re-layouts: 0.81 us -> 0.16 us
    unnamed x8 -> x10, local copies, waits for them, and re-layouts: 0.8 us -> 0.15 us
    select_n x3 -> x4, other arithmetic: 0.83 us -> 0.8 us  [mine(): return jnp.where(core == 0, x[0], x[1])]
where the time goes in v12:
time: 30.7 us; the launch traced here: 30.5 us
  starting transfers between devices  15.5 us (50%)
  Pallas kernels  7.25 us (24%)
  waiting for transfers between devices  5.8 us (19%)
  other arithmetic  0.95 us (3%)
  between operations  0.82 us (3%)
    ppermute x4, starting transfers between devices, shift(): return lax.ppermute(x, 'ctx', moves)  11.7 us
    ppermute x4, waiting for transfers between devices, shift(): return lax.ppermute(x, 'ctx', moves)  4.32 us
    ppermute x8, starting transfers between devices, swapped(): return lax.ppermute(x, 'ctx', swap)  3.81 us
    pallas_call x1, Pallas kernels, shards(): pl.pallas_call(scores_kernel, out_shape=(jax.ShapeDtypeStruct((pair, pair...  2.43 us
    pallas_call x2, Pallas kernels, arranged(): pl.pallas_call(functools.partial(rows_kernel, unit), out_shape=(stacked,...  2.03 us
    pallas_call x1, Pallas kernels, shards(): pl.pallas_call(rest_kernel, out_shape=(jax.ShapeDtypeStruct((slots, token...  2.02 us
    ppermute x8, waiting for transfers between devices, swapped(): return lax.ppermute(x, 'ctx', swap)  1.48 us
    select_n x4, other arithmetic, mine(): return jnp.where(core == 0, x[0], x[1])  0.8 us
  transfers between devices with their start and end apart: 12, of which 6 were waited for; matrix products, arithmetic and copies ran while one was open for 3% of the time, Pallas kernels for 13%

profile of v12, /device:TPU:13, one launch (start us, length us, event | category | flops | bytes accessed | tf_op | source)
XLA Modules:
  0.0 30.5 jit_solution(17970292747013091243)
XLA Ops:
  0.6 0.0 copy-start.4
  0.6 0.0 copy-start
  0.7 0.7 %collective-permute-start.1 = (bf16[2,64,256]{2,1,0:T(8,128)(2,1)}, bf16[2,64,256]{2,1,0:T(8,128)(2,1)S(1)}, u32[]{:S(2)}, u32[]{:S(2)}) collective-permute-start(bf16[2,64,256]{2,1,0:T(8,128)(2,1)} %bitcast.30), channel_id=1, source_target_pairs={{0,4},{4,0},{8,12},{12,8},{16,20},{20,16},{24,28},{28,24},{1,5},{5... | collective-permute-start | bytes 196616 | tf_op jit(solution)/shard_map/ppermute | solution.py:230
  1.4 0.1 collective-permute-start
  1.5 0.8 %select_bitcast_fusion.1 = bf16[64,256]{1,0:T(8,128)(2,1)S(1)} fusion(bf16[1,2,64,256]{3,2,1,0:T(8,128)(2,1)} %param.7, pred[]{:T(512)} %bitcast.2), kind=kLoop, calls=%fused_computation.8 | loop fusion | flops 16384 | bytes 98305 | tf_op jit(solution)/shard_map/jit(_where)/select_n | solution.py:233
  2.3 0.0 copy-done.4
  2.3 0.2 collective-permute-done.1
  2.5 0.3 %collective-permute-done = bf16[2,64,256]{2,1,0:T(8,128)(2,1)S(1)} collective-permute-done((bf16[2,64,256]{2,1,0:T(8,128)(2,1)}, bf16[2,64,256]{2,1,0:T(8,128)(2,1)S(1)}, u32[]{:S(2)}, u32[]{:S(2)}) %collective-permute-start) | collective-permute-done | bytes 65568 | tf_op jit(solution)/shard_map/ppermute | solution.py:230
  2.9 0.0 copy-start.3
  2.9 0.0 copy-done
  2.9 0.2 collective-permute-start.3
  3.1 0.4 %collective-permute-start.4 = (bf16[2,64,2048]{2,1,0:T(8,128)(2,1)}, bf16[2,64,2048]{2,1,0:T(8,128)(2,1)S(1)}, u32[]{:S(2)}, u32[]{:S(2)}) collective-permute-start(bf16[2,64,2048]{2,1,0:T(8,128)(2,1)} %bitcast.22), channel_id=1, source_target_pairs={{0,4},{4,0},{8,12},{12,8},{16,20},{20,16},{24,28},{28,24},{1,5},{5... | collective-permute-start | bytes 1572872 | tf_op jit(solution)/shard_map/ppermute | solution.py:230
  3.5 0.2 collective-permute-start.5
  3.6 0.0 copy-done.3
  3.6 0.4 %collective-permute-start.2 = (s32[2,64]{1,0:T(2,128)S(1)}, s32[2,64]{1,0:T(2,128)S(1)}, u32[]{:S(2)}, u32[]{:S(2)}) collective-permute-start(s32[2,64]{1,0:T(2,128)S(1)} %bitcast.26), channel_id=1, source_target_pairs={{0,4},{4,0},{8,12},{12,8},{16,20},{20,16},{24,28},{28,24},{1,5},{5... | collective-permute-start | bytes 1544 | tf_op jit(solution)/shard_map/ppermute | solution.py:230
  4.0 2.1 %collective-permute-start.7 = (bf16[128,512]{1,0:T(8,128)(2,1)S(1)}, bf16[128,512]{1,0:T(8,128)(2,1)S(1)}, u32[]{:S(2)}, u32[]{:S(2)}) collective-permute-start(bf16[128,512]{1,0:T(8,128)(2,1)S(1)} %maximum_maximum_fusion.own_ref), channel_id=1, source_target_pairs={{0,8},{8,16},{16,24},{24,28},{28,20},{20,12},{12,4},{1,9},{9,17},{... | collective-permute-start | bytes 393224 | tf_op jit(solution)/shard_map/ppermute | solution.py:223
  6.1 0.0 collective-permute-done.2.starts_ref.starts_in_ref
  6.1 1.3 %collective-permute-start.6 = (bf16[128,512]{1,0:T(8,128)(2,1)S(1)}, bf16[128,512]{1,0:T(8,128)(2,1)S(1)}, u32[]{:S(2)}, u32[]{:S(2)}) collective-permute-start(bf16[128,512]{1,0:T(8,128)(2,1)S(1)} %maximum_maximum_fusion.own_ref), channel_id=1, source_target_pairs={{0,16},{8,24},{16,28},{24,20},{28,12},{20,4},{1,17},{9,25},{17,29}... | collective-permute-start | bytes 393224 | tf_op jit(solution)/shard_map/ppermute | solution.py:223
  7.4 0.1 pad_add_fusion.place_ref
  7.5 0.0 copy-start.1
  7.5 0.0 copy-start.2
  7.5 0.0 collective-permute-done.3.q_ref
  7.5 0.0 collective-permute-done.4.do_ref
  7.5 0.0 collective-permute-done.5.o_ref
  7.5 1.0 %rows.2 = (bf16[2,512,128]{2,1,0:T(8,128)(2,1)S(1)}, bf16[2,512,128]{2,1,0:T(8,128)(2,1)S(1)}, f32[2,128,512]{2,1,0:T(8,128)S(1)}, f32[2,128,512]{2,1,0:T(8,128)S(1)}, f32[2,8,512]{2,1,0:T(8,128)S(1)}) custom-call(s32[2]{0:T(128)S(1)} %pad_add_fusion.place_ref, s32[2,64]{1,0:T(2,128)S(1)} %collective-permute-done.2.starts_ref.starts_in_ref, ...), custom_call_target="tpu_custom_call" | custom-call | flops 33554432 | bytes 4194304 | tf_op jit(solution)/shard_map/rows/pallas_call | solution.py:250
  8.5 0.0 copy-done.1
  8.5 0.1 copy-done.2
  8.7 1.0 %rows.3 = (bf16[2,512,128]{2,1,0:T(8,128)(2,1)S(1)}, bf16[2,512,128]{2,1,0:T(8,128)(2,1)S(1)}, f32[2,64,512]{2,1,0:T(8,128)S(1)}, f32[2,64,512]{2,1,0:T(8,128)S(1)}, f32[2,8,512]{2,1,0:T(8,128)S(1)}) custom-call(s32[2]{0:T(128)S(1)} %pad_add_fusion.place_ref, s32[2,64]{1,0:T(2,128)S(1)} %bitcast.27, bf16[128,512]{1,0:T(8,128)(2,1)S(1)} %maximum_maximum_fusion.own_ref, ...), custom_call_target="tpu_custom_call" | custom-call | flops 33554432 | bytes 4194304 | tf_op jit(solution)/shard_map/rows/pallas_call | solution.py:250
  9.7 0.3 %collective-permute-done.7.near_ref = bf16[128,512]{1,0:T(8,128)(2,1)S(1)} collective-permute-done((bf16[128,512]{1,0:T(8,128)(2,1)S(1)}, bf16[128,512]{1,0:T(8,128)(2,1)S(1)}, u32[]{:S(2)}, u32[]{:S(2)}) %collective-permute-start.7) | collective-permute-done | bytes 131104 | tf_op jit(solution)/shard_map/ppermute | solution.py:223
  10.0 3.5 %collective-permute-done.6.far_ref = bf16[128,512]{1,0:T(8,128)(2,1)S(1)} collective-permute-done((bf16[128,512]{1,0:T(8,128)(2,1)S(1)}, bf16[128,512]{1,0:T(8,128)(2,1)S(1)}, u32[]{:S(2)}, u32[]{:S(2)}) %collective-permute-start.6) | collective-permute-done | bytes 131104 | tf_op jit(solution)/shard_map/ppermute | solution.py:223
  13.4 2.4 %scores.1 = (bf16[128,512]{1,0:T(8,128)(2,1)S(1)}, bf16[128,512]{1,0:T(8,128)(2,1)S(1)}, bf16[2,2,256,512]{3,2,1,0:T(8,128)(2,1)S(1)}, f32[2,2,8,512]{3,2,1,0:T(8,128)S(1)}) custom-call(s32[2]{0:T(128)S(1)} %pad_add_fusion.place_ref, s32[2,64]{1,0:T(2,128)S(1)} %bitcast.28, bf16[2,512,128]{2,1,0:T(8,128)(2,1)S(1)} %get-tuple-element.44.q_ref, ...), custom_call_target="tpu_custom_call" | custom-call | flops 402653184 | bytes 12582912 | tf_op jit(solution)/shard_map/scores/pallas_call | solution.py:273
  15.9 2.8 %collective-permute-start.9 = (bf16[128,512]{1,0:T(8,128)(2,1)S(1)}, bf16[128,512]{1,0:T(8,128)(2,1)S(1)}, u32[]{:S(2)}, u32[]{:S(2)}) collective-permute-start(bf16[128,512]{1,0:T(8,128)(2,1)S(1)} %get-tuple-element.57), channel_id=1, source_target_pairs={{8,0},{16,8},{24,16},{28,24},{20,28},{12,20},{4,12},{9,1},{17,9},{... | collective-permute-start | bytes 393224 | tf_op jit(solution)/shard_map/ppermute | solution.py:223
  18.7 5.5 %collective-permute-start.10 = (bf16[128,512]{1,0:T(8,128)(2,1)S(1)}, bf16[128,512]{1,0:T(8,128)(2,1)S(1)}, u32[]{:S(2)}, u32[]{:S(2)}) collective-permute-start(bf16[128,512]{1,0:T(8,128)(2,1)S(1)} %get-tuple-element.58), channel_id=1, source_target_pairs={{16,0},{24,8},{28,16},{20,24},{12,28},{4,20},{17,1},{25,9},{29,17}... | collective-permute-start | bytes 393224 | tf_op jit(solution)/shard_map/ppermute | solution.py:223
  24.2 2.0 %rest.1 = (bf16[2,64,2048]{2,1,0:T(8,128)(2,1)}, bf16[64,2048]{1,0:T(8,128)(2,1)S(1)}, f32[128,512]{1,0:T(8,128)S(1)}) custom-call(s32[2]{0:T(128)S(1)} %pad_add_fusion.place_ref, bf16[2,512,128]{2,1,0:T(8,128)(2,1)S(1)} %get-tuple-element.44.q_ref, bf16[2,512,128]{2,1,0:T(8,128)(2,1)S(1)} %get-tuple-element.45.do_ref, ...), custom_call_target="tpu_custom_call" | custom-call | flops 201326592 | bytes 8388608 | tf_op jit(solution)/shard_map/rest/pallas_call | solution.py:293
  26.2 0.1 collective-permute-start.8
  26.3 0.0 collective-permute-done.9
  26.3 0.6 %collective-permute-done.10 = bf16[128,512]{1,0:T(8,128)(2,1)S(1)} collective-permute-done((bf16[128,512]{1,0:T(8,128)(2,1)S(1)}, bf16[128,512]{1,0:T(8,128)(2,1)S(1)}, u32[]{:S(2)}, u32[]{:S(2)}) %collective-permute-start.10) | collective-permute-done | bytes 131104 | tf_op jit(solution)/shard_map/ppermute | solution.py:223
  26.9 0.1 add_convert_fusion
  26.9 1.8 %collective-permute-start.11 = (bf16[64,512]{1,0:T(8,128)(2,1)S(1)}, bf16[64,512]{1,0:T(8,128)(2,1)S(1)}, u32[]{:S(2)}, u32[]{:S(2)}) collective-permute-start(bf16[64,512]{1,0:T(8,128)(2,1)S(1)} %get-tuple-element.63), channel_id=1, source_target_pairs={{0,4},{4,0},{8,12},{12,8},{16,20},{20,16},{24,28},{28,24},{1,5},{5... | collective-permute-start | bytes 196616 | tf_op jit(solution)/shard_map/ppermute | solution.py:230
  28.8 0.9 %collective-permute-done.11.given_ref = bf16[64,512]{1,0:T(8,128)(2,1)S(1)} collective-permute-done((bf16[64,512]{1,0:T(8,128)(2,1)S(1)}, bf16[64,512]{1,0:T(8,128)(2,1)S(1)}, u32[]{:S(2)}, u32[]{:S(2)}) %collective-permute-start.11) | collective-permute-done | bytes 65568 | tf_op jit(solution)/shard_map/ppermute | solution.py:230
  29.7 0.0 collective-permute-done.8.rows_ref
  29.7 0.8 %store.1 = (bf16[2,64,2048]{2,1,0:T(8,128)(2,1)}, bf16[2,64,256]{2,1,0:T(8,128)(2,1)}, bf16[2,64,256]{2,1,0:T(8,128)(2,1)}) custom-call(s32[1]{0:T(128)} %bitcast.core_ref, bf16[64,2048]{1,0:T(8,128)(2,1)S(1)} %collective-permute-done.8.rows_ref, bf16[64,512]{1,0:T(8,128)(2,1)S(1)} %get-tuple-element.64.kept_ref, ...), custom_call_target="tpu_custom_call", output_to_operand_aliasing={{0}: (4, {})} | custom-call | tf_op jit(solution)/shard_map/store/pallas_call | solution.py:316
  (6 shorter events, 0.1 us)
Async XLA Ops:
  0.6 1.6 %copy-start.4 = (bf16[1,2,64,256]{3,2,1,0:T(8,128)(2,1)S(1)}, bf16[1,2,64,256]{3,2,1,0:T(8,128)(2,1)}, u32[]{:S(2)}) copy-start(bf16[1,2,64,256]{3,2,1,0:T(8,128)(2,1)} %param.8) | copy-start | bytes 196612
  0.6 2.3 %copy-start = (bf16[1,2,64,2048]{3,2,1,0:T(8,128)(2,1)S(1)}, bf16[1,2,64,2048]{3,2,1,0:T(8,128)(2,1)}, u32[]{:S(2)}) copy-start(bf16[1,2,64,2048]{3,2,1,0:T(8,128)(2,1)} %param.6) | copy-start | bytes 1572868
  0.7 1.9 %collective-permute-start.1 = (bf16[2,64,256]{2,1,0:T(8,128)(2,1)}, bf16[2,64,256]{2,1,0:T(8,128)(2,1)S(1)}, u32[]{:S(2)}, u32[]{:S(2)}) collective-permute-start(bf16[2,64,256]{2,1,0:T(8,128)(2,1)} %bitcast.30), channel_id=1, source_target_pairs={{0,4},{4,0},{8,12},{12,8},{16,20},{20,16},{24,28},{28,24},{1,5},{5... | collective-permute-start | bytes 196616 | tf_op jit(solution)/shard_map/ppermute | solution.py:230
  1.4 1.5 %collective-permute-start = (bf16[2,64,256]{2,1,0:T(8,128)(2,1)}, bf16[2,64,256]{2,1,0:T(8,128)(2,1)S(1)}, u32[]{:S(2)}, u32[]{:S(2)}) collective-permute-start(bf16[2,64,256]{2,1,0:T(8,128)(2,1)} %bitcast.31), channel_id=1, source_target_pairs={{0,4},{4,0},{8,12},{12,8},{16,20},{20,16},{24,28},{28,24},{1,5},{5... | collective-permute-start | bytes 196616 | tf_op jit(solution)/shard_map/ppermute | solution.py:230
  2.9 0.8 %copy-start.3 = (s32[1,2,64]{2,1,0:T(2,128)S(1)}, s32[1,2,64]{2,1,0:T(2,128)}, u32[]{:S(2)}) copy-start(s32[1,2,64]{2,1,0:T(2,128)} %param.11) | copy-start | bytes 1540
  2.9 4.6 %collective-permute-start.3 = (bf16[2,64,2048]{2,1,0:T(8,128)(2,1)S(1)}, bf16[2,64,2048]{2,1,0:T(8,128)(2,1)S(1)}, u32[]{:S(2)}, u32[]{:S(2)}) collective-permute-start(bf16[2,64,2048]{2,1,0:T(8,128)(2,1)S(1)} %bitcast.20), channel_id=1, source_target_pairs={{0,4},{4,0},{8,12},{12,8},{16,20},{20,16},{24,28},{28,24},{1,5},{5... | collective-permute-start | bytes 1572872 | tf_op jit(solution)/shard_map/ppermute | solution.py:230
  3.1 4.4 %collective-permute-start.4 = (bf16[2,64,2048]{2,1,0:T(8,128)(2,1)}, bf16[2,64,2048]{2,1,0:T(8,128)(2,1)S(1)}, u32[]{:S(2)}, u32[]{:S(2)}) collective-permute-start(bf16[2,64,2048]{2,1,0:T(8,128)(2,1)} %bitcast.22), channel_id=1, source_target_pairs={{0,4},{4,0},{8,12},{12,8},{16,20},{20,16},{24,28},{28,24},{1,5},{5... | collective-permute-start | bytes 1572872 | tf_op jit(solution)/shard_map/ppermute | solution.py:230
  3.5 4.0 %collective-permute-start.5 = (bf16[2,64,2048]{2,1,0:T(8,128)(2,1)}, bf16[2,64,2048]{2,1,0:T(8,128)(2,1)S(1)}, u32[]{:S(2)}, u32[]{:S(2)}) collective-permute-start(bf16[2,64,2048]{2,1,0:T(8,128)(2,1)} %bitcast.24), channel_id=1, source_target_pairs={{0,4},{4,0},{8,12},{12,8},{16,20},{20,16},{24,28},{28,24},{1,5},{5... | collective-permute-start | bytes 1572872 | tf_op jit(solution)/shard_map/ppermute | solution.py:230
  3.6 2.4 %collective-permute-start.2 = (s32[2,64]{1,0:T(2,128)S(1)}, s32[2,64]{1,0:T(2,128)S(1)}, u32[]{:S(2)}, u32[]{:S(2)}) collective-permute-start(s32[2,64]{1,0:T(2,128)S(1)} %bitcast.26), channel_id=1, source_target_pairs={{0,4},{4,0},{8,12},{12,8},{16,20},{20,16},{24,28},{28,24},{1,5},{5... | collective-permute-start | bytes 1544 | tf_op jit(solution)/shard_map/ppermute | solution.py:230
  4.0 6.0 %collective-permute-start.7 = (bf16[128,512]{1,0:T(8,128)(2,1)S(1)}, bf16[128,512]{1,0:T(8,128)(2,1)S(1)}, u32[]{:S(2)}, u32[]{:S(2)}) collective-permute-start(bf16[128,512]{1,0:T(8,128)(2,1)S(1)} %maximum_maximum_fusion.own_ref), channel_id=1, source_target_pairs={{0,8},{8,16},{16,24},{24,28},{28,20},{20,12},{12,4},{1,9},{9,17},{... | collective-permute-start | bytes 393224 | tf_op jit(solution)/shard_map/ppermute | solution.py:223
  6.1 7.4 %collective-permute-start.6 = (bf16[128,512]{1,0:T(8,128)(2,1)S(1)}, bf16[128,512]{1,0:T(8,128)(2,1)S(1)}, u32[]{:S(2)}, u32[]{:S(2)}) collective-permute-start(bf16[128,512]{1,0:T(8,128)(2,1)S(1)} %maximum_maximum_fusion.own_ref), channel_id=1, source_target_pairs={{0,16},{8,24},{16,28},{24,20},{28,12},{20,4},{1,17},{9,25},{17,29}... | collective-permute-start | bytes 393224 | tf_op jit(solution)/shard_map/ppermute | solution.py:223
  7.5 1.1 %copy-start.1 = (bf16[1,2,64,2048]{3,2,1,0:T(8,128)(2,1)S(1)}, bf16[1,2,64,2048]{3,2,1,0:T(8,128)(2,1)}, u32[]{:S(2)}) copy-start(bf16[1,2,64,2048]{3,2,1,0:T(8,128)(2,1)} %param.9) | copy-start | bytes 1572868
  7.5 1.2 %copy-start.2 = (bf16[1,2,64,2048]{3,2,1,0:T(8,128)(2,1)S(1)}, bf16[1,2,64,2048]{3,2,1,0:T(8,128)(2,1)}, u32[]{:S(2)}) copy-start(bf16[1,2,64,2048]{3,2,1,0:T(8,128)(2,1)} %param.10) | copy-start | bytes 1572868
  15.9 10.4 %collective-permute-start.9 = (bf16[128,512]{1,0:T(8,128)(2,1)S(1)}, bf16[128,512]{1,0:T(8,128)(2,1)S(1)}, u32[]{:S(2)}, u32[]{:S(2)}) collective-permute-start(bf16[128,512]{1,0:T(8,128)(2,1)S(1)} %get-tuple-element.57), channel_id=1, source_target_pairs={{8,0},{16,8},{24,16},{28,24},{20,28},{12,20},{4,12},{9,1},{17,9},{... | collective-permute-start | bytes 393224 | tf_op jit(solution)/shard_map/ppermute | solution.py:223
  18.7 8.1 %collective-permute-start.10 = (bf16[128,512]{1,0:T(8,128)(2,1)S(1)}, bf16[128,512]{1,0:T(8,128)(2,1)S(1)}, u32[]{:S(2)}, u32[]{:S(2)}) collective-permute-start(bf16[128,512]{1,0:T(8,128)(2,1)S(1)} %get-tuple-element.58), channel_id=1, source_target_pairs={{16,0},{24,8},{28,16},{20,24},{12,28},{4,20},{17,1},{25,9},{29,17}... | collective-permute-start | bytes 393224 | tf_op jit(solution)/shard_map/ppermute | solution.py:223
  26.2 3.5 %collective-permute-start.8 = (bf16[64,2048]{1,0:T(8,128)(2,1)S(1)}, bf16[64,2048]{1,0:T(8,128)(2,1)S(1)}, u32[]{:S(2)}, u32[]{:S(2)}) collective-permute-start(bf16[64,2048]{1,0:T(8,128)(2,1)S(1)} %get-tuple-element.55), channel_id=1, source_target_pairs={{0,4},{4,0},{8,12},{12,8},{16,20},{20,16},{24,28},{28,24},{1,5},{5... | collective-permute-start | bytes 786440 | tf_op jit(solution)/shard_map/ppermute | solution.py:230
  26.9 2.7 %collective-permute-start.11 = (bf16[64,512]{1,0:T(8,128)(2,1)S(1)}, bf16[64,512]{1,0:T(8,128)(2,1)S(1)}, u32[]{:S(2)}, u32[]{:S(2)}) collective-permute-start(bf16[64,512]{1,0:T(8,128)(2,1)S(1)} %get-tuple-element.63), channel_id=1, source_target_pairs={{0,4},{4,0},{8,12},{12,8},{16,20},{20,16},{24,28},{28,24},{1,5},{5... | collective-permute-start | bytes 196616 | tf_op jit(solution)/shard_map/ppermute | solution.py:230

commit v13 on v12

--- a/solution.py
+++ b/solution.py
@@ -100,11 +100,11 @@
         return scores, dot(values, do_side[g], CONTRACT_LAST)
 
     order = [(unit, g) for unit in range(2) for g in range(kv_heads)]
-    ahead = products(*order[0])
+    ahead = [products(*item) for item in order[:2]]
     for step, (unit, g) in enumerate(order):
-        scores, dprobs = ahead
-        if step + 1 < len(order):
-            ahead = products(*order[step + 1])
+        scores, dprobs = ahead.pop(0)
+        if step + 2 < len(order):
+            ahead.append(products(*order[step + 2]))
         _, q_side, do_side, held_side, delta_side = sides[unit]
         first = unit * tokens
         before = 2 * pair - first
@@ -122,7 +122,7 @@
         dscores = (probs * (dprobs - delta_side[g, :1])).astype(jnp.bfloat16)
         dscores_ref[unit, g, :before] = dscores
         for part, column in (
-            (dot(dscores, q_side[g]) * scale, g * HEAD_SIZE),
+            (dot(dscores, q_side[g]), g * HEAD_SIZE),
             (dot(probs.astype(jnp.bfloat16), do_side[g]), kv_width + g * HEAD_SIZE),
         ):
             columns = slice(column, column + HEAD_SIZE)
@@ -130,6 +130,7 @@
                 part_ref[:, columns] = part
             else:
                 part_ref[first:, columns] += part
+    part_ref[:, :kv_width] *= scale
     far_part_ref[...] = part_ref[:pair, :].astype(jnp.bfloat16)
     near_part_ref[...] = part_ref[pair:, :].astype(jnp.bfloat16)
 

time: 30.7 us -> 30.7 us (level)
  no operation moved by 1% of the time
where the time goes in v13:
time: 30.7 us; the launch traced here: 30.5 us
  starting transfers between devices  15.5 us (50%)
  Pallas kernels  7.26 us (24%)
  waiting for transfers between devices  5.8 us (19%)
  other arithmetic  0.95 us (3%)
  between operations  0.82 us (3%)
    ppermute x4, starting transfers between devices, shift(): return lax.ppermute(x, 'ctx', moves)  11.7 us
    ppermute x4, waiting for transfers between devices, shift(): return lax.ppermute(x, 'ctx', moves)  4.32 us
    ppermute x8, starting transfers between devices, swapped(): return lax.ppermute(x, 'ctx', swap)  3.81 us
    pallas_call x1, Pallas kernels, shards(): pl.pallas_call(scores_kernel, out_shape=(jax.ShapeDtypeStruct((pair, pair...  2.43 us
    pallas_call x2, Pallas kernels, arranged(): pl.pallas_call(functools.partial(rows_kernel, unit), out_shape=(stacked,...  2.03 us
    pallas_call x1, Pallas kernels, shards(): pl.pallas_call(rest_kernel, out_shape=(jax.ShapeDtypeStruct((slots, token...  2.02 us
    ppermute x8, waiting for transfers between devices, swapped(): return lax.ppermute(x, 'ctx', swap)  1.48 us
    select_n x4, other arithmetic, mine(): return jnp.where(core == 0, x[0], x[1])  0.8 us
  transfers between devices with their start and end apart: 12, of which 6 were waited for; matrix products, arithmetic and copies ran while one was open for 3% of the time, Pallas kernels for 13%

profile of v13, /device:TPU:13, one launch (start us, length us, event | category | flops | bytes accessed | tf_op | source)
XLA Modules:
  0.0 30.5 jit_solution(9522537225574449528)
XLA Ops:
  0.6 0.0 copy-start.4
  0.6 0.0 copy-start
  0.7 0.7 %collective-permute-start.1 = (bf16[2,64,256]{2,1,0:T(8,128)(2,1)}, bf16[2,64,256]{2,1,0:T(8,128)(2,1)S(1)}, u32[]{:S(2)}, u32[]{:S(2)}) collective-permute-start(bf16[2,64,256]{2,1,0:T(8,128)(2,1)} %bitcast.30), channel_id=1, source_target_pairs={{0,4},{4,0},{8,12},{12,8},{16,20},{20,16},{24,28},{28,24},{1,5},{5... | collective-permute-start | bytes 196616 | tf_op jit(solution)/shard_map/ppermute | solution.py:231
  1.4 0.1 collective-permute-start
  1.5 0.8 %select_bitcast_fusion.1 = bf16[64,256]{1,0:T(8,128)(2,1)S(1)} fusion(bf16[1,2,64,256]{3,2,1,0:T(8,128)(2,1)} %param.7, pred[]{:T(512)} %bitcast.2), kind=kLoop, calls=%fused_computation.8 | loop fusion | flops 16384 | bytes 98305 | tf_op jit(solution)/shard_map/jit(_where)/select_n | solution.py:234
  2.3 0.0 copy-done.4
  2.3 0.2 collective-permute-done.1
  2.5 0.3 %collective-permute-done = bf16[2,64,256]{2,1,0:T(8,128)(2,1)S(1)} collective-permute-done((bf16[2,64,256]{2,1,0:T(8,128)(2,1)}, bf16[2,64,256]{2,1,0:T(8,128)(2,1)S(1)}, u32[]{:S(2)}, u32[]{:S(2)}) %collective-permute-start) | collective-permute-done | bytes 65568 | tf_op jit(solution)/shard_map/ppermute | solution.py:231
  2.9 0.0 copy-start.3
  2.9 0.0 copy-done
  2.9 0.2 collective-permute-start.3
  3.1 0.4 %collective-permute-start.4 = (bf16[2,64,2048]{2,1,0:T(8,128)(2,1)}, bf16[2,64,2048]{2,1,0:T(8,128)(2,1)S(1)}, u32[]{:S(2)}, u32[]{:S(2)}) collective-permute-start(bf16[2,64,2048]{2,1,0:T(8,128)(2,1)} %bitcast.22), channel_id=1, source_target_pairs={{0,4},{4,0},{8,12},{12,8},{16,20},{20,16},{24,28},{28,24},{1,5},{5... | collective-permute-start | bytes 1572872 | tf_op jit(solution)/shard_map/ppermute | solution.py:231
  3.5 0.2 collective-permute-start.5
  3.6 0.0 copy-done.3
  3.6 0.4 %collective-permute-start.2 = (s32[2,64]{1,0:T(2,128)S(1)}, s32[2,64]{1,0:T(2,128)S(1)}, u32[]{:S(2)}, u32[]{:S(2)}) collective-permute-start(s32[2,64]{1,0:T(2,128)S(1)} %bitcast.26), channel_id=1, source_target_pairs={{0,4},{4,0},{8,12},{12,8},{16,20},{20,16},{24,28},{28,24},{1,5},{5... | collective-permute-start | bytes 1544 | tf_op jit(solution)/shard_map/ppermute | solution.py:231
  4.0 2.1 %collective-permute-start.7 = (bf16[128,512]{1,0:T(8,128)(2,1)S(1)}, bf16[128,512]{1,0:T(8,128)(2,1)S(1)}, u32[]{:S(2)}, u32[]{:S(2)}) collective-permute-start(bf16[128,512]{1,0:T(8,128)(2,1)S(1)} %maximum_maximum_fusion.own_ref), channel_id=1, source_target_pairs={{0,8},{8,16},{16,24},{24,28},{28,20},{20,12},{12,4},{1,9},{9,17},{... | collective-permute-start | bytes 393224 | tf_op jit(solution)/shard_map/ppermute | solution.py:224
  6.1 0.0 collective-permute-done.2.starts_ref.starts_in_ref
  6.1 1.3 %collective-permute-start.6 = (bf16[128,512]{1,0:T(8,128)(2,1)S(1)}, bf16[128,512]{1,0:T(8,128)(2,1)S(1)}, u32[]{:S(2)}, u32[]{:S(2)}) collective-permute-start(bf16[128,512]{1,0:T(8,128)(2,1)S(1)} %maximum_maximum_fusion.own_ref), channel_id=1, source_target_pairs={{0,16},{8,24},{16,28},{24,20},{28,12},{20,4},{1,17},{9,25},{17,29}... | collective-permute-start | bytes 393224 | tf_op jit(solution)/shard_map/ppermute | solution.py:224
  7.4 0.1 pad_add_fusion.place_ref
  7.5 0.0 copy-start.1
  7.5 0.0 copy-start.2
  7.5 0.0 collective-permute-done.3.q_ref
  7.5 0.0 collective-permute-done.4.do_ref
  7.5 0.0 collective-permute-done.5.o_ref
  7.5 1.0 %rows.2 = (bf16[2,512,128]{2,1,0:T(8,128)(2,1)S(1)}, bf16[2,512,128]{2,1,0:T(8,128)(2,1)S(1)}, f32[2,128,512]{2,1,0:T(8,128)S(1)}, f32[2,128,512]{2,1,0:T(8,128)S(1)}, f32[2,8,512]{2,1,0:T(8,128)S(1)}) custom-call(s32[2]{0:T(128)S(1)} %pad_add_fusion.place_ref, s32[2,64]{1,0:T(2,128)S(1)} %collective-permute-done.2.starts_ref.starts_in_ref, ...), custom_call_target="tpu_custom_call" | custom-call | flops 33554432 | bytes 4194304 | tf_op jit(solution)/shard_map/rows/pallas_call | solution.py:251
  8.5 0.0 copy-done.1
  8.5 0.1 copy-done.2
  8.7 1.0 %rows.3 = (bf16[2,512,128]{2,1,0:T(8,128)(2,1)S(1)}, bf16[2,512,128]{2,1,0:T(8,128)(2,1)S(1)}, f32[2,64,512]{2,1,0:T(8,128)S(1)}, f32[2,64,512]{2,1,0:T(8,128)S(1)}, f32[2,8,512]{2,1,0:T(8,128)S(1)}) custom-call(s32[2]{0:T(128)S(1)} %pad_add_fusion.place_ref, s32[2,64]{1,0:T(2,128)S(1)} %bitcast.27, bf16[128,512]{1,0:T(8,128)(2,1)S(1)} %maximum_maximum_fusion.own_ref, ...), custom_call_target="tpu_custom_call" | custom-call | flops 33554432 | bytes 4194304 | tf_op jit(solution)/shard_map/rows/pallas_call | solution.py:251
  9.7 0.3 %collective-permute-done.7.near_ref = bf16[128,512]{1,0:T(8,128)(2,1)S(1)} collective-permute-done((bf16[128,512]{1,0:T(8,128)(2,1)S(1)}, bf16[128,512]{1,0:T(8,128)(2,1)S(1)}, u32[]{:S(2)}, u32[]{:S(2)}) %collective-permute-start.7) | collective-permute-done | bytes 131104 | tf_op jit(solution)/shard_map/ppermute | solution.py:224
  10.0 3.5 %collective-permute-done.6.far_ref = bf16[128,512]{1,0:T(8,128)(2,1)S(1)} collective-permute-done((bf16[128,512]{1,0:T(8,128)(2,1)S(1)}, bf16[128,512]{1,0:T(8,128)(2,1)S(1)}, u32[]{:S(2)}, u32[]{:S(2)}) %collective-permute-start.6) | collective-permute-done | bytes 131104 | tf_op jit(solution)/shard_map/ppermute | solution.py:224
  13.4 2.4 %scores.1 = (bf16[128,512]{1,0:T(8,128)(2,1)S(1)}, bf16[128,512]{1,0:T(8,128)(2,1)S(1)}, bf16[2,2,256,512]{3,2,1,0:T(8,128)(2,1)S(1)}, f32[2,2,8,512]{3,2,1,0:T(8,128)S(1)}) custom-call(s32[2]{0:T(128)S(1)} %pad_add_fusion.place_ref, s32[2,64]{1,0:T(2,128)S(1)} %bitcast.28, bf16[2,512,128]{2,1,0:T(8,128)(2,1)S(1)} %get-tuple-element.44.q_ref, ...), custom_call_target="tpu_custom_call" | custom-call | flops 402653184 | bytes 12582912 | tf_op jit(solution)/shard_map/scores/pallas_call | solution.py:274
  15.9 2.8 %collective-permute-start.9 = (bf16[128,512]{1,0:T(8,128)(2,1)S(1)}, bf16[128,512]{1,0:T(8,128)(2,1)S(1)}, u32[]{:S(2)}, u32[]{:S(2)}) collective-permute-start(bf16[128,512]{1,0:T(8,128)(2,1)S(1)} %get-tuple-element.57), channel_id=1, source_target_pairs={{8,0},{16,8},{24,16},{28,24},{20,28},{12,20},{4,12},{9,1},{17,9},{... | collective-permute-start | bytes 393224 | tf_op jit(solution)/shard_map/ppermute | solution.py:224
  18.7 5.5 %collective-permute-start.10 = (bf16[128,512]{1,0:T(8,128)(2,1)S(1)}, bf16[128,512]{1,0:T(8,128)(2,1)S(1)}, u32[]{:S(2)}, u32[]{:S(2)}) collective-permute-start(bf16[128,512]{1,0:T(8,128)(2,1)S(1)} %get-tuple-element.58), channel_id=1, source_target_pairs={{16,0},{24,8},{28,16},{20,24},{12,28},{4,20},{17,1},{25,9},{29,17}... | collective-permute-start | bytes 393224 | tf_op jit(solution)/shard_map/ppermute | solution.py:224
  24.2 2.0 %rest.1 = (bf16[2,64,2048]{2,1,0:T(8,128)(2,1)}, bf16[64,2048]{1,0:T(8,128)(2,1)S(1)}, f32[128,512]{1,0:T(8,128)S(1)}) custom-call(s32[2]{0:T(128)S(1)} %pad_add_fusion.place_ref, bf16[2,512,128]{2,1,0:T(8,128)(2,1)S(1)} %get-tuple-element.44.q_ref, bf16[2,512,128]{2,1,0:T(8,128)(2,1)S(1)} %get-tuple-element.45.do_ref, ...), custom_call_target="tpu_custom_call" | custom-call | flops 201326592 | bytes 8388608 | tf_op jit(solution)/shard_map/rest/pallas_call | solution.py:294
  26.2 0.1 collective-permute-start.8
  26.3 0.0 collective-permute-done.9
  26.3 0.6 %collective-permute-done.10 = bf16[128,512]{1,0:T(8,128)(2,1)S(1)} collective-permute-done((bf16[128,512]{1,0:T(8,128)(2,1)S(1)}, bf16[128,512]{1,0:T(8,128)(2,1)S(1)}, u32[]{:S(2)}, u32[]{:S(2)}) %collective-permute-start.10) | collective-permute-done | bytes 131104 | tf_op jit(solution)/shard_map/ppermute | solution.py:224
  26.9 0.1 add_convert_fusion
  27.0 1.8 %collective-permute-start.11 = (bf16[64,512]{1,0:T(8,128)(2,1)S(1)}, bf16[64,512]{1,0:T(8,128)(2,1)S(1)}, u32[]{:S(2)}, u32[]{:S(2)}) collective-permute-start(bf16[64,512]{1,0:T(8,128)(2,1)S(1)} %get-tuple-element.63), channel_id=1, source_target_pairs={{0,4},{4,0},{8,12},{12,8},{16,20},{20,16},{24,28},{28,24},{1,5},{5... | collective-permute-start | bytes 196616 | tf_op jit(solution)/shard_map/ppermute | solution.py:231
  28.8 0.9 %collective-permute-done.11.given_ref = bf16[64,512]{1,0:T(8,128)(2,1)S(1)} collective-permute-done((bf16[64,512]{1,0:T(8,128)(2,1)S(1)}, bf16[64,512]{1,0:T(8,128)(2,1)S(1)}, u32[]{:S(2)}, u32[]{:S(2)}) %collective-permute-start.11) | collective-permute-done | bytes 65568 | tf_op jit(solution)/shard_map/ppermute | solution.py:231
  29.7 0.0 collective-permute-done.8.rows_ref
  29.7 0.8 %store.1 = (bf16[2,64,2048]{2,1,0:T(8,128)(2,1)}, bf16[2,64,256]{2,1,0:T(8,128)(2,1)}, bf16[2,64,256]{2,1,0:T(8,128)(2,1)}) custom-call(s32[1]{0:T(128)} %bitcast.core_ref, bf16[64,2048]{1,0:T(8,128)(2,1)S(1)} %collective-permute-done.8.rows_ref, bf16[64,512]{1,0:T(8,128)(2,1)S(1)} %get-tuple-element.64.kept_ref, ...), custom_call_target="tpu_custom_call", output_to_operand_aliasing={{0}: (4, {})} | custom-call | tf_op jit(solution)/shard_map/store/pallas_call | solution.py:317
  (6 shorter events, 0.1 us)
Async XLA Ops:
  0.6 1.6 %copy-start.4 = (bf16[1,2,64,256]{3,2,1,0:T(8,128)(2,1)S(1)}, bf16[1,2,64,256]{3,2,1,0:T(8,128)(2,1)}, u32[]{:S(2)}) copy-start(bf16[1,2,64,256]{3,2,1,0:T(8,128)(2,1)} %param.8) | copy-start | bytes 196612
  0.6 2.3 %copy-start = (bf16[1,2,64,2048]{3,2,1,0:T(8,128)(2,1)S(1)}, bf16[1,2,64,2048]{3,2,1,0:T(8,128)(2,1)}, u32[]{:S(2)}) copy-start(bf16[1,2,64,2048]{3,2,1,0:T(8,128)(2,1)} %param.6) | copy-start | bytes 1572868
  0.7 1.9 %collective-permute-start.1 = (bf16[2,64,256]{2,1,0:T(8,128)(2,1)}, bf16[2,64,256]{2,1,0:T(8,128)(2,1)S(1)}, u32[]{:S(2)}, u32[]{:S(2)}) collective-permute-start(bf16[2,64,256]{2,1,0:T(8,128)(2,1)} %bitcast.30), channel_id=1, source_target_pairs={{0,4},{4,0},{8,12},{12,8},{16,20},{20,16},{24,28},{28,24},{1,5},{5... | collective-permute-start | bytes 196616 | tf_op jit(solution)/shard_map/ppermute | solution.py:231
  1.4 1.5 %collective-permute-start = (bf16[2,64,256]{2,1,0:T(8,128)(2,1)}, bf16[2,64,256]{2,1,0:T(8,128)(2,1)S(1)}, u32[]{:S(2)}, u32[]{:S(2)}) collective-permute-start(bf16[2,64,256]{2,1,0:T(8,128)(2,1)} %bitcast.31), channel_id=1, source_target_pairs={{0,4},{4,0},{8,12},{12,8},{16,20},{20,16},{24,28},{28,24},{1,5},{5... | collective-permute-start | bytes 196616 | tf_op jit(solution)/shard_map/ppermute | solution.py:231
  2.9 0.8 %copy-start.3 = (s32[1,2,64]{2,1,0:T(2,128)S(1)}, s32[1,2,64]{2,1,0:T(2,128)}, u32[]{:S(2)}) copy-start(s32[1,2,64]{2,1,0:T(2,128)} %param.11) | copy-start | bytes 1540
  2.9 4.6 %collective-permute-start.3 = (bf16[2,64,2048]{2,1,0:T(8,128)(2,1)S(1)}, bf16[2,64,2048]{2,1,0:T(8,128)(2,1)S(1)}, u32[]{:S(2)}, u32[]{:S(2)}) collective-permute-start(bf16[2,64,2048]{2,1,0:T(8,128)(2,1)S(1)} %bitcast.20), channel_id=1, source_target_pairs={{0,4},{4,0},{8,12},{12,8},{16,20},{20,16},{24,28},{28,24},{1,5},{5... | collective-permute-start | bytes 1572872 | tf_op jit(solution)/shard_map/ppermute | solution.py:231
  3.1 4.4 %collective-permute-start.4 = (bf16[2,64,2048]{2,1,0:T(8,128)(2,1)}, bf16[2,64,2048]{2,1,0:T(8,128)(2,1)S(1)}, u32[]{:S(2)}, u32[]{:S(2)}) collective-permute-start(bf16[2,64,2048]{2,1,0:T(8,128)(2,1)} %bitcast.22), channel_id=1, source_target_pairs={{0,4},{4,0},{8,12},{12,8},{16,20},{20,16},{24,28},{28,24},{1,5},{5... | collective-permute-start | bytes 1572872 | tf_op jit(solution)/shard_map/ppermute | solution.py:231
  3.5 4.0 %collective-permute-start.5 = (bf16[2,64,2048]{2,1,0:T(8,128)(2,1)}, bf16[2,64,2048]{2,1,0:T(8,128)(2,1)S(1)}, u32[]{:S(2)}, u32[]{:S(2)}) collective-permute-start(bf16[2,64,2048]{2,1,0:T(8,128)(2,1)} %bitcast.24), channel_id=1, source_target_pairs={{0,4},{4,0},{8,12},{12,8},{16,20},{20,16},{24,28},{28,24},{1,5},{5... | collective-permute-start | bytes 1572872 | tf_op jit(solution)/shard_map/ppermute | solution.py:231
  3.6 2.4 %collective-permute-start.2 = (s32[2,64]{1,0:T(2,128)S(1)}, s32[2,64]{1,0:T(2,128)S(1)}, u32[]{:S(2)}, u32[]{:S(2)}) collective-permute-start(s32[2,64]{1,0:T(2,128)S(1)} %bitcast.26), channel_id=1, source_target_pairs={{0,4},{4,0},{8,12},{12,8},{16,20},{20,16},{24,28},{28,24},{1,5},{5... | collective-permute-start | bytes 1544 | tf_op jit(solution)/shard_map/ppermute | solution.py:231
  4.0 6.0 %collective-permute-start.7 = (bf16[128,512]{1,0:T(8,128)(2,1)S(1)}, bf16[128,512]{1,0:T(8,128)(2,1)S(1)}, u32[]{:S(2)}, u32[]{:S(2)}) collective-permute-start(bf16[128,512]{1,0:T(8,128)(2,1)S(1)} %maximum_maximum_fusion.own_ref), channel_id=1, source_target_pairs={{0,8},{8,16},{16,24},{24,28},{28,20},{20,12},{12,4},{1,9},{9,17},{... | collective-permute-start | bytes 393224 | tf_op jit(solution)/shard_map/ppermute | solution.py:224
  6.1 7.4 %collective-permute-start.6 = (bf16[128,512]{1,0:T(8,128)(2,1)S(1)}, bf16[128,512]{1,0:T(8,128)(2,1)S(1)}, u32[]{:S(2)}, u32[]{:S(2)}) collective-permute-start(bf16[128,512]{1,0:T(8,128)(2,1)S(1)} %maximum_maximum_fusion.own_ref), channel_id=1, source_target_pairs={{0,16},{8,24},{16,28},{24,20},{28,12},{20,4},{1,17},{9,25},{17,29}... | collective-permute-start | bytes 393224 | tf_op jit(solution)/shard_map/ppermute | solution.py:224
  7.5 1.1 %copy-start.1 = (bf16[1,2,64,2048]{3,2,1,0:T(8,128)(2,1)S(1)}, bf16[1,2,64,2048]{3,2,1,0:T(8,128)(2,1)}, u32[]{:S(2)}) copy-start(bf16[1,2,64,2048]{3,2,1,0:T(8,128)(2,1)} %param.9) | copy-start | bytes 1572868
  7.5 1.2 %copy-start.2 = (bf16[1,2,64,2048]{3,2,1,0:T(8,128)(2,1)S(1)}, bf16[1,2,64,2048]{3,2,1,0:T(8,128)(2,1)}, u32[]{:S(2)}) copy-start(bf16[1,2,64,2048]{3,2,1,0:T(8,128)(2,1)} %param.10) | copy-start | bytes 1572868
  15.9 10.4 %collective-permute-start.9 = (bf16[128,512]{1,0:T(8,128)(2,1)S(1)}, bf16[128,512]{1,0:T(8,128)(2,1)S(1)}, u32[]{:S(2)}, u32[]{:S(2)}) collective-permute-start(bf16[128,512]{1,0:T(8,128)(2,1)S(1)} %get-tuple-element.57), channel_id=1, source_target_pairs={{8,0},{16,8},{24,16},{28,24},{20,28},{12,20},{4,12},{9,1},{17,9},{... | collective-permute-start | bytes 393224 | tf_op jit(solution)/shard_map/ppermute | solution.py:224
  18.7 8.1 %collective-permute-start.10 = (bf16[128,512]{1,0:T(8,128)(2,1)S(1)}, bf16[128,512]{1,0:T(8,128)(2,1)S(1)}, u32[]{:S(2)}, u32[]{:S(2)}) collective-permute-start(bf16[128,512]{1,0:T(8,128)(2,1)S(1)} %get-tuple-element.58), channel_id=1, source_target_pairs={{16,0},{24,8},{28,16},{20,24},{12,28},{4,20},{17,1},{25,9},{29,17}... | collective-permute-start | bytes 393224 | tf_op jit(solution)/shard_map/ppermute | solution.py:224
  26.2 3.5 %collective-permute-start.8 = (bf16[64,2048]{1,0:T(8,128)(2,1)S(1)}, bf16[64,2048]{1,0:T(8,128)(2,1)S(1)}, u32[]{:S(2)}, u32[]{:S(2)}) collective-permute-start(bf16[64,2048]{1,0:T(8,128)(2,1)S(1)} %get-tuple-element.55), channel_id=1, source_target_pairs={{0,4},{4,0},{8,12},{12,8},{16,20},{20,16},{24,28},{28,24},{1,5},{5... | collective-permute-start | bytes 786440 | tf_op jit(solution)/shard_map/ppermute | solution.py:231
  27.0 2.7 %collective-permute-start.11 = (bf16[64,512]{1,0:T(8,128)(2,1)S(1)}, bf16[64,512]{1,0:T(8,128)(2,1)S(1)}, u32[]{:S(2)}, u32[]{:S(2)}) collective-permute-start(bf16[64,512]{1,0:T(8,128)(2,1)S(1)} %get-tuple-element.63), channel_id=1, source_target_pairs={{0,4},{4,0},{8,12},{12,8},{16,20},{20,16},{24,28},{28,24},{1,5},{5... | collective-permute-start | bytes 196616 | tf_op jit(solution)/shard_map/ppermute | solution.py:231
